TPU v7x, 32 devices: a whole 2x2x4 slice. The times are simulated.
32 devices in a mesh: dp: 8 (over z, x), mp: 4 (over y, core).
Axes of the slice: x: 2, y: 2, z: 4, core: 2. Of those that a mesh axis runs over, the one named last changes fastest.
Arguments:
- inputs: bfloat16 [16, 512, 512], P('dp'), may hold values from -6 to 6
- memory: bfloat16 [16, 512, 512], P(None, 'dp'), may hold values from -6 to 6
- segment_ids: int32 [16, 512], P('dp'), may hold values from 0 to 7, never falling along the last dimension, each value on 1 to 128 neighbouring positions
- mem_lengths: int32 [16, 8], P('dp'), may hold values from 1 to 128, 512 in all within a row
- bucket_group: int32 [8], replicated, may hold values from 0 to 5
- group_tokens: int32 [6], replicated, may hold values from 64 to 1023
- norm_gain: bfloat16 [3, 512], replicated, may hold values from 0.5 to 1.5
- norm_bias: bfloat16 [3, 512], replicated, may hold values from -3 to 3
- self_qkv: bfloat16 [3, 512, 512], P(None, None, 'mp'), may hold values from -0.25 to 0.25
- self_bias: bfloat16 [2, 512], P(None, 'mp'), may hold values from -3 to 3
- self_out: bfloat16 [512, 512], P('mp'), may hold values from -0.75 to 0.75
- cross_q: bfloat16 [512, 512], P(None, 'mp'), may hold values from -0.25 to 0.25
- cross_kv: bfloat16 [2, 512, 512], P(None, None, 'mp'), may hold values from -0.25 to 0.25
- cross_bias: bfloat16 [2, 512], P(None, 'mp'), may hold values from -3 to 3
- cross_out: bfloat16 [512, 512], P('mp'), may hold values from -0.75 to 0.75
- ffn_in: bfloat16 [512, 2048], P(None, 'mp'), may hold values from -0.25 to 0.25
- ffn_bias: bfloat16 [2048], P('mp'), may hold values from -3 to 3
- ffn_out: bfloat16 [2048, 512], P('mp'), may hold values from -0.125 to 0.125
- out_bias: bfloat16 [3, 512], replicated, may hold values from -3 to 3
- cotangent: bfloat16 [16, 512, 512], P('dp'), may hold values from -6 to 6
Outputs:
- mixed: bfloat16 [16, 512, 512], P('dp')
- grad_inputs: float32 [16, 512, 512], P('dp')
- grad_memory: float32 [16, 512, 512], P(None, 'dp', 'mp')
- grad_norm_gain: float32 [3, 512], replicated
- grad_norm_bias: float32 [3, 512], replicated
- grad_self_qkv: float32 [3, 512, 512], P(None, None, 'mp')
- grad_self_bias: float32 [2, 512], P(None, 'mp')
- grad_self_out: float32 [512, 512], P('mp')
- grad_cross_q: float32 [512, 512], P(None, 'mp')
- grad_cross_kv: float32 [2, 512, 512], P(None, None, 'mp')
- grad_cross_bias: float32 [2, 512], P(None, 'mp')
- grad_cross_out: float32 [512, 512], P('mp')
- grad_ffn_in: float32 [512, 2048], P(None, 'mp')
- grad_ffn_bias: float32 [2048], P('mp')
- grad_ffn_out: float32 [2048, 512], P('mp')
- grad_out_bias: float32 [3, 512], replicated
Inputs may be any that keep to these rules, and one draw needn't show every extreme that they name: `segment_ids`: each row holds 8 target molecules, numbered 0 to 7 in order, each of 1 to 128 tokens, one of exactly 128. `mem_lengths`: the token counts of a row's 8 source molecules in its memory, in order, summing to 512; target molecule k reads source molecule k; the longest is exactly 128.
All inputs are finite; a program needn't handle non-finite values.
Results may differ from a plain program's by a relative error of at most 0.02.
Values may be sent and summed in bfloat16 or wider, within the bound.
No kernel may reach another device: no remote copies, remote signals or barrier semaphores. Data moves between devices by JAX's collectives and lax.ppermute only.
A program may use at most 64 MiB of HBM per device.

v0:
```python
import functools

import jax
import jax.numpy as jnp
from jax import lax
from jax.experimental import pallas as pl
from jax.experimental.pallas import tpu as pltpu
from jax.sharding import PartitionSpec as P

HDIM = 64
LANES = 128
BLOCK = 128
SMALL = 16
EPSILON = 1e-05
F32 = jnp.float32
BF16 = jnp.bfloat16


def dot(left, right):
    return lax.dot_general(left, right, (((1,), (0,)), ((), ())), preferred_element_type=F32)


def dot_right(left, right):
    return lax.dot_general(left, right, (((1,), (1,)), ((), ())), preferred_element_type=F32)


def dot_left(left, right):
    return lax.dot_general(left, right, (((0,), (0,)), ((), ())), preferred_element_type=F32)


class Far:
    def __init__(self, value, pick=False):
        self.value, self.pick = value, pick


class Scalars:
    def __init__(self, value):
        self.value = value


class Flow:
    def __init__(self):
        self.loads, self.stores, self.sent = {}, {}, []

    def need(self, *refs):
        for ref in refs:
            copy = self.loads.pop(id(ref), None)
            if copy is not None:
                copy.wait()

    def send(self, *refs):
        for ref in refs:
            copy = self.stores.pop(id(ref), None)
            if copy is not None:
                copy.start()
                self.sent.append(copy)


class Steps:
    def __init__(self, where):
        self.where, self.token = where, None

    def __call__(self, kernel, ins, outs, scratch=(), name=None):
        near = pl.BlockSpec(memory_space=pltpu.VMEM)
        far = pl.BlockSpec(memory_space=pltpu.HBM)
        words = pl.BlockSpec(memory_space=pltpu.SMEM)
        values, specs, stages = [], [], []
        for v in ins:
            if isinstance(v, Scalars):
                values.append(v.value)
                specs.append(words)
            elif isinstance(v, Far):
                values.append(pltpu.with_memory_space_constraint(v.value, pltpu.HBM))
                specs.append(far)
                stages.append(pltpu.VMEM(v.value.shape[1:] if v.pick else v.value.shape, v.value.dtype))
            else:
                values.append(pltpu.with_memory_space_constraint(v, pltpu.VMEM))
                specs.append(near)
        after = [] if self.token is None else [pltpu.with_memory_space_constraint(self.token, pltpu.HBM)]
        for v in outs:
            if isinstance(v, Far):
                stages.append(pltpu.VMEM(*v.value))
        shapes = [pltpu.HBM(*v.value) if isinstance(v, Far) else pltpu.VMEM(*v) for v in outs]
        count, n_in, n_out, n_after = len(stages), len(ins), len(outs), len(after)

        def body(where_ref, *refs):
            refs = list(refs)
            in_refs, refs = refs[:n_in], refs[n_in + n_after :]
            out_refs, refs = refs[:n_out], refs[n_out + 1 :]
            stage_refs, refs = refs[:count], refs[count:]
            flow = Flow()
            if count:
                sems, refs = refs[0], refs[1:]
            given, k = [], 0
            for v, ref in zip(ins, in_refs):
                if isinstance(v, Far):
                    source = ref.at[where_ref[0]] if v.pick else ref
                    copy = pltpu.make_async_copy(source, stage_refs[k], sems.at[k])
                    copy.start()
                    flow.loads[id(stage_refs[k])] = copy
                    ref, k = stage_refs[k], k + 1
                given.append(ref)
            for v, ref in zip(outs, out_refs):
                if isinstance(v, Far):
                    flow.stores[id(stage_refs[k])] = pltpu.make_async_copy(stage_refs[k], ref, sems.at[k])
                    ref, k = stage_refs[k], k + 1
                given.append(ref)
            kernel(flow, where_ref, *given, *refs)
            for copy in flow.loads.values():
                copy.wait()
            for copy in flow.stores.values():
                copy.start()
            for copy in [*flow.sent, *flow.stores.values()]:
                copy.wait()

        results = pl.pallas_call(
            body,
            in_specs=[words] + specs + [far] * n_after,
            out_specs=[far if isinstance(v, Far) else near for v in outs] + [far],
            out_shape=shapes + [pltpu.HBM((8, LANES), F32)],
            scratch_shapes=stages + ([pltpu.SemaphoreType.DMA((count,))] if count else []) + list(scratch),
            compiler_params=pltpu.CompilerParams(vmem_limit_bytes=24 * 1024 * 1024),
            cost_estimate=pl.CostEstimate(flops=10**6, bytes_accessed=10**5, transcendentals=0),
            name=name,
        )(self.where, *values, *after)
        self.token = results[-1]
        return list(results[:-1])


def row_blocks(seq):
    return [slice(start, start + BLOCK) for start in range(0, seq, BLOCK)]


def row_of(ref, i):
    return ref[i : i + 1, :].astype(F32)


GAIN, SHIFT, OUT, SCALE, VECTORS = 0, 3, 6, 9, 16


def norm_parts(value):
    centre = value - jnp.mean(value, axis=-1, keepdims=True)
    spread = jnp.mean(centre * centre, axis=-1, keepdims=True)
    scale = lax.rsqrt(spread + EPSILON)
    return centre * scale, scale


def norm_backward(value, gain, incoming):
    xhat, scale = norm_parts(value)
    weighted = incoming * gain
    grad = scale * (
        weighted
        - jnp.mean(weighted, axis=-1, keepdims=True)
        - xhat * jnp.mean(weighted * xhat, axis=-1, keepdims=True)
    )
    return grad, jnp.sum(incoming * xhat, axis=0, keepdims=True), jnp.sum(incoming, axis=0, keepdims=True)


def head_lanes(value, j):
    lane = lax.broadcasted_iota(jnp.int32, value.shape, 1)
    return jnp.where((lane >= HDIM) == bool(j), value, jnp.zeros_like(value))


def span_of(block, seq, banded):
    if not banded:
        return slice(0, seq)
    return slice(max(block.start - BLOCK, 0), block.stop)


def setup_kernel(flow, where, group_tokens, bucket_group, lengths, segments, gains, shifts, biases, vectors, molecules):
    flow.need(segments, gains, shifts, biases)
    width = vectors.shape[1]
    total, own = 0, 0
    for b in range(bucket_group.shape[0]):
        tokens = group_tokens[bucket_group[b]]
        total = total + tokens
        own = own + jnp.where(where[2] == b, tokens, 0)
    scaled = jnp.full((1, width), bucket_group.shape[0] * own, jnp.int32).astype(F32)
    scale = scaled / jnp.full((1, width), total, jnp.int32).astype(F32)
    rows = [r[...].astype(F32) for r in (gains, shifts, biases)] + [scale]
    vectors[...] = jnp.concatenate(rows + [jnp.zeros((VECTORS - 10, width), F32)], axis=0)
    size = molecules.shape[1]
    place = lax.broadcasted_iota(jnp.int32, (1, size), 1)
    count, end = jnp.zeros((1, size), jnp.int32), 0
    for k in range(lengths.shape[1]):
        end = end + lengths[where[0], k]
        count = count + (end <= place).astype(jnp.int32)
    molecules[0:1, :] = segments[pl.ds(where[0], 1), :]
    molecules[1:2, :] = count


def allowed_of(own, keys, block, span, banded):
    column = jnp.broadcast_to(own[:, block], (LANES, BLOCK)).T
    wide = span.stop - span.start
    allowed = jnp.concatenate([column] * (wide // LANES), axis=1) == keys[:, span]
    if banded:
        query = lax.broadcasted_iota(jnp.int32, (BLOCK, wide), 0) + block.start
        key = lax.broadcasted_iota(jnp.int32, (BLOCK, wide), 1) + span.start
        allowed = allowed & (key <= query)
    return allowed


def attend_forward(q, k, v, own, keys, heads, totals, banded):
    seq, wide = q.shape
    for block in row_blocks(seq):
        span = span_of(block, k.shape[0], banded)
        allowed = allowed_of(own, keys, block, span, banded)
        lane = lax.broadcasted_iota(jnp.int32, (BLOCK, LANES), 1)
        kept = jnp.zeros((BLOCK, LANES), F32)
        for pair in range(wide // LANES):
            lanes = slice(pair * LANES, (pair + 1) * LANES)
            query, keyset, values = q[block, lanes] * 0.125, k[span, lanes], v[span, lanes]
            mixed = None
            for j in (0, 1):
                scores = jnp.where(allowed, dot_right(head_lanes(query, j), keyset), -1e30)
                maxima = jnp.max(scores, axis=-1, keepdims=True)
                raised = jnp.exp(scores - maxima)
                total = jnp.sum(raised, axis=-1, keepdims=True)
                chances = (raised * (1.0 / total)).astype(BF16)
                term = dot(chances, head_lanes(values, j))
                mixed = term if mixed is None else mixed + term
                kept = jnp.where(lane == 2 * pair + j, maxima + jnp.log(total), kept)
            heads[block, lanes] = mixed.astype(BF16)
        totals[block, :] = kept


def attend_backward(q, k, v, own, keys, totals, grad_heads, dq, dk, dv, sum_k, sum_v, banded):
    seq, wide = q.shape
    sum_k[...] = jnp.zeros_like(sum_k)
    sum_v[...] = jnp.zeros_like(sum_v)
    for block in row_blocks(seq):
        span = span_of(block, k.shape[0], banded)
        allowed = allowed_of(own, keys, block, span, banded)
        for pair in range(wide // LANES):
            lanes = slice(pair * LANES, (pair + 1) * LANES)
            query, keyset, values = q[block, lanes], k[span, lanes], v[span, lanes]
            grad = grad_heads[block, lanes]
            grad_query = grad_key = grad_value = 0.0
            for j in (0, 1):
                head = 2 * pair + j
                part = head_lanes(query, j) * 0.125
                scores = jnp.where(allowed, dot_right(part, keyset), -1e30)
                chances = jnp.exp(scores - totals[block, head : head + 1])
                own_grad = head_lanes(grad, j)
                grad_value += dot_left(chances.astype(BF16), own_grad)
                weighted = chances * dot_right(own_grad, values)
                mean = jnp.sum(weighted, axis=-1, keepdims=True)
                grad_scores = (weighted - chances * mean).astype(BF16)
                grad_query += dot(grad_scores, head_lanes(keyset, j))
                grad_key += dot_left(grad_scores, part)
            dq[block, lanes] = (grad_query * 0.125).astype(BF16)
            sum_k[span, lanes] += grad_key
            sum_v[span, lanes] += grad_value
    dk[...] = sum_k[...].astype(BF16)
    dv[...] = sum_v[...].astype(BF16)


def self_forward_kernel(n, i, flow, where, *refs):
    last = i == n - 1
    first, vectors, molecules, w, bias, refs = *refs[:5], refs[5:]
    if last:
        w_out, done, refs = refs[:n], refs[n : 2 * n - 1], refs[2 * n - 1 :]
    if i == 0:
        normed, refs = refs[0], refs[1:]
        flow.need(first)
        for block in row_blocks(first.shape[0]):
            norm = norm_parts(first[block, :].astype(F32))[0]
            normed[block, :] = (norm * row_of(vectors, GAIN) + row_of(vectors, SHIFT)).astype(BF16)
    else:
        normed = first
    q, k, v, heads, totals = refs[:5]
    flow.need(w)
    q[...] = (dot(normed[...], w[0]) + row_of(bias, 0)).astype(BF16)
    k[...] = dot(normed[...], w[1]).astype(BF16)
    v[...] = (dot(normed[...], w[2]) + row_of(bias, 1)).astype(BF16)
    own = molecules[0:1, :]
    attend_forward(q, k, v, own, own, heads, totals, True)
    if last:
        project_out(flow, [*done, heads], w_out, refs[5])


def project_out(flow, heads, w_out, part):
    flow.need(*w_out)
    for block in row_blocks(part.shape[0]):
        part[block, :] = sum(dot(h[block, :], w[...]) for h, w in zip(heads, w_out)).astype(BF16)


def memory_kernel(flow, where, memory, w, bias, k, v):
    flow.need(w)
    k[...] = dot(memory[...], w[0]).astype(BF16)
    v[...] = (dot(memory[...], w[1]) + row_of(bias, 3)).astype(BF16)


def cross_forward_kernel(n, i, flow, where, *refs):
    last = i == n - 1
    if i == 0:
        x, mine, theirs, refs = *refs[:3], refs[3:]
    else:
        normed, refs = refs[0], refs[1:]
    vectors, molecules, w, bias, k, v, refs = *refs[:6], refs[6:]
    if last:
        w_out, done, refs = refs[:n], refs[n : 2 * n - 1], refs[2 * n - 1 :]
    if i == 0:
        after_self, normed, refs = refs[0], refs[1], refs[2:]
    q, heads, totals = refs[:3]
    if i == 0:
        flow.need(x)
        for block in row_blocks(x.shape[0]):
            both = mine[block, :].astype(F32) + theirs[block, :].astype(F32)
            value = x[block, :].astype(F32) + both + row_of(vectors, OUT)
            after_self[block, :] = value
            norm = norm_parts(value)[0]
            normed[block, :] = (norm * row_of(vectors, GAIN + 1) + row_of(vectors, SHIFT + 1)).astype(BF16)
    flow.need(w)
    q[...] = (dot(normed[...], w[...]) + row_of(bias, 2)).astype(BF16)
    attend_forward(q, k, v, molecules[0:1, :], molecules[1:2, :], heads, totals, False)
    if last:
        project_out(flow, [*done, heads], w_out, refs[3])


def ffn_kernel(i, flow, where, *refs):
    if i == 0:
        after_self, mine, theirs, cotangent, vectors, w_in, bias, w_out, refs = *refs[:8], refs[8:]
        after_cross, normed, low, active, grad_hidden, part, part_grad = refs
        flow.need(cotangent)
    else:
        normed, low, begun, begun_grad, w_in, bias, w_out, refs = *refs[:7], refs[7:]
        active, grad_hidden, part, part_grad = refs
    flow.need(w_in, w_out)
    if bias.shape[0] == 1:
        row = row_of(bias, 0)
    else:
        row = jnp.concatenate([row_of(bias, k) for k in range(4, bias.shape[0])], axis=1)
    for block in row_blocks(normed.shape[0]):
        if i == 0:
            both = mine[block, :].astype(F32) + theirs[block, :].astype(F32)
            value = after_self[block, :] + both + row_of(vectors, OUT + 1)
            after_cross[block, :] = value
            norm = norm_parts(value)[0]
            norm = (norm * row_of(vectors, GAIN + 2) + row_of(vectors, SHIFT + 2)).astype(BF16)
            normed[block, :] = norm
            grad = (cotangent[block, :].astype(F32) * row_of(vectors, SCALE)).astype(BF16)
            low[block, :] = grad
        else:
            norm, grad = normed[block, :], low[block, :]
        hidden = dot(norm, w_in[...]) + row
        cdf = 0.5 * (1.0 + lax.erf(hidden * 0.7071067811865476))
        act = (hidden * cdf).astype(BF16)
        active[block, :] = act
        slope = cdf + hidden * (0.3989422804014327 * jnp.exp(-0.5 * hidden * hidden))
        back = (slope * dot_right(grad, w_out[...])).astype(BF16)
        grad_hidden[block, :] = back
        out, out_grad = dot(act, w_out[...]), dot_right(back, w_in[...])
        if i == 0:
            part[block, :], part_grad[block, :] = out, out_grad
        else:
            part[block, :] = (begun[block, :] + out).astype(BF16)
            part_grad[block, :] = (begun_grad[block, :] + out_grad).astype(BF16)


def ffn_weights_kernel(flow, where, *refs):
    hidden, active, normed, low, sums = refs[:2], refs[2:4], refs[4], refs[5], refs[6]
    keep_out, send_out, keep_in, send_in = refs[7:]
    half = keep_in.shape[1]
    for i in (0, 1):
        for target, bit in ((keep_in, where[3]), (send_in, 1 - where[3])):
            lanes = pl.ds(pl.multiple_of(bit * half, half), half)
            target[i] = dot_left(hidden[i][:, lanes], normed[...]).astype(target.dtype)
        sums[i : i + 1, :] = jnp.sum(hidden[i][...].astype(F32), axis=0, keepdims=True)
    keep_out[0] = dot_left(active[0][...], low[...])
    send_out[0] = dot_left(active[1][...], low[...]).astype(BF16)


def spread_grad_heads(low, w_out, grad_heads):
    for piece, target in zip(w_out, grad_heads):
        target[...] = dot_right(low[...], piece[...]).astype(BF16)


def column_sums(sums, values):
    for i, value in enumerate(values):
        sums[i : i + 1, :] = jnp.sum(value[...].astype(F32), axis=0, keepdims=True)


def cross_backward_kernel(n, flow, where, *refs):
    after_cross, mine, theirs, cotangent, vectors, molecules, refs = *refs[:6], refs[6:]
    (q, k, v, totals, w_out, w), refs = [refs[i * n : (i + 1) * n] for i in range(6)], refs[6 * n :]
    grad_cross, low, refs = refs[0], refs[1], refs[2:]
    (dq, dk, dv, bias_sums), refs = [refs[i * n : (i + 1) * n] for i in range(4)], refs[4 * n :]
    part, sums, refs = refs[0], refs[1], refs[2:]
    grad_heads, sum_k, sum_v = refs[:n], refs[n], refs[n + 1]
    seq, width = after_cross.shape
    rows = [jnp.zeros((1, width), F32)] * 3
    flow.need(cotangent)
    for block in row_blocks(seq):
        incoming = mine[block, :].astype(F32) + theirs[block, :].astype(F32)
        grad_result = cotangent[block, :].astype(F32) * row_of(vectors, SCALE)
        back, by_gain, by_shift = norm_backward(after_cross[block, :], row_of(vectors, GAIN + 2), incoming)
        value = grad_result + back
        grad_cross[block, :] = value
        low[block, :] = value.astype(BF16)
        parts = (by_gain, by_shift, jnp.sum(grad_result, axis=0, keepdims=True))
        rows = [a + b for a, b in zip(rows, parts)]
    for i, row in enumerate(rows):
        sums[i : i + 1, :] = row
    flow.need(*w_out)
    spread_grad_heads(low, w_out, grad_heads)
    own, keys = molecules[0:1, :], molecules[1:2, :]
    for i in range(n):
        attend_backward(
            q[i], k[i], v[i], own, keys, totals[i], grad_heads[i], dq[i], dk[i], dv[i], sum_k, sum_v, False
        )
        column_sums(bias_sums[i], (dq[i], dv[i]))
    flow.need(*w)
    for block in row_blocks(seq):
        part[block, :] = sum(dot_right(d[block, :], m[...]) for d, m in zip(dq, w)).astype(BF16)


def shard_grads(kinds):
    grads = ([], [])
    for kind in kinds:
        if len(kind) == 2:
            for i in (0, 1):
                grads[i].append(dot_left(kind[i][0][...], kind[i][1][...]))
        else:
            left, right = kind[0]
            both, half = dot_left(left[...], right[...]), left.shape[1] // 2
            grads[0].append(both[:half])
            grads[1].append(both[half:])
    return grads


def cross_weights_kernel(n, flow, where, *refs):
    (dq, dk, dv, heads, w), refs = [refs[i * n : (i + 1) * n] for i in range(5)], refs[5 * n :]
    normed, memory, low, after_cross, mine, theirs, vectors, refs = *refs[:7], refs[7:]
    keep, send, terms, result, result_part = refs
    flow.need(*w)
    pairs = [[(a, b) for a in left] for left, b in ((dq, normed), (dk, memory), (dv, memory), (heads, low))]
    first = where[4] == 0
    for i, grads in enumerate(shard_grads(pairs)):
        upper, lower = jnp.concatenate(grads[:2], axis=0), jnp.concatenate(grads[2:], axis=0)
        keep[i] = jnp.where(first, upper, lower)
        send[i] = jnp.where(first, lower, upper).astype(BF16)
    for block in row_blocks(memory.shape[0]):
        total = sum(
            dot_right(a[block, :], m[0]) + dot_right(b[block, :], m[1]) for a, b, m in zip(dk, dv, w)
        )
        terms[block, :] = total.astype(BF16)
    for block in row_blocks(after_cross.shape[0]):
        both = mine[block, :].astype(F32) + theirs[block, :].astype(F32)
        result[block, :] = (after_cross[block, :] + both + row_of(vectors, OUT + 2)).astype(BF16)
    size = result_part.shape[0]
    result_part[...] = result[pl.ds(pl.multiple_of(where[1] * size, size), size), :]


def self_backward_kernel(n, flow, where, *refs):
    after_self, mine, theirs, grad_cross, vectors, molecules, refs = *refs[:6], refs[6:]
    (q, k, v, totals, w_out, w), refs = [refs[i * n : (i + 1) * n] for i in range(6)], refs[6 * n :]
    grad_self, low, refs = refs[0], refs[1], refs[2:]
    (dq, dk, dv, bias_sums), refs = [refs[i * n : (i + 1) * n] for i in range(4)], refs[4 * n :]
    part, sums, refs = refs[0], refs[1], refs[2:]
    grad_heads, sum_k, sum_v = refs[:n], refs[n], refs[n + 1]
    seq, width = after_self.shape
    rows = [jnp.zeros((1, width), F32)] * 3
    for block in row_blocks(seq):
        incoming = mine[block, :].astype(F32) + theirs[block, :].astype(F32)
        back, by_gain, by_shift = norm_backward(after_self[block, :], row_of(vectors, GAIN + 1), incoming)
        upper = grad_cross[block, :]
        value = upper + back
        grad_self[block, :] = value
        low[block, :] = value.astype(BF16)
        parts = (by_gain, by_shift, jnp.sum(upper, axis=0, keepdims=True))
        rows = [a + b for a, b in zip(rows, parts)]
    for i, row in enumerate(rows):
        sums[i : i + 1, :] = row
    flow.need(*w_out)
    spread_grad_heads(low, w_out, grad_heads)
    own = molecules[0:1, :]
    for i in range(n):
        attend_backward(
            q[i], k[i], v[i], own, own, totals[i], grad_heads[i], dq[i], dk[i], dv[i], sum_k, sum_v, True
        )
        column_sums(bias_sums[i], (dq[i], dv[i]))
    flow.need(*w)
    for block in row_blocks(seq):
        total = 0.0
        for i in range(n):
            for which, d in enumerate((dq[i], dk[i], dv[i])):
                total += dot_right(d[block, :], w[i][which])
        part[block, :] = total.astype(BF16)


def input_backward_kernel(flow, where, x, mine, theirs, grad_self, vectors, grad_inputs, inputs_part, sums):
    rows = [jnp.zeros((1, x.shape[1]), F32)] * 3
    flow.need(x)
    for block in row_blocks(x.shape[0]):
        incoming = mine[block, :].astype(F32) + theirs[block, :].astype(F32)
        back, by_gain, by_shift = norm_backward(x[block, :].astype(F32), row_of(vectors, GAIN), incoming)
        upper = grad_self[block, :]
        grad_inputs[block, :] = (upper + back).astype(BF16)
        parts = (by_gain, by_shift, jnp.sum(upper, axis=0, keepdims=True))
        rows = [a + b for a, b in zip(rows, parts)]
    for i, row in enumerate(rows):
        sums[i : i + 1, :] = row
    size = inputs_part.shape[0]
    inputs_part[...] = grad_inputs[pl.ds(pl.multiple_of(where[1] * size, size), size), :]


def self_weights_kernel(n, flow, where, *refs):
    (dq, dk, dv, heads), refs = [refs[i * n : (i + 1) * n] for i in range(4)], refs[4 * n :]
    normed, low, by_self, by_cross, by_ffn, refs = *refs[:5], refs[5:]
    shard_rows, (keep, send) = refs[:-2], refs[-2:]
    width = normed.shape[1]
    common = [r[k : k + 1, :] for k in range(3) for r in (by_self, by_cross, by_ffn)]
    if len(shard_rows) == 1:
        lines = [shard_rows[0][i] for i in (0, 1)]
    else:
        sums_self, sums_cross, sums_ffn = shard_rows[:n], shard_rows[n : 2 * n], shard_rows[2 * n]
        lines = []
        for i in (0, 1):
            pieces = [r[k : k + 1, :] for r in (sums_self[i], sums_cross[i]) for k in (0, 1)]
            lines.append(jnp.concatenate([jnp.concatenate(pieces, axis=1), sums_ffn[i : i + 1, :]], axis=0))
    rest = jnp.zeros((SMALL - 9 - lines[0].shape[0], width), F32)
    pairs = [[(a, b) for a in left] for left, b in ((dq, normed), (dk, normed), (dv, normed), (heads, low))]
    for target, grads, line in zip((keep, send), shard_grads(pairs), lines):
        small = jnp.concatenate([*common, line, rest], axis=0).astype(BF16).astype(F32)
        target[0] = jnp.concatenate([*grads, small], axis=0).astype(target.dtype)


def fold_kernel(count, small, mode, bit, flow, where, *refs):
    keeps, gots, outs = refs[:count], refs[count : 2 * count], refs[2 * count :]

    def part(k, p, rows):
        return keeps[k][p, rows, :].astype(F32) + gots[k][p, rows, :].astype(F32)

    planes = [(k, p) for k in range(count) for p in range(keeps[k].shape[0])]
    size = keeps[0].shape[1]
    main = size - small
    if mode == "half":
        keep, send = outs
        half = main // 2
        for at, (k, p) in enumerate(planes):
            for target, side in ((keep, where[3 + bit]), (send, 1 - where[3 + bit])):
                rows = pl.ds(pl.multiple_of(side * half, half), half)
                value = part(k, p, rows)
                if small:
                    tail = part(k, p, slice(main, size)).astype(BF16).astype(F32)
                    value = jnp.concatenate([value, tail], axis=0)
                target[at] = value.astype(target.dtype)
    elif mode == "shard":
        keep, send = outs
        for target, (k, p) in zip((keep, send), planes):
            target[0] = part(k, p, slice(0, size)).astype(target.dtype)
    else:
        for at, (k, p) in enumerate(planes):
            outs[0][at] = part(k, p, slice(0, main if mode == "last" else size)).astype(outs[0].dtype)
        if mode == "last" and small:
            outs[1][...] = part(*planes[0], slice(main, size))


def join_kernel(bit, flow, where, near, got, out):
    half = near.shape[1]
    for value, side in ((near, where[3 + bit]), (got, 1 - where[3 + bit])):
        rows = pl.ds(pl.multiple_of(side * half, half), half)
        for p in range(near.shape[0]):
            out[p, rows, :] = value[p]


def joined(where, bit, near, got, p):
    first = where[3 + bit] == 0
    a, b = near[p], got[p]
    rows = [jnp.where(first, a, b), jnp.where(first, b, a)]
    return jnp.concatenate(rows, axis=0).astype(F32)


def self_grads_kernel(bit, flow, where, near, got, qkv, out):
    value = joined(where, bit, near, got, 0)
    size = out.shape[0]
    for k in range(3):
        qkv[k] = value[k * size : (k + 1) * size].T
    out[...] = value[3 * size :]


def cross_grads_kernel(bit, flow, where, near, got, query, kv, out):
    value = joined(where, bit, near, got, 0)
    size = out.shape[0]
    query[...] = value[:size].T
    for k in (0, 1):
        kv[k] = value[(k + 1) * size : (k + 2) * size].T
    out[...] = value[3 * size :]


def ffn_grads_kernel(bit, flow, where, near, got, grad_in, grad_out):
    grad_out[...] = joined(where, bit, near, got, 0)
    flow.send(grad_out)
    grad_in[...] = joined(where, bit, near, got, 1).T


def place_rows_kernel(flow, where, own, near, got, out):
    kind = out.dtype
    out[where[0]] = own[...].astype(kind)
    size = near.shape[0]
    mine, theirs = near[...].astype(kind), got[...].astype(kind)
    first = where[1] == 0
    out[1 - where[0], :size, :] = jnp.where(first, mine, theirs)
    out[1 - where[0], size:, :] = jnp.where(first, theirs, mine)


def memory_blocks_kernel(flow, where, mine, theirs, out):
    dp, rows, tokens, share = out.shape
    team = mine.shape[1] // (rows * share)
    for r in range(rows):
        lanes = pl.ds(pl.multiple_of((r * team + where[1]) * share, share), share)
        total = (mine[:, lanes].astype(F32) + theirs[:, lanes].astype(F32)).astype(BF16)
        for d in range(dp):
            out[d, r] = total[d * tokens : (d + 1) * tokens]


def pack_ffn_kernel(flow, where, w_in, w_out, half_in, half_out):
    flow.need(w_in, w_out)
    for source, target in ((w_in, half_in), (w_out, half_out)):
        half = target.shape[0]
        target[...] = source[pl.ds(pl.multiple_of(where[3] * half, half), half), :]


def join_weights_kernel(flow, where, *refs):
    count = len(refs) // 3
    for near, got, out in zip(refs[:count], refs[count : 2 * count], refs[2 * count :]):
        half = near.shape[0]
        for value, bit in ((near, where[3]), (got, 1 - where[3])):
            out[pl.ds(pl.multiple_of(bit * half, half), half), :] = value[...]


def shards(
    inputs,
    memory,
    segment_ids,
    mem_lengths,
    bucket_group,
    group_tokens,
    norm_gain,
    norm_bias,
    self_qkv,
    self_bias,
    self_out,
    cross_q,
    cross_kv,
    cross_bias,
    cross_out,
    ffn_in,
    ffn_bias,
    ffn_out,
    out_bias,
    cotangent,
):
    dp, mp = lax.axis_size("dp"), lax.axis_size("mp")
    rows, seq, width = inputs.shape
    team = mp // rows
    data, place = lax.axis_index("dp"), lax.axis_index("mp")
    row, seat = place // team, place % team
    bits = dp.bit_length() - 1
    where = jnp.stack([row, seat, data] + [(data >> k) & 1 for k in range(bits)]).astype(jnp.int32)
    run, far = Steps(where), Far

    across = [(i, (i + team) % mp) for i in range(mp)]

    def other(value):
        return lax.ppermute(value, "mp", across)

    def seat_swap(value, step):
        return lax.ppermute(value, "mp", [(i, i ^ step) for i in range(mp)])

    def data_swap(value, k):
        return lax.ppermute(value, "dp", [(i, i ^ (1 << k)) for i in range(dp)])

    def swap(value, axis):
        return other(value) if axis == "row" else data_swap(value, axis)

    def later(value, *after):
        return lax.optimization_barrier((value, *after))[0]

    def team_parts(value):
        step = 1
        while 2 * step < team:
            value = (value.astype(F32) + seat_swap(value, step).astype(F32)).astype(BF16)
            step *= 2
        return value, seat_swap(value, step)

    def team_gather(value):
        step = 1
        while 2 * step < team:
            got = seat_swap(value, step)
            low = (seat // step) % 2 == 0
            value = jnp.where(low, jnp.concatenate([value, got]), jnp.concatenate([got, value]))
            step *= 2
        return value, seat_swap(value, step)

    head, unit = self_bias.shape[1], ffn_bias.shape[0]
    mem_len = memory.shape[1] * dp
    apart = head % LANES == 0
    n = 2 if apart else 1
    wide = head if apart else 2 * head

    other_qkv = other(self_qkv)
    memory_part = lax.dynamic_index_in_dim(memory.reshape((dp, rows) + memory.shape[1:]), row, 1, keepdims=False)
    memory_row = lax.all_to_all(memory_part, "dp", split_axis=0, concat_axis=0, tiled=True).reshape(mem_len, width)
    other_self_out = other(self_out)
    bias_own = jnp.concatenate([self_bias, cross_bias, ffn_bias.reshape(-1, head)])
    bias_other = other(bias_own)
    other_cross_q = other(later(cross_q, other_qkv))
    other_cross_kv = other(later(cross_kv, other_qkv))
    other_cross_out = other(later(cross_out, other_qkv))

    def pieces(own, theirs, axis):
        return [far(own), theirs] if apart else [jnp.concatenate([own, theirs], axis=axis)]

    w_qkv = pieces(self_qkv, other_qkv, 2)
    w_self_out = pieces(self_out, other_self_out, 0)
    w_cross_q = pieces(cross_q, other_cross_q, 1)
    w_cross_kv = pieces(cross_kv, other_cross_kv, 2)
    w_cross_out = pieces(cross_out, other_cross_out, 0)
    b_heads = [bias_own, bias_other] if apart else [jnp.concatenate([bias_own, bias_other], axis=1)]
    b_in = b_heads if apart else [b[4:].reshape(1, unit) for b in (bias_own, bias_other)]

    whole, full = ((seq, width), BF16), ((seq, width), F32)
    local, totals = ((seq, wide), BF16), ((seq, LANES), F32)
    units = ((seq, unit), BF16)

    vectors, molecules = run(
        setup_kernel,
        [Scalars(group_tokens), Scalars(bucket_group), Scalars(mem_lengths)]
        + [far(segment_ids), far(norm_gain), far(norm_bias), far(out_bias)],
        [((VECTORS, width), F32), ((2, seq), jnp.int32)],
        name="setup",
    )

    heads_self, saved_self, part = [], [], None
    for i in range(n):
        last = i == n - 1
        ins = [far(inputs, True) if i == 0 else normed_self, vectors, molecules, w_qkv[i], b_heads[i]]
        outs = ([whole] if i == 0 else []) + [local] * 4 + [totals]
        if last:
            ins += [*w_self_out, *heads_self]
            outs += [whole]
        got = run(functools.partial(self_forward_kernel, n, i), ins, outs, name=f"self_forward_{i}")
        if i == 0:
            normed_self, got = got[0], got[1:]
        saved_self.append((got[0], got[1], got[2], got[4]))
        heads_self.append(got[3])
    mine, theirs = team_parts(got[5])

    heads_cross, saved_cross = [], []
    for i in range(n):
        last = i == n - 1
        kv = run(memory_kernel, [memory_row, w_cross_kv[i], b_heads[i]], [((mem_len, wide), BF16)] * 2, name=f"memory_{i}")
        if i == 0:
            half_in, half_out = run(
                pack_ffn_kernel,
                [far(ffn_in), far(ffn_out)],
                [((width // 2, unit), BF16), ((unit // 2, width), BF16)],
                name="pack_ffn",
            )
        first = [far(inputs, True), mine, theirs] if i == 0 else [normed_cross]
        ins = first + [vectors, molecules, w_cross_q[i], b_heads[i], *kv]
        outs = ([full, whole] if i == 0 else []) + [local] * 2 + [totals]
        if last:
            ins += [*w_cross_out, *heads_cross]
            outs += [whole]
        got = run(functools.partial(cross_forward_kernel, n, i), ins, outs, name=f"cross_forward_{i}")
        if i == 0:
            after_self, normed_cross, got = got[0], got[1], got[2:]
            near_in = other(later(half_in, other_cross_kv))
            near_out = other(later(half_out, other_cross_kv))
        saved_cross.append((got[0], *kv, got[2]))
        heads_cross.append(got[1])
    mine, theirs = team_parts(got[3])

    far_in, far_out = data_swap(near_in, 0), data_swap(near_out, 0)
    after_cross, normed_ffn, low_ffn, act_own, hid_own, part, part_grad = run(
        functools.partial(ffn_kernel, 0),
        [after_self, mine, theirs, far(cotangent, True), vectors, far(ffn_in), b_in[0], far(ffn_out)],
        [full, whole, whole, units, units, full, full],
        name="ffn_0",
    )
    other_in, other_out = run(
        join_weights_kernel,
        [near_in, near_out, far_in, far_out],
        [(ffn_in.shape, BF16), (ffn_out.shape, BF16)],
        name="join_ffn",
    )
    act_other, hid_other, part, part_grad = run(
        functools.partial(ffn_kernel, 1),
        [normed_ffn, low_ffn, part, part_grad, other_in, b_in[1], other_out],
        [units, units, whole, whole],
        name="ffn_1",
    )
    mine, theirs = team_parts(part_grad)
    out_mine, out_theirs = team_parts(part)

    class Reduction:
        def __init__(self, name, keeps, sends, axes, small=0):
            self.name, self.keeps, self.small = name, keeps, small
            self.axes = axes
            self.gots = [swap(s, a) for s, a in zip(sends, axes[0])]
            self.halved = [b for b in axes[0] if b != "row"][:1]
            self.chunk = None

        def fold(self):
            axes, small, keeps = self.axes, self.small, self.keeps
            planes = sum(k.shape[0] for k in keeps)
            size = keeps[0].shape[1]
            bit = 0
            if len(axes) == 1:
                mode, outs = "last", [((planes, size - small, width), BF16)]
                if small:
                    outs.append(((small, width), F32))
            elif len(keeps) > 1 and len(axes[1]) > 1:
                mode = None
            elif axes[1][0] == "row":
                mode, shape = "shard", (1, size, width)
                outs = [(shape, F32), (shape, BF16)]
            elif len(axes) == 2:
                mode, outs = "full", [((planes, size, width), BF16)]
            else:
                mode, bit, shape = "half", axes[1][0], (planes, (size - small) // 2 + small, width)
                outs = [(shape, F32), (shape, BF16)]
                self.halved.append(bit)
            got = run(
                functools.partial(fold_kernel, len(keeps), small, mode, bit),
                [*keeps, *self.gots],
                outs,
                name=f"{self.name}_{mode}_{len(axes)}",
            )
            self.axes = axes[1:]
            if mode == "last":
                self.chunk = got[0]
                self.rest = got[1] if small else None
                self.keeps = None
                self.got = swap(self.chunk, self.halved[-1])
            else:
                self.keeps = [got[0]]
                self.gots = [swap(got[-1], axes[1][0])]

        def join(self):
            bit = self.halved.pop()
            planes, size, _ = self.chunk.shape
            (self.chunk,) = run(
                functools.partial(join_kernel, bit),
                [self.chunk, self.got],
                [((planes, 2 * size, width), BF16)],
                name=f"{self.name}_join_{bit}",
            )
            self.got = swap(self.chunk, self.halved[-1])

        def ready(self):
            return self.chunk is not None and len(self.halved) == 1

        def step(self):
            if self.chunk is None:
                self.fold()
            elif not self.ready():
                self.join()

    ffn_sums, keep_out, send_out, keep_in, send_in = run(
        ffn_weights_kernel,
        [hid_own, hid_other, act_own, act_other, normed_ffn, low_ffn],
        [((2, unit), F32), ((1, unit, width), F32), ((1, unit, width), BF16)]
        + [((2, unit // 2, width), F32), ((2, unit // 2, width), BF16)],
        name="ffn_weights",
    )
    by_out = Reduction("ffn_out", [keep_out], [send_out], [["row"], [0], [1]])
    by_in = Reduction("ffn_in", [keep_in], [send_in], [[0], ["row"], [1]])

    scratch = [pltpu.VMEM((seq, wide), BF16)] * n + [pltpu.VMEM((seq, wide), F32)] * 2
    bias_sum = ((2, wide), F32)

    def saved_of(saved):
        return [s[k] for k in range(4) for s in saved]

    got = run(
        functools.partial(cross_backward_kernel, n),
        [after_cross, mine, theirs, far(cotangent, True), vectors, molecules]
        + saved_of(saved_cross) + [*w_cross_out, *w_cross_q],
        [full, whole] + [local] * (3 * n) + [bias_sum] * n + [whole, ((3, width), F32)],
        scratch=scratch,
        name="cross_backward",
    )
    grad_cross, low_cross, got = got[0], got[1], got[2:]
    cross_grads, cross_bias_sums, got = got[: 3 * n], got[3 * n : 4 * n], got[4 * n :]
    part, small_ffn = got
    mine, theirs = team_parts(part)
    part_rows = seq // team
    keep, send, memory_terms, result, result_part = run(
        functools.partial(cross_weights_kernel, n),
        [*cross_grads, *heads_cross, *w_cross_kv]
        + [normed_cross, memory_row, low_cross, after_cross, out_mine, out_theirs, vectors],
        [((2, 2 * head, width), F32), ((2, 2 * head, width), BF16), whole, whole, ((part_rows, width), BF16)],
        name="cross_weights",
    )
    by_cross = Reduction("cross", [keep], [send], [[1], [0], ["row"]] + [[k] for k in range(2, bits)])
    by_out.fold()
    by_in.fold()

    got = run(
        functools.partial(self_backward_kernel, n),
        [after_self, mine, theirs, grad_cross, vectors, molecules] + saved_of(saved_self) + [*w_self_out, *w_qkv],
        [full, whole] + [local] * (3 * n) + [bias_sum] * n + [whole, ((3, width), F32)],
        scratch=scratch,
        name="self_backward",
    )
    grad_self, low_self, got = got[0], got[1], got[2:]
    self_grads, self_bias_sums, got = got[: 3 * n], got[3 * n : 4 * n], got[4 * n :]
    part, small_cross = got
    mine, theirs = team_parts(part)
    by_ffn = by_out
    by_ffn.name, by_ffn.keeps, by_ffn.gots = "ffn", by_out.keeps + by_in.keeps, by_out.gots + by_in.gots
    by_ffn.axes = [[0]] + [[k] for k in range(1, bits)]
    by_ffn.fold()
    grad_row, grad_part, small_self = run(
        input_backward_kernel,
        [far(inputs, True), mine, theirs, grad_self, vectors],
        [whole, ((part_rows, width), BF16), ((3, width), F32)],
        name="input_backward",
    )
    if apart and 4 * head == width and unit == width:
        shard_rows = [*self_bias_sums, *cross_bias_sums, ffn_sums]
        lines = 2
    else:
        def by_shard(sums):
            return sums if n == 2 else [sums[0][:, :head], sums[0][:, head:]]

        shard_rows = [
            jnp.stack(
                [
                    jnp.concatenate([a.reshape(-1), b.reshape(-1), ffn_sums[i]]).reshape(-1, width)
                    for i, (a, b) in enumerate(zip(by_shard(self_bias_sums), by_shard(cross_bias_sums)))
                ]
            )
        ]
        lines = shard_rows[0].shape[1]
    size = 4 * head + SMALL
    keep, send = run(
        functools.partial(self_weights_kernel, n),
        [*self_grads, *heads_self, normed_self, low_self, small_self, small_cross, small_ffn, *shard_rows],
        [((1, size, width), F32), ((1, size, width), BF16)],
        name="self_weights",
    )
    by_self = Reduction("self", [keep], [send], [["row"]] + [[k] for k in range(bits)], SMALL)

    by_cross.fold()
    by_ffn.fold()
    by_cross.fold()
    by_self.fold()
    groups = [by_ffn, by_cross, by_self]
    while not all(g.ready() for g in groups):
        for g in groups:
            g.step()

    grad_ffn_out, grad_ffn_in = ffn_result = [None, None]
    grad_ffn_in, grad_ffn_out = run(
        functools.partial(ffn_grads_kernel, by_ffn.halved[0]),
        [by_ffn.chunk, by_ffn.got],
        [far(((width, unit), F32)), far(((unit, width), F32))],
        name="ffn_grads",
    )
    grad_cross_q, grad_cross_kv, grad_cross_out = run(
        functools.partial(cross_grads_kernel, by_cross.halved[0]),
        [by_cross.chunk, by_cross.got],
        [far(((width, head), F32)), far(((2, width, head), F32)), far(((head, width), F32))],
        name="cross_grads",
    )

    mem_mine, mem_theirs = team_parts(memory_terms)
    share = width // mp
    if share % LANES == 0 and team == 2:
        (blocks,) = run(
            memory_blocks_kernel,
            [mem_mine, mem_theirs],
            [((dp, rows, mem_len // dp, share), BF16)],
            name="memory_blocks",
        )
    else:
        total = (mem_mine.astype(F32) + mem_theirs.astype(F32)).astype(BF16)
        total = total.reshape(dp, mem_len // dp, rows, team, share)
        blocks = lax.dynamic_index_in_dim(total, seat, 3, keepdims=False).swapaxes(1, 2)
    blocks = blocks.reshape(dp * rows, mem_len // dp, share)
    same_seat = [[d * mp + m for d in range(dp) for m in range(mp) if m % team == s] for s in range(team)]
    grad_memory = lax.all_to_all(
        blocks, ("dp", "mp"), split_axis=0, concat_axis=0, tiled=True, axis_index_groups=same_seat
    ).astype(F32)

    def both_rows(own, part, kind, name):
        near, got = team_gather(other(part))
        top = where if team == 2 else jnp.stack([row, seat // (team // 2)]).astype(jnp.int32)
        run.where = top
        (out,) = run(place_rows_kernel, [own, near, got], [far(((rows, seq, width), kind))], name=name)
        run.where = where
        return out

    mixed = both_rows(result, result_part, BF16, "place_mixed")
    grad_inputs = both_rows(grad_row, grad_part, F32, "place_grad_inputs")
    grad_self_qkv, grad_self_out = run(
        functools.partial(self_grads_kernel, by_self.halved[0]),
        [by_self.chunk, by_self.got],
        [far(((3, width, head), F32)), far(((head, width), F32))],
        name="self_grads",
    )
    small = by_self.rest
    own_small = small[9 : 9 + lines].reshape(-1)
    grad_self_bias = own_small[: 2 * head].reshape(2, head)
    grad_cross_bias = own_small[2 * head : 4 * head].reshape(2, head)
    grad_ffn_bias = own_small[4 * head :]
    return (
        mixed,
        grad_inputs,
        grad_memory,
        small[0:3],
        small[3:6],
        grad_self_qkv,
        grad_self_bias,
        grad_self_out,
        grad_cross_q,
        grad_cross_kv,
        grad_cross_bias,
        grad_cross_out,
        grad_ffn_in,
        grad_ffn_bias,
        grad_ffn_out,
        small[6:9],
    )


def solution(mesh):
    placed = (
        P("dp", None, None),
        P(None, "dp", None),
        P("dp", None),
        P("dp", None),
        P(),
        P(),
        P(),
        P(),
        P(None, None, "mp"),
        P(None, "mp"),
        P("mp", None),
        P(None, "mp"),
        P(None, None, "mp"),
        P(None, "mp"),
        P("mp", None),
        P(None, "mp"),
        P("mp"),
        P("mp", None),
        P(),
        P("dp", None, None),
    )
    return jax.shard_map(
        shards,
        mesh=mesh,
        in_specs=placed,
        out_specs=(
            P("dp", None, None),
            P("dp", None, None),
            P(None, "dp", "mp"),
            P(),
            P(),
            P(None, None, "mp"),
            P(None, "mp"),
            P("mp", None),
            P(None, "mp"),
            P(None, None, "mp"),
            P(None, "mp"),
            P("mp", None),
            P(None, "mp"),
            P("mp"),
            P("mp", None),
            P(),
        ),
        check_vma=False,
    )
```

profile of v0, /device:TPU:0, one launch (start us, length us, event | category | flops | bytes accessed | tf_op | source)
XLA Modules:
  0.0 195.6 jit_solution(6474417080784370958)
XLA Ops:
  2.7 7.3 %all-to-all-start = ((bf16[8,64,512]{2,1,0:T(8,128)(2,1)}), bf16[8,64,512]{2,1,0:T(8,128)(2,1)S(1)}, u32[]{:S(2)}, u32[]{:S(2)}) async-start(bf16[8,64,512]{2,1,0:T(8,128)(2,1)} %dynamic-slice_bitcast_fusion), calls=%async_computation | async-start | bytes 1048576 | tf_op jit(solution)/shard_map/all_to_all | solution.py:705
  10.0 1.6 collective-permute-start
  12.1 1.6 collective-permute-start.1
  15.2 4.0 %self_forward_0.1 = (bf16[512,512]{1,0:T(8,128)(2,1)S(1)}, bf16[512,128]{1,0:T(8,128)(2,1)S(1)}, bf16[512,128]{1,0:T(8,128)(2,1)S(1)}, bf16[512,128]{1,0:T(8,128...) custom-call(s32[6]{0:T(128)S(1)} %stack.27.where_ref, ...), custom_call_target="tpu_custom_call" | custom-call | flops 1000000 | bytes 100000 | tf_op jit(solution)/shard_map/self_forward_0/pallas_call | solution.py:116
  20.5 2.9 %collective-permute-done.1.refs_4_.refs_2_.refs_5_ = bf16[8,128]{1,0:T(8,128)(2,1)S(1)} collective-permute-done((bf16[8,128]{1,0:T(8,128)(2,1)S(1)}, bf16[8,128]{1,0:T(8,128)(2,1)S(1)}, u32[]{:S(2)}, u32[]{:S(2)}) %collective-permute-start.1) | collective-permute-done | bytes 2080 | tf_op jit(solution)/shard_map/ppermute | solution.py:667
  23.5 3.1 %self_forward_1.1 = (bf16[512,128]{1,0:T(8,128)(2,1)S(1)}, bf16[512,128]{1,0:T(8,128)(2,1)S(1)}, bf16[512,128]{1,0:T(8,128)(2,1)S(1)}, bf16[512,128]{1,0:T(8,128...) custom-call(s32[6]{0:T(128)S(1)} %stack.27.where_ref, ...), custom_call_target="tpu_custom_call" | custom-call | flops 1000000 | bytes 100000 | tf_op jit(solution)/shard_map/self_forward_1/pallas_call | solution.py:116
  29.9 1.6 collective-permute-start.5
  33.5 1.9 memory_0.1
  35.5 1.8 pack_ffn.1
  37.3 5.1 %cross_forward_0.1 = (f32[512,512]{1,0:T(8,128)S(1)}, bf16[512,512]{1,0:T(8,128)(2,1)S(1)}, bf16[512,128]{1,0:T(8,128)(2,1)S(1)}, bf16[512,128]{1,0:T(8,128)(2,1...) custom-call(s32[6]{0:T(128)S(1)} %stack.27.where_ref, bf16[2,512,512]{2,1,0:T(8,128)(2,1)} %refs_0_.9, ...), custom_call_target="tpu_custom_call" | custom-call | flops 1000000 | bytes 100000 | tf_op jit(solution)/shard_map/cross_forward_0/pallas_call | solution.py:116
  44.5 4.6 %cross_forward_1.1 = (bf16[512,128]{1,0:T(8,128)(2,1)S(1)}, bf16[512,128]{1,0:T(8,128)(2,1)S(1)}, f32[512,128]{1,0:T(8,128)S(1)}, bf16[512,512]{1,0:T(8,128)(2,1)S(1)}, f32[8,128]{1,0:T(8,128)}) custom-call(s32[6]{0:T(128)S(1)} %stack.27.where_ref, bf16[512,512]{1,0:T(8,128)(2,1)S(1)} %get-tuple-element.187.refs_0_.refs_10_, ...), custom_call_target="tpu_custom_call" | custom-call | flops 1000000 | bytes 100000 | tf_op jit(solution)/shard_map/cross_forward_1/pallas_call | solution.py:116
  49.3 1.6 collective-permute-start.8
  51.4 7.1 %collective-permute-done.8.refs_0_ = bf16[256,512]{1,0:T(8,128)(2,1)S(1)} collective-permute-done((bf16[256,512]{1,0:T(8,128)(2,1)S(1)}, bf16[256,512]{1,0:T(8,128)(2,1)S(1)}, u32[]{:S(2)}, u32[]{:S(2)}) %collective-permute-start.8) | collective-permute-done | bytes 262176 | tf_op jit(solution)/shard_map/ppermute | solution.py:667
  58.4 1.7 collective-permute-start.10
  60.1 3.5 %collective-permute-done.9.refs_1_ = bf16[256,512]{1,0:T(8,128)(2,1)S(1)} collective-permute-done((bf16[256,512]{1,0:T(8,128)(2,1)S(1)}, bf16[256,512]{1,0:T(8,128)(2,1)S(1)}, u32[]{:S(2)}, u32[]{:S(2)}) %collective-permute-start.9) | collective-permute-done | bytes 262176 | tf_op jit(solution)/shard_map/ppermute | solution.py:667
  63.6 1.7 collective-permute-start.11
  65.3 4.3 %ffn_0.1 = (f32[512,512]{1,0:T(8,128)S(1)}, bf16[512,512]{1,0:T(8,128)(2,1)S(1)}, bf16[512,512]{1,0:T(8,128)(2,1)S(1)}, bf16[512,512]{1,0:T(8,128)(2,1)S(1)}, bf...) custom-call(s32[6]{0:T(128)S(1)} %stack.27.where_ref, ...), custom_call_target="tpu_custom_call" | custom-call | flops 1000000 | bytes 100000 | tf_op jit(solution)/shard_map/ffn_0/pallas_call | solution.py:116
  69.6 1.9 collective-permute-done.11.refs_3_
  72.1 3.0 %ffn_1.1 = (bf16[512,512]{1,0:T(8,128)(2,1)S(1)}, bf16[512,512]{1,0:T(8,128)(2,1)S(1)}, bf16[512,512]{1,0:T(8,128)(2,1)S(1)}, bf16[512,512]{1,0:T(8,128)(2,1)S(1)}, f32[8,128]{1,0:T(8,128)}) custom-call(s32[6]{0:T(128)S(1)} %stack.27.where_ref, bf16[512,512]{1,0:T(8,128)(2,1)S(1)} %get-tuple-element.199.refs_0_.refs_4_, ...), custom_call_target="tpu_custom_call" | custom-call | flops 1000000 | bytes 100000 | tf_op jit(solution)/shard_map/ffn_1/pallas_call | solution.py:116
  75.7 1.9 ffn_weights.1
  79.1 1.7 collective-permute-start.19
  80.8 8.5 %cross_backward.1 = (f32[512,512]{1,0:T(8,128)S(1)}, bf16[512,512]{1,0:T(8,128)(2,1)S(1)}, bf16[512,128]{1,0:T(8,128)(2,1)S(1)}, bf16[512,128]{1,0:T(8,128)(2,1)...) custom-call(s32[6]{0:T(128)S(1)} %stack.27.where_ref, ...), custom_call_target="tpu_custom_call" | custom-call | flops 1000000 | bytes 100000 | tf_op jit(solution)/shard_map/cross_backward/pallas_call | solution.py:116
  89.4 3.8 %cross_weights.1 = (f32[2,256,512]{2,1,0:T(8,128)S(1)}, bf16[2,256,512]{2,1,0:T(8,128)(2,1)S(1)}, bf16[512,512]{1,0:T(8,128)(2,1)S(1)}, bf16[512,512]{1,0:T(8,12...) custom-call(s32[6]{0:T(128)S(1)} %stack.27.where_ref, bf16[512,128]{1,0:T(8,128)(2,1)S(1)} %get-tuple-element.222.refs_0_, ...), custom_call_target="tpu_custom_call" | custom-call | flops 1000000 | bytes 100000 | tf_op jit(solution)/shard_map/cross_weights/pallas_call | solution.py:116
  94.8 6.4 %self_backward.1 = (f32[512,512]{1,0:T(8,128)S(1)}, bf16[512,512]{1,0:T(8,128)(2,1)S(1)}, bf16[512,128]{1,0:T(8,128)(2,1)S(1)}, bf16[512,128]{1,0:T(8,128)(2,1)S...) custom-call(s32[6]{0:T(128)S(1)} %stack.27.where_ref, ...), custom_call_target="tpu_custom_call" | custom-call | flops 1000000 | bytes 100000 | tf_op jit(solution)/shard_map/self_backward/pallas_call | solution.py:116
  102.7 1.6 collective-permute-start.17
  104.3 5.7 %collective-permute-done.23.refs_3_ = bf16[1,256,512]{2,1,0:T(8,128)(2,1)S(1)} collective-permute-done((bf16[1,256,512]{2,1,0:T(8,128)(2,1)S(1)}, bf16[1,256,512]{2,1,0:T(8,128)(2,1)S(1)}, u32[]{:S(2)}, u32[]{:S(2)}) %collective-permute-start.23) | collective-permute-done | bytes 262176 | tf_op jit(solution)/shard_map/ppermute | solution.py:667
  110.9 3.2 %input_backward.1 = (bf16[512,512]{1,0:T(8,128)(2,1)S(1)}, bf16[256,512]{1,0:T(8,128)(2,1)}, f32[3,512]{1,0:T(4,128)S(1)}, f32[8,128]{1,0:T(8,128)}) custom-call(s32[6]{0:T(128)S(1)} %stack.27.where_ref, bf16[2,512,512]{2,1,0:T(8,128)(2,1)} %refs_0_.9, bf16[512,512]{1,0:T(8,128)(2,1)S(1)} %get-tuple-element.262.refs_1_, ...), custom_call_target="tpu_custom_call" | custom-call | flops 1000000 | bytes 100000 | tf_op jit(solution)/shard_map/input_backward/pallas_call | solution.py:116
  115.5 1.6 collective-permute-start.28
  119.9 4.1 %collective-permute-done.25.refs_1_ = bf16[2,128,512]{2,1,0:T(8,128)(2,1)S(1)} collective-permute-done((bf16[2,128,512]{2,1,0:T(8,128)(2,1)S(1)}, bf16[2,128,512]{2,1,0:T(8,128)(2,1)S(1)}, u32[]{:S(2)}, u32[]{:S(2)}) %collective-permute-start.25) | collective-permute-done | bytes 262176 | tf_op jit(solution)/shard_map/ppermute | solution.py:673
  124.6 2.4 %collective-permute-start.27 = (bf16[2,128,512]{2,1,0:T(8,128)(2,1)S(1)}, bf16[2,128,512]{2,1,0:T(8,128)(2,1)S(1)}, u32[]{:S(2)}, u32[]{:S(2)}) collective-permute-start(bf16[2,128,512]{2,1,0:T(8,128)(2,1)S(1)} %get-tuple-element.288.refs_0_), channel_id=1, source_target_pairs={{0,16},{4,20},{8,24},{12,28},{16,0},{20,4},{24,8},{28,12},{1,17},{... | collective-permute-start | bytes 786440 | tf_op jit(solution)/shard_map/ppermute | solution.py:673
  130.6 6.4 %collective-permute-done.27.refs_1_ = bf16[2,128,512]{2,1,0:T(8,128)(2,1)S(1)} collective-permute-done((bf16[2,128,512]{2,1,0:T(8,128)(2,1)S(1)}, bf16[2,128,512]{2,1,0:T(8,128)(2,1)S(1)}, u32[]{:S(2)}, u32[]{:S(2)}) %collective-permute-start.27) | collective-permute-done | bytes 262176 | tf_op jit(solution)/shard_map/ppermute | solution.py:673
  138.9 4.3 %collective-permute-done.26.refs_1_ = bf16[1,128,512]{2,1,0:T(8,128)(2,1)S(1)} collective-permute-done((bf16[1,128,512]{2,1,0:T(8,128)(2,1)S(1)}, bf16[1,128,512]{2,1,0:T(8,128)(2,1)S(1)}, u32[]{:S(2)}, u32[]{:S(2)}) %collective-permute-start.26) | collective-permute-done | bytes 131104 | tf_op jit(solution)/shard_map/ppermute | solution.py:667
  144.3 1.6 collective-permute-start.33
  146.0 1.9 collective-permute-start.29
  149.1 3.5 %collective-permute-done.29.refs_1_ = bf16[1,128,512]{2,1,0:T(8,128)(2,1)S(1)} collective-permute-done((bf16[1,128,512]{2,1,0:T(8,128)(2,1)S(1)}, bf16[1,128,512]{2,1,0:T(8,128)(2,1)S(1)}, u32[]{:S(2)}, u32[]{:S(2)}) %collective-permute-start.29) | collective-permute-done | bytes 131104 | tf_op jit(solution)/shard_map/ppermute | solution.py:673
  153.9 1.7 collective-permute-start.36
  156.1 7.2 %collective-permute-done.32.refs_1_ = bf16[1,128,512]{2,1,0:T(8,128)(2,1)S(1)} collective-permute-done((bf16[1,128,512]{2,1,0:T(8,128)(2,1)S(1)}, bf16[1,128,512]{2,1,0:T(8,128)(2,1)S(1)}, u32[]{:S(2)}, u32[]{:S(2)}) %collective-permute-start.32) | collective-permute-done | bytes 131104 | tf_op jit(solution)/shard_map/ppermute | solution.py:673
  164.5 1.7 collective-permute-start.37
  167.5 2.5 %collective-permute-done.37.refs_1_ = bf16[1,128,512]{2,1,0:T(8,128)(2,1)S(1)} collective-permute-done((bf16[1,128,512]{2,1,0:T(8,128)(2,1)S(1)}, bf16[1,128,512]{2,1,0:T(8,128)(2,1)S(1)}, u32[]{:S(2)}, u32[]{:S(2)}) %collective-permute-start.37) | collective-permute-done | bytes 131104 | tf_op jit(solution)/shard_map/ppermute | solution.py:673
  171.6 2.2 %ffn_grads.1 = (f32[512,512]{1,0:T(8,128)}, f32[512,512]{1,0:T(8,128)}, f32[8,128]{1,0:T(8,128)}) custom-call(s32[6]{0:T(128)S(1)} %stack.27.where_ref, bf16[2,256,512]{2,1,0:T(8,128)(2,1)S(1)} %get-tuple-element.307.refs_0_, bf16[2,256,512]{2,1,0:T(8,128)(2,1)S(1)} %collective-permute-done.35.refs_1_, f32[8,128]{1,0:T(8,128)} %get-tuple-element.312.refs_2_), custom_call_target="tpu_custom_call" | custom-call | flops 1000000 | bytes 100000 | tf_op jit(solution)/shard_map/ffn_grads/pallas_call | solution.py:116
  173.8 1.6 cross_grads.1
  176.8 4.6 %all-to-all-start.1 = ((bf16[16,64,128]{2,1,0:T(8,128)(2,1)}), bf16[16,64,128]{2,1,0:T(8,128)(2,1)}, u32[]{:S(2)}, u32[]{:S(2)}) async-start(bf16[16,64,128]{2,1,0:T(8,128)(2,1)} %bitcast.10), calls=%async_computation.1 | async-start | bytes 524288 | tf_op jit(solution)/shard_map/all_to_all | solution.py:987
  182.0 1.9 collective-permute-start.40
  185.7 2.0 %place_mixed.1 = (bf16[2,512,512]{2,1,0:T(8,128)(2,1)}, f32[8,128]{1,0:T(8,128)}) custom-call(s32[6]{0:T(128)S(1)} %stack.27.where_ref, bf16[512,512]{1,0:T(8,128)(2,1)S(1)} %copy-done.4, bf16[256,512]{1,0:T(8,128)(2,1)} %collective-permute-done.14.refs_1_, bf16[256,512]{1,0:T(8,128)(2,1)S(1)} %collective-permute-done.15.refs_2_, ...), custom_call_target="tpu_custom_call" | custom-call | flops 1000000 | bytes 100000 | tf_op jit(solution)/shard_map/place_mixed/pallas_call | solution.py:116
  187.7 2.0 %place_grad_inputs.1 = (f32[2,512,512]{2,1,0:T(8,128)}, f32[8,128]{1,0:T(8,128)}) custom-call(s32[6]{0:T(128)S(1)} %stack.27.where_ref, bf16[512,512]{1,0:T(8,128)(2,1)S(1)} %get-tuple-element.317.refs_0_, bf16[256,512]{1,0:T(8,128)(2,1)S(1)} %collective-permute-done.38.refs_1_, bf16[256,512]{1,0:T(8,128)(2,1)S(1)} %collective-permute-done.39.refs_2_, ...), custom_call_target="tpu_custom_call" | custom-call | flops 1000000 | bytes 100000 | tf_op jit(solution)/shard_map/place_grad_inputs/pallas_call | solution.py:116
  189.8 2.3 %collective-permute-done.40.refs_1_ = bf16[1,256,512]{2,1,0:T(8,128)(2,1)S(1)} collective-permute-done((bf16[1,256,512]{2,1,0:T(8,128)(2,1)S(1)}, bf16[1,256,512]{2,1,0:T(8,128)(2,1)S(1)}, u32[]{:S(2)}, u32[]{:S(2)}) %collective-permute-start.40) | collective-permute-done | bytes 262176 | tf_op jit(solution)/shard_map/ppermute | solution.py:673
  192.1 1.7 self_grads.1
  193.8 1.8 convert_element_type.3
  (146 shorter events, 41.7 us)
Async XLA Ops:
  0.7 13.1 %copy-start.23 = (s32[2,8]{1,0:T(2,128)S(1)}, s32[2,8]{1,0:T(2,128)}, u32[]{:S(2)}) copy-start(s32[2,8]{1,0:T(2,128)} %refs_2_.1) | copy-start | bytes 196
  0.7 13.1 %copy-start.25 = (s32[8]{0:T(128)S(1)}, s32[8]{0:T(128)}, u32[]{:S(2)}) copy-start(s32[8]{0:T(128)} %refs_1_.3) | copy-start | bytes 100
  0.7 13.0 %copy-start.24 = (s32[6]{0:T(128)S(1)}, s32[6]{0:T(128)}, u32[]{:S(2)}) copy-start(s32[6]{0:T(128)} %refs_0_.5) | copy-start | bytes 76
  2.7 30.8 %all-to-all-start = ((bf16[8,64,512]{2,1,0:T(8,128)(2,1)}), bf16[8,64,512]{2,1,0:T(8,128)(2,1)S(1)}, u32[]{:S(2)}, u32[]{:S(2)}) async-start(bf16[8,64,512]{2,1,0:T(8,128)(2,1)} %dynamic-slice_bitcast_fusion), calls=%async_computation | async-start | bytes 1048576 | tf_op jit(solution)/shard_map/all_to_all | solution.py:705
  10.0 13.5 %collective-permute-start = (bf16[3,512,128]{2,1,0:T(8,128)(2,1)S(1)}, bf16[3,512,128]{2,1,0:T(8,128)(2,1)S(1)}, u32[]{:S(2)}, u32[]{:S(2)}) collective-permute-start(bf16[3,512,128]{2,1,0:T(8,128)(2,1)S(1)} %copy-done.26), channel_id=1, source_target_pairs={{0,2},{1,3},{2,0},{3,1},{4,6},{5,7},{6,4},{7,5},{8,10},{9,11},{10,... | collective-permute-start | bytes 1179656 | tf_op jit(solution)/shard_map/ppermute | solution.py:667
  11.6 11.9 %collective-permute-start.2 = (bf16[128,512]{1,0:T(8,128)(2,1)}, bf16[128,512]{1,0:T(8,128)(2,1)S(1)}, u32[]{:S(2)}, u32[]{:S(2)}) collective-permute-start(bf16[128,512]{1,0:T(8,128)(2,1)} %refs_14_.3), channel_id=1, source_target_pairs={{0,2},{1,3},{2,0},{3,1},{4,6},{5,7},{6,4},{7,5},{8,10},{9,11},{10,... | collective-permute-start | bytes 393224 | tf_op jit(solution)/shard_map/ppermute | solution.py:667
  12.1 11.4 %collective-permute-start.1 = (bf16[8,128]{1,0:T(8,128)(2,1)S(1)}, bf16[8,128]{1,0:T(8,128)(2,1)S(1)}, u32[]{:S(2)}, u32[]{:S(2)}) collective-permute-start(bf16[8,128]{1,0:T(8,128)(2,1)S(1)} %pad_maximum_fusion.refs_4_.refs_2_.refs_6_), channel_id=1, source_target_pairs={{0,2},{1,3},{2,0},{3,1},{4,6},{5,7},{6,4},{7,5},{8,10},{9,11},{10,... | collective-permute-start | bytes 6152 | tf_op jit(solution)/shard_map/ppermute | solution.py:667
  20.5 11.4 %copy-start.5 = (f32[512,128]{1,0:T(8,128)}, f32[512,128]{1,0:T(8,128)S(1)}, u32[]{:S(2)}) copy-start(f32[512,128]{1,0:T(8,128)S(1)} %get-tuple-element.245.refs_12_) | copy-start | bytes 786436
  29.9 7.4 %collective-permute-start.3 = (bf16[512,512]{1,0:T(8,128)(2,1)S(1)}, bf16[512,512]{1,0:T(8,128)(2,1)}, u32[]{:S(2)}, u32[]{:S(2)}) collective-permute-start(bf16[512,512]{1,0:T(8,128)(2,1)S(1)} %get-tuple-element.180.refs_1_), channel_id=1, source_target_pairs={{0,1},{1,0},{2,3},{3,2},{4,5},{5,4},{6,7},{7,6},{8,9},{9,8},{10,11... | collective-permute-start | bytes 1572872 | tf_op jit(solution)/shard_map/ppermute | solution.py:670
  29.9 12.5 %collective-permute-start.5 = (bf16[2,512,128]{2,1,0:T(8,128)(2,1)}, bf16[2,512,128]{2,1,0:T(8,128)(2,1)S(1)}, u32[]{:S(2)}, u32[]{:S(2)}) collective-permute-start(bf16[2,512,128]{2,1,0:T(8,128)(2,1)} %refs_8_.1), channel_id=1, source_target_pairs={{0,2},{1,3},{2,0},{3,1},{4,6},{5,7},{6,4},{7,5},{8,10},{9,11},{10,... | collective-permute-start | bytes 786440 | tf_op jit(solution)/shard_map/ppermute | solution.py:667
  31.5 11.9 %collective-permute-start.4 = (bf16[512,128]{1,0:T(8,128)(2,1)}, bf16[512,128]{1,0:T(8,128)(2,1)}, u32[]{:S(2)}, u32[]{:S(2)}) collective-permute-start(bf16[512,128]{1,0:T(8,128)(2,1)} %refs_16_.2), channel_id=1, source_target_pairs={{0,2},{1,3},{2,0},{3,1},{4,6},{5,7},{6,4},{7,5},{8,10},{9,11},{10,... | collective-permute-start | bytes 393224 | tf_op jit(solution)/shard_map/ppermute | solution.py:667
  32.0 12.6 %collective-permute-start.6 = (bf16[128,512]{1,0:T(8,128)(2,1)}, bf16[128,512]{1,0:T(8,128)(2,1)}, u32[]{:S(2)}, u32[]{:S(2)}) collective-permute-start(bf16[128,512]{1,0:T(8,128)(2,1)} %refs_14_.2), channel_id=1, source_target_pairs={{0,2},{1,3},{2,0},{3,1},{4,6},{5,7},{6,4},{7,5},{8,10},{9,11},{10,... | collective-permute-start | bytes 393224 | tf_op jit(solution)/shard_map/ppermute | solution.py:667
  49.2 16.1 %collective-permute-start.7 = (bf16[512,512]{1,0:T(8,128)(2,1)S(1)}, bf16[512,512]{1,0:T(8,128)(2,1)S(1)}, u32[]{:S(2)}, u32[]{:S(2)}) collective-permute-start(bf16[512,512]{1,0:T(8,128)(2,1)S(1)} %get-tuple-element.196.refs_1_), channel_id=1, source_target_pairs={{0,1},{1,0},{2,3},{3,2},{4,5},{5,4},{6,7},{7,6},{8,9},{9,8},{10,11... | collective-permute-start | bytes 1572872 | tf_op jit(solution)/shard_map/ppermute | solution.py:670
  49.3 9.2 %collective-permute-start.8 = (bf16[256,512]{1,0:T(8,128)(2,1)S(1)}, bf16[256,512]{1,0:T(8,128)(2,1)S(1)}, u32[]{:S(2)}, u32[]{:S(2)}) collective-permute-start(bf16[256,512]{1,0:T(8,128)(2,1)S(1)} %get-tuple-element.204), channel_id=1, source_target_pairs={{0,2},{1,3},{2,0},{3,1},{4,6},{5,7},{6,4},{7,5},{8,10},{9,11},{10,... | collective-permute-start | bytes 786440 | tf_op jit(solution)/shard_map/ppermute | solution.py:667
  50.9 12.8 %collective-permute-start.9 = (bf16[256,512]{1,0:T(8,128)(2,1)S(1)}, bf16[256,512]{1,0:T(8,128)(2,1)S(1)}, u32[]{:S(2)}, u32[]{:S(2)}) collective-permute-start(bf16[256,512]{1,0:T(8,128)(2,1)S(1)} %get-tuple-element.206), channel_id=1, source_target_pairs={{0,2},{1,3},{2,0},{3,1},{4,6},{5,7},{6,4},{7,5},{8,10},{9,11},{10,... | collective-permute-start | bytes 786440 | tf_op jit(solution)/shard_map/ppermute | solution.py:667
  58.4 11.2 %collective-permute-start.10 = (bf16[256,512]{1,0:T(8,128)(2,1)S(1)}, bf16[256,512]{1,0:T(8,128)(2,1)S(1)}, u32[]{:S(2)}, u32[]{:S(2)}) collective-permute-start(bf16[256,512]{1,0:T(8,128)(2,1)S(1)} %collective-permute-done.8.refs_0_), channel_id=1, source_target_pairs={{0,4},{4,0},{8,12},{12,8},{16,20},{20,16},{24,28},{28,24},{1,5},{5... | collective-permute-start | bytes 786440 | tf_op jit(solution)/shard_map/ppermute | solution.py:673
  63.6 7.9 %collective-permute-start.11 = (bf16[256,512]{1,0:T(8,128)(2,1)S(1)}, bf16[256,512]{1,0:T(8,128)(2,1)S(1)}, u32[]{:S(2)}, u32[]{:S(2)}) collective-permute-start(bf16[256,512]{1,0:T(8,128)(2,1)S(1)} %collective-permute-done.9.refs_1_), channel_id=1, source_target_pairs={{0,4},{4,0},{8,12},{12,8},{16,20},{20,16},{24,28},{28,24},{1,5},{5... | collective-permute-start | bytes 786440 | tf_op jit(solution)/shard_map/ppermute | solution.py:673
  75.1 5.7 %collective-permute-start.12 = (bf16[512,512]{1,0:T(8,128)(2,1)S(1)}, bf16[512,512]{1,0:T(8,128)(2,1)S(1)}, u32[]{:S(2)}, u32[]{:S(2)}) collective-permute-start(bf16[512,512]{1,0:T(8,128)(2,1)S(1)} %get-tuple-element.211.refs_1_), channel_id=1, source_target_pairs={{0,1},{1,0},{2,3},{3,2},{4,5},{5,4},{6,7},{7,6},{8,9},{9,8},{10,11... | collective-permute-start | bytes 1572872 | tf_op jit(solution)/shard_map/ppermute | solution.py:670
  75.2 14.3 %collective-permute-start.13 = (bf16[512,512]{1,0:T(8,128)(2,1)S(1)}, bf16[512,512]{1,0:T(8,128)(2,1)S(1)}, u32[]{:S(2)}, u32[]{:S(2)}) collective-permute-start(bf16[512,512]{1,0:T(8,128)(2,1)S(1)} %get-tuple-element.230.refs_14_), channel_id=1, source_target_pairs={{0,1},{1,0},{2,3},{3,2},{4,5},{5,4},{6,7},{7,6},{8,9},{9,8},{10,11... | collective-permute-start | bytes 1572872 | tf_op jit(solution)/shard_map/ppermute | solution.py:670
  77.5 15.8 %collective-permute-start.20 = (bf16[1,512,512]{2,1,0:T(8,128)(2,1)S(1)}, bf16[1,512,512]{2,1,0:T(8,128)(2,1)S(1)}, u32[]{:S(2)}, u32[]{:S(2)}) collective-permute-start(bf16[1,512,512]{2,1,0:T(8,128)(2,1)S(1)} %get-tuple-element.250), channel_id=1, source_target_pairs={{0,2},{1,3},{2,0},{3,1},{4,6},{5,7},{6,4},{7,5},{8,10},{9,11},{10,... | collective-permute-start | bytes 1572872 | tf_op jit(solution)/shard_map/ppermute | solution.py:667
  79.1 14.9 %collective-permute-start.19 = (bf16[2,256,512]{2,1,0:T(8,128)(2,1)S(1)}, bf16[2,256,512]{2,1,0:T(8,128)(2,1)S(1)}, u32[]{:S(2)}, u32[]{:S(2)}) collective-permute-start(bf16[2,256,512]{2,1,0:T(8,128)(2,1)S(1)} %get-tuple-element.248), channel_id=1, source_target_pairs={{0,4},{4,0},{8,12},{12,8},{16,20},{20,16},{24,28},{28,24},{1,5},{5... | collective-permute-start | bytes 1572872 | tf_op jit(solution)/shard_map/ppermute | solution.py:673
  89.3 5.3 %collective-permute-start.18 = (bf16[512,512]{1,0:T(8,128)(2,1)S(1)}, bf16[512,512]{1,0:T(8,128)(2,1)S(1)}, u32[]{:S(2)}, u32[]{:S(2)}) collective-permute-start(bf16[512,512]{1,0:T(8,128)(2,1)S(1)} %get-tuple-element.237.refs_1_), channel_id=1, source_target_pairs={{0,1},{1,0},{2,3},{3,2},{4,5},{5,4},{6,7},{7,6},{8,9},{9,8},{10,11... | collective-permute-start | bytes 1572872 | tf_op jit(solution)/shard_map/ppermute | solution.py:670
  101.2 9.7 %collective-permute-start.21 = (bf16[512,512]{1,0:T(8,128)(2,1)S(1)}, bf16[512,512]{1,0:T(8,128)(2,1)S(1)}, u32[]{:S(2)}, u32[]{:S(2)}) collective-permute-start(bf16[512,512]{1,0:T(8,128)(2,1)S(1)} %get-tuple-element.262.refs_1_), channel_id=1, source_target_pairs={{0,1},{1,0},{2,3},{3,2},{4,5},{5,4},{6,7},{7,6},{8,9},{9,8},{10,11... | collective-permute-start | bytes 1572872 | tf_op jit(solution)/shard_map/ppermute | solution.py:670
  101.8 8.3 %collective-permute-start.23 = (bf16[1,256,512]{2,1,0:T(8,128)(2,1)S(1)}, bf16[1,256,512]{2,1,0:T(8,128)(2,1)S(1)}, u32[]{:S(2)}, u32[]{:S(2)}) collective-permute-start(bf16[1,256,512]{2,1,0:T(8,128)(2,1)S(1)} %get-tuple-element.267), channel_id=1, source_target_pairs={{0,2},{1,3},{2,0},{3,1},{4,6},{5,7},{6,4},{7,5},{8,10},{9,11},{10,... | collective-permute-start | bytes 786440 | tf_op jit(solution)/shard_map/ppermute | solution.py:667
  102.3 8.0 %collective-permute-start.22 = (bf16[1,256,512]{2,1,0:T(8,128)(2,1)S(1)}, bf16[1,256,512]{2,1,0:T(8,128)(2,1)S(1)}, u32[]{:S(2)}, u32[]{:S(2)}) collective-permute-start(bf16[1,256,512]{2,1,0:T(8,128)(2,1)S(1)} %get-tuple-element.266), channel_id=1, source_target_pairs={{0,4},{4,0},{8,12},{12,8},{16,20},{20,16},{24,28},{28,24},{1,5},{5... | collective-permute-start | bytes 786440 | tf_op jit(solution)/shard_map/ppermute | solution.py:673
  102.7 15.9 %collective-permute-start.17 = (bf16[2,256,512]{2,1,0:T(8,128)(2,1)S(1)}, bf16[2,256,512]{2,1,0:T(8,128)(2,1)S(1)}, u32[]{:S(2)}, u32[]{:S(2)}) collective-permute-start(bf16[2,256,512]{2,1,0:T(8,128)(2,1)S(1)} %get-tuple-element.236), channel_id=1, source_target_pairs={{0,8},{4,12},{8,0},{12,4},{16,24},{20,28},{24,16},{28,20},{1,9},{5... | collective-permute-start | bytes 1572872 | tf_op jit(solution)/shard_map/ppermute | solution.py:673
  115.5 13.3 %collective-permute-start.28 = (bf16[1,528,512]{2,1,0:T(8,128)(2,1)S(1)}, bf16[1,528,512]{2,1,0:T(8,128)(2,1)S(1)}, u32[]{:S(2)}, u32[]{:S(2)}) collective-permute-start(bf16[1,528,512]{2,1,0:T(8,128)(2,1)S(1)} %get-tuple-element.290), channel_id=1, source_target_pairs={{0,2},{1,3},{2,0},{3,1},{4,6},{5,7},{6,4},{7,5},{8,10},{9,11},{10,... | collective-permute-start | bytes 1622024 | tf_op jit(solution)/shard_map/ppermute | solution.py:667
  117.1 6.8 %collective-permute-start.25 = (bf16[2,128,512]{2,1,0:T(8,128)(2,1)S(1)}, bf16[2,128,512]{2,1,0:T(8,128)(2,1)S(1)}, u32[]{:S(2)}, u32[]{:S(2)}) collective-permute-start(bf16[2,128,512]{2,1,0:T(8,128)(2,1)S(1)} %get-tuple-element.283), channel_id=1, source_target_pairs={{0,8},{4,12},{8,0},{12,4},{16,24},{20,28},{24,16},{28,20},{1,9},{5... | collective-permute-start | bytes 786440 | tf_op jit(solution)/shard_map/ppermute | solution.py:673
  119.2 7.8 %collective-permute-start.24 = (bf16[2,128,512]{2,1,0:T(8,128)(2,1)S(1)}, bf16[2,128,512]{2,1,0:T(8,128)(2,1)S(1)}, u32[]{:S(2)}, u32[]{:S(2)}) collective-permute-start(bf16[2,128,512]{2,1,0:T(8,128)(2,1)S(1)} %get-tuple-element.281), channel_id=1, source_target_pairs={{0,4},{4,0},{8,12},{12,8},{16,20},{20,16},{24,28},{28,24},{1,5},{5... | collective-permute-start | bytes 786440 | tf_op jit(solution)/shard_map/ppermute | solution.py:673
  124.6 12.5 %collective-permute-start.27 = (bf16[2,128,512]{2,1,0:T(8,128)(2,1)S(1)}, bf16[2,128,512]{2,1,0:T(8,128)(2,1)S(1)}, u32[]{:S(2)}, u32[]{:S(2)}) collective-permute-start(bf16[2,128,512]{2,1,0:T(8,128)(2,1)S(1)} %get-tuple-element.288.refs_0_), channel_id=1, source_target_pairs={{0,16},{4,20},{8,24},{12,28},{16,0},{20,4},{24,8},{28,12},{1,17},{... | collective-permute-start | bytes 786440 | tf_op jit(solution)/shard_map/ppermute | solution.py:673
  129.4 14.3 %collective-permute-start.31 = (bf16[1,272,512]{2,1,0:T(8,128)(2,1)S(1)}, bf16[1,272,512]{2,1,0:T(8,128)(2,1)S(1)}, u32[]{:S(2)}, u32[]{:S(2)}) collective-permute-start(bf16[1,272,512]{2,1,0:T(8,128)(2,1)S(1)} %get-tuple-element.297), channel_id=1, source_target_pairs={{0,4},{4,0},{8,12},{12,8},{16,20},{20,16},{24,28},{28,24},{1,5},{5... | collective-permute-start | bytes 835592 | tf_op jit(solution)/shard_map/ppermute | solution.py:673
  137.7 10.2 %collective-permute-start.30 = (bf16[2,128,512]{2,1,0:T(8,128)(2,1)S(1)}, bf16[2,128,512]{2,1,0:T(8,128)(2,1)S(1)}, u32[]{:S(2)}, u32[]{:S(2)}) collective-permute-start(bf16[2,128,512]{2,1,0:T(8,128)(2,1)S(1)} %get-tuple-element.295.refs_0_), channel_id=1, source_target_pairs={{0,8},{4,12},{8,0},{12,4},{16,24},{20,28},{24,16},{28,20},{1,9},{5... | collective-permute-start | bytes 786440 | tf_op jit(solution)/shard_map/ppermute | solution.py:673
  138.2 5.0 %collective-permute-start.26 = (bf16[1,128,512]{2,1,0:T(8,128)(2,1)S(1)}, bf16[1,128,512]{2,1,0:T(8,128)(2,1)S(1)}, u32[]{:S(2)}, u32[]{:S(2)}) collective-permute-start(bf16[1,128,512]{2,1,0:T(8,128)(2,1)S(1)} %get-tuple-element.287), channel_id=1, source_target_pairs={{0,2},{1,3},{2,0},{3,1},{4,6},{5,7},{6,4},{7,5},{8,10},{9,11},{10,... | collective-permute-start | bytes 393224 | tf_op jit(solution)/shard_map/ppermute | solution.py:667
  144.3 8.9 %collective-permute-start.33 = (bf16[1,144,512]{2,1,0:T(8,128)(2,1)S(1)}, bf16[1,144,512]{2,1,0:T(8,128)(2,1)S(1)}, u32[]{:S(2)}, u32[]{:S(2)}) collective-permute-start(bf16[1,144,512]{2,1,0:T(8,128)(2,1)S(1)} %get-tuple-element.303), channel_id=1, source_target_pairs={{0,8},{4,12},{8,0},{12,4},{16,24},{20,28},{24,16},{28,20},{1,9},{5... | collective-permute-start | bytes 442376 | tf_op jit(solution)/shard_map/ppermute | solution.py:673
  146.0 6.7 %collective-permute-start.29 = (bf16[1,128,512]{2,1,0:T(8,128)(2,1)S(1)}, bf16[1,128,512]{2,1,0:T(8,128)(2,1)S(1)}, u32[]{:S(2)}, u32[]{:S(2)}) collective-permute-start(bf16[1,128,512]{2,1,0:T(8,128)(2,1)S(1)} %get-tuple-element.294.refs_0_), channel_id=1, source_target_pairs={{0,16},{4,20},{8,24},{12,28},{16,0},{20,4},{24,8},{28,12},{1,17},{... | collective-permute-start | bytes 393224 | tf_op jit(solution)/shard_map/ppermute | solution.py:673
  148.5 23.1 %collective-permute-start.35 = (bf16[2,256,512]{2,1,0:T(8,128)(2,1)S(1)}, bf16[2,256,512]{2,1,0:T(8,128)(2,1)S(1)}, u32[]{:S(2)}, u32[]{:S(2)}) collective-permute-start(bf16[2,256,512]{2,1,0:T(8,128)(2,1)S(1)} %get-tuple-element.307.refs_0_), channel_id=1, source_target_pairs={{0,4},{4,0},{8,12},{12,8},{16,20},{20,16},{24,28},{28,24},{1,5},{5... | collective-permute-start | bytes 1572872 | tf_op jit(solution)/shard_map/ppermute | solution.py:673
  149.1 26.3 %collective-permute-start.16 = (bf16[512,512]{1,0:T(8,128)(2,1)S(1)}, bf16[512,512]{1,0:T(8,128)(2,1)S(1)}, u32[]{:S(2)}, u32[]{:S(2)}) collective-permute-start(bf16[512,512]{1,0:T(8,128)(2,1)S(1)} %get-tuple-element.234.refs_0_), channel_id=1, source_target_pairs={{0,1},{1,0},{2,3},{3,2},{4,5},{5,4},{6,7},{7,6},{8,9},{9,8},{10,11... | collective-permute-start | bytes 1572872 | tf_op jit(solution)/shard_map/ppermute | solution.py:670
  153.8 31.8 %copy-start.4 = (bf16[512,512]{1,0:T(8,128)(2,1)S(1)}, bf16[512,512]{1,0:T(8,128)(2,1)}, u32[]{:S(2)}) copy-start(bf16[512,512]{1,0:T(8,128)(2,1)} %copy-done.3) | copy-start | bytes 1572868
  153.9 10.1 %collective-permute-start.36 = (bf16[1,144,512]{2,1,0:T(8,128)(2,1)S(1)}, bf16[1,144,512]{2,1,0:T(8,128)(2,1)S(1)}, u32[]{:S(2)}, u32[]{:S(2)}) collective-permute-start(bf16[1,144,512]{2,1,0:T(8,128)(2,1)S(1)} %get-tuple-element.308.refs_0_), channel_id=1, source_target_pairs={{0,16},{4,20},{8,24},{12,28},{16,0},{20,4},{24,8},{28,12},{1,17},{... | collective-permute-start | bytes 442376 | tf_op jit(solution)/shard_map/ppermute | solution.py:673
  155.6 7.8 %collective-permute-start.32 = (bf16[1,128,512]{2,1,0:T(8,128)(2,1)S(1)}, bf16[1,128,512]{2,1,0:T(8,128)(2,1)S(1)}, u32[]{:S(2)}, u32[]{:S(2)}) collective-permute-start(bf16[1,128,512]{2,1,0:T(8,128)(2,1)S(1)} %get-tuple-element.301.refs_0_), channel_id=1, source_target_pairs={{0,4},{4,0},{8,12},{12,8},{16,20},{20,16},{24,28},{28,24},{1,5},{5... | collective-permute-start | bytes 393224 | tf_op jit(solution)/shard_map/ppermute | solution.py:673
  164.5 5.5 %collective-permute-start.37 = (bf16[1,128,512]{2,1,0:T(8,128)(2,1)S(1)}, bf16[1,128,512]{2,1,0:T(8,128)(2,1)S(1)}, u32[]{:S(2)}, u32[]{:S(2)}) collective-permute-start(bf16[1,128,512]{2,1,0:T(8,128)(2,1)S(1)} %get-tuple-element.310.refs_0_), channel_id=1, source_target_pairs={{0,8},{4,12},{8,0},{12,4},{16,24},{20,28},{24,16},{28,20},{1,9},{5... | collective-permute-start | bytes 393224 | tf_op jit(solution)/shard_map/ppermute | solution.py:673
  166.2 7.5 %collective-permute-start.34 = (bf16[1,256,512]{2,1,0:T(8,128)(2,1)S(1)}, bf16[1,256,512]{2,1,0:T(8,128)(2,1)S(1)}, u32[]{:S(2)}, u32[]{:S(2)}) collective-permute-start(bf16[1,256,512]{2,1,0:T(8,128)(2,1)S(1)} %get-tuple-element.306.refs_0_), channel_id=1, source_target_pairs={{0,8},{4,12},{8,0},{12,4},{16,24},{20,28},{24,16},{28,20},{1,9},{5... | collective-permute-start | bytes 786440 | tf_op jit(solution)/shard_map/ppermute | solution.py:673
  166.6 14.8 %collective-permute-start.14 = (bf16[256,512]{1,0:T(8,128)(2,1)}, bf16[256,512]{1,0:T(8,128)(2,1)}, u32[]{:S(2)}, u32[]{:S(2)}) collective-permute-start(bf16[256,512]{1,0:T(8,128)(2,1)} %get-tuple-element.233), channel_id=1, source_target_pairs={{0,2},{1,3},{2,0},{3,1},{4,6},{5,7},{6,4},{7,5},{8,10},{9,11},{10,... | collective-permute-start | bytes 786440 | tf_op jit(solution)/shard_map/ppermute | solution.py:667
  170.0 11.4 %collective-permute-start.38 = (bf16[256,512]{1,0:T(8,128)(2,1)}, bf16[256,512]{1,0:T(8,128)(2,1)S(1)}, u32[]{:S(2)}, u32[]{:S(2)}) collective-permute-start(bf16[256,512]{1,0:T(8,128)(2,1)} %get-tuple-element.318), channel_id=1, source_target_pairs={{0,2},{1,3},{2,0},{3,1},{4,6},{5,7},{6,4},{7,5},{8,10},{9,11},{10,... | collective-permute-start | bytes 786440 | tf_op jit(solution)/shard_map/ppermute | solution.py:667
  176.8 17.0 %all-to-all-start.1 = ((bf16[16,64,128]{2,1,0:T(8,128)(2,1)}), bf16[16,64,128]{2,1,0:T(8,128)(2,1)}, u32[]{:S(2)}, u32[]{:S(2)}) async-start(bf16[16,64,128]{2,1,0:T(8,128)(2,1)} %bitcast.10), calls=%async_computation.1 | async-start | bytes 524288 | tf_op jit(solution)/shard_map/all_to_all | solution.py:987
  181.4 4.3 %collective-permute-start.15 = (bf16[256,512]{1,0:T(8,128)(2,1)}, bf16[256,512]{1,0:T(8,128)(2,1)S(1)}, u32[]{:S(2)}, u32[]{:S(2)}) collective-permute-start(bf16[256,512]{1,0:T(8,128)(2,1)} %collective-permute-done.14.refs_1_), channel_id=1, source_target_pairs={{0,1},{1,0},{2,3},{3,2},{4,5},{5,4},{6,7},{7,6},{8,9},{9,8},{10,11... | collective-permute-start | bytes 786440 | tf_op jit(solution)/shard_map/ppermute | solution.py:670
  181.5 6.2 %collective-permute-start.39 = (bf16[256,512]{1,0:T(8,128)(2,1)S(1)}, bf16[256,512]{1,0:T(8,128)(2,1)S(1)}, u32[]{:S(2)}, u32[]{:S(2)}) collective-permute-start(bf16[256,512]{1,0:T(8,128)(2,1)S(1)} %collective-permute-done.38.refs_1_), channel_id=1, source_target_pairs={{0,1},{1,0},{2,3},{3,2},{4,5},{5,4},{6,7},{7,6},{8,9},{9,8},{10,11... | collective-permute-start | bytes 786440 | tf_op jit(solution)/shard_map/ppermute | solution.py:670
  182.0 10.1 %collective-permute-start.40 = (bf16[1,256,512]{2,1,0:T(8,128)(2,1)S(1)}, bf16[1,256,512]{2,1,0:T(8,128)(2,1)S(1)}, u32[]{:S(2)}, u32[]{:S(2)}) collective-permute-start(bf16[1,256,512]{2,1,0:T(8,128)(2,1)S(1)} %get-tuple-element.323.refs_0_), channel_id=1, source_target_pairs={{0,4},{4,0},{8,12},{12,8},{16,20},{20,16},{24,28},{28,24},{1,5},{5... | collective-permute-start | bytes 786440 | tf_op jit(solution)/shard_map/ppermute | solution.py:673
  (25 other events, 83.8 us)
where the time goes:
time: 196 us
  Pallas kernels  76.6 us (39%)
  waiting for transfers between devices  54.2 us (28%)
  starting transfers between devices  53 us (27%)
  local copies, waits for them, and re-layouts  8.55 us (4%)
    pallas_call x39, Pallas kernels, __call__(): pl.pallas_call(body, in_specs=[words] + specs + [far] * n_after, out_spec...  76.6 us
    ppermute x18, waiting for transfers between devices, data_swap(): return lax.ppermute(value, 'dp', [(i, i ^ 1 << k) for i in range(dp)])  28.2 us
    ppermute x14, waiting for transfers between devices, other(): return lax.ppermute(value, 'mp', across)  25.9 us
    ppermute x18, starting transfers between devices, data_swap(): return lax.ppermute(value, 'dp', [(i, i ^ 1 << k) for i in range(dp)])  23.8 us
    ppermute x14, starting transfers between devices, other(): return lax.ppermute(value, 'mp', across)  15.6 us
    all_to_all x1, starting transfers between devices, shards(): lax.all_to_all(memory_part, 'dp', split_axis=0, concat_axis=0, tiled=True)  7.25 us
    unnamed x60, local copies, waits for them, and re-layouts  5.84 us
    all_to_all x1, starting transfers between devices, shards(): lax.all_to_all(blocks, ('dp', 'mp'), split_axis=0, concat_axis=0, tiled=T...  4.58 us
  transfers between devices with their start and end apart: 43, of which 15 were waited for; matrix products, arithmetic and copies ran while one was open for 1% of the time, Pallas kernels for 32%

commit v1 on v0

v1 whole, which is shorter than its diff:
```python
import functools

import jax
import jax.numpy as jnp
from jax import lax
from jax.experimental import pallas as pl
from jax.experimental.pallas import tpu as pltpu
from jax.sharding import PartitionSpec as P

HDIM = 64
LANES = 128
BLOCK = 128
SMALL = 16
FRONT = 2
BACK = 2
EPSILON = 1e-05
F32 = jnp.float32
BF16 = jnp.bfloat16


def dot(left, right):
    return lax.dot_general(left, right, (((1,), (0,)), ((), ())), preferred_element_type=F32)


def dot_right(left, right):
    return lax.dot_general(left, right, (((1,), (1,)), ((), ())), preferred_element_type=F32)


def dot_left(left, right):
    return lax.dot_general(left, right, (((0,), (0,)), ((), ())), preferred_element_type=F32)


class Far:
    def __init__(self, value, pick=False):
        self.value, self.pick = value, pick


class Raw:
    def __init__(self, value):
        self.value = value


class Scalars:
    def __init__(self, value):
        self.value = value


class Flow:
    def __init__(self):
        self.loads, self.stores, self.sent = {}, {}, []

    def need(self, *refs):
        for ref in refs:
            copy = self.loads.pop(id(ref), None)
            if copy is not None:
                copy.wait()

    def send(self, *refs):
        for ref in refs:
            copy = self.stores.pop(id(ref), None)
            if copy is not None:
                copy.start()
                self.sent.append(copy)


class Steps:
    def __init__(self, where):
        self.where, self.token = where, None

    def batch(self, parts, name=None, cost=0.1):
        def kernel(flow, where, *refs):
            at, to = 0, sum(len(ins) for _, ins, _ in parts)
            for part, ins, outs in parts:
                part(flow, where, *refs[at : at + len(ins)], *refs[to : to + len(outs)])
                at, to = at + len(ins), to + len(outs)

        got = self(
            kernel, [v for _, ins, _ in parts for v in ins], [v for _, _, outs in parts for v in outs], name=name, cost=cost
        )
        results = []
        for _, _, outs in parts:
            results.append(got[: len(outs)])
            got = got[len(outs) :]
        return results

    def __call__(self, kernel, ins, outs, scratch=(), name=None, cost=0.1, hold=()):
        near = pl.BlockSpec(memory_space=pltpu.VMEM)
        far = pl.BlockSpec(memory_space=pltpu.HBM)
        words = pl.BlockSpec(memory_space=pltpu.SMEM)
        values, specs, stages = [], [], []
        for v in ins:
            if isinstance(v, Scalars):
                values.append(v.value)
                specs.append(words)
            elif isinstance(v, Raw):
                values.append(pltpu.with_memory_space_constraint(v.value, pltpu.HBM))
                specs.append(far)
            elif isinstance(v, Far):
                values.append(pltpu.with_memory_space_constraint(v.value, pltpu.HBM))
                specs.append(far)
                stages.append(pltpu.VMEM(v.value.shape[1:] if v.pick else v.value.shape, v.value.dtype))
            else:
                values.append(pltpu.with_memory_space_constraint(v, pltpu.VMEM))
                specs.append(near)
        after = [pltpu.with_memory_space_constraint(v, pltpu.VMEM) for v in hold]
        after_specs = [near] * len(after)
        if self.token is not None:
            after.append(pltpu.with_memory_space_constraint(self.token, pltpu.HBM))
            after_specs.append(far)
        for v in outs:
            if isinstance(v, Far):
                stages.append(pltpu.VMEM(*v.value))
        shapes = [pltpu.HBM(*v.value) if isinstance(v, (Far, Raw)) else pltpu.VMEM(*v) for v in outs]
        count, n_in, n_out, n_after = len(stages), len(ins), len(outs), len(after)

        def body(where_ref, *refs):
            refs = list(refs)
            in_refs, refs = refs[:n_in], refs[n_in + n_after :]
            out_refs, refs = refs[:n_out], refs[n_out + 1 :]
            stage_refs, refs = refs[:count], refs[count:]
            flow = Flow()
            if count:
                sems, refs = refs[0], refs[1:]
            given, k = [], 0
            for v, ref in zip(ins, in_refs):
                if isinstance(v, Far):
                    source = ref.at[where_ref[0]] if v.pick else ref
                    copy = pltpu.make_async_copy(source, stage_refs[k], sems.at[k])
                    copy.start()
                    flow.loads[id(stage_refs[k])] = copy
                    ref, k = stage_refs[k], k + 1
                given.append(ref)
            for v, ref in zip(outs, out_refs):
                if isinstance(v, Far):
                    flow.stores[id(stage_refs[k])] = pltpu.make_async_copy(stage_refs[k], ref, sems.at[k])
                    ref, k = stage_refs[k], k + 1
                given.append(ref)
            kernel(flow, where_ref, *given, *refs)
            for copy in flow.loads.values():
                copy.wait()
            for copy in flow.stores.values():
                copy.start()
            for copy in [*flow.sent, *flow.stores.values()]:
                copy.wait()

        results = pl.pallas_call(
            body,
            in_specs=[words] + specs + after_specs,
            out_specs=[far if isinstance(v, (Far, Raw)) else near for v in outs] + [far],
            out_shape=shapes + [pltpu.HBM((8, LANES), F32)],
            scratch_shapes=stages + ([pltpu.SemaphoreType.DMA((count,))] if count else []) + list(scratch),
            compiler_params=pltpu.CompilerParams(vmem_limit_bytes=24 * 1024 * 1024),
            cost_estimate=pl.CostEstimate(flops=10**6, bytes_accessed=int(cost * 3 * 10**6), transcendentals=0),
            name=name,
        )(self.where, *values, *after)
        self.token = results[-1]
        return list(results[:-1])


def row_blocks(seq):
    return [slice(start, start + BLOCK) for start in range(0, seq, BLOCK)]


def row_of(ref, i):
    return ref[i : i + 1, :].astype(F32)


GAIN, SHIFT, OUT, SCALE, VECTORS = 0, 3, 6, 9, 16


def norm_parts(value):
    centre = value - jnp.mean(value, axis=-1, keepdims=True)
    spread = jnp.mean(centre * centre, axis=-1, keepdims=True)
    scale = lax.rsqrt(spread + EPSILON)
    return centre * scale, scale


def norm_backward(value, gain, incoming):
    xhat, scale = norm_parts(value)
    weighted = incoming * gain
    grad = scale * (
        weighted
        - jnp.mean(weighted, axis=-1, keepdims=True)
        - xhat * jnp.mean(weighted * xhat, axis=-1, keepdims=True)
    )
    return grad, jnp.sum(incoming * xhat, axis=0, keepdims=True), jnp.sum(incoming, axis=0, keepdims=True)


def head_lanes(value, j):
    lane = lax.broadcasted_iota(jnp.int32, value.shape, 1)
    return jnp.where((lane >= HDIM) == bool(j), value, jnp.zeros_like(value))


def span_of(block, seq, banded):
    if not banded:
        return slice(0, seq)
    return slice(max(block.start - BLOCK, 0), block.stop)


def start_all(moves, sems):
    copies = [pltpu.make_async_copy(a, b, sems.at[i]) for i, (a, b) in enumerate(moves)]
    for copy in copies:
        copy.start()
    return copies


def setup_kernel(packing, flow, where, *refs):
    group_tokens, bucket_group, lengths, inputs, cotangent, memory, segments, gains, shifts, biases, refs = *refs[:10], refs[10:]
    if packing:
        query, kv, out, cross, refs = *refs[:4], refs[4:]
    x, cot, memory_part, vectors, molecules, tokens_now, group_now, lengths_now, word_sems, sems = refs
    words = start_all([(group_tokens, tokens_now), (bucket_group, group_now), (lengths, lengths_now)], word_sems)
    moves = [(memory.at[:, where[0]], memory_part), (inputs.at[where[0]], x), (cotangent.at[where[0]], cot)]
    if packing:
        full, wide = query.shape
        half = full // 2
        rows = pl.ds(pl.multiple_of(where[3] * half, half), half)
        moves += [
            (query.at[rows, :], cross.at[0:half, :]),
            (kv.at[0, rows, :], cross.at[half : 2 * half, :]),
            (kv.at[1, rows, :], cross.at[2 * half : 3 * half, :]),
        ]
        count, size = out.shape[1] // wide // 2, out.shape[0]
        for k in range(count):
            lanes = pl.ds(pl.multiple_of((where[3] * count + k) * wide, wide), wide)
            moves.append((out.at[:, lanes], cross.at[3 * half + k * size : 3 * half + (k + 1) * size, :]))
    copies = start_all(moves, sems)
    for copy in words:
        copy.wait()
    width = vectors.shape[1]
    total, own = 0, 0
    for b in range(bucket_group.shape[0]):
        tokens = tokens_now[group_now[b]]
        total = total + tokens
        own = own + jnp.where(where[2] == b, tokens, 0)
    scaled = jnp.full((1, width), bucket_group.shape[0] * own, jnp.int32).astype(F32)
    scale = scaled / jnp.full((1, width), total, jnp.int32).astype(F32)
    size = molecules.shape[1]
    place = lax.broadcasted_iota(jnp.int32, (1, size), 1)
    count, end = jnp.zeros((1, size), jnp.int32), 0
    for k in range(lengths.shape[1]):
        end = end + lengths_now[where[0], k]
        count = count + (end <= place).astype(jnp.int32)
    molecules[1:2, :] = count
    flow.need(segments, gains, shifts, biases)
    molecules[0:1, :] = segments[pl.ds(where[0], 1), :]
    rows = [r[...].astype(F32) for r in (gains, shifts, biases)] + [scale]
    vectors[...] = jnp.concatenate(rows + [jnp.zeros((VECTORS - 10, width), F32)], axis=0)
    for copy in copies:
        copy.wait()


def key_columns(keys):
    size = keys.shape[1]
    tiles = [jnp.broadcast_to(keys[:, at : at + BLOCK], (LANES, BLOCK)).T for at in range(0, size, BLOCK)]
    return jnp.concatenate(tiles, axis=0)


def allowed_of(own, columns, block, span, banded):
    allowed = columns[span] == own[:, block]
    if banded:
        query = lax.broadcasted_iota(jnp.int32, allowed.shape, 1) + block.start
        key = lax.broadcasted_iota(jnp.int32, allowed.shape, 0) + span.start
        allowed = allowed & (key <= query)
    return allowed


def head_rows(value, j):
    row = lax.broadcasted_iota(jnp.int32, value.shape, 0)
    return jnp.where((row >= HDIM) == bool(j), value, jnp.zeros_like(value))


def attend_forward(q, k, v, own, keys, heads, totals, banded):
    seq, wide = q.shape
    columns = key_columns(keys)
    for pair in range(wide // LANES):
        lanes = slice(pair * LANES, (pair + 1) * LANES)
        turned = [head_rows(v[:, lanes].T, j) for j in (0, 1)]
        for block in row_blocks(seq):
            span = span_of(block, k.shape[0], banded)
            allowed = allowed_of(own, columns, block, span, banded)
            query, keyset = q[block, lanes] * 0.125, k[span, lanes]
            mixed = None
            for j in (0, 1):
                scores = jnp.where(allowed, dot_right(keyset, head_lanes(query, j)), -1e30)
                maxima = jnp.max(scores, axis=0, keepdims=True)
                raised = jnp.exp(scores - maxima)
                total = jnp.sum(raised, axis=0, keepdims=True)
                chances = (raised * (1.0 / total)).astype(BF16)
                term = dot(turned[j][:, span], chances)
                mixed = term if mixed is None else mixed + term
                totals[2 * pair + j : 2 * pair + j + 1, block] = maxima + jnp.log(total)
            heads[block, lanes] = mixed.T.astype(BF16)


def attend_backward(q, k, v, own, keys, totals, grad_heads, dq, dk, dv, sum_k, sum_v, banded):
    seq, wide = q.shape
    columns = key_columns(keys)
    for pair in range(wide // LANES):
        lanes = slice(pair * LANES, (pair + 1) * LANES)
        turned = [head_rows(k[:, lanes].T, j) for j in (0, 1)]
        for at, block in enumerate(row_blocks(seq)):
            span = span_of(block, k.shape[0], banded)
            allowed = allowed_of(own, columns, block, span, banded)
            query, keyset, values = q[block, lanes] * 0.125, k[span, lanes], v[span, lanes]
            grad = grad_heads[block, lanes]
            grad_query = grad_key = grad_value = None
            for j in (0, 1):
                head = 2 * pair + j
                part, own_grad = head_lanes(query, j), head_lanes(grad, j)
                scores = jnp.where(allowed, dot_right(keyset, part), -1e30)
                chances = jnp.exp(scores - totals[head : head + 1, block])
                by_value = dot(chances.astype(BF16), own_grad)
                weighted = chances * dot_right(values, own_grad)
                mean = jnp.sum(weighted, axis=0, keepdims=True)
                grad_scores = (weighted - chances * mean).astype(BF16)
                by_query, by_key = dot(turned[j][:, span], grad_scores), dot(grad_scores, part)
                if j == 0:
                    grad_query, grad_key, grad_value = by_query, by_key, by_value
                else:
                    grad_query, grad_key, grad_value = grad_query + by_query, grad_key + by_key, grad_value + by_value
            dq[block, lanes] = (grad_query.T * 0.125).astype(BF16)
            if banded:
                early = block.start - span.start
                sum_k[block, lanes] = grad_key[early:]
                sum_v[block, lanes] = grad_value[early:]
                if early:
                    sum_k[span.start : block.start, lanes] += grad_key[:early]
                    sum_v[span.start : block.start, lanes] += grad_value[:early]
            elif at == 0:
                sum_k[:, lanes] = grad_key
                sum_v[:, lanes] = grad_value
            else:
                sum_k[:, lanes] += grad_key
                sum_v[:, lanes] += grad_value
    dk[...] = sum_k[...].astype(BF16)
    dv[...] = sum_v[...].astype(BF16)


def team_total(mine, theirs, block):
    half = mine[0].shape[0]
    k, rows = block.start // half, slice(block.start % half, block.start % half + BLOCK)
    return mine[k][rows, :].astype(F32) + theirs[k][rows, :].astype(F32)


def put_half(parts, block, value):
    half = parts[0].shape[0]
    start = block.start % half
    parts[block.start // half][start : start + BLOCK, :] = value.astype(parts[0].dtype)


def self_forward_kernel(n, i, flow, where, *refs):
    last = i == n - 1
    first, vectors, molecules, w, bias, refs = *refs[:5], refs[5:]
    if last:
        w_out, done, refs = refs[:n], refs[n : 2 * n - 1], refs[2 * n - 1 :]
    if i == 0:
        normed, refs = refs[0], refs[1:]
        for block in row_blocks(first.shape[0]):
            norm = norm_parts(first[block, :].astype(F32))[0]
            normed[block, :] = (norm * row_of(vectors, GAIN) + row_of(vectors, SHIFT)).astype(BF16)
    else:
        normed = first
    q, k, v, heads, totals = refs[:5]
    flow.need(w)
    q[...] = (dot(normed[...], w[0]) + row_of(bias, 0)).astype(BF16)
    k[...] = dot(normed[...], w[1]).astype(BF16)
    v[...] = (dot(normed[...], w[2]) + row_of(bias, 1)).astype(BF16)
    own = molecules[0:1, :]
    flow.send(q, k, v)
    attend_forward(q, k, v, own, own, heads, totals, True)
    flow.send(totals)
    if last:
        project_out(flow, [*done, heads], w_out, refs[5 : 5 + FRONT])


def project_out(flow, heads, w_out, parts):
    flow.need(*w_out)
    for block in row_blocks(heads[0].shape[0]):
        put_half(parts, block, sum(dot(h[block, :], w[...]) for h, w in zip(heads, w_out)))


def memory_kernel(flow, where, memory, w, bias, k, v):
    flow.need(w)
    k[...] = dot(memory[...], w[0]).astype(BF16)
    v[...] = (dot(memory[...], w[1]) + row_of(bias, 3)).astype(BF16)


def unpack_memory_kernel(flow, where, near, got, memory, bias, query, kv, out, k, v):
    full, wide = query.shape
    half, size = full // 2, out.shape[0]
    count = out.shape[1] // wide // 2
    for packed, bit in ((near, where[3]), (got, 1 - where[3])):
        rows = pl.ds(pl.multiple_of(bit * half, half), half)
        query[rows, :] = packed[:half]
        for i in (0, 1):
            kv[i, rows, :] = packed[(i + 1) * half : (i + 2) * half]
        for i in range(count):
            lanes = pl.ds(pl.multiple_of((bit * count + i) * wide, wide), wide)
            out[:, lanes] = packed[3 * half + i * size : 3 * half + (i + 1) * size]
    memory_kernel(flow, where, memory, kv, bias, k, v)


def cross_forward_kernel(n, i, flow, where, *refs):
    last = i == n - 1
    if i == 0:
        x, mine, theirs, refs = refs[0], refs[1 : 1 + FRONT], refs[1 + FRONT : 1 + 2 * FRONT], refs[1 + 2 * FRONT :]
    else:
        normed, refs = refs[0], refs[1:]
    vectors, molecules, w, bias, k, v, refs = *refs[:6], refs[6:]
    if last:
        w_out, done, refs = refs[:n], refs[n : 2 * n - 1], refs[2 * n - 1 :]
    if i == 0:
        after_self, normed, refs = refs[0], refs[1], refs[2:]
    q, heads, totals = refs[:3]
    if i == 0:
        for block in row_blocks(x.shape[0]):
            value = x[block, :].astype(F32) + team_total(mine, theirs, block) + row_of(vectors, OUT)
            after_self[block, :] = value
            norm = norm_parts(value)[0]
            normed[block, :] = (norm * row_of(vectors, GAIN + 1) + row_of(vectors, SHIFT + 1)).astype(BF16)
    flow.need(w)
    q[...] = (dot(normed[...], w[...]) + row_of(bias, 2)).astype(BF16)
    attend_forward(q, k, v, molecules[0:1, :], molecules[1:2, :], heads, totals, False)
    if last:
        project_out(flow, [*done, heads], w_out, refs[3 : 3 + FRONT])


def ffn_kernel(i, flow, where, *refs):
    if i == 0:
        after_self, mine, theirs, refs = refs[0], refs[1 : 1 + FRONT], refs[1 + FRONT : 1 + 2 * FRONT], refs[1 + 2 * FRONT :]
        cotangent, vectors, w_in, bias, w_out, refs = *refs[:5], refs[5:]
        after_cross, normed, low, active, grad_hidden, part, part_grad = refs
    else:
        normed, low, begun, begun_grad, w_in, w_out, bias, refs = *refs[:7], refs[7:]
        active, grad_hidden, parts, parts_grad = refs[0], refs[1], refs[2 : 2 + BACK], refs[2 + BACK :]
    if bias.shape[0] == 1:
        row = row_of(bias, 0)
    else:
        row = jnp.concatenate([row_of(bias, k) for k in range(4, bias.shape[0])], axis=1)
    if i == 0:
        for block in row_blocks(normed.shape[0]):
            value = after_self[block, :] + team_total(mine, theirs, block) + row_of(vectors, OUT + 1)
            after_cross[block, :] = value
            norm = norm_parts(value)[0]
            normed[block, :] = (norm * row_of(vectors, GAIN + 2) + row_of(vectors, SHIFT + 2)).astype(BF16)
            low[block, :] = (cotangent[block, :].astype(F32) * row_of(vectors, SCALE)).astype(BF16)
    flow.need(w_in, w_out)
    for block in row_blocks(normed.shape[0]):
        hidden = dot(normed[block, :], w_in[...]) + row
        cdf = 0.5 * (1.0 + lax.erf(hidden * 0.7071067811865476))
        act = (hidden * cdf).astype(BF16)
        active[block, :] = act
        slope = cdf + hidden * (0.3989422804014327 * jnp.exp(-0.5 * hidden * hidden))
        back = (slope * dot_right(low[block, :], w_out[...])).astype(BF16)
        grad_hidden[block, :] = back
        out, out_grad = dot(act, w_out[...]), dot_right(back, w_in[...])
        if i == 0:
            part[block, :], part_grad[block, :] = out, out_grad
        else:
            put_half(parts, block, begun[block, :] + out)
            put_half(parts_grad, block, begun_grad[block, :] + out_grad)


def ffn_weights_kernel(flow, where, *refs):
    hidden, active, normed, low, sums = refs[:2], refs[2:4], refs[4], refs[5], refs[6]
    keep_out, send_out, keep_in, send_in = refs[7:]
    half = keep_in.shape[1]
    for i in (0, 1):
        for target, bit in ((keep_in, where[3]), (send_in, 1 - where[3])):
            lanes = pl.ds(pl.multiple_of(bit * half, half), half)
            target[i] = dot_left(hidden[i][:, lanes], normed[...]).astype(target.dtype)
        sums[i : i + 1, :] = jnp.sum(hidden[i][...].astype(F32), axis=0, keepdims=True)
    keep_out[0] = dot_left(active[0][...], low[...])
    send_out[0] = dot_left(active[1][...], low[...]).astype(BF16)


def spread_grad_heads(low, w_out, grad_heads):
    for piece, target in zip(w_out, grad_heads):
        target[...] = dot_right(low[...], piece[...]).astype(BF16)


def column_sums(sums, values):
    for i, value in enumerate(values):
        sums[i : i + 1, :] = jnp.sum(value[...].astype(F32), axis=0, keepdims=True)


def cross_backward_kernel(n, flow, where, *refs):
    after_cross, mine, theirs, refs = refs[0], refs[1 : 1 + BACK], refs[1 + BACK : 1 + 2 * BACK], refs[1 + 2 * BACK :]
    cotangent, vectors, molecules, refs = *refs[:3], refs[3:]
    (q, k, v, totals, w_out, w), refs = [refs[i * n : (i + 1) * n] for i in range(6)], refs[6 * n :]
    grad_cross, low, refs = refs[0], refs[1], refs[2:]
    (dq, dk, dv, bias_sums), refs = [refs[i * n : (i + 1) * n] for i in range(4)], refs[4 * n :]
    parts_out, sums, refs = refs[:BACK], refs[BACK], refs[BACK + 1 :]
    grad_heads, sum_k, sum_v = refs[:n], refs[n], refs[n + 1]
    seq, width = after_cross.shape
    rows = [jnp.zeros((1, width), F32)] * 3
    for block in row_blocks(seq):
        incoming = team_total(mine, theirs, block)
        grad_result = cotangent[block, :].astype(F32) * row_of(vectors, SCALE)
        back, by_gain, by_shift = norm_backward(after_cross[block, :], row_of(vectors, GAIN + 2), incoming)
        value = grad_result + back
        grad_cross[block, :] = value
        low[block, :] = value.astype(BF16)
        parts = (by_gain, by_shift, jnp.sum(grad_result, axis=0, keepdims=True))
        rows = [a + b for a, b in zip(rows, parts)]
    for i, row in enumerate(rows):
        sums[i : i + 1, :] = row
    flow.need(*w_out)
    spread_grad_heads(low, w_out, grad_heads)
    own, keys = molecules[0:1, :], molecules[1:2, :]
    for i in range(n):
        attend_backward(
            q[i], k[i], v[i], own, keys, totals[i], grad_heads[i], dq[i], dk[i], dv[i], sum_k, sum_v, False
        )
        column_sums(bias_sums[i], (dq[i], dv[i]))
    flow.need(*w)
    for block in row_blocks(seq):
        put_half(parts_out, block, sum(dot_right(d[block, :], m[...]) for d, m in zip(dq, w)))


def shard_grads(kinds):
    grads = ([], [])
    for kind in kinds:
        if len(kind) == 2:
            for i in (0, 1):
                grads[i].append(dot_left(kind[i][0][...], kind[i][1][...]))
        else:
            left, right = kind[0]
            both, half = dot_left(left[...], right[...]), left.shape[1] // 2
            grads[0].append(both[:half])
            grads[1].append(both[half:])
    return grads


def cross_weights_kernel(n, flow, where, *refs):
    (dq, dk, dv, heads, w), refs = [refs[i * n : (i + 1) * n] for i in range(5)], refs[5 * n :]
    normed, memory, low, after_cross, refs = *refs[:4], refs[4:]
    mine, theirs, vectors, refs = refs[:BACK], refs[BACK : 2 * BACK], refs[2 * BACK], refs[2 * BACK + 1 :]
    keep, send, terms, result = refs[0], refs[1], refs[2 : 2 + BACK], refs[-1]
    flow.need(*w)
    pairs = [[(a, b) for a in left] for left, b in ((dq, normed), (dk, memory), (dv, memory), (heads, low))]
    first = where[4] == 0
    for i, grads in enumerate(shard_grads(pairs)):
        upper, lower = jnp.concatenate(grads[:2], axis=0), jnp.concatenate(grads[2:], axis=0)
        keep[i] = jnp.where(first, upper, lower)
        send[i] = jnp.where(first, lower, upper).astype(BF16)
    for block in row_blocks(memory.shape[0]):
        total = sum(
            dot_right(a[block, :], m[0]) + dot_right(b[block, :], m[1]) for a, b, m in zip(dk, dv, w)
        )
        put_half(terms, block, total)
    for block in row_blocks(after_cross.shape[0]):
        both = team_total(mine, theirs, block)
        result[block, :] = (after_cross[block, :] + both + row_of(vectors, OUT + 2)).astype(BF16)


def self_backward_kernel(n, flow, where, *refs):
    after_self, mine, theirs, refs = refs[0], refs[1 : 1 + BACK], refs[1 + BACK : 1 + 2 * BACK], refs[1 + 2 * BACK :]
    grad_cross, vectors, molecules, refs = *refs[:3], refs[3:]
    (q, k, v, totals, w_out), refs = [refs[i * n : (i + 1) * n] for i in range(5)], refs[5 * n :]
    grad_self, low, refs = refs[0], refs[1], refs[2:]
    (dq, dk, dv, bias_sums), refs = [refs[i * n : (i + 1) * n] for i in range(4)], refs[4 * n :]
    sums, refs = refs[0], refs[1:]
    grad_heads, sum_k, sum_v = refs[:n], refs[n], refs[n + 1]
    seq, width = after_self.shape
    rows = [jnp.zeros((1, width), F32)] * 3
    for block in row_blocks(seq):
        incoming = team_total(mine, theirs, block)
        back, by_gain, by_shift = norm_backward(after_self[block, :], row_of(vectors, GAIN + 1), incoming)
        upper = grad_cross[block, :]
        value = upper + back
        grad_self[block, :] = value
        low[block, :] = value.astype(BF16)
        parts = (by_gain, by_shift, jnp.sum(upper, axis=0, keepdims=True))
        rows = [a + b for a, b in zip(rows, parts)]
    for i, row in enumerate(rows):
        sums[i : i + 1, :] = row
    flow.need(*w_out)
    spread_grad_heads(low, w_out, grad_heads)
    own = molecules[0:1, :]
    flow.need(*q, *k, *v, *totals)
    for i in range(n):
        attend_backward(
            q[i], k[i], v[i], own, own, totals[i], grad_heads[i], dq[i], dk[i], dv[i], sum_k, sum_v, True
        )
        column_sums(bias_sums[i], (dq[i], dv[i]))


def input_backward_kernel(n, flow, where, x, *refs):
    mine, theirs, refs = refs[:BACK], refs[BACK : 2 * BACK], refs[2 * BACK :]
    grad_self, vectors, result, by_cross, by_ffn, refs = *refs[:5], refs[5:]
    shard_rows, (both, small_own, small_other) = refs[:-3], refs[-3:]
    seq = x.shape[0]
    both[:seq, :] = result[...]
    width = x.shape[1]
    rows = [jnp.zeros((1, width), F32)] * 3
    for block in row_blocks(x.shape[0]):
        incoming = team_total(mine, theirs, block)
        back, by_gain, by_shift = norm_backward(x[block, :].astype(F32), row_of(vectors, GAIN), incoming)
        upper = grad_self[block, :]
        both[seq + block.start : seq + block.stop, :] = (upper + back).astype(BF16)
        parts = (by_gain, by_shift, jnp.sum(upper, axis=0, keepdims=True))
        rows = [a + b for a, b in zip(rows, parts)]
    common = [r for k in range(3) for r in (rows[k], by_cross[k : k + 1, :], by_ffn[k : k + 1, :])]
    if len(shard_rows) == 1:
        lines = [shard_rows[0][i] for i in (0, 1)]
    else:
        sums_self, sums_cross, sums_ffn = shard_rows[:n], shard_rows[n : 2 * n], shard_rows[2 * n]
        lines = []
        for i in (0, 1):
            pieces = [r[k : k + 1, :] for r in (sums_self[i], sums_cross[i]) for k in (0, 1)]
            lines.append(jnp.concatenate([jnp.concatenate(pieces, axis=1), sums_ffn[i : i + 1, :]], axis=0))
    rest = jnp.zeros((SMALL - 9 - lines[0].shape[0], width), F32)
    small = [jnp.concatenate([*common, line, rest], axis=0).astype(BF16) for line in lines]
    small_own[...] = small[0]
    small_other[...] = small[1]


def self_weights_kernel(n, flow, where, *refs):
    (dq, dk, dv, heads, w), refs = [refs[i * n : (i + 1) * n] for i in range(5)], refs[5 * n :]
    normed, low, parts_out, keep, send = refs[0], refs[1], refs[2 : 2 + BACK], refs[-2], refs[-1]
    pairs = [[(a, b) for a in left] for left, b in ((dq, normed), (dk, normed), (dv, normed), (heads, low))]
    for target, grads in zip((keep, send), shard_grads(pairs)):
        size = grads[0].shape[0]
        for k, grad in enumerate(grads):
            target[0, k * size : (k + 1) * size, :] = grad.astype(target.dtype)
    flow.need(*w)
    for block in row_blocks(normed.shape[0]):
        total = 0.0
        for i in range(n):
            for which, d in enumerate((dq[i], dk[i], dv[i])):
                total += dot_right(d[block, :], w[i][which])
        put_half(parts_out, block, total)


def fold_kernel(count, ride, mode, bit, flow, where, *refs):
    keeps, gots, refs = refs[:count], refs[count : 2 * count], refs[2 * count :]
    planes = [(k, p) for k in range(count) for p in range(keeps[k].shape[0])]
    size = keeps[0].shape[1]

    def part(at, rows):
        k, p = planes[at]
        return keeps[k][p, rows, :].astype(F32) + gots[k][p, rows, :].astype(F32)

    if mode == "half":
        keep, send = refs
        half = size // 2
        for at in range(len(planes)):
            for target, side in ((keep, where[3 + bit]), (send, 1 - where[3 + bit])):
                rows = pl.ds(pl.multiple_of(side * half, half), half)
                target[at] = part(at, rows).astype(target.dtype)
    elif mode == "shard":
        if ride:
            refs[2][0, size:, :] = refs[0][...]
        for at, target in enumerate(refs[-2:]):
            target[0, :size, :] = part(at, slice(0, size)).astype(target.dtype)
    else:
        out = refs[-1]
        for at in range(len(planes)):
            value = part(at, slice(0, size))
            if ride and mode == "full":
                own, came = refs[:2]
                last = came.shape[1]
                small = own[...].astype(F32) + came[0, last - SMALL : last, :].astype(F32)
                value = jnp.concatenate([value, small], axis=0)
            out[at] = value.astype(out.dtype)


def join_kernel(ride, bit, flow, where, near, got, out):
    half = near.shape[1] - (SMALL if ride else 0)
    for value, side in ((near, where[3 + bit]), (got, 1 - where[3 + bit])):
        rows = pl.ds(pl.multiple_of(side * half, half), half)
        for p in range(near.shape[0]):
            out[p, rows, :] = value[p, :half]
    if ride:
        out[0, 2 * half :, :] = (near[0, half:].astype(F32) + got[0, half:].astype(F32)).astype(BF16)


def joined(where, bit, near, got, p, ride=0):
    first = where[3 + bit] == 0
    size = near.shape[1] - ride
    a, b = near[p, :size], got[p, :size]
    rows = [jnp.where(first, a, b), jnp.where(first, b, a)]
    return jnp.concatenate(rows, axis=0).astype(F32)


def self_grads_kernel(bit, flow, where, near, got, qkv, out, gains, shifts, biases, *rest):
    size = near.shape[1] - SMALL
    small = near[0, size:].astype(F32) + got[0, size:].astype(F32)
    for k, target in enumerate((gains, shifts, biases)):
        target[...] = small[3 * k : 3 * k + 3]
    if len(rest) == 1:
        rest[0][...] = small[9 : 9 + rest[0].shape[0]]
    else:
        for k, target in enumerate(rest[:2]):
            wide = target.shape[1]
            for i in (0, 1):
                at = (2 * k + i) * wide
                target[i : i + 1, :] = small[9:10, at : at + wide]
        rest[2][...] = small[10:11]
    flow.send(gains, shifts, biases, *rest)
    value = joined(where, bit, near, got, 0, SMALL)
    size = out.shape[0]
    for k in range(3):
        qkv[k] = value[k * size : (k + 1) * size].T
    out[...] = value[3 * size :]


def cross_grads_kernel(bit, flow, where, near, got, query, kv, out):
    half = near.shape[1] // 2
    value = [joined(where, bit, near[:, k * half : (k + 1) * half], got[:, k * half : (k + 1) * half], 0) for k in (0, 1)]
    value = jnp.concatenate(value, axis=0)
    size = out.shape[0]
    query[...] = value[:size].T
    for k in (0, 1):
        kv[k] = value[(k + 1) * size : (k + 2) * size].T
    out[...] = value[3 * size :]


def widen_kernel(flow, where, value, out):
    out[...] = value[...].astype(out.dtype)


def ffn_grads_kernel(bit, flow, where, near, got, grad_in, grad_out):
    grad_out[...] = joined(where, bit, near, got, 0)
    flow.send(grad_out)
    grad_in[...] = joined(where, bit, near, got, 1).T


def place_rows_kernel(flow, where, own, got, mixed, grad):
    seq = own.shape[0] // 2
    for k, out in enumerate((mixed, grad)):
        for row, value in ((where[0], own), (1 - where[0], got)):
            out[row] = value[k * seq : (k + 1) * seq, :].astype(out.dtype)
        flow.send(out)


def memory_blocks_kernel(flow, where, *refs):
    mine, theirs, out = refs[:BACK], refs[BACK : 2 * BACK], refs[2 * BACK]
    dp, rows, tokens, share = out.shape
    half, width = mine[0].shape
    team = width // (rows * share)
    for r in range(rows):
        lanes = pl.ds(pl.multiple_of((r * team + where[1]) * share, share), share)
        for k in range(BACK):
            total = (mine[k][:, lanes].astype(F32) + theirs[k][:, lanes].astype(F32)).astype(BF16)
            for d in range(half // tokens):
                out[k * half // tokens + d, r] = total[d * tokens : (d + 1) * tokens]


def shards(
    inputs,
    memory,
    segment_ids,
    mem_lengths,
    bucket_group,
    group_tokens,
    norm_gain,
    norm_bias,
    self_qkv,
    self_bias,
    self_out,
    cross_q,
    cross_kv,
    cross_bias,
    cross_out,
    ffn_in,
    ffn_bias,
    ffn_out,
    out_bias,
    cotangent,
):
    dp, mp = lax.axis_size("dp"), lax.axis_size("mp")
    rows, seq, width = inputs.shape
    team = mp // rows
    data, place = lax.axis_index("dp"), lax.axis_index("mp")
    row, seat = place // team, place % team
    bits = dp.bit_length() - 1
    where = jnp.stack([row, seat, data] + [(data >> k) & 1 for k in range(bits)]).astype(jnp.int32)
    run, far = Steps(where), Far

    across = [(i, (i + team) % mp) for i in range(mp)]

    def other(value):
        return lax.ppermute(value, "mp", across)

    def seat_swap(value, step):
        return lax.ppermute(value, "mp", [(i, i ^ step) for i in range(mp)])

    def data_swap(value, k):
        return lax.ppermute(value, "dp", [(i, i ^ (1 << k)) for i in range(dp)])

    def swap(value, axis):
        return other(value) if axis == "row" else data_swap(value, axis)

    def later(value, *after):
        return lax.optimization_barrier((value, *after))[0]

    def team_parts(values):
        step = 1
        while 2 * step < team:
            values = [(v.astype(F32) + seat_swap(v, step).astype(F32)).astype(BF16) for v in values]
            step *= 2
        return [*values, *(seat_swap(v, step) for v in values)]

    head, unit = self_bias.shape[1], ffn_bias.shape[0]
    mem_len = memory.shape[1] * dp
    apart = head % LANES == 0
    n = 2 if apart else 1
    wide = head if apart else 2 * head

    front = [((seq // FRONT, width), BF16)] * FRONT
    back = [((seq // BACK, width), BF16)] * BACK
    whole, full = ((seq, width), BF16), ((seq, width), F32)
    local, totals = ((seq, wide), BF16), ((2 * wide // LANES, seq), F32)
    units = ((seq, unit), BF16)

    other_qkv = other(self_qkv)
    bias_own = jnp.concatenate([self_bias, cross_bias, ffn_bias.reshape(-1, head)])
    bias_other = other(bias_own)
    other_self_out = other(self_out)
    memory_rows = memory.reshape((dp, rows) + memory.shape[1:])
    packing = apart and width % (2 * head) == 0
    ins = [Raw(group_tokens), Raw(bucket_group), Raw(mem_lengths), Raw(inputs), Raw(cotangent), Raw(memory_rows)]
    ins += [far(segment_ids), far(norm_gain), far(norm_bias), far(out_bias)]
    outs = [whole, whole, ((dp,) + memory.shape[1:], BF16), ((VECTORS, width), F32), ((2, seq), jnp.int32)]
    if packing:
        ins += [Raw(v) for v in (cross_q, cross_kv, cross_out)]
        outs = [((3 * width // 2 + cross_out.size // head // 2, head), BF16)] + outs
    *packed, x, cot, memory_part, vectors, molecules = run(
        functools.partial(setup_kernel, packing),
        ins,
        outs,
        scratch=[pltpu.SMEM(v.shape, jnp.int32) for v in (group_tokens, bucket_group, mem_lengths)]
        + [pltpu.SemaphoreType.DMA((3,)), pltpu.SemaphoreType.DMA((6 + width // head // 2,))],
        name="setup",
    )
    memory_row = lax.all_to_all(memory_part, "dp", split_axis=0, concat_axis=0, tiled=True).reshape(mem_len, width)
    def pieces(own, theirs, axis):
        return [far(own), theirs] if apart else [jnp.concatenate([own, theirs], axis=axis)]

    w_qkv = pieces(self_qkv, other_qkv, 2)
    w_self_out = pieces(self_out, other_self_out, 0)
    b_heads = [bias_own, bias_other] if apart else [jnp.concatenate([bias_own, bias_other], axis=1)]
    b_in = b_heads if apart else [b[4:].reshape(1, unit) for b in (bias_own, bias_other)]

    heads_self, saved_self = [], []
    for i in range(n):
        last = i == n - 1
        ins = [x if i == 0 else normed_self, vectors, molecules, w_qkv[i], b_heads[i]]
        outs = ([whole] if i == 0 else []) + [far(local)] * 3 + [local, far(totals)]
        if last:
            ins += [*w_self_out, *heads_self]
            outs += front
        hold = [near_cross] if packing and i == 1 else []
        got = run(functools.partial(self_forward_kernel, n, i), ins, outs, name=f"self_forward_{i}", hold=hold)
        if i == 0:
            normed_self, got = got[0], got[1:]
            early = (normed_self, other_qkv, bias_other, other_self_out)
            if packing:
                near_cross = other(later(packed[0], *early))
                got_cross = data_swap(near_cross, 0)
                other_in, other_out = [other(later(w, near_cross)) for w in (ffn_in, ffn_out)]
            else:
                other_cross = [other(later(w, *early)) for w in (cross_q, cross_kv, cross_out)]
                other_in, other_out = [other(later(w, *other_cross)) for w in (ffn_in, ffn_out)]
        saved_self.append((got[0], got[1], got[2], got[4]))
        heads_self.append(got[3])
    terms = team_parts(got[5:])

    heads_cross, saved_cross = [], []
    if apart:
        w_cross_q, w_cross_kv, w_cross_out = [far(cross_q)], [far(cross_kv)], [far(cross_out)]
    else:
        w_cross_q = pieces(cross_q, other_cross[0], 1)
        w_cross_kv = pieces(cross_kv, other_cross[1], 2)
        w_cross_out = pieces(cross_out, other_cross[2], 0)
    projected = ((mem_len, wide), BF16)
    for i in range(n):
        last = i == n - 1
        if i == 1 and packing:
            query, both, out, *kv = run(
                unpack_memory_kernel,
                [near_cross, got_cross, memory_row, b_heads[1]],
                [(v.shape, BF16) for v in (cross_q, cross_kv, cross_out)] + [projected] * 2,
                name="memory_1",
            )
            for pieces_of, w in ((w_cross_q, query), (w_cross_kv, both), (w_cross_out, out)):
                pieces_of.append(w)
        else:
            if i == 1:
                for pieces_of, w in zip((w_cross_q, w_cross_kv, w_cross_out), other_cross):
                    pieces_of.append(w)
            kv = run(memory_kernel, [memory_row, w_cross_kv[i], b_heads[i]], [projected] * 2, name=f"memory_{i}")
        first = [x, *terms] if i == 0 else [normed_cross]
        ins = first + [vectors, molecules, w_cross_q[i], b_heads[i], *kv]
        outs = ([full, whole] if i == 0 else []) + [local] * 2 + [totals]
        if last:
            ins += [*w_cross_out, *heads_cross]
            outs += front
        got = run(functools.partial(cross_forward_kernel, n, i), ins, outs, name=f"cross_forward_{i}")
        if i == 0:
            after_self, normed_cross, got = got[0], got[1], got[2:]
        saved_cross.append((got[0], *kv, got[2]))
        heads_cross.append(got[1])
    terms = team_parts(got[3:])

    after_cross, normed_ffn, low_ffn, act_own, hid_own, begun, begun_grad = run(
        functools.partial(ffn_kernel, 0),
        [after_self, *terms, cot, vectors, far(ffn_in), b_in[0], far(ffn_out)],
        [full, whole, whole, units, units, full, full],
        name="ffn_0",
    )
    ins = [other_in, other_out, b_in[1]]
    act_other, hid_other, *parts = run(
        functools.partial(ffn_kernel, 1),
        [normed_ffn, low_ffn, begun, begun_grad, *ins],
        [units, units] + back + back,
        name="ffn_1",
    )
    terms = team_parts(parts[BACK:])
    out_terms = team_parts(parts[:BACK])

    class Reduction:
        def __init__(self, keeps, sends, axes):
            self.keeps, self.axes, self.ride, self.carry, self.turned = keeps, axes, [], [], False
            self.gots = [swap(s, a) for s, a in zip(sends, axes[0])]
            self.halved = [b for b in axes[0] if b != "row"][:1]
            self.chunk = None

        def plan(self):
            extra = SMALL if self.ride else 0
            if self.chunk is not None:
                bit = self.halved.pop()
                planes, size, _ = self.chunk.shape
                outs = [((planes, 2 * size - extra, width), BF16)]
                return functools.partial(join_kernel, bool(extra), bit), [self.chunk, self.got], outs
            axes, keeps, ride = self.axes, self.keeps, []
            planes = sum(k.shape[0] for k in keeps)
            size = keeps[0].shape[1]
            bit = 0
            if len(axes) == 1:
                mode, outs = "last", [((planes, size, width), BF16)]
            elif axes[1][0] == "row":
                mode, ride = "shard", self.carry
                outs = [((1, size, width), F32), ((1, size + (SMALL if ride else 0), width), BF16)]
            elif len(axes) == 2:
                mode, ride, outs = "full", self.ride, [((planes, size + extra, width), BF16)]
            else:
                mode, bit, shape = "half", axes[1][0], (planes, size // 2, width)
                outs = [(shape, F32), (shape, BF16)]
                self.halved.append(bit)
            return functools.partial(fold_kernel, len(keeps), bool(ride), mode, bit), [*keeps, *self.gots, *ride], outs

        def take(self, got):
            if self.chunk is not None or len(self.axes) == 1:
                if self.chunk is None and self.turned:
                    self.halved[:2] = self.halved[1::-1]
                self.chunk = got[0]
                self.got = swap(self.chunk, self.halved[-1])
            else:
                self.axes = self.axes[1:]
                self.keeps = [got[0]]
                self.gots = [swap(got[-1], self.axes[0][0])]

        def ready(self):
            return self.chunk is not None and len(self.halved) == 1

    def advance(name, *groups, cost=0.1):
        groups = [g for g in groups if not g.ready()]
        if groups:
            for g, got in zip(groups, run.batch([g.plan() for g in groups], name=name, cost=cost)):
                g.take(got)

    ffn_sums, keep_out, send_out, keep_in, send_in = run(
        ffn_weights_kernel,
        [hid_own, hid_other, act_own, act_other, normed_ffn, low_ffn],
        [((2, unit), F32), ((1, unit, width), F32), ((1, unit, width), BF16)]
        + [((2, unit // 2, width), F32), ((2, unit // 2, width), BF16)],
        name="ffn_weights",
    )
    by_out = Reduction([keep_out], [send_out], [["row"], [0], [1]])
    by_in = Reduction([keep_in], [send_in], [[0], ["row"], [1]])

    scratch = [pltpu.VMEM((seq, wide), BF16)] * n + [pltpu.VMEM((seq, wide), F32)] * 2
    bias_sum = ((2, wide), F32)

    def saved_of(saved):
        return [s[k] for k in range(4) for s in saved]

    got = run(
        functools.partial(cross_backward_kernel, n),
        [after_cross, *terms, cot, vectors, molecules]
        + saved_of(saved_cross) + [*w_cross_out, *w_cross_q],
        [full, whole] + [local] * (3 * n) + [bias_sum] * n + back + [((3, width), F32)],
        scratch=scratch,
        name="cross_backward",
    )
    grad_cross, low_cross, got = got[0], got[1], got[2:]
    cross_grads, cross_bias_sums, got = got[: 3 * n], got[3 * n : 4 * n], got[4 * n :]
    terms, small_ffn = team_parts(got[:BACK]), got[BACK]
    keep, send, *memory_terms, result = run(
        functools.partial(cross_weights_kernel, n),
        [*cross_grads, *heads_cross, *w_cross_kv]
        + [normed_cross, memory_row, low_cross, after_cross, *out_terms, vectors],
        [((2, 2 * head, width), F32), ((2, 2 * head, width), BF16)] + back + [whole],
        name="cross_weights",
    )
    by_cross = Reduction([keep], [send], [[1], [0], ["row"]] + [[k] for k in range(2, bits)])
    by_cross.turned = True
    advance("fold_ffn", by_out, by_in)

    got = run(
        functools.partial(self_backward_kernel, n),
        [after_self, *terms, grad_cross, vectors, molecules] + [far(v) for v in saved_of(saved_self)] + [*w_self_out],
        [full, whole] + [local] * (3 * n) + [bias_sum] * n + [((3, width), F32)],
        scratch=scratch,
        name="self_backward",
    )
    grad_self, low_self, got = got[0], got[1], got[2:]
    self_grads, self_bias_sums, small_cross = got[: 3 * n], got[3 * n : 4 * n], got[4 * n]
    by_ffn = by_out
    by_ffn.keeps, by_ffn.gots = by_out.keeps + by_in.keeps, by_out.gots + by_in.gots
    by_ffn.axes = [[0]] + [[k] for k in range(1, bits)]
    advance("ffn_1", by_ffn)
    *parts, keep, send = run(
        functools.partial(self_weights_kernel, n),
        [*self_grads, *heads_self, *w_qkv, normed_self, low_self],
        back + [((1, 4 * head, width), F32), ((1, 4 * head, width), BF16)],
        name="self_weights",
    )
    by_self = Reduction([keep], [send], [["row"]] + [[k] for k in range(bits)])
    terms = team_parts(parts)
    advance("cross_1", by_cross)
    advance("ffn_2", by_ffn)
    mem_terms = team_parts(memory_terms)
    share = width // mp
    if share % LANES == 0 and team == 2:
        (blocks,) = run(
            memory_blocks_kernel, mem_terms, [((dp, rows, mem_len // dp, share), BF16)], name="memory_blocks"
        )
    else:
        mine, theirs = jnp.concatenate(mem_terms[:BACK]), jnp.concatenate(mem_terms[BACK:])
        total = (mine.astype(F32) + theirs.astype(F32)).astype(BF16)
        total = total.reshape(dp, mem_len // dp, rows, team, share)
        blocks = lax.dynamic_index_in_dim(total, seat, 3, keepdims=False).swapaxes(1, 2)
    blocks = blocks.reshape(dp * rows, mem_len // dp, share)
    same_seat = [[d * mp + m for d in range(dp) for m in range(mp) if m % team == s] for s in range(team)]
    memory_got = lax.all_to_all(
        blocks, ("dp", "mp"), split_axis=0, concat_axis=0, tiled=True, axis_index_groups=same_seat
    )


    fits = apart and 4 * head == width and unit == width
    if fits:
        shard_rows = [*self_bias_sums, *cross_bias_sums, ffn_sums]
        lines = 2
    else:

        def by_shard(sums):
            return sums if n == 2 else [sums[0][:, :head], sums[0][:, head:]]

        shard_rows = [
            jnp.stack(
                [
                    jnp.concatenate([a.reshape(-1), b.reshape(-1), ffn_sums[i]]).reshape(-1, width)
                    for i, (a, b) in enumerate(zip(by_shard(self_bias_sums), by_shard(cross_bias_sums)))
                ]
            )
        ]
        lines = shard_rows[0].shape[1]
    both, small_own, small_other = run(
        functools.partial(input_backward_kernel, n),
        [x, *terms, grad_self, vectors, result, small_cross, small_ffn, *shard_rows],
        [((2 * seq, width), BF16)] + [((SMALL, width), BF16)] * 2,
        name="input_backward",
    )

    by_cross.carry = [small_other]

    advance("cross_2", by_cross)
    by_self.ride = [small_own, by_cross.gots[0]]
    advance("self_1", by_self)
    advance("all_1", by_self, by_ffn, by_cross)
    got_both = other(later(both, by_self.keeps[0]))
    (grad_memory,) = run(widen_kernel, [memory_got], [far((memory_got.shape, F32))], name="widen_memory")
    advance("all_2", by_self, by_ffn, by_cross)
    advance("self_cross_3", by_self, by_cross)
    while not (by_self.ready() and by_cross.ready() and by_ffn.ready()):
        advance("rest", by_self, by_cross, by_ffn)
    mixed, grad_inputs = run(
        place_rows_kernel,
        [both, got_both],
        [far(((rows, seq, width), BF16)), far(((rows, seq, width), F32))],
        name="place_rows",
    )
    grad_ffn_in, grad_ffn_out = run(
        functools.partial(ffn_grads_kernel, by_ffn.halved[0]),
        [by_ffn.chunk, by_ffn.got],
        [far(((width, unit), F32)), far(((unit, width), F32))],
        name="ffn_grads",
    )
    grad_cross_q, grad_cross_kv, grad_cross_out = run(
        functools.partial(cross_grads_kernel, by_cross.halved[0]),
        [by_cross.chunk, by_cross.got],
        [far(((width, head), F32)), far(((2, width, head), F32)), far(((head, width), F32))],
        name="cross_grads",
    )
    if fits:
        outs = [((2, head), F32), ((2, head), F32), ((1, unit), F32)]
    else:
        outs = [((lines, width), F32)]
    grad_self_qkv, grad_self_out, grad_gain, grad_shift, grad_out_bias, *rest = run(
        functools.partial(self_grads_kernel, by_self.halved[0]),
        [by_self.chunk, by_self.got],
        [far(((3, width, head), F32)), far(((head, width), F32))] + [far(((3, width), F32))] * 3 + [far(v) for v in outs],
        name="self_grads",
    )
    if fits:
        grad_self_bias, grad_cross_bias, grad_ffn_bias = rest[0], rest[1], rest[2].reshape(-1)
    else:
        own_small = rest[0].reshape(-1)
        grad_self_bias = own_small[: 2 * head].reshape(2, head)
        grad_cross_bias = own_small[2 * head : 4 * head].reshape(2, head)
        grad_ffn_bias = own_small[4 * head :]
    return (
        mixed,
        grad_inputs,
        grad_memory,
        grad_gain,
        grad_shift,
        grad_self_qkv,
        grad_self_bias,
        grad_self_out,
        grad_cross_q,
        grad_cross_kv,
        grad_cross_bias,
        grad_cross_out,
        grad_ffn_in,
        grad_ffn_bias,
        grad_ffn_out,
        grad_out_bias,
    )


def solution(mesh):
    placed = (
        P("dp", None, None),
        P(None, "dp", None),
        P("dp", None),
        P("dp", None),
        P(),
        P(),
        P(),
        P(),
        P(None, None, "mp"),
        P(None, "mp"),
        P("mp", None),
        P(None, "mp"),
        P(None, None, "mp"),
        P(None, "mp"),
        P("mp", None),
        P(None, "mp"),
        P("mp"),
        P("mp", None),
        P(),
        P("dp", None, None),
    )
    return jax.shard_map(
        shards,
        mesh=mesh,
        in_specs=placed,
        out_specs=(
            P("dp", None, None),
            P("dp", None, None),
            P(None, "dp", "mp"),
            P(),
            P(),
            P(None, None, "mp"),
            P(None, "mp"),
            P("mp", None),
            P(None, "mp"),
            P(None, None, "mp"),
            P(None, "mp"),
            P("mp", None),
            P(None, "mp"),
            P("mp"),
            P("mp", None),
            P(),
        ),
        check_vma=False,
    )
```

time: 196 us -> 165 us (0.84)
  waiting for transfers between devices: 54.2 us -> 41.6 us
  Pallas kernels: 76.6 us -> 69.5 us
  local copies, waits for them, and re-layouts: 8.55 us -> 2.42 us
  starting transfers between devices: 53 us -> 49 us
    ppermute x14 -> x11, waiting for transfers between devices: 25.9 us -> 12 us  [other(): return lax.ppermute(value, 'mp', across)]
    pallas_call x39 -> x31, Pallas kernels: 76.6 us -> 69.5 us  [__call__(): pl.pallas_call(body, in_specs=[words] + specs + after_specs, out_specs=[f...]
    unnamed x60 -> x20, local copies, waits for them, and re-layouts: 5.84 us -> 2.34 us
    ppermute x9 -> x14, waiting for transfers between devices: 0.02 us -> 2.45 us  [seat_swap(): return lax.ppermute(value, 'mp', [(i, i ^ step) for i in range(mp)])]
    ppermute x18 -> x17, starting transfers between devices: 23.8 us -> 21.4 us  [data_swap(): return lax.ppermute(value, 'dp', [(i, i ^ 1 << k) for i in range(dp)])]
    ppermute x18 -> x17, waiting for transfers between devices: 28.2 us -> 26 us  [data_swap(): return lax.ppermute(value, 'dp', [(i, i ^ 1 << k) for i in range(dp)])]
    ppermute x14 -> x11, starting transfers between devices: 15.6 us -> 13.5 us  [other(): return lax.ppermute(value, 'mp', across)]
  transfers between devices with their start and end apart: 43 -> 44, of which waited for: 15 -> 15; matrix products, arithmetic and copies ran while one was open for 1% -> 0% of each run, Pallas kernels for 32% -> 39%
where the time goes in v1:
time: 165 us; the launch traced here: 164 us
  Pallas kernels  69.5 us (42%)
  starting transfers between devices  49 us (30%)
  waiting for transfers between devices  41.6 us (25%)
  local copies, waits for them, and re-layouts  2.42 us (1%)
    pallas_call x31, Pallas kernels, __call__(): pl.pallas_call(body, in_specs=[words] + specs + after_specs, out_specs=[f...  69.5 us
    ppermute x17, waiting for transfers between devices, data_swap(): return lax.ppermute(value, 'dp', [(i, i ^ 1 << k) for i in range(dp)])  26 us
    ppermute x17, starting transfers between devices, data_swap(): return lax.ppermute(value, 'dp', [(i, i ^ 1 << k) for i in range(dp)])  21.4 us
    ppermute x11, starting transfers between devices, other(): return lax.ppermute(value, 'mp', across)  13.5 us
    ppermute x11, waiting for transfers between devices, other(): return lax.ppermute(value, 'mp', across)  12 us
    all_to_all x1, starting transfers between devices, shards(): lax.all_to_all(memory_part, 'dp', split_axis=0, concat_axis=0, tiled=True)  5.82 us
    all_to_all x1, starting transfers between devices, shards(): lax.all_to_all(blocks, ('dp', 'mp'), split_axis=0, concat_axis=0, tiled=T...  5.39 us
  transfers between devices with their start and end apart: 44, of which 15 were waited for; matrix products, arithmetic and copies ran while one was open for 0% of the time, Pallas kernels for 39%

profile of v1, /device:TPU:0, one launch (start us, length us, event | category | flops | bytes accessed | tf_op | source)
XLA Modules:
  0.0 163.8 jit_solution(2583222595635214223)
XLA Ops:
  0.6 3.0 %collective-permute-start = (bf16[3,512,128]{2,1,0:T(8,128)(2,1)}, bf16[3,512,128]{2,1,0:T(8,128)(2,1)S(1)}, u32[]{:S(2)}, u32[]{:S(2)}) collective-permute-start(bf16[3,512,128]{2,1,0:T(8,128)(2,1)} %refs_8_.5), channel_id=1, source_target_pairs={{0,2},{1,3},{2,0},{3,1},{4,6},{5,7},{6,4},{7,5},{8,10},{9,11},{10,... | collective-permute-start | bytes 1179656 | tf_op jit(solution)/shard_map/ppermute | solution.py:786
  3.8 2.9 %setup.1 = (bf16[1024,128]{1,0:T(8,128)(2,1)S(1)}, bf16[512,512]{1,0:T(8,128)(2,1)S(1)}, bf16[512,512]{1,0:T(8,128)(2,1)S(1)}, bf16[8,64,512]{2,1,0:T(8,128)(2,1...) custom-call(s32[6]{0:T(128)S(1)} %stack.27.where_ref, s32[6]{0:T(128)} %refs_0_.1, s32[8]{0:T(128)} %refs_1_.2, ...), custom_call_target="tpu_custom_call" | custom-call | flops 1000000 | bytes 300000 | tf_op jit(solution)/shard_map/setup/pallas_call | solution.py:146
  6.7 5.8 %all-to-all-start = ((bf16[8,64,512]{2,1,0:T(8,128)(2,1)}), bf16[8,64,512]{2,1,0:T(8,128)(2,1)S(1)}, u32[]{:S(2)}, u32[]{:S(2)}) async-start(bf16[8,64,512]{2,1,0:T(8,128)(2,1)} %get-tuple-element.191), calls=%async_computation | async-start | bytes 1048576 | tf_op jit(solution)/shard_map/all_to_all | solution.py:839
  13.1 1.6 collective-permute-start.1
  14.7 3.8 %self_forward_0.1 = (bf16[512,512]{1,0:T(8,128)(2,1)S(1)}, bf16[512,128]{1,0:T(8,128)(2,1)}, bf16[512,128]{1,0:T(8,128)(2,1)}, bf16[512,128]{1,0:T(8,128)(2,1)},...) custom-call(s32[6]{0:T(128)S(1)} %stack.27.where_ref, ...), custom_call_target="tpu_custom_call" | custom-call | flops 1000000 | bytes 300000 | tf_op jit(solution)/shard_map/self_forward_0/pallas_call | solution.py:146
  19.1 6.4 %collective-permute-done.3.refs_8_.refs_0_ = bf16[1024,128]{1,0:T(8,128)(2,1)S(1)} collective-permute-done((bf16[1024,128]{1,0:T(8,128)(2,1)S(1)}, bf16[1024,128]{1,0:T(8,128)(2,1)S(1)}, u32[]{:S(2)}, u32[]{:S(2)}) %collective-permute-start.3) | collective-permute-done | bytes 262176 | tf_op jit(solution)/shard_map/ppermute | solution.py:786
  25.5 3.7 %self_forward_1.1 = (bf16[512,128]{1,0:T(8,128)(2,1)}, bf16[512,128]{1,0:T(8,128)(2,1)}, bf16[512,128]{1,0:T(8,128)(2,1)}, bf16[512,128]{1,0:T(8,128)(2,1)S(1)},...) custom-call(s32[6]{0:T(128)S(1)} %stack.27.where_ref, ...), custom_call_target="tpu_custom_call" | custom-call | flops 1000000 | bytes 300000 | tf_op jit(solution)/shard_map/self_forward_1/pallas_call | solution.py:146
  30.4 1.7 %collective-permute-start.6 = (bf16[1024,128]{1,0:T(8,128)(2,1)S(1)}, bf16[1024,128]{1,0:T(8,128)(2,1)}, u32[]{:S(2)}, u32[]{:S(2)}) collective-permute-start(bf16[1024,128]{1,0:T(8,128)(2,1)S(1)} %collective-permute-done.3.refs_8_.refs_0_), channel_id=1, source_target_pairs={{0,4},{4,0},{8,12},{12,8},{16,20},{20,16},{24,28},{28,24},{1,5},{5... | collective-permute-start | bytes 786440 | tf_op jit(solution)/shard_map/ppermute | solution.py:792
  32.5 1.5 collective-permute-start.9
  34.1 1.9 %memory_0.1 = (bf16[512,128]{1,0:T(8,128)(2,1)S(1)}, bf16[512,128]{1,0:T(8,128)(2,1)S(1)}, f32[8,128]{1,0:T(8,128)}) custom-call(s32[6]{0:T(128)S(1)} %stack.27.where_ref, bf16[512,512]{1,0:T(8,128)(2,1)S(1)} %bitcast.11, bf16[2,512,128]{2,1,0:T(8,128)(2,1)} %refs_8_.4, bf16[8,128]{1,0:T(8,128)(2,1)S(1)} %pad_maximum_fusion.refs_4_.refs_2_.refs_8_, ...), custom_call_target="tpu_custom_call" | custom-call | flops 1000000 | bytes 300000 | tf_op jit(solution)/shard_map/memory_0/pallas_call | solution.py:146
  36.0 4.5 %cross_forward_0.1 = (f32[512,512]{1,0:T(8,128)S(1)}, bf16[512,512]{1,0:T(8,128)(2,1)S(1)}, bf16[512,128]{1,0:T(8,128)(2,1)S(1)}, bf16[512,128]{1,0:T(8,128)(2,1...) custom-call(s32[6]{0:T(128)S(1)} %stack.27.where_ref, bf16[512,512]{1,0:T(8,128)(2,1)S(1)} %get-tuple-element.180.refs_0_, ...), custom_call_target="tpu_custom_call" | custom-call | flops 1000000 | bytes 300000 | tf_op jit(solution)/shard_map/cross_forward_0/pallas_call | solution.py:146
  40.5 1.5 memory_1.1
  42.0 3.3 %cross_forward_1.1 = (bf16[512,128]{1,0:T(8,128)(2,1)S(1)}, bf16[512,128]{1,0:T(8,128)(2,1)S(1)}, f32[2,512]{1,0:T(2,128)S(1)}, bf16[256,512]{1,0:T(8,128)(2,1)S...) custom-call(s32[6]{0:T(128)S(1)} %stack.27.where_ref, bf16[512,512]{1,0:T(8,128)(2,1)S(1)} %get-tuple-element.197.refs_0_.refs_10_, ...), custom_call_target="tpu_custom_call" | custom-call | flops 1000000 | bytes 300000 | tf_op jit(solution)/shard_map/cross_forward_1/pallas_call | solution.py:146
  47.3 4.3 %ffn_0.1 = (f32[512,512]{1,0:T(8,128)S(1)}, bf16[512,512]{1,0:T(8,128)(2,1)S(1)}, bf16[512,512]{1,0:T(8,128)(2,1)S(1)}, bf16[512,512]{1,0:T(8,128)(2,1)S(1)}, bf...) custom-call(s32[6]{0:T(128)S(1)} %stack.27.where_ref, ...), custom_call_target="tpu_custom_call" | custom-call | flops 1000000 | bytes 300000 | tf_op jit(solution)/shard_map/ffn_0/pallas_call | solution.py:146
  51.6 5.6 %collective-permute-done.9.refs_4_ = bf16[512,512]{1,0:T(8,128)(2,1)} collective-permute-done((bf16[512,512]{1,0:T(8,128)(2,1)}, bf16[512,512]{1,0:T(8,128)(2,1)}, u32[]{:S(2)}, u32[]{:S(2)}) %collective-permute-start.9) | collective-permute-done | bytes 524320 | tf_op jit(solution)/shard_map/ppermute | solution.py:786
  57.1 3.5 %ffn_1.2 = (bf16[512,512]{1,0:T(8,128)(2,1)S(1)}, bf16[512,512]{1,0:T(8,128)(2,1)S(1)}, bf16[256,512]{1,0:T(8,128)(2,1)S(1)}, bf16[256,512]{1,0:T(8,128)(2,1)S(1...) custom-call(s32[6]{0:T(128)S(1)} %stack.27.where_ref, ...), custom_call_target="tpu_custom_call" | custom-call | flops 1000000 | bytes 300000 | tf_op jit(solution)/shard_map/ffn_1/pallas_call | solution.py:146
  60.7 1.8 %ffn_weights.1 = (f32[2,512]{1,0:T(2,128)S(1)}, f32[1,512,512]{2,1,0:T(8,128)S(1)}, bf16[1,512,512]{2,1,0:T(8,128)(2,1)S(1)}, f32[2,256,512]{2,1,0:T(8,128)S(1)}...) custom-call(s32[6]{0:T(128)S(1)} %stack.27.where_ref, bf16[512,512]{1,0:T(8,128)(2,1)S(1)} %get-tuple-element.223.refs_0_, ...), custom_call_target="tpu_custom_call" | custom-call | flops 1000000 | bytes 300000 | tf_op jit(solution)/shard_map/ffn_weights/pallas_call | solution.py:146
  65.0 6.5 %cross_backward.1 = (f32[512,512]{1,0:T(8,128)S(1)}, bf16[512,512]{1,0:T(8,128)(2,1)S(1)}, bf16[512,128]{1,0:T(8,128)(2,1)S(1)}, bf16[512,128]{1,0:T(8,128)(2,1)...) custom-call(s32[6]{0:T(128)S(1)} %stack.27.where_ref, ...), custom_call_target="tpu_custom_call" | custom-call | flops 1000000 | bytes 300000 | tf_op jit(solution)/shard_map/cross_backward/pallas_call | solution.py:146
  72.1 3.1 %cross_weights.1 = (f32[2,256,512]{2,1,0:T(8,128)S(1)}, bf16[2,256,512]{2,1,0:T(8,128)(2,1)S(1)}, bf16[256,512]{1,0:T(8,128)(2,1)S(1)}, bf16[256,512]{1,0:T(8,12...) custom-call(s32[6]{0:T(128)S(1)} %stack.27.where_ref, bf16[512,128]{1,0:T(8,128)(2,1)S(1)} %get-tuple-element.244.refs_0_, ...), custom_call_target="tpu_custom_call" | custom-call | flops 1000000 | bytes 300000 | tf_op jit(solution)/shard_map/cross_weights/pallas_call | solution.py:146
  75.2 1.7 %collective-permute-start.26 = (bf16[2,256,512]{2,1,0:T(8,128)(2,1)S(1)}, bf16[2,256,512]{2,1,0:T(8,128)(2,1)S(1)}, u32[]{:S(2)}, u32[]{:S(2)}) collective-permute-start(bf16[2,256,512]{2,1,0:T(8,128)(2,1)S(1)} %get-tuple-element.288), channel_id=1, source_target_pairs={{0,8},{4,12},{8,0},{12,4},{16,24},{20,28},{24,16},{28,20},{1,9},{5... | collective-permute-start | bytes 1572872 | tf_op jit(solution)/shard_map/ppermute | solution.py:792
  77.9 1.3 collective-permute-start.19
  79.2 1.5 collective-permute-start.20
  80.8 6.2 %self_backward.1 = (f32[512,512]{1,0:T(8,128)S(1)}, bf16[512,512]{1,0:T(8,128)(2,1)S(1)}, bf16[512,128]{1,0:T(8,128)(2,1)S(1)}, bf16[512,128]{1,0:T(8,128)(2,1)S...) custom-call(s32[6]{0:T(128)S(1)} %stack.27.where_ref, ...), custom_call_target="tpu_custom_call" | custom-call | flops 1000000 | bytes 300000 | tf_op jit(solution)/shard_map/self_backward/pallas_call | solution.py:146
  88.5 2.5 %self_weights.1 = (bf16[256,512]{1,0:T(8,128)(2,1)S(1)}, bf16[256,512]{1,0:T(8,128)(2,1)S(1)}, f32[1,512,512]{2,1,0:T(8,128)S(1)}, bf16[1,512,512]{2,1,0:T(8,128)(2,1)S(1)}, f32[8,128]{1,0:T(8,128)}) custom-call(s32[6]{0:T(128)S(1)} %stack.27.where_ref, bf16[512,128]{1,0:T(8,128)(2,1)S(1)} %get-tuple-element.258.refs_0_, ...), custom_call_target="tpu_custom_call" | custom-call | flops 1000000 | bytes 300000 | tf_op jit(solution)/shard_map/self_weights/pallas_call | solution.py:146
  91.0 1.4 collective-permute-start.27
  93.6 2.8 %collective-permute-done.25.refs_1_ = bf16[2,128,512]{2,1,0:T(8,128)(2,1)S(1)} collective-permute-done((bf16[2,128,512]{2,1,0:T(8,128)(2,1)S(1)}, bf16[2,128,512]{2,1,0:T(8,128)(2,1)S(1)}, u32[]{:S(2)}, u32[]{:S(2)}) %collective-permute-start.25) | collective-permute-done | bytes 262176 | tf_op jit(solution)/shard_map/ppermute | solution.py:792
  97.8 2.4 %collective-permute-start.30 = (bf16[2,128,512]{2,1,0:T(8,128)(2,1)S(1)}, bf16[2,128,512]{2,1,0:T(8,128)(2,1)S(1)}, u32[]{:S(2)}, u32[]{:S(2)}) collective-permute-start(bf16[2,128,512]{2,1,0:T(8,128)(2,1)S(1)} %get-tuple-element.303.refs_2_), channel_id=1, source_target_pairs={{0,16},{4,20},{8,24},{12,28},{16,0},{20,4},{24,8},{28,12},{1,17},{... | collective-permute-start | bytes 786440 | tf_op jit(solution)/shard_map/ppermute | solution.py:792
  100.2 1.3 memory_blocks.1
  101.5 1.5 input_backward.1
  103.0 1.2 collective-permute-done.28.refs_1_
  104.3 1.2 cross_2.1
  107.8 5.4 %all-to-all-start.1 = ((bf16[16,64,128]{2,1,0:T(8,128)(2,1)}), bf16[16,64,128]{2,1,0:T(8,128)(2,1)S(1)}, u32[]{:S(2)}, u32[]{:S(2)}) async-start(bf16[16,64,128]{2,1,0:T(8,128)(2,1)} %bitcast.9), calls=%async_computation.1 | async-start | bytes 524288 | tf_op jit(solution)/shard_map/all_to_all | solution.py:1050
  113.4 1.3 all_1.1
  115.4 1.7 %collective-permute-start.32 = (bf16[1024,512]{1,0:T(8,128)(2,1)S(1)}, bf16[1024,512]{1,0:T(8,128)(2,1)S(1)}, u32[]{:S(2)}, u32[]{:S(2)}) collective-permute-start(bf16[1024,512]{1,0:T(8,128)(2,1)S(1)} %get-tuple-element.308.refs_0_), channel_id=1, source_target_pairs={{0,2},{1,3},{2,0},{3,1},{4,6},{5,7},{6,4},{7,5},{8,10},{9,11},{10,... | collective-permute-start | bytes 3145736 | tf_op jit(solution)/shard_map/ppermute | solution.py:786
  117.2 1.5 collective-permute-start.34
  119.2 2.4 %collective-permute-start.35 = (bf16[1,128,512]{2,1,0:T(8,128)(2,1)S(1)}, bf16[1,128,512]{2,1,0:T(8,128)(2,1)S(1)}, u32[]{:S(2)}, u32[]{:S(2)}) collective-permute-start(bf16[1,128,512]{2,1,0:T(8,128)(2,1)S(1)} %get-tuple-element.312.refs_6_), channel_id=1, source_target_pairs={{0,16},{4,20},{8,24},{12,28},{16,0},{20,4},{24,8},{28,12},{1,17},{... | collective-permute-start | bytes 393224 | tf_op jit(solution)/shard_map/ppermute | solution.py:792
  122.7 1.4 widen_memory.1
  124.1 6.5 %collective-permute-done.33.refs_1_ = bf16[1,128,512]{2,1,0:T(8,128)(2,1)S(1)} collective-permute-done((bf16[1,128,512]{2,1,0:T(8,128)(2,1)}, bf16[1,128,512]{2,1,0:T(8,128)(2,1)S(1)}, u32[]{:S(2)}, u32[]{:S(2)}) %collective-permute-start.33) | collective-permute-done | bytes 131104 | tf_op jit(solution)/shard_map/ppermute | solution.py:792
  133.6 2.3 %collective-permute-start.37 = (bf16[1,128,512]{2,1,0:T(8,128)(2,1)S(1)}, bf16[1,128,512]{2,1,0:T(8,128)(2,1)S(1)}, u32[]{:S(2)}, u32[]{:S(2)}) collective-permute-start(bf16[1,128,512]{2,1,0:T(8,128)(2,1)S(1)} %get-tuple-element.317.refs_2_), channel_id=1, source_target_pairs={{0,8},{4,12},{8,0},{12,4},{16,24},{20,28},{24,16},{28,20},{1,9},{5... | collective-permute-start | bytes 393224 | tf_op jit(solution)/shard_map/ppermute | solution.py:792
  135.9 1.3 collective-permute-start.41
  137.2 2.9 %collective-permute-done.37.refs_3_ = bf16[1,128,512]{2,1,0:T(8,128)(2,1)S(1)} collective-permute-done((bf16[1,128,512]{2,1,0:T(8,128)(2,1)S(1)}, bf16[1,128,512]{2,1,0:T(8,128)(2,1)S(1)}, u32[]{:S(2)}, u32[]{:S(2)}) %collective-permute-start.37) | collective-permute-done | bytes 131104 | tf_op jit(solution)/shard_map/ppermute | solution.py:792
  141.9 5.0 %collective-permute-done.38.refs_1_ = bf16[1,144,512]{2,1,0:T(8,128)(2,1)S(1)} collective-permute-done((bf16[1,144,512]{2,1,0:T(8,128)(2,1)S(1)}, bf16[1,144,512]{2,1,0:T(8,128)(2,1)S(1)}, u32[]{:S(2)}, u32[]{:S(2)}) %collective-permute-start.38) | collective-permute-done | bytes 147488 | tf_op jit(solution)/shard_map/ppermute | solution.py:792
  147.5 1.7 %collective-permute-start.39 = (bf16[1,272,512]{2,1,0:T(8,128)(2,1)S(1)}, bf16[1,272,512]{2,1,0:T(8,128)(2,1)S(1)}, u32[]{:S(2)}, u32[]{:S(2)}) collective-permute-start(bf16[1,272,512]{2,1,0:T(8,128)(2,1)S(1)} %get-tuple-element.325.refs_0_), channel_id=1, source_target_pairs={{0,4},{4,0},{8,12},{12,8},{16,20},{20,16},{24,28},{28,24},{1,5},{5... | collective-permute-start | bytes 835592 | tf_op jit(solution)/shard_map/ppermute | solution.py:792
  149.6 2.3 %place_rows.1 = (bf16[2,512,512]{2,1,0:T(8,128)(2,1)}, f32[2,512,512]{2,1,0:T(8,128)}, f32[8,128]{1,0:T(8,128)}) custom-call(s32[6]{0:T(128)S(1)} %stack.27.where_ref, bf16[1024,512]{1,0:T(8,128)(2,1)S(1)} %get-tuple-element.308.refs_0_, bf16[1024,512]{1,0:T(8,128)(2,1)S(1)} %collective-permute-done.32.refs_1_, f32[8,128]{1,0:T(8,128)} %get-tuple-element.321.refs_2_), custom_call_target="tpu_custom_call" | custom-call | flops 1000000 | bytes 300000 | tf_op jit(solution)/shard_map/place_rows/pallas_call | solution.py:146
  151.9 2.2 %ffn_grads.1 = (f32[512,512]{1,0:T(8,128)}, f32[512,512]{1,0:T(8,128)}, f32[8,128]{1,0:T(8,128)}) custom-call(s32[6]{0:T(128)S(1)} %stack.27.where_ref, bf16[2,256,512]{2,1,0:T(8,128)(2,1)S(1)} %get-tuple-element.327.refs_0_, bf16[2,256,512]{2,1,0:T(8,128)(2,1)S(1)} %collective-permute-done.41.refs_1_, f32[8,128]{1,0:T(8,128)} %get-tuple-element.328.refs_2_), custom_call_target="tpu_custom_call" | custom-call | flops 1000000 | bytes 300000 | tf_op jit(solution)/shard_map/ffn_grads/pallas_call | solution.py:146
  154.1 6.1 %collective-permute-done.40.refs_1_ = bf16[1,256,512]{2,1,0:T(8,128)(2,1)S(1)} collective-permute-done((bf16[1,256,512]{2,1,0:T(8,128)(2,1)S(1)}, bf16[1,256,512]{2,1,0:T(8,128)(2,1)S(1)}, u32[]{:S(2)}, u32[]{:S(2)}) %collective-permute-start.40) | collective-permute-done | bytes 262176 | tf_op jit(solution)/shard_map/ppermute | solution.py:792
  160.2 1.6 %cross_grads.1 = (f32[512,128]{1,0:T(8,128)}, f32[2,512,128]{2,1,0:T(8,128)}, f32[128,512]{1,0:T(8,128)}, f32[8,128]{1,0:T(8,128)}) custom-call(s32[6]{0:T(128)S(1)} %stack.27.where_ref, bf16[1,256,512]{2,1,0:T(8,128)(2,1)S(1)} %get-tuple-element.326.refs_0_, bf16[1,256,512]{2,1,0:T(8,128)(2,1)S(1)} %collective-permute-done.40.refs_1_, ...), custom_call_target="tpu_custom_call" | custom-call | flops 1000000 | bytes 300000 | tf_op jit(solution)/shard_map/cross_grads/pallas_call | solution.py:146
  161.9 1.8 %self_grads.1 = (f32[3,512,128]{2,1,0:T(8,128)}, f32[128,512]{1,0:T(8,128)}, f32[3,512]{1,0:T(4,128)}, f32[3,512]{1,0:T(4,128)}, f32[3,512]{1,0:T(4,128)}, /*ind...) custom-call(s32[6]{0:T(128)S(1)} %stack.27.where_ref, ...), custom_call_target="tpu_custom_call" | custom-call | flops 1000000 | bytes 300000 | tf_op jit(solution)/shard_map/self_grads/pallas_call | solution.py:146
  (93 shorter events, 23.7 us)
Async XLA Ops:
  0.6 17.9 %collective-permute-start = (bf16[3,512,128]{2,1,0:T(8,128)(2,1)}, bf16[3,512,128]{2,1,0:T(8,128)(2,1)S(1)}, u32[]{:S(2)}, u32[]{:S(2)}) collective-permute-start(bf16[3,512,128]{2,1,0:T(8,128)(2,1)} %refs_8_.5), channel_id=1, source_target_pairs={{0,2},{1,3},{2,0},{3,1},{4,6},{5,7},{6,4},{7,5},{8,10},{9,11},{10,... | collective-permute-start | bytes 1179656 | tf_op jit(solution)/shard_map/ppermute | solution.py:786
  3.8 9.3 %copy-start.7 = (bf16[512]{0:T(512)(128)(2,1)S(1)}, bf16[512]{0:T(512)(128)(2,1)}, u32[]{:S(2)}) copy-start(bf16[512]{0:T(512)(128)(2,1)} %param.36) | copy-start | bytes 3076
  3.8 9.3 %copy-start.8 = (bf16[2,128]{1,0:T(2,128)(2,1)S(1)}, bf16[2,128]{1,0:T(2,128)(2,1)}, u32[]{:S(2)}) copy-start(bf16[2,128]{1,0:T(2,128)(2,1)} %param.33) | copy-start | bytes 1540
  3.8 9.3 %copy-start.9 = (bf16[2,128]{1,0:T(2,128)(2,1)S(1)}, bf16[2,128]{1,0:T(2,128)(2,1)}, u32[]{:S(2)}) copy-start(bf16[2,128]{1,0:T(2,128)(2,1)} %param.29) | copy-start | bytes 1540
  6.7 27.4 %all-to-all-start = ((bf16[8,64,512]{2,1,0:T(8,128)(2,1)}), bf16[8,64,512]{2,1,0:T(8,128)(2,1)S(1)}, u32[]{:S(2)}, u32[]{:S(2)}) async-start(bf16[8,64,512]{2,1,0:T(8,128)(2,1)} %get-tuple-element.191), calls=%async_computation | async-start | bytes 1048576 | tf_op jit(solution)/shard_map/all_to_all | solution.py:839
  12.5 6.0 %collective-permute-start.2 = (bf16[128,512]{1,0:T(8,128)(2,1)S(1)}, bf16[128,512]{1,0:T(8,128)(2,1)S(1)}, u32[]{:S(2)}, u32[]{:S(2)}) collective-permute-start(bf16[128,512]{1,0:T(8,128)(2,1)S(1)} %copy-done.6), channel_id=1, source_target_pairs={{0,2},{1,3},{2,0},{3,1},{4,6},{5,7},{6,4},{7,5},{8,10},{9,11},{10,... | collective-permute-start | bytes 393224 | tf_op jit(solution)/shard_map/ppermute | solution.py:786
  13.1 5.4 %collective-permute-start.1 = (bf16[8,128]{1,0:T(8,128)(2,1)S(1)}, bf16[8,128]{1,0:T(8,128)(2,1)S(1)}, u32[]{:S(2)}, u32[]{:S(2)}) collective-permute-start(bf16[8,128]{1,0:T(8,128)(2,1)S(1)} %pad_maximum_fusion.refs_4_.refs_2_.refs_8_), channel_id=1, source_target_pairs={{0,2},{1,3},{2,0},{3,1},{4,6},{5,7},{6,4},{7,5},{8,10},{9,11},{10,... | collective-permute-start | bytes 6152 | tf_op jit(solution)/shard_map/ppermute | solution.py:786
  18.5 14.0 %copy-start = (bf16[128,512]{1,0:T(8,128)(2,1)}, bf16[128,512]{1,0:T(8,128)(2,1)S(1)}, u32[]{:S(2)}) copy-start(bf16[128,512]{1,0:T(8,128)(2,1)S(1)} %collective-permute-done.2.refs_6_.refs_17_) | copy-start | bytes 393220
  18.5 7.0 %collective-permute-start.3 = (bf16[1024,128]{1,0:T(8,128)(2,1)S(1)}, bf16[1024,128]{1,0:T(8,128)(2,1)S(1)}, u32[]{:S(2)}, u32[]{:S(2)}) collective-permute-start(bf16[1024,128]{1,0:T(8,128)(2,1)S(1)} %get-tuple-element.187), channel_id=1, source_target_pairs={{0,2},{1,3},{2,0},{3,1},{4,6},{5,7},{6,4},{7,5},{8,10},{9,11},{10,... | collective-permute-start | bytes 786440 | tf_op jit(solution)/shard_map/ppermute | solution.py:786
  29.9 6.2 %collective-permute-start.4 = (bf16[256,512]{1,0:T(8,128)(2,1)}, bf16[256,512]{1,0:T(8,128)(2,1)}, u32[]{:S(2)}, u32[]{:S(2)}) collective-permute-start(bf16[256,512]{1,0:T(8,128)(2,1)} %get-tuple-element.189.refs_1_), channel_id=1, source_target_pairs={{0,1},{1,0},{2,3},{3,2},{4,5},{5,4},{6,7},{7,6},{8,9},{9,8},{10,11... | collective-permute-start | bytes 786440 | tf_op jit(solution)/shard_map/ppermute | solution.py:789
  29.9 6.2 %collective-permute-start.5 = (bf16[256,512]{1,0:T(8,128)(2,1)}, bf16[256,512]{1,0:T(8,128)(2,1)}, u32[]{:S(2)}, u32[]{:S(2)}) collective-permute-start(bf16[256,512]{1,0:T(8,128)(2,1)} %get-tuple-element.190.refs_2_), channel_id=1, source_target_pairs={{0,1},{1,0},{2,3},{3,2},{4,5},{5,4},{6,7},{7,6},{8,9},{9,8},{10,11... | collective-permute-start | bytes 786440 | tf_op jit(solution)/shard_map/ppermute | solution.py:789
  30.4 10.1 %collective-permute-start.6 = (bf16[1024,128]{1,0:T(8,128)(2,1)S(1)}, bf16[1024,128]{1,0:T(8,128)(2,1)}, u32[]{:S(2)}, u32[]{:S(2)}) collective-permute-start(bf16[1024,128]{1,0:T(8,128)(2,1)S(1)} %collective-permute-done.3.refs_8_.refs_0_), channel_id=1, source_target_pairs={{0,4},{4,0},{8,12},{12,8},{16,20},{20,16},{24,28},{28,24},{1,5},{5... | collective-permute-start | bytes 786440 | tf_op jit(solution)/shard_map/ppermute | solution.py:792
  32.0 19.5 %collective-permute-start.10 = (bf16[512,512]{1,0:T(8,128)(2,1)}, bf16[512,512]{1,0:T(8,128)(2,1)S(1)}, u32[]{:S(2)}, u32[]{:S(2)}) collective-permute-start(bf16[512,512]{1,0:T(8,128)(2,1)} %refs_9_.3), channel_id=1, source_target_pairs={{0,2},{1,3},{2,0},{3,1},{4,6},{5,7},{6,4},{7,5},{8,10},{9,11},{10,... | collective-permute-start | bytes 1572872 | tf_op jit(solution)/shard_map/ppermute | solution.py:786
  32.5 24.6 %collective-permute-start.9 = (bf16[512,512]{1,0:T(8,128)(2,1)}, bf16[512,512]{1,0:T(8,128)(2,1)}, u32[]{:S(2)}, u32[]{:S(2)}) collective-permute-start(bf16[512,512]{1,0:T(8,128)(2,1)} %refs_7_.7), channel_id=1, source_target_pairs={{0,2},{1,3},{2,0},{3,1},{4,6},{5,7},{6,4},{7,5},{8,10},{9,11},{10,... | collective-permute-start | bytes 1572872 | tf_op jit(solution)/shard_map/ppermute | solution.py:786
  45.3 1.6 collective-permute-start.7
  45.4 1.9 %collective-permute-start.8 = (bf16[256,512]{1,0:T(8,128)(2,1)S(1)}, bf16[256,512]{1,0:T(8,128)(2,1)S(1)}, u32[]{:S(2)}, u32[]{:S(2)}) collective-permute-start(bf16[256,512]{1,0:T(8,128)(2,1)S(1)} %get-tuple-element.206.refs_2_), channel_id=1, source_target_pairs={{0,1},{1,0},{2,3},{3,2},{4,5},{5,4},{6,7},{7,6},{8,9},{9,8},{10,11... | collective-permute-start | bytes 786440 | tf_op jit(solution)/shard_map/ppermute | solution.py:789
  60.6 3.4 %collective-permute-start.11 = (bf16[256,512]{1,0:T(8,128)(2,1)S(1)}, bf16[256,512]{1,0:T(8,128)(2,1)S(1)}, u32[]{:S(2)}, u32[]{:S(2)}) collective-permute-start(bf16[256,512]{1,0:T(8,128)(2,1)S(1)} %get-tuple-element.217.refs_1_), channel_id=1, source_target_pairs={{0,1},{1,0},{2,3},{3,2},{4,5},{5,4},{6,7},{7,6},{8,9},{9,8},{10,11... | collective-permute-start | bytes 786440 | tf_op jit(solution)/shard_map/ppermute | solution.py:789
  62.5 14.4 %collective-permute-start.15 = (bf16[1,512,512]{2,1,0:T(8,128)(2,1)S(1)}, bf16[1,512,512]{2,1,0:T(8,128)(2,1)S(1)}, u32[]{:S(2)}, u32[]{:S(2)}) collective-permute-start(bf16[1,512,512]{2,1,0:T(8,128)(2,1)S(1)} %get-tuple-element.241), channel_id=1, source_target_pairs={{0,2},{1,3},{2,0},{3,1},{4,6},{5,7},{6,4},{7,5},{8,10},{9,11},{10,... | collective-permute-start | bytes 1572872 | tf_op jit(solution)/shard_map/ppermute | solution.py:786
  63.1 14.0 %collective-permute-start.16 = (bf16[2,256,512]{2,1,0:T(8,128)(2,1)S(1)}, bf16[2,256,512]{2,1,0:T(8,128)(2,1)S(1)}, u32[]{:S(2)}, u32[]{:S(2)}) collective-permute-start(bf16[2,256,512]{2,1,0:T(8,128)(2,1)S(1)} %get-tuple-element.243), channel_id=1, source_target_pairs={{0,4},{4,0},{8,12},{12,8},{16,20},{20,16},{24,28},{28,24},{1,5},{5... | collective-permute-start | bytes 1572872 | tf_op jit(solution)/shard_map/ppermute | solution.py:792
  63.5 1.5 collective-permute-start.12
  63.5 8.3 %collective-permute-start.17 = (bf16[256,512]{1,0:T(8,128)(2,1)S(1)}, bf16[256,512]{1,0:T(8,128)(2,1)S(1)}, u32[]{:S(2)}, u32[]{:S(2)}) collective-permute-start(bf16[256,512]{1,0:T(8,128)(2,1)S(1)} %get-tuple-element.253.refs_14_), channel_id=1, source_target_pairs={{0,1},{1,0},{2,3},{3,2},{4,5},{5,4},{6,7},{7,6},{8,9},{9,8},{10,11... | collective-permute-start | bytes 786440 | tf_op jit(solution)/shard_map/ppermute | solution.py:789
  64.0 8.1 %collective-permute-start.18 = (bf16[256,512]{1,0:T(8,128)(2,1)S(1)}, bf16[256,512]{1,0:T(8,128)(2,1)S(1)}, u32[]{:S(2)}, u32[]{:S(2)}) collective-permute-start(bf16[256,512]{1,0:T(8,128)(2,1)S(1)} %get-tuple-element.254.refs_15_), channel_id=1, source_target_pairs={{0,1},{1,0},{2,3},{3,2},{4,5},{5,4},{6,7},{7,6},{8,9},{9,8},{10,11... | collective-permute-start | bytes 786440 | tf_op jit(solution)/shard_map/ppermute | solution.py:789
  71.6 9.2 %collective-permute-start.13 = (bf16[256,512]{1,0:T(8,128)(2,1)S(1)}, bf16[256,512]{1,0:T(8,128)(2,1)S(1)}, u32[]{:S(2)}, u32[]{:S(2)}) collective-permute-start(bf16[256,512]{1,0:T(8,128)(2,1)S(1)} %get-tuple-element.229.refs_1_), channel_id=1, source_target_pairs={{0,1},{1,0},{2,3},{3,2},{4,5},{5,4},{6,7},{7,6},{8,9},{9,8},{10,11... | collective-permute-start | bytes 786440 | tf_op jit(solution)/shard_map/ppermute | solution.py:789
  71.8 9.0 %collective-permute-start.14 = (bf16[256,512]{1,0:T(8,128)(2,1)S(1)}, bf16[256,512]{1,0:T(8,128)(2,1)S(1)}, u32[]{:S(2)}, u32[]{:S(2)}) collective-permute-start(bf16[256,512]{1,0:T(8,128)(2,1)S(1)} %get-tuple-element.230.refs_2_), channel_id=1, source_target_pairs={{0,1},{1,0},{2,3},{3,2},{4,5},{5,4},{6,7},{7,6},{8,9},{9,8},{10,11... | collective-permute-start | bytes 786440 | tf_op jit(solution)/shard_map/ppermute | solution.py:789
  75.2 17.7 %collective-permute-start.26 = (bf16[2,256,512]{2,1,0:T(8,128)(2,1)S(1)}, bf16[2,256,512]{2,1,0:T(8,128)(2,1)S(1)}, u32[]{:S(2)}, u32[]{:S(2)}) collective-permute-start(bf16[2,256,512]{2,1,0:T(8,128)(2,1)S(1)} %get-tuple-element.288), channel_id=1, source_target_pairs={{0,8},{4,12},{8,0},{12,4},{16,24},{20,28},{24,16},{28,20},{1,9},{5... | collective-permute-start | bytes 1572872 | tf_op jit(solution)/shard_map/ppermute | solution.py:792
  77.9 9.1 %collective-permute-start.19 = (bf16[1,256,512]{2,1,0:T(8,128)(2,1)S(1)}, bf16[1,256,512]{2,1,0:T(8,128)(2,1)S(1)}, u32[]{:S(2)}, u32[]{:S(2)}) collective-permute-start(bf16[1,256,512]{2,1,0:T(8,128)(2,1)S(1)} %get-tuple-element.268), channel_id=1, source_target_pairs={{0,4},{4,0},{8,12},{12,8},{16,20},{20,16},{24,28},{28,24},{1,5},{5... | collective-permute-start | bytes 786440 | tf_op jit(solution)/shard_map/ppermute | solution.py:792
  79.2 7.8 %collective-permute-start.20 = (bf16[1,256,512]{2,1,0:T(8,128)(2,1)S(1)}, bf16[1,256,512]{2,1,0:T(8,128)(2,1)S(1)}, u32[]{:S(2)}, u32[]{:S(2)}) collective-permute-start(bf16[1,256,512]{2,1,0:T(8,128)(2,1)S(1)} %get-tuple-element.269), channel_id=1, source_target_pairs={{0,2},{1,3},{2,0},{3,1},{4,6},{5,7},{6,4},{7,5},{8,10},{9,11},{10,... | collective-permute-start | bytes 786440 | tf_op jit(solution)/shard_map/ppermute | solution.py:786
  80.7 11.7 %collective-permute-start.23 = (bf16[256,512]{1,0:T(8,128)(2,1)S(1)}, bf16[256,512]{1,0:T(8,128)(2,1)S(1)}, u32[]{:S(2)}, u32[]{:S(2)}) collective-permute-start(bf16[256,512]{1,0:T(8,128)(2,1)S(1)} %get-tuple-element.283.refs_0_), channel_id=1, source_target_pairs={{0,1},{1,0},{2,3},{3,2},{4,5},{5,4},{6,7},{7,6},{8,9},{9,8},{10,11... | collective-permute-start | bytes 786440 | tf_op jit(solution)/shard_map/ppermute | solution.py:789
  87.6 8.7 %collective-permute-start.25 = (bf16[2,128,512]{2,1,0:T(8,128)(2,1)S(1)}, bf16[2,128,512]{2,1,0:T(8,128)(2,1)S(1)}, u32[]{:S(2)}, u32[]{:S(2)}) collective-permute-start(bf16[2,128,512]{2,1,0:T(8,128)(2,1)S(1)} %get-tuple-element.286), channel_id=1, source_target_pairs={{0,8},{4,12},{8,0},{12,4},{16,24},{20,28},{24,16},{28,20},{1,9},{5... | collective-permute-start | bytes 786440 | tf_op jit(solution)/shard_map/ppermute | solution.py:792
  91.0 14.5 %collective-permute-start.27 = (bf16[1,512,512]{2,1,0:T(8,128)(2,1)S(1)}, bf16[1,512,512]{2,1,0:T(8,128)(2,1)S(1)}, u32[]{:S(2)}, u32[]{:S(2)}) collective-permute-start(bf16[1,512,512]{2,1,0:T(8,128)(2,1)S(1)} %get-tuple-element.295), channel_id=1, source_target_pairs={{0,2},{1,3},{2,0},{3,1},{4,6},{5,7},{6,4},{7,5},{8,10},{9,11},{10,... | collective-permute-start | bytes 1572872 | tf_op jit(solution)/shard_map/ppermute | solution.py:786
  92.4 5.4 %collective-permute-start.24 = (bf16[256,512]{1,0:T(8,128)(2,1)S(1)}, bf16[256,512]{1,0:T(8,128)(2,1)S(1)}, u32[]{:S(2)}, u32[]{:S(2)}) collective-permute-start(bf16[256,512]{1,0:T(8,128)(2,1)S(1)} %get-tuple-element.284.refs_1_), channel_id=1, source_target_pairs={{0,1},{1,0},{2,3},{3,2},{4,5},{5,4},{6,7},{7,6},{8,9},{9,8},{10,11... | collective-permute-start | bytes 786440 | tf_op jit(solution)/shard_map/ppermute | solution.py:789
  92.4 9.1 %collective-permute-start.21 = (bf16[256,512]{1,0:T(8,128)(2,1)S(1)}, bf16[256,512]{1,0:T(8,128)(2,1)S(1)}, u32[]{:S(2)}, u32[]{:S(2)}) collective-permute-start(bf16[256,512]{1,0:T(8,128)(2,1)S(1)} %get-tuple-element.272.refs_1_), channel_id=1, source_target_pairs={{0,1},{1,0},{2,3},{3,2},{4,5},{5,4},{6,7},{7,6},{8,9},{9,8},{10,11... | collective-permute-start | bytes 786440 | tf_op jit(solution)/shard_map/ppermute | solution.py:789
  92.9 8.6 %collective-permute-start.22 = (bf16[256,512]{1,0:T(8,128)(2,1)S(1)}, bf16[256,512]{1,0:T(8,128)(2,1)S(1)}, u32[]{:S(2)}, u32[]{:S(2)}) collective-permute-start(bf16[256,512]{1,0:T(8,128)(2,1)S(1)} %get-tuple-element.273.refs_2_), channel_id=1, source_target_pairs={{0,1},{1,0},{2,3},{3,2},{4,5},{5,4},{6,7},{7,6},{8,9},{9,8},{10,11... | collective-permute-start | bytes 786440 | tf_op jit(solution)/shard_map/ppermute | solution.py:789
  96.4 7.9 %collective-permute-start.28 = (bf16[2,128,512]{2,1,0:T(8,128)(2,1)S(1)}, bf16[2,128,512]{2,1,0:T(8,128)(2,1)S(1)}, u32[]{:S(2)}, u32[]{:S(2)}) collective-permute-start(bf16[2,128,512]{2,1,0:T(8,128)(2,1)S(1)} %get-tuple-element.297), channel_id=1, source_target_pairs={{0,4},{4,0},{8,12},{12,8},{16,20},{20,16},{24,28},{28,24},{1,5},{5... | collective-permute-start | bytes 786440 | tf_op jit(solution)/shard_map/ppermute | solution.py:792
  97.8 15.4 %collective-permute-start.30 = (bf16[2,128,512]{2,1,0:T(8,128)(2,1)S(1)}, bf16[2,128,512]{2,1,0:T(8,128)(2,1)S(1)}, u32[]{:S(2)}, u32[]{:S(2)}) collective-permute-start(bf16[2,128,512]{2,1,0:T(8,128)(2,1)S(1)} %get-tuple-element.303.refs_2_), channel_id=1, source_target_pairs={{0,16},{4,20},{8,24},{12,28},{16,0},{20,4},{24,8},{28,12},{1,17},{... | collective-permute-start | bytes 786440 | tf_op jit(solution)/shard_map/ppermute | solution.py:792
  106.2 7.2 %collective-permute-start.29 = (bf16[1,256,512]{2,1,0:T(8,128)(2,1)S(1)}, bf16[1,256,512]{2,1,0:T(8,128)(2,1)S(1)}, u32[]{:S(2)}, u32[]{:S(2)}) collective-permute-start(bf16[1,256,512]{2,1,0:T(8,128)(2,1)S(1)} %get-tuple-element.302), channel_id=1, source_target_pairs={{0,4},{4,0},{8,12},{12,8},{16,20},{20,16},{24,28},{28,24},{1,5},{5... | collective-permute-start | bytes 786440 | tf_op jit(solution)/shard_map/ppermute | solution.py:792
  107.3 5.9 %collective-permute-start.31 = (bf16[1,144,512]{2,1,0:T(8,128)(2,1)}, bf16[1,144,512]{2,1,0:T(8,128)(2,1)S(1)}, u32[]{:S(2)}, u32[]{:S(2)}) collective-permute-start(bf16[1,144,512]{2,1,0:T(8,128)(2,1)} %get-tuple-element.305), channel_id=1, source_target_pairs={{0,2},{1,3},{2,0},{3,1},{4,6},{5,7},{6,4},{7,5},{8,10},{9,11},{10,... | collective-permute-start | bytes 442376 | tf_op jit(solution)/shard_map/ppermute | solution.py:786
  107.8 14.9 %all-to-all-start.1 = ((bf16[16,64,128]{2,1,0:T(8,128)(2,1)}), bf16[16,64,128]{2,1,0:T(8,128)(2,1)S(1)}, u32[]{:S(2)}, u32[]{:S(2)}) async-start(bf16[16,64,128]{2,1,0:T(8,128)(2,1)} %bitcast.9), calls=%async_computation.1 | async-start | bytes 524288 | tf_op jit(solution)/shard_map/all_to_all | solution.py:1050
  115.4 34.2 %collective-permute-start.32 = (bf16[1024,512]{1,0:T(8,128)(2,1)S(1)}, bf16[1024,512]{1,0:T(8,128)(2,1)S(1)}, u32[]{:S(2)}, u32[]{:S(2)}) collective-permute-start(bf16[1024,512]{1,0:T(8,128)(2,1)S(1)} %get-tuple-element.308.refs_0_), channel_id=1, source_target_pairs={{0,2},{1,3},{2,0},{3,1},{4,6},{5,7},{6,4},{7,5},{8,10},{9,11},{10,... | collective-permute-start | bytes 3145736 | tf_op jit(solution)/shard_map/ppermute | solution.py:786
  117.2 13.4 %collective-permute-start.34 = (bf16[2,128,512]{2,1,0:T(8,128)(2,1)}, bf16[2,128,512]{2,1,0:T(8,128)(2,1)S(1)}, u32[]{:S(2)}, u32[]{:S(2)}) collective-permute-start(bf16[2,128,512]{2,1,0:T(8,128)(2,1)} %get-tuple-element.311.refs_4_), channel_id=1, source_target_pairs={{0,8},{4,12},{8,0},{12,4},{16,24},{20,28},{24,16},{28,20},{1,9},{5... | collective-permute-start | bytes 786440 | tf_op jit(solution)/shard_map/ppermute | solution.py:792
  118.6 12.0 %collective-permute-start.33 = (bf16[1,128,512]{2,1,0:T(8,128)(2,1)}, bf16[1,128,512]{2,1,0:T(8,128)(2,1)S(1)}, u32[]{:S(2)}, u32[]{:S(2)}) collective-permute-start(bf16[1,128,512]{2,1,0:T(8,128)(2,1)} %get-tuple-element.309), channel_id=1, source_target_pairs={{0,8},{4,12},{8,0},{12,4},{16,24},{20,28},{24,16},{28,20},{1,9},{5... | collective-permute-start | bytes 393224 | tf_op jit(solution)/shard_map/ppermute | solution.py:792
  119.2 11.4 %collective-permute-start.35 = (bf16[1,128,512]{2,1,0:T(8,128)(2,1)S(1)}, bf16[1,128,512]{2,1,0:T(8,128)(2,1)S(1)}, u32[]{:S(2)}, u32[]{:S(2)}) collective-permute-start(bf16[1,128,512]{2,1,0:T(8,128)(2,1)S(1)} %get-tuple-element.312.refs_6_), channel_id=1, source_target_pairs={{0,16},{4,20},{8,24},{12,28},{16,0},{20,4},{24,8},{28,12},{1,17},{... | collective-permute-start | bytes 393224 | tf_op jit(solution)/shard_map/ppermute | solution.py:792
  132.6 8.5 %collective-permute-start.36 = (bf16[1,144,512]{2,1,0:T(8,128)(2,1)S(1)}, bf16[1,144,512]{2,1,0:T(8,128)(2,1)S(1)}, u32[]{:S(2)}, u32[]{:S(2)}) collective-permute-start(bf16[1,144,512]{2,1,0:T(8,128)(2,1)S(1)} %get-tuple-element.316.refs_0_), channel_id=1, source_target_pairs={{0,16},{4,20},{8,24},{12,28},{16,0},{20,4},{24,8},{28,12},{1,17},{... | collective-permute-start | bytes 442376 | tf_op jit(solution)/shard_map/ppermute | solution.py:792
  133.6 6.4 %collective-permute-start.37 = (bf16[1,128,512]{2,1,0:T(8,128)(2,1)S(1)}, bf16[1,128,512]{2,1,0:T(8,128)(2,1)S(1)}, u32[]{:S(2)}, u32[]{:S(2)}) collective-permute-start(bf16[1,128,512]{2,1,0:T(8,128)(2,1)S(1)} %get-tuple-element.317.refs_2_), channel_id=1, source_target_pairs={{0,8},{4,12},{8,0},{12,4},{16,24},{20,28},{24,16},{28,20},{1,9},{5... | collective-permute-start | bytes 393224 | tf_op jit(solution)/shard_map/ppermute | solution.py:792
  135.9 16.0 %collective-permute-start.41 = (bf16[2,256,512]{2,1,0:T(8,128)(2,1)S(1)}, bf16[2,256,512]{2,1,0:T(8,128)(2,1)S(1)}, u32[]{:S(2)}, u32[]{:S(2)}) collective-permute-start(bf16[2,256,512]{2,1,0:T(8,128)(2,1)S(1)} %get-tuple-element.327.refs_0_), channel_id=1, source_target_pairs={{0,4},{4,0},{8,12},{12,8},{16,20},{20,16},{24,28},{28,24},{1,5},{5... | collective-permute-start | bytes 1572872 | tf_op jit(solution)/shard_map/ppermute | solution.py:792
  141.7 5.2 %collective-permute-start.38 = (bf16[1,144,512]{2,1,0:T(8,128)(2,1)S(1)}, bf16[1,144,512]{2,1,0:T(8,128)(2,1)S(1)}, u32[]{:S(2)}, u32[]{:S(2)}) collective-permute-start(bf16[1,144,512]{2,1,0:T(8,128)(2,1)S(1)} %get-tuple-element.319.refs_0_), channel_id=1, source_target_pairs={{0,8},{4,12},{8,0},{12,4},{16,24},{20,28},{24,16},{28,20},{1,9},{5... | collective-permute-start | bytes 442376 | tf_op jit(solution)/shard_map/ppermute | solution.py:792
  147.5 14.3 %collective-permute-start.39 = (bf16[1,272,512]{2,1,0:T(8,128)(2,1)S(1)}, bf16[1,272,512]{2,1,0:T(8,128)(2,1)S(1)}, u32[]{:S(2)}, u32[]{:S(2)}) collective-permute-start(bf16[1,272,512]{2,1,0:T(8,128)(2,1)S(1)} %get-tuple-element.325.refs_0_), channel_id=1, source_target_pairs={{0,4},{4,0},{8,12},{12,8},{16,20},{20,16},{24,28},{28,24},{1,5},{5... | collective-permute-start | bytes 835592 | tf_op jit(solution)/shard_map/ppermute | solution.py:792
  149.2 11.0 %collective-permute-start.40 = (bf16[1,256,512]{2,1,0:T(8,128)(2,1)S(1)}, bf16[1,256,512]{2,1,0:T(8,128)(2,1)S(1)}, u32[]{:S(2)}, u32[]{:S(2)}) collective-permute-start(bf16[1,256,512]{2,1,0:T(8,128)(2,1)S(1)} %get-tuple-element.326.refs_0_), channel_id=1, source_target_pairs={{0,4},{4,0},{8,12},{12,8},{16,20},{20,16},{24,28},{28,24},{1,5},{5... | collective-permute-start | bytes 786440 | tf_op jit(solution)/shard_map/ppermute | solution.py:792
  (6 other events, 24.3 us)

commit v2 on v1

--- a/solution.py
+++ b/solution.py
@@ -207,7 +207,7 @@
 def setup_kernel(packing, flow, where, *refs):
     group_tokens, bucket_group, lengths, inputs, cotangent, memory, segments, gains, shifts, biases, refs = *refs[:10], refs[10:]
     if packing:
-        query, kv, out, cross, refs = *refs[:4], refs[4:]
+        query, kv, out, w_in, w_out, cross, ffn, refs = *refs[:7], refs[7:]
     x, cot, memory_part, vectors, molecules, tokens_now, group_now, lengths_now, word_sems, sems = refs
     words = start_all([(group_tokens, tokens_now), (bucket_group, group_now), (lengths, lengths_now)], word_sems)
     moves = [(memory.at[:, where[0]], memory_part), (inputs.at[where[0]], x), (cotangent.at[where[0]], cot)]
@@ -224,6 +224,7 @@
         for k in range(count):
             lanes = pl.ds(pl.multiple_of((where[3] * count + k) * wide, wide), wide)
             moves.append((out.at[:, lanes], cross.at[3 * half + k * size : 3 * half + (k + 1) * size, :]))
+        moves += [(w_in, ffn.at[0]), (w_out, ffn.at[1])]
     copies = start_all(moves, sems)
     for copy in words:
         copy.wait()
@@ -432,7 +433,11 @@
         cotangent, vectors, w_in, bias, w_out, refs = *refs[:5], refs[5:]
         after_cross, normed, low, active, grad_hidden, part, part_grad = refs
     else:
-        normed, low, begun, begun_grad, w_in, w_out, bias, refs = *refs[:7], refs[7:]
+        normed, low, begun, begun_grad, w_in, bias, refs = *refs[:6], refs[6:]
+        if len(w_in.shape) == 3:
+            w_in, w_out = w_in.at[0], w_in.at[1]
+        else:
+            w_out, refs = refs[0], refs[1:]
         active, grad_hidden, parts, parts_grad = refs[0], refs[1], refs[2 : 2 + BACK], refs[2 + BACK :]
     if bias.shape[0] == 1:
         row = row_of(bias, 0)
@@ -540,7 +545,7 @@
     keep, send, terms, result = refs[0], refs[1], refs[2 : 2 + BACK], refs[-1]
     flow.need(*w)
     pairs = [[(a, b) for a in left] for left, b in ((dq, normed), (dk, memory), (dv, memory), (heads, low))]
-    first = where[4] == 0
+    first = where[3] == 0
     for i, grads in enumerate(shard_grads(pairs)):
         upper, lower = jnp.concatenate(grads[:2], axis=0), jnp.concatenate(grads[2:], axis=0)
         keep[i] = jnp.where(first, upper, lower)
@@ -555,14 +560,18 @@
         result[block, :] = (after_cross[block, :] + both + row_of(vectors, OUT + 2)).astype(BF16)
 
 
+def put_grads(target, grads):
+    size = grads[0].shape[0]
+    for k, grad in enumerate(grads):
+        target[0, k * size : (k + 1) * size, :] = grad.astype(target.dtype)
+
+
 def self_backward_kernel(n, flow, where, *refs):
     after_self, mine, theirs, refs = refs[0], refs[1 : 1 + BACK], refs[1 + BACK : 1 + 2 * BACK], refs[1 + 2 * BACK :]
-    grad_cross, vectors, molecules, refs = *refs[:3], refs[3:]
-    (q, k, v, totals, w_out), refs = [refs[i * n : (i + 1) * n] for i in range(5)], refs[5 * n :]
-    grad_self, low, refs = refs[0], refs[1], refs[2:]
-    (dq, dk, dv, bias_sums), refs = [refs[i * n : (i + 1) * n] for i in range(4)], refs[4 * n :]
-    sums, refs = refs[0], refs[1:]
-    grad_heads, sum_k, sum_v = refs[:n], refs[n], refs[n + 1]
+    grad_cross, vectors, molecules, q, k, v, totals, refs = *refs[:7], refs[7:]
+    w_out, refs = refs[:n], refs[n:]
+    normed, heads, grad_self, low, dq, dk, dv, bias_sums, sums, refs = *refs[:9], refs[9:]
+    first, send, grad_heads, sum_k, sum_v = refs
     seq, width = after_self.shape
     rows = [jnp.zeros((1, width), F32)] * 3
     for block in row_blocks(seq):
@@ -577,14 +586,42 @@
     for i, row in enumerate(rows):
         sums[i : i + 1, :] = row
     flow.need(*w_out)
-    spread_grad_heads(low, w_out, grad_heads)
+    spread_grad_heads(low, w_out, [first, grad_heads] if n == 2 else [grad_heads])
     own = molecules[0:1, :]
-    flow.need(*q, *k, *v, *totals)
-    for i in range(n):
-        attend_backward(
-            q[i], k[i], v[i], own, own, totals[i], grad_heads[i], dq[i], dk[i], dv[i], sum_k, sum_v, True
-        )
-        column_sums(bias_sums[i], (dq[i], dv[i]))
+    flow.need(q, k, v, totals)
+    attend_backward(q, k, v, own, own, totals, grad_heads, dq, dk, dv, sum_k, sum_v, True)
+    column_sums(bias_sums, (dq, dv))
+    grads = [dot_left(a[...], b[...]) for a, b in ((dq, normed), (dk, normed), (dv, normed), (heads, low))]
+    if n == 2:
+        put_grads(send, grads)
+    else:
+        half = grads[0].shape[0] // 2
+        put_grads(first, [g[:half] for g in grads])
+        put_grads(send, [g[half:] for g in grads])
+
+
+def self_backward_rest_kernel(n, flow, where, *refs):
+    w, grads_last, refs = refs[:n], refs[n : n + 3], refs[n + 3 :]
+    pieces = [grads_last]
+    if n == 2:
+        molecules, q, k, v, totals, grad_heads, normed, heads, low, refs = *refs[:9], refs[9:]
+        bias_sums, keep, parts_out, refs = refs[0], refs[1], refs[2 : 2 + BACK], refs[2 + BACK :]
+        dq, dk, dv, sum_k, sum_v = refs
+        own = molecules[0:1, :]
+        flow.need(q, k, v, totals)
+        attend_backward(q, k, v, own, own, totals, grad_heads, dq, dk, dv, sum_k, sum_v, True)
+        column_sums(bias_sums, (dq, dv))
+        put_grads(keep, [dot_left(a[...], b[...]) for a, b in ((dq, normed), (dk, normed), (dv, normed), (heads, low))])
+        pieces = [(dq, dk, dv), grads_last]
+    else:
+        parts_out = refs[:BACK]
+    flow.need(*w)
+    for block in row_blocks(grads_last[0].shape[0]):
+        total = 0.0
+        for matrices, grads in zip(w, pieces):
+            for which, d in enumerate(grads):
+                total += dot_right(d[block, :], matrices[which])
+        put_half(parts_out, block, total)
 
 
 def input_backward_kernel(n, flow, where, x, *refs):
@@ -617,27 +654,9 @@
     small_other[...] = small[1]
 
 
-def self_weights_kernel(n, flow, where, *refs):
-    (dq, dk, dv, heads, w), refs = [refs[i * n : (i + 1) * n] for i in range(5)], refs[5 * n :]
-    normed, low, parts_out, keep, send = refs[0], refs[1], refs[2 : 2 + BACK], refs[-2], refs[-1]
-    pairs = [[(a, b) for a in left] for left, b in ((dq, normed), (dk, normed), (dv, normed), (heads, low))]
-    for target, grads in zip((keep, send), shard_grads(pairs)):
-        size = grads[0].shape[0]
-        for k, grad in enumerate(grads):
-            target[0, k * size : (k + 1) * size, :] = grad.astype(target.dtype)
-    flow.need(*w)
-    for block in row_blocks(normed.shape[0]):
-        total = 0.0
-        for i in range(n):
-            for which, d in enumerate((dq[i], dk[i], dv[i])):
-                total += dot_right(d[block, :], w[i][which])
-        put_half(parts_out, block, total)
-
-
-def fold_kernel(count, ride, mode, bit, flow, where, *refs):
+def fold_kernel(count, size, ride, mode, bit, flow, where, *refs):
     keeps, gots, refs = refs[:count], refs[count : 2 * count], refs[2 * count :]
     planes = [(k, p) for k in range(count) for p in range(keeps[k].shape[0])]
-    size = keeps[0].shape[1]
 
     def part(at, rows):
         k, p = planes[at]
@@ -649,22 +668,81 @@
         for at in range(len(planes)):
             for target, side in ((keep, where[3 + bit]), (send, 1 - where[3 + bit])):
                 rows = pl.ds(pl.multiple_of(side * half, half), half)
-                target[at] = part(at, rows).astype(target.dtype)
+                target[at, :half, :] = part(at, rows).astype(target.dtype)
     elif mode == "shard":
-        if ride:
-            refs[2][0, size:, :] = refs[0][...]
+        if ride is not None:
+            refs[-1][0, size : size + SMALL, :] = refs[0][...]
         for at, target in enumerate(refs[-2:]):
             target[0, :size, :] = part(at, slice(0, size)).astype(target.dtype)
     else:
         out = refs[-1]
         for at in range(len(planes)):
-            value = part(at, slice(0, size))
-            if ride and mode == "full":
-                own, came = refs[:2]
-                last = came.shape[1]
-                small = own[...].astype(F32) + came[0, last - SMALL : last, :].astype(F32)
-                value = jnp.concatenate([value, small], axis=0)
-            out[at] = value.astype(out.dtype)
+            out[at, :size, :] = part(at, slice(0, size)).astype(out.dtype)
+        if ride is not None:
+            own, came = refs[:2]
+            small = own[...].astype(F32) + came[0, ride : ride + SMALL, :].astype(F32)
+            out[0, size : size + SMALL, :] = small.astype(out.dtype)
+
+
+def memory_pairs(axis):
+    step = 1 if axis == "row" else 2 << axis
+    return [(k, k | step) for k in range(16) if not k & step]
+
+
+def memory_bit(where, axis):
+    return where[0] if axis == "row" else where[3 + axis]
+
+
+def send_blocks(where, axis, blocks, send, offset):
+    low = memory_bit(where, axis) == 0
+    per = 8 // send.shape[0]
+    for k, (a, b) in enumerate(memory_pairs(axis)):
+        at = offset + k % per * SMALL
+        send[k // per, at : at + SMALL, :] = jnp.where(low, blocks[b], blocks[a])
+
+
+def take_blocks(where, axis, kept, got, offset):
+    low = memory_bit(where, axis) == 0
+    per = 8 // got.shape[0]
+    blocks = {}
+    for k, (a, b) in enumerate(memory_pairs(axis)):
+        at = offset + k % per * SMALL
+        came = got[k // per, at : at + SMALL, :]
+        blocks[a] = jnp.where(low, kept[a], came)
+        blocks[b] = jnp.where(low, came, kept[b])
+    return blocks
+
+
+def memory_start_kernel(axis, flow, where, *refs, send, offset):
+    mine, theirs, kept = refs[:BACK], refs[BACK : 2 * BACK], refs[2 * BACK]
+    half, width = mine[0].shape
+    tokens = half * BACK // 8
+    share = LANES
+    blocks = {}
+    for r in (0, 1):
+        lanes = pl.ds(pl.multiple_of((2 * r + where[1]) * share, share), share)
+        for k in range(BACK):
+            total = (mine[k][:, lanes].astype(F32) + theirs[k][:, lanes].astype(F32)).astype(BF16)
+            for d in range(half // tokens):
+                block = total[d * tokens : (d + 1) * tokens]
+                parts = [block[q : q + SMALL] for q in range(0, tokens, SMALL)]
+                at = 2 * (k * half // tokens + d) + r
+                blocks[at] = jnp.concatenate(parts, axis=1)
+                kept[at] = blocks[at]
+    send_blocks(where, axis, blocks, send, offset)
+
+
+def memory_send_kernel(before, at, axis, flow, where, old, got, kept, send):
+    blocks = take_blocks(where, before, old, got, at)
+    for k, block in blocks.items():
+        kept[k] = block
+    send_blocks(where, axis, blocks, send, 0)
+
+
+def memory_end_kernel(before, at, flow, where, old, got, out):
+    for k, block in take_blocks(where, before, old, got, at).items():
+        parts = [block[:, q : q + LANES] for q in range(0, block.shape[1], LANES)]
+        out[k] = jnp.concatenate(parts, axis=0).astype(out.dtype)
 
 
 def join_kernel(ride, bit, flow, where, near, got, out):
@@ -708,18 +786,12 @@
 
 
 def cross_grads_kernel(bit, flow, where, near, got, query, kv, out):
-    half = near.shape[1] // 2
-    value = [joined(where, bit, near[:, k * half : (k + 1) * half], got[:, k * half : (k + 1) * half], 0) for k in (0, 1)]
-    value = jnp.concatenate(value, axis=0)
+    value = joined(where, bit, near, got, 0)
     size = out.shape[0]
     query[...] = value[:size].T
     for k in (0, 1):
         kv[k] = value[(k + 1) * size : (k + 2) * size].T
     out[...] = value[3 * size :]
-
-
-def widen_kernel(flow, where, value, out):
-    out[...] = value[...].astype(out.dtype)
 
 
 def ffn_grads_kernel(bit, flow, where, near, got, grad_in, grad_out):
@@ -734,19 +806,6 @@
         for row, value in ((where[0], own), (1 - where[0], got)):
             out[row] = value[k * seq : (k + 1) * seq, :].astype(out.dtype)
         flow.send(out)
-
-
-def memory_blocks_kernel(flow, where, *refs):
-    mine, theirs, out = refs[:BACK], refs[BACK : 2 * BACK], refs[2 * BACK]
-    dp, rows, tokens, share = out.shape
-    half, width = mine[0].shape
-    team = width // (rows * share)
-    for r in range(rows):
-        lanes = pl.ds(pl.multiple_of((r * team + where[1]) * share, share), share)
-        for k in range(BACK):
-            total = (mine[k][:, lanes].astype(F32) + theirs[k][:, lanes].astype(F32)).astype(BF16)
-            for d in range(half // tokens):
-                out[k * half // tokens + d, r] = total[d * tokens : (d + 1) * tokens]
 
 
 def shards(
@@ -821,21 +880,24 @@
     bias_other = other(bias_own)
     other_self_out = other(self_out)
     memory_rows = memory.reshape((dp, rows) + memory.shape[1:])
-    packing = apart and width % (2 * head) == 0
+    packing = apart and width % (2 * head) == 0 and ffn_in.shape == ffn_out.shape
     ins = [Raw(group_tokens), Raw(bucket_group), Raw(mem_lengths), Raw(inputs), Raw(cotangent), Raw(memory_rows)]
     ins += [far(segment_ids), far(norm_gain), far(norm_bias), far(out_bias)]
     outs = [whole, whole, ((dp,) + memory.shape[1:], BF16), ((VECTORS, width), F32), ((2, seq), jnp.int32)]
     if packing:
-        ins += [Raw(v) for v in (cross_q, cross_kv, cross_out)]
-        outs = [((3 * width // 2 + cross_out.size // head // 2, head), BF16)] + outs
+        ins += [Raw(v) for v in (cross_q, cross_kv, cross_out, ffn_in, ffn_out)]
+        outs = [((3 * width // 2 + cross_out.size // head // 2, head), BF16), ((2,) + ffn_in.shape, BF16)] + outs
     *packed, x, cot, memory_part, vectors, molecules = run(
         functools.partial(setup_kernel, packing),
         ins,
         outs,
         scratch=[pltpu.SMEM(v.shape, jnp.int32) for v in (group_tokens, bucket_group, mem_lengths)]
-        + [pltpu.SemaphoreType.DMA((3,)), pltpu.SemaphoreType.DMA((6 + width // head // 2,))],
+        + [pltpu.SemaphoreType.DMA((3,)), pltpu.SemaphoreType.DMA((8 + width // head // 2,))],
         name="setup",
     )
+    if packing:
+        near_cross = other(packed[0])
+        got_cross = data_swap(near_cross, 0)
     memory_row = lax.all_to_all(memory_part, "dp", split_axis=0, concat_axis=0, tiled=True).reshape(mem_len, width)
     def pieces(own, theirs, axis):
         return [far(own), theirs] if apart else [jnp.concatenate([own, theirs], axis=axis)]
@@ -853,15 +915,12 @@
         if last:
             ins += [*w_self_out, *heads_self]
             outs += front
-        hold = [near_cross] if packing and i == 1 else []
-        got = run(functools.partial(self_forward_kernel, n, i), ins, outs, name=f"self_forward_{i}", hold=hold)
+        got = run(functools.partial(self_forward_kernel, n, i), ins, outs, name=f"self_forward_{i}")
         if i == 0:
             normed_self, got = got[0], got[1:]
             early = (normed_self, other_qkv, bias_other, other_self_out)
             if packing:
-                near_cross = other(later(packed[0], *early))
-                got_cross = data_swap(near_cross, 0)
-                other_in, other_out = [other(later(w, near_cross)) for w in (ffn_in, ffn_out)]
+                other_ffn = other(later(packed[1], *early, near_cross))
             else:
                 other_cross = [other(later(w, *early)) for w in (cross_q, cross_kv, cross_out)]
                 other_in, other_out = [other(later(w, *other_cross)) for w in (ffn_in, ffn_out)]
@@ -912,7 +971,7 @@
         [full, whole, whole, units, units, full, full],
         name="ffn_0",
     )
-    ins = [other_in, other_out, b_in[1]]
+    ins = [other_ffn if packing else other_in, b_in[1]] + ([] if packing else [other_out])
     act_other, hid_other, *parts = run(
         functools.partial(ffn_kernel, 1),
         [normed_ffn, low_ffn, begun, begun_grad, *ins],
@@ -924,39 +983,57 @@
 
     class Reduction:
         def __init__(self, keeps, sends, axes):
-            self.keeps, self.axes, self.ride, self.carry, self.turned = keeps, axes, [], [], False
+            self.keeps, self.axes, self.ride, self.carry = keeps, axes, [], []
             self.gots = [swap(s, a) for s, a in zip(sends, axes[0])]
             self.halved = [b for b in axes[0] if b != "row"][:1]
+            self.size = sends[0].shape[1]
             self.chunk = None
 
-        def plan(self):
-            extra = SMALL if self.ride else 0
+        def plan(self, extra=None):
             if self.chunk is not None:
-                bit = self.halved.pop()
+                bit, small = self.halved.pop(), SMALL if self.ride else 0
                 planes, size, _ = self.chunk.shape
-                outs = [((planes, 2 * size - extra, width), BF16)]
-                return functools.partial(join_kernel, bool(extra), bit), [self.chunk, self.got], outs
-            axes, keeps, ride = self.axes, self.keeps, []
+                outs = [((planes, 2 * size - small, width), BF16)]
+                return functools.partial(join_kernel, bool(small), bit), [self.chunk, self.got], outs
+            axes, keeps, size = self.axes, self.keeps, self.size
             planes = sum(k.shape[0] for k in keeps)
-            size = keeps[0].shape[1]
-            bit = 0
+            bit, ride, at, rows = 0, [], None, size
             if len(axes) == 1:
-                mode, outs = "last", [((planes, size, width), BF16)]
+                mode = "last"
             elif axes[1][0] == "row":
-                mode, ride = "shard", self.carry
-                outs = [((1, size, width), F32), ((1, size + (SMALL if ride else 0), width), BF16)]
+                mode, planes = "shard", 1
+                if self.carry:
+                    ride, at, rows = self.carry, size, size + SMALL
             elif len(axes) == 2:
-                mode, ride, outs = "full", self.ride, [((planes, size + extra, width), BF16)]
+                mode = "full"
+                if self.ride:
+                    ride, at, rows = self.ride, self.ride_at, size + SMALL
+                    self.size += SMALL
             else:
-                mode, bit, shape = "half", axes[1][0], (planes, size // 2, width)
-                outs = [(shape, F32), (shape, BF16)]
+                mode, bit, rows = "half", axes[1][0], size // 2
+                self.size = rows
                 self.halved.append(bit)
-            return functools.partial(fold_kernel, len(keeps), bool(ride), mode, bit), [*keeps, *self.gots, *ride], outs
+            more = 8 // planes * SMALL if extra else 0
+            outs = [((planes, rows + more, width), BF16)]
+            if mode in ("half", "shard"):
+                outs = [((planes, self.size, width), F32)] + outs
+            ins = [*keeps, *self.gots, *ride]
+            kernel = functools.partial(fold_kernel, len(keeps), size, at, mode, bit)
+            if not extra:
+                return kernel, ins, outs
+            second, second_ins, second_outs = extra
+            self.extra_at = rows
+
+            def both(flow, where, *refs):
+                a, b = len(ins), len(ins) + len(second_ins)
+                c = b + len(second_outs)
+                kernel(flow, where, *refs[:a], *refs[c:])
+                second(flow, where, *refs[a:c], send=refs[-1], offset=rows)
+
+            return both, ins + second_ins, second_outs + outs
 
         def take(self, got):
             if self.chunk is not None or len(self.axes) == 1:
-                if self.chunk is None and self.turned:
-                    self.halved[:2] = self.halved[1::-1]
                 self.chunk = got[0]
                 self.got = swap(self.chunk, self.halved[-1])
             else:
@@ -967,11 +1044,17 @@
         def ready(self):
             return self.chunk is not None and len(self.halved) == 1
 
-    def advance(name, *groups, cost=0.1):
+    def advance(name, *groups, extra=None, more=None):
         groups = [g for g in groups if not g.ready()]
-        if groups:
-            for g, got in zip(groups, run.batch([g.plan() for g in groups], name=name, cost=cost)):
-                g.take(got)
+        parts = [g.plan(extra if i == 0 else None) for i, g in enumerate(groups)] + ([more] if more else [])
+        results = run.batch(parts, name=name) if parts else []
+        given = results.pop() if more else []
+        for i, (g, got) in enumerate(zip(groups, results)):
+            if extra and i == 0:
+                count = len(extra[2])
+                given, got = got[:count], got[count:]
+            g.take(got)
+        return given
 
     ffn_sums, keep_out, send_out, keep_in, send_in = run(
         ffn_weights_kernel,
@@ -1007,50 +1090,49 @@
         [((2, 2 * head, width), F32), ((2, 2 * head, width), BF16)] + back + [whole],
         name="cross_weights",
     )
-    by_cross = Reduction([keep], [send], [[1], [0], ["row"]] + [[k] for k in range(2, bits)])
-    by_cross.turned = True
+    by_cross = Reduction([keep], [send], [[0], [1], ["row"]] + [[k] for k in range(2, bits)])
     advance("fold_ffn", by_out, by_in)
 
-    got = run(
+    group = ((1, 4 * head, width), F32)
+    ins = [after_self, *terms, grad_cross, vectors, molecules] + [far(v) for v in saved_self[-1]]
+    grad_self, low_self, *last_grads, last_sums, small_cross, first, send = run(
         functools.partial(self_backward_kernel, n),
-        [after_self, *terms, grad_cross, vectors, molecules] + [far(v) for v in saved_of(saved_self)] + [*w_self_out],
-        [full, whole] + [local] * (3 * n) + [bias_sum] * n + [((3, width), F32)],
-        scratch=scratch,
+        ins + [*w_self_out, normed_self, heads_self[-1]],
+        [full, whole] + [local] * 3 + [bias_sum, ((3, width), F32), local if n == 2 else group, (group[0], BF16)],
+        scratch=scratch[-3:],
         name="self_backward",
     )
-    grad_self, low_self, got = got[0], got[1], got[2:]
-    self_grads, self_bias_sums, small_cross = got[: 3 * n], got[3 * n : 4 * n], got[4 * n]
+    by_self = Reduction([first], [send], [["row"]] + [[k] for k in range(bits)])
     by_ffn = by_out
     by_ffn.keeps, by_ffn.gots = by_out.keeps + by_in.keeps, by_out.gots + by_in.gots
     by_ffn.axes = [[0]] + [[k] for k in range(1, bits)]
-    advance("ffn_1", by_ffn)
-    *parts, keep, send = run(
-        functools.partial(self_weights_kernel, n),
-        [*self_grads, *heads_self, *w_qkv, normed_self, low_self],
-        back + [((1, 4 * head, width), F32), ((1, 4 * head, width), BF16)],
-        name="self_weights",
-    )
-    by_self = Reduction([keep], [send], [["row"]] + [[k] for k in range(bits)])
-    terms = team_parts(parts)
-    advance("cross_1", by_cross)
-    advance("ffn_2", by_ffn)
     mem_terms = team_parts(memory_terms)
     share = width // mp
-    if share % LANES == 0 and team == 2:
-        (blocks,) = run(
-            memory_blocks_kernel, mem_terms, [((dp, rows, mem_len // dp, share), BF16)], name="memory_blocks"
-        )
-    else:
-        mine, theirs = jnp.concatenate(mem_terms[:BACK]), jnp.concatenate(mem_terms[BACK:])
-        total = (mine.astype(F32) + theirs.astype(F32)).astype(BF16)
-        total = total.reshape(dp, mem_len // dp, rows, team, share)
-        blocks = lax.dynamic_index_in_dim(total, seat, 3, keepdims=False).swapaxes(1, 2)
-    blocks = blocks.reshape(dp * rows, mem_len // dp, share)
-    same_seat = [[d * mp + m for d in range(dp) for m in range(mp) if m % team == s] for s in range(team)]
-    memory_got = lax.all_to_all(
-        blocks, ("dp", "mp"), split_axis=0, concat_axis=0, tiled=True, axis_index_groups=same_seat
-    )
-
+    along = share == LANES and team == 2 and dp == 8 and mem_len // dp * LANES == SMALL * width
+    blocks = ((16, SMALL, width), BF16)
+    extra = (functools.partial(memory_start_kernel, 1), mem_terms, [blocks]) if along else None
+    given = advance("ffn_1", by_ffn, extra=extra)
+    ins = [*w_qkv, *last_grads]
+    if n == 2:
+        ins += [molecules] + [far(v) for v in saved_self[0]] + [first, normed_self, heads_self[0], low_self]
+    outs = ([bias_sum, group] if n == 2 else []) + back
+    got = run(
+        functools.partial(self_backward_rest_kernel, n),
+        ins,
+        outs,
+        scratch=[pltpu.VMEM((seq, wide), BF16)] * 3 + scratch[-2:] if n == 2 else [],
+        name="self_backward_rest",
+    )
+    self_bias_sums = [last_sums]
+    if n == 2:
+        self_bias_sums, by_self.keeps, got = [got[0], last_sums], [got[1]], got[2:]
+    terms = team_parts(got)
+    sent, more = [blocks, ((1, 8 * SMALL, width), BF16)], None
+    if along:
+        more = (functools.partial(memory_send_kernel, 1, by_ffn.extra_at, 0), [*given, by_ffn.gots[0]], sent)
+    given = advance("cross_1", by_cross, more=more)
+    advance("ffn_2", by_ffn)
+    advance("self_1", by_self)
 
     fits = apart and 4 * head == width and unit == width
     if fits:
@@ -1078,17 +1160,44 @@
     )
 
     by_cross.carry = [small_other]
-
-    advance("cross_2", by_cross)
-    by_self.ride = [small_own, by_cross.gots[0]]
-    advance("self_1", by_self)
-    advance("all_1", by_self, by_ffn, by_cross)
+    if along:
+        more = (functools.partial(memory_send_kernel, 0, 0, "row"), [given[0], data_swap(given[1], 0)], sent)
+    given = advance("cross_2", by_cross, more=more)
+    by_self.ride, by_self.ride_at = [small_own, by_cross.gots[0]], by_cross.size
+    if along:
+        memory_state = [given[0], other(given[1])]
+    advance("all_1", by_cross, by_self, by_ffn)
     got_both = other(later(both, by_self.keeps[0]))
-    (grad_memory,) = run(widen_kernel, [memory_got], [far((memory_got.shape, F32))], name="widen_memory")
     advance("all_2", by_self, by_ffn, by_cross)
+    if not along:
+        mine, theirs = jnp.concatenate(mem_terms[:BACK]), jnp.concatenate(mem_terms[BACK:])
+        total = (mine.astype(F32) + theirs.astype(F32)).astype(BF16)
+        total = total.reshape(dp, mem_len // dp, rows, team, share)
+        blocks = lax.dynamic_index_in_dim(total, seat, 3, keepdims=False).swapaxes(1, 2)
+        blocks = blocks.reshape(dp * rows, mem_len // dp, share)
+        same_seat = [[d * mp + m for d in range(dp) for m in range(mp) if m % team == s] for s in range(team)]
+        grad_memory = lax.all_to_all(
+            blocks, ("dp", "mp"), split_axis=0, concat_axis=0, tiled=True, axis_index_groups=same_seat
+        ).astype(F32)
     advance("self_cross_3", by_self, by_cross)
-    while not (by_self.ready() and by_cross.ready() and by_ffn.ready()):
-        advance("rest", by_self, by_cross, by_ffn)
+
+    def cross_grads():
+        return run(
+            functools.partial(cross_grads_kernel, by_cross.halved[0]),
+            [by_cross.chunk, by_cross.got],
+            [far(((width, head), F32)), far(((2, width, head), F32)), far(((head, width), F32))],
+            name="cross_grads",
+        )
+
+    cross_results = None
+    if by_cross.ready():
+        cross_results = cross_grads()
+    more = (functools.partial(memory_send_kernel, "row", 0, 2), memory_state, sent) if along else None
+    while more or not (by_self.ready() and by_cross.ready() and by_ffn.ready()):
+        given = advance("rest", by_self, by_cross, by_ffn, more=more)
+        if more:
+            memory_state, more = [given[0], data_swap(given[1], 2)], None
+    grad_cross_q, grad_cross_kv, grad_cross_out = cross_results or cross_grads()
     mixed, grad_inputs = run(
         place_rows_kernel,
         [both, got_both],
@@ -1101,12 +1210,13 @@
         [far(((width, unit), F32)), far(((unit, width), F32))],
         name="ffn_grads",
     )
-    grad_cross_q, grad_cross_kv, grad_cross_out = run(
-        functools.partial(cross_grads_kernel, by_cross.halved[0]),
-        [by_cross.chunk, by_cross.got],
-        [far(((width, head), F32)), far(((2, width, head), F32)), far(((head, width), F32))],
-        name="cross_grads",
-    )
+    if along:
+        (grad_memory,) = run(
+            functools.partial(memory_end_kernel, 2, 0),
+            memory_state,
+            [far(((16, mem_len // dp, share), F32))],
+            name="memory_end",
+        )
     if fits:
         outs = [((2, head), F32), ((2, head), F32), ((1, unit), F32)]
     else:

time: 165 us -> 153 us (0.927)
  waiting for transfers between devices: 41.6 us -> 31.1 us
  starting transfers between devices: 49 us -> 51.2 us
    ppermute x11, waiting for transfers between devices: 12 us -> 1.73 us  [other(): return lax.ppermute(value, 'mp', across)]
    ppermute x17 -> x19, starting transfers between devices: 21.4 us -> 27.9 us  [data_swap(): return lax.ppermute(value, 'dp', [(i, i ^ 1 << k) for i in range(dp)])]
    all_to_all x1 -> x0, starting transfers between devices: 5.39 us -> none  [shards(): lax.all_to_all(blocks, ('dp', 'mp'), split_axis=0, concat_axis=0, tiled=T...]
    ppermute x17 -> x19, waiting for transfers between devices: 26 us -> 27.9 us  [data_swap(): return lax.ppermute(value, 'dp', [(i, i ^ 1 << k) for i in range(dp)])]
    pallas_call x31 -> x30, Pallas kernels: 69.5 us -> 68 us  [__call__(): pl.pallas_call(body, in_specs=[words] + specs + after_specs, out_specs=[f...]
  transfers between devices with their start and end apart: 44 -> 45, of which waited for: 15 -> 15; matrix products, arithmetic and copies ran while one was open for 0% -> 0% of each run, Pallas kernels for 39% -> 41%
where the time goes in v2:
time: 153 us
  Pallas kernels  68 us (44%)
  starting transfers between devices  51.2 us (33%)
  waiting for transfers between devices  31.1 us (20%)
    pallas_call x30, Pallas kernels, __call__(): pl.pallas_call(body, in_specs=[words] + specs + after_specs, out_specs=[f...  68 us
    ppermute x19, waiting for transfers between devices, data_swap(): return lax.ppermute(value, 'dp', [(i, i ^ 1 << k) for i in range(dp)])  27.9 us
    ppermute x19, starting transfers between devices, data_swap(): return lax.ppermute(value, 'dp', [(i, i ^ 1 << k) for i in range(dp)])  27.9 us
    ppermute x11, starting transfers between devices, other(): return lax.ppermute(value, 'mp', across)  13.6 us
    all_to_all x1, starting transfers between devices, shards(): lax.all_to_all(memory_part, 'dp', split_axis=0, concat_axis=0, tiled=True)  6.27 us
    ppermute x14, starting transfers between devices, seat_swap(): return lax.ppermute(value, 'mp', [(i, i ^ step) for i in range(mp)])  3.36 us
  transfers between devices with their start and end apart: 45, of which 15 were waited for; matrix products, arithmetic and copies ran while one was open for 0% of the time, Pallas kernels for 41%

profile of v2, /device:TPU:0, one launch (start us, length us, event | category | flops | bytes accessed | tf_op | source)
XLA Modules:
  0.0 152.6 jit_solution(8724588900277819686)
XLA Ops:
  0.6 3.0 %collective-permute-start = (bf16[3,512,128]{2,1,0:T(8,128)(2,1)}, bf16[3,512,128]{2,1,0:T(8,128)(2,1)S(1)}, u32[]{:S(2)}, u32[]{:S(2)}) collective-permute-start(bf16[3,512,128]{2,1,0:T(8,128)(2,1)} %refs_0_.3), channel_id=1, source_target_pairs={{0,2},{1,3},{2,0},{3,1},{4,6},{5,7},{6,4},{7,5},{8,10},{9,11},{10,... | collective-permute-start | bytes 1179656 | tf_op jit(solution)/shard_map/ppermute | solution.py:845
  3.8 3.3 %setup.1 = (bf16[1024,128]{1,0:T(8,128)(2,1)S(1)}, bf16[2,512,512]{2,1,0:T(8,128)(2,1)S(1)}, bf16[512,512]{1,0:T(8,128)(2,1)S(1)}, bf16[512,512]{1,0:T(8,128)(2,...) custom-call(s32[6]{0:T(128)S(1)} %stack.27.where_ref, ...), custom_call_target="tpu_custom_call" | custom-call | flops 1000000 | bytes 300000 | tf_op jit(solution)/shard_map/setup/pallas_call | solution.py:146
  8.1 6.3 %all-to-all-start = ((bf16[8,64,512]{2,1,0:T(8,128)(2,1)}), bf16[8,64,512]{2,1,0:T(8,128)(2,1)S(1)}, u32[]{:S(2)}, u32[]{:S(2)}) async-start(bf16[8,64,512]{2,1,0:T(8,128)(2,1)} %get-tuple-element.191), calls=%async_computation | async-start | bytes 1048576 | tf_op jit(solution)/shard_map/all_to_all | solution.py:901
  14.4 1.5 collective-permute-start.2
  16.5 3.8 %self_forward_0.1 = (bf16[512,512]{1,0:T(8,128)(2,1)S(1)}, bf16[512,128]{1,0:T(8,128)(2,1)}, bf16[512,128]{1,0:T(8,128)(2,1)}, bf16[512,128]{1,0:T(8,128)(2,1)},...) custom-call(s32[6]{0:T(128)S(1)} %stack.27.where_ref, ...), custom_call_target="tpu_custom_call" | custom-call | flops 1000000 | bytes 300000 | tf_op jit(solution)/shard_map/self_forward_0/pallas_call | solution.py:146
  20.3 1.2 collective-permute-done.1.refs_4_.refs_3_.refs_5_
  21.5 1.8 %collective-permute-start.9 = (bf16[2,512,512]{2,1,0:T(8,128)(2,1)}, bf16[2,512,512]{2,1,0:T(8,128)(2,1)}, u32[]{:S(2)}, u32[]{:S(2)}) collective-permute-start(bf16[2,512,512]{2,1,0:T(8,128)(2,1)} %copy-done), channel_id=1, source_target_pairs={{0,2},{1,3},{2,0},{3,1},{4,6},{5,7},{6,4},{7,5},{8,10},{9,11},{10,... | collective-permute-start | bytes 3145736 | tf_op jit(solution)/shard_map/ppermute | solution.py:845
  23.3 3.7 %self_forward_1.1 = (bf16[512,128]{1,0:T(8,128)(2,1)}, bf16[512,128]{1,0:T(8,128)(2,1)}, bf16[512,128]{1,0:T(8,128)(2,1)}, bf16[512,128]{1,0:T(8,128)(2,1)S(1)},...) custom-call(s32[6]{0:T(128)S(1)} %stack.27.where_ref, ...), custom_call_target="tpu_custom_call" | custom-call | flops 1000000 | bytes 300000 | tf_op jit(solution)/shard_map/self_forward_1/pallas_call | solution.py:146
  27.6 1.5 collective-permute-start.6
  29.0 1.9 %memory_0.1 = (bf16[512,128]{1,0:T(8,128)(2,1)S(1)}, bf16[512,128]{1,0:T(8,128)(2,1)S(1)}, f32[8,128]{1,0:T(8,128)}) custom-call(s32[6]{0:T(128)S(1)} %stack.27.where_ref, bf16[512,512]{1,0:T(8,128)(2,1)S(1)} %bitcast.10, bf16[2,512,128]{2,1,0:T(8,128)(2,1)} %refs_8_.3, bf16[8,128]{1,0:T(8,128)(2,1)S(1)} %pad_maximum_fusion.refs_4_.refs_2_.refs_8_, ...), custom_call_target="tpu_custom_call" | custom-call | flops 1000000 | bytes 300000 | tf_op jit(solution)/shard_map/memory_0/pallas_call | solution.py:146
  31.0 4.5 %cross_forward_0.1 = (f32[512,512]{1,0:T(8,128)S(1)}, bf16[512,512]{1,0:T(8,128)(2,1)S(1)}, bf16[512,128]{1,0:T(8,128)(2,1)S(1)}, bf16[512,128]{1,0:T(8,128)(2,1...) custom-call(s32[6]{0:T(128)S(1)} %stack.27.where_ref, bf16[512,512]{1,0:T(8,128)(2,1)S(1)} %get-tuple-element.182.refs_0_, ...), custom_call_target="tpu_custom_call" | custom-call | flops 1000000 | bytes 300000 | tf_op jit(solution)/shard_map/cross_forward_0/pallas_call | solution.py:146
  36.9 3.3 %cross_forward_1.1 = (bf16[512,128]{1,0:T(8,128)(2,1)S(1)}, bf16[512,128]{1,0:T(8,128)(2,1)S(1)}, f32[2,512]{1,0:T(2,128)S(1)}, bf16[256,512]{1,0:T(8,128)(2,1)S...) custom-call(s32[6]{0:T(128)S(1)} %stack.27.where_ref, bf16[512,512]{1,0:T(8,128)(2,1)S(1)} %get-tuple-element.197.refs_0_.refs_10_, ...), custom_call_target="tpu_custom_call" | custom-call | flops 1000000 | bytes 300000 | tf_op jit(solution)/shard_map/cross_forward_1/pallas_call | solution.py:146
  42.2 4.3 %ffn_0.1 = (f32[512,512]{1,0:T(8,128)S(1)}, bf16[512,512]{1,0:T(8,128)(2,1)S(1)}, bf16[512,512]{1,0:T(8,128)(2,1)S(1)}, bf16[512,512]{1,0:T(8,128)(2,1)S(1)}, bf...) custom-call(s32[6]{0:T(128)S(1)} %stack.27.where_ref, ...), custom_call_target="tpu_custom_call" | custom-call | flops 1000000 | bytes 300000 | tf_op jit(solution)/shard_map/ffn_0/pallas_call | solution.py:146
  46.5 3.6 %ffn_1.2 = (bf16[512,512]{1,0:T(8,128)(2,1)S(1)}, bf16[512,512]{1,0:T(8,128)(2,1)S(1)}, bf16[256,512]{1,0:T(8,128)(2,1)S(1)}, bf16[256,512]{1,0:T(8,128)(2,1)S(1...) custom-call(s32[6]{0:T(128)S(1)} %stack.27.where_ref, ...), custom_call_target="tpu_custom_call" | custom-call | flops 1000000 | bytes 300000 | tf_op jit(solution)/shard_map/ffn_1/pallas_call | solution.py:146
  50.3 1.8 %ffn_weights.1 = (f32[2,512]{1,0:T(2,128)S(1)}, f32[1,512,512]{2,1,0:T(8,128)S(1)}, bf16[1,512,512]{2,1,0:T(8,128)(2,1)S(1)}, f32[2,256,512]{2,1,0:T(8,128)S(1)}...) custom-call(s32[6]{0:T(128)S(1)} %stack.27.where_ref, bf16[512,512]{1,0:T(8,128)(2,1)S(1)} %get-tuple-element.224.refs_0_, ...), custom_call_target="tpu_custom_call" | custom-call | flops 1000000 | bytes 300000 | tf_op jit(solution)/shard_map/ffn_weights/pallas_call | solution.py:146
  53.5 1.5 collective-permute-start.15
  55.5 6.5 %cross_backward.1 = (f32[512,512]{1,0:T(8,128)S(1)}, bf16[512,512]{1,0:T(8,128)(2,1)S(1)}, bf16[512,128]{1,0:T(8,128)(2,1)S(1)}, bf16[512,128]{1,0:T(8,128)(2,1)...) custom-call(s32[6]{0:T(128)S(1)} %stack.27.where_ref, ...), custom_call_target="tpu_custom_call" | custom-call | flops 1000000 | bytes 300000 | tf_op jit(solution)/shard_map/cross_backward/pallas_call | solution.py:146
  62.6 3.1 %cross_weights.1 = (f32[2,256,512]{2,1,0:T(8,128)S(1)}, bf16[2,256,512]{2,1,0:T(8,128)(2,1)S(1)}, bf16[256,512]{1,0:T(8,128)(2,1)S(1)}, bf16[256,512]{1,0:T(8,12...) custom-call(s32[6]{0:T(128)S(1)} %stack.27.where_ref, bf16[512,128]{1,0:T(8,128)(2,1)S(1)} %get-tuple-element.242.refs_0_, ...), custom_call_target="tpu_custom_call" | custom-call | flops 1000000 | bytes 300000 | tf_op jit(solution)/shard_map/cross_weights/pallas_call | solution.py:146
  66.4 1.2 collective-permute-done.15.refs_3_
  68.3 1.6 %collective-permute-start.18 = (bf16[1,256,512]{2,1,0:T(8,128)(2,1)S(1)}, bf16[1,256,512]{2,1,0:T(8,128)(2,1)S(1)}, u32[]{:S(2)}, u32[]{:S(2)}) collective-permute-start(bf16[1,256,512]{2,1,0:T(8,128)(2,1)S(1)} %get-tuple-element.267), channel_id=1, source_target_pairs={{0,4},{4,0},{8,12},{12,8},{16,20},{20,16},{24,28},{28,24},{1,5},{5... | collective-permute-start | bytes 786440 | tf_op jit(solution)/shard_map/ppermute | solution.py:851
  71.4 5.1 %self_backward.1 = (f32[512,512]{1,0:T(8,128)S(1)}, bf16[512,512]{1,0:T(8,128)(2,1)S(1)}, bf16[512,128]{1,0:T(8,128)(2,1)S(1)}, bf16[512,128]{1,0:T(8,128)(2,1)S...) custom-call(s32[6]{0:T(128)S(1)} %stack.27.where_ref, ...), custom_call_target="tpu_custom_call" | custom-call | flops 1000000 | bytes 300000 | tf_op jit(solution)/shard_map/self_backward/pallas_call | solution.py:146
  78.4 1.7 %collective-permute-start.25 = (bf16[2,192,512]{2,1,0:T(8,128)(2,1)S(1)}, bf16[2,192,512]{2,1,0:T(8,128)(2,1)S(1)}, u32[]{:S(2)}, u32[]{:S(2)}) collective-permute-start(bf16[2,192,512]{2,1,0:T(8,128)(2,1)S(1)} %get-tuple-element.287), channel_id=1, source_target_pairs={{0,8},{4,12},{8,0},{12,4},{16,24},{20,28},{24,16},{28,20},{1,9},{5... | collective-permute-start | bytes 1179656 | tf_op jit(solution)/shard_map/ppermute | solution.py:851
  81.0 4.8 %self_backward_rest.1 = (f32[2,128]{1,0:T(2,128)S(1)}, f32[1,512,512]{2,1,0:T(8,128)S(1)}, bf16[256,512]{1,0:T(8,128)(2,1)S(1)}, bf16[256,512]{1,0:T(8,128)(2,1)S(1)}, f32[8,128]{1,0:T(8,128)}) custom-call(s32[6]{0:T(128)S(1)} %stack.27.where_ref, bf16[3,512,128]{2,1,0:T(8,128)(2,1)} %refs_0_.3, ...), custom_call_target="tpu_custom_call" | custom-call | flops 1000000 | bytes 300000 | tf_op jit(solution)/shard_map/self_backward_rest/pallas_call | solution.py:146
  88.1 1.6 %collective-permute-start.27 = (bf16[2,128,512]{2,1,0:T(8,128)(2,1)S(1)}, bf16[2,128,512]{2,1,0:T(8,128)(2,1)S(1)}, u32[]{:S(2)}, u32[]{:S(2)}) collective-permute-start(bf16[2,128,512]{2,1,0:T(8,128)(2,1)S(1)} %get-tuple-element.297), channel_id=1, source_target_pairs={{0,8},{4,12},{8,0},{12,4},{16,24},{20,28},{24,16},{28,20},{1,9},{5... | collective-permute-start | bytes 786440 | tf_op jit(solution)/shard_map/ppermute | solution.py:851
  89.7 1.4 collective-permute-start.28
  92.4 1.2 collective-permute-start.30
  93.6 2.6 %collective-permute-start.31 = (bf16[2,128,512]{2,1,0:T(8,128)(2,1)S(1)}, bf16[2,128,512]{2,1,0:T(8,128)(2,1)S(1)}, u32[]{:S(2)}, u32[]{:S(2)}) collective-permute-start(bf16[2,128,512]{2,1,0:T(8,128)(2,1)S(1)} %get-tuple-element.306.refs_4_), channel_id=1, source_target_pairs={{0,16},{4,20},{8,24},{12,28},{16,0},{20,4},{24,8},{28,12},{1,17},{... | collective-permute-start | bytes 786440 | tf_op jit(solution)/shard_map/ppermute | solution.py:851
  96.2 1.5 %input_backward.1 = (bf16[1024,512]{1,0:T(8,128)(2,1)S(1)}, bf16[16,512]{1,0:T(8,128)(2,1)S(1)}, bf16[16,512]{1,0:T(8,128)(2,1)S(1)}, f32[8,128]{1,0:T(8,128)}) custom-call(s32[6]{0:T(128)S(1)} %stack.27.where_ref, bf16[512,512]{1,0:T(8,128)(2,1)S(1)} %get-tuple-element.182.refs_0_, bf16[256,512]{1,0:T(8,128)(2,1)S(1)} %get-tuple-element.273.refs_1_, ...), custom_call_target="tpu_custom_call" | custom-call | flops 1000000 | bytes 300000 | tf_op jit(solution)/shard_map/input_backward/pallas_call | solution.py:146
  100.1 5.4 %collective-permute-done.31.refs_5_ = bf16[2,128,512]{2,1,0:T(8,128)(2,1)S(1)} collective-permute-done((bf16[2,128,512]{2,1,0:T(8,128)(2,1)S(1)}, bf16[2,128,512]{2,1,0:T(8,128)(2,1)S(1)}, u32[]{:S(2)}, u32[]{:S(2)}) %collective-permute-start.31) | collective-permute-done | bytes 262176 | tf_op jit(solution)/shard_map/ppermute | solution.py:851
  106.2 1.4 collective-permute-start.32
  107.5 2.0 %collective-permute-start.33 = (bf16[1,128,512]{2,1,0:T(8,128)(2,1)S(1)}, bf16[1,128,512]{2,1,0:T(8,128)(2,1)S(1)}, u32[]{:S(2)}, u32[]{:S(2)}) collective-permute-start(bf16[1,128,512]{2,1,0:T(8,128)(2,1)S(1)} %get-tuple-element.310), channel_id=1, source_target_pairs={{0,8},{4,12},{8,0},{12,4},{16,24},{20,28},{24,16},{28,20},{1,9},{5... | collective-permute-start | bytes 393224 | tf_op jit(solution)/shard_map/ppermute | solution.py:851
  109.6 1.3 collective-permute-start.35
  110.9 8.3 %collective-permute-done.33.refs_1_ = bf16[1,128,512]{2,1,0:T(8,128)(2,1)S(1)} collective-permute-done((bf16[1,128,512]{2,1,0:T(8,128)(2,1)S(1)}, bf16[1,128,512]{2,1,0:T(8,128)(2,1)S(1)}, u32[]{:S(2)}, u32[]{:S(2)}) %collective-permute-start.33) | collective-permute-done | bytes 131104 | tf_op jit(solution)/shard_map/ppermute | solution.py:851
  119.8 1.4 collective-permute-start.36
  121.2 2.5 %collective-permute-start.37 = (bf16[1,128,512]{2,1,0:T(8,128)(2,1)S(1)}, bf16[1,128,512]{2,1,0:T(8,128)(2,1)S(1)}, u32[]{:S(2)}, u32[]{:S(2)}) collective-permute-start(bf16[1,128,512]{2,1,0:T(8,128)(2,1)S(1)} %get-tuple-element.316.refs_2_), channel_id=1, source_target_pairs={{0,8},{4,12},{8,0},{12,4},{16,24},{20,28},{24,16},{28,20},{1,9},{5... | collective-permute-start | bytes 393224 | tf_op jit(solution)/shard_map/ppermute | solution.py:851
  123.7 3.6 %collective-permute-done.37.refs_3_ = bf16[1,128,512]{2,1,0:T(8,128)(2,1)S(1)} collective-permute-done((bf16[1,128,512]{2,1,0:T(8,128)(2,1)S(1)}, bf16[1,128,512]{2,1,0:T(8,128)(2,1)S(1)}, u32[]{:S(2)}, u32[]{:S(2)}) %collective-permute-start.37) | collective-permute-done | bytes 131104 | tf_op jit(solution)/shard_map/ppermute | solution.py:851
  127.9 1.6 %collective-permute-start.40 = (bf16[1,256,512]{2,1,0:T(8,128)(2,1)S(1)}, bf16[1,256,512]{2,1,0:T(8,128)(2,1)S(1)}, u32[]{:S(2)}, u32[]{:S(2)}) collective-permute-start(bf16[1,256,512]{2,1,0:T(8,128)(2,1)S(1)} %get-tuple-element.321.refs_0_), channel_id=1, source_target_pairs={{0,4},{4,0},{8,12},{12,8},{16,20},{20,16},{24,28},{28,24},{1,5},{5... | collective-permute-start | bytes 786440 | tf_op jit(solution)/shard_map/ppermute | solution.py:851
  130.0 1.4 collective-permute-start.38
  131.4 1.3 collective-permute-start.39
  132.6 4.6 %collective-permute-done.40.refs_1_ = bf16[1,256,512]{2,1,0:T(8,128)(2,1)S(1)} collective-permute-done((bf16[1,256,512]{2,1,0:T(8,128)(2,1)S(1)}, bf16[1,256,512]{2,1,0:T(8,128)(2,1)S(1)}, u32[]{:S(2)}, u32[]{:S(2)}) %collective-permute-start.40) | collective-permute-done | bytes 262176 | tf_op jit(solution)/shard_map/ppermute | solution.py:851
  137.2 1.6 %cross_grads.1 = (f32[512,128]{1,0:T(8,128)}, f32[2,512,128]{2,1,0:T(8,128)}, f32[128,512]{1,0:T(8,128)}, f32[8,128]{1,0:T(8,128)}) custom-call(s32[6]{0:T(128)S(1)} %stack.27.where_ref, bf16[1,256,512]{2,1,0:T(8,128)(2,1)S(1)} %get-tuple-element.321.refs_0_, bf16[1,256,512]{2,1,0:T(8,128)(2,1)S(1)} %collective-permute-done.40.refs_1_, ...), custom_call_target="tpu_custom_call" | custom-call | flops 1000000 | bytes 300000 | tf_op jit(solution)/shard_map/cross_grads/pallas_call | solution.py:146
  139.5 1.6 %collective-permute-start.43 = (bf16[1,272,512]{2,1,0:T(8,128)(2,1)S(1)}, bf16[1,272,512]{2,1,0:T(8,128)(2,1)S(1)}, u32[]{:S(2)}, u32[]{:S(2)}) collective-permute-start(bf16[1,272,512]{2,1,0:T(8,128)(2,1)S(1)} %get-tuple-element.333.refs_0_), channel_id=1, source_target_pairs={{0,4},{4,0},{8,12},{12,8},{16,20},{20,16},{24,28},{28,24},{1,5},{5... | collective-permute-start | bytes 835592 | tf_op jit(solution)/shard_map/ppermute | solution.py:851
  141.1 2.1 %collective-permute-start.41 = (bf16[1,128,512]{2,1,0:T(8,128)(2,1)S(1)}, bf16[1,128,512]{2,1,0:T(8,128)(2,1)S(1)}, u32[]{:S(2)}, u32[]{:S(2)}) collective-permute-start(bf16[1,128,512]{2,1,0:T(8,128)(2,1)S(1)} %get-tuple-element.328), channel_id=1, source_target_pairs={{0,16},{4,20},{8,24},{12,28},{16,0},{20,4},{24,8},{28,12},{1,17},{... | collective-permute-start | bytes 393224 | tf_op jit(solution)/shard_map/ppermute | solution.py:851
  143.2 2.3 %place_rows.1 = (bf16[2,512,512]{2,1,0:T(8,128)(2,1)}, f32[2,512,512]{2,1,0:T(8,128)}, f32[8,128]{1,0:T(8,128)}) custom-call(s32[6]{0:T(128)S(1)} %stack.27.where_ref, bf16[1024,512]{1,0:T(8,128)(2,1)S(1)} %get-tuple-element.309.refs_0_, bf16[1024,512]{1,0:T(8,128)(2,1)S(1)} %collective-permute-done.32.refs_1_, f32[8,128]{1,0:T(8,128)} %get-tuple-element.324.refs_2_), custom_call_target="tpu_custom_call" | custom-call | flops 1000000 | bytes 300000 | tf_op jit(solution)/shard_map/place_rows/pallas_call | solution.py:146
  145.5 1.6 %collective-permute-done.42.refs_1_ = bf16[2,256,512]{2,1,0:T(8,128)(2,1)S(1)} collective-permute-done((bf16[2,256,512]{2,1,0:T(8,128)(2,1)S(1)}, bf16[2,256,512]{2,1,0:T(8,128)(2,1)S(1)}, u32[]{:S(2)}, u32[]{:S(2)}) %collective-permute-start.42) | collective-permute-done | bytes 524320 | tf_op jit(solution)/shard_map/ppermute | solution.py:851
  147.0 2.2 %ffn_grads.1 = (f32[512,512]{1,0:T(8,128)}, f32[512,512]{1,0:T(8,128)}, f32[8,128]{1,0:T(8,128)}) custom-call(s32[6]{0:T(128)S(1)} %stack.27.where_ref, bf16[2,256,512]{2,1,0:T(8,128)(2,1)S(1)} %get-tuple-element.329.refs_0_, bf16[2,256,512]{2,1,0:T(8,128)(2,1)S(1)} %collective-permute-done.42.refs_1_, f32[8,128]{1,0:T(8,128)} %get-tuple-element.330.refs_2_), custom_call_target="tpu_custom_call" | custom-call | flops 1000000 | bytes 300000 | tf_op jit(solution)/shard_map/ffn_grads/pallas_call | solution.py:146
  149.3 1.4 memory_end.1
  150.7 1.8 %self_grads.1 = (f32[3,512,128]{2,1,0:T(8,128)}, f32[128,512]{1,0:T(8,128)}, f32[3,512]{1,0:T(4,128)}, f32[3,512]{1,0:T(4,128)}, f32[3,512]{1,0:T(4,128)}, /*ind...) custom-call(s32[6]{0:T(128)S(1)} %stack.27.where_ref, ...), custom_call_target="tpu_custom_call" | custom-call | flops 1000000 | bytes 300000 | tf_op jit(solution)/shard_map/self_grads/pallas_call | solution.py:146
  (82 shorter events, 22.8 us)
Async XLA Ops:
  0.6 20.8 %collective-permute-start = (bf16[3,512,128]{2,1,0:T(8,128)(2,1)}, bf16[3,512,128]{2,1,0:T(8,128)(2,1)S(1)}, u32[]{:S(2)}, u32[]{:S(2)}) collective-permute-start(bf16[3,512,128]{2,1,0:T(8,128)(2,1)} %refs_0_.3), channel_id=1, source_target_pairs={{0,2},{1,3},{2,0},{3,1},{4,6},{5,7},{6,4},{7,5},{8,10},{9,11},{10,... | collective-permute-start | bytes 1179656 | tf_op jit(solution)/shard_map/ppermute | solution.py:845
  3.8 12.1 %copy-start.1 = (bf16[512]{0:T(512)(128)(2,1)S(1)}, bf16[512]{0:T(512)(128)(2,1)}, u32[]{:S(2)}) copy-start(bf16[512]{0:T(512)(128)(2,1)} %param.36) | copy-start | bytes 3076
  3.8 12.1 %copy-start.2 = (bf16[2,128]{1,0:T(2,128)(2,1)S(1)}, bf16[2,128]{1,0:T(2,128)(2,1)}, u32[]{:S(2)}) copy-start(bf16[2,128]{1,0:T(2,128)(2,1)} %param.33) | copy-start | bytes 1540
  3.8 12.1 %copy-start.3 = (bf16[2,128]{1,0:T(2,128)(2,1)S(1)}, bf16[2,128]{1,0:T(2,128)(2,1)}, u32[]{:S(2)}) copy-start(bf16[2,128]{1,0:T(2,128)(2,1)} %param.29) | copy-start | bytes 1540
  8.0 13.4 %collective-permute-start.5 = (bf16[1024,128]{1,0:T(8,128)(2,1)S(1)}, bf16[1024,128]{1,0:T(8,128)(2,1)S(1)}, u32[]{:S(2)}, u32[]{:S(2)}) collective-permute-start(bf16[1024,128]{1,0:T(8,128)(2,1)S(1)} %get-tuple-element.198), channel_id=1, source_target_pairs={{0,2},{1,3},{2,0},{3,1},{4,6},{5,7},{6,4},{7,5},{8,10},{9,11},{10,... | collective-permute-start | bytes 786440 | tf_op jit(solution)/shard_map/ppermute | solution.py:845
  8.1 21.0 %all-to-all-start = ((bf16[8,64,512]{2,1,0:T(8,128)(2,1)}), bf16[8,64,512]{2,1,0:T(8,128)(2,1)S(1)}, u32[]{:S(2)}, u32[]{:S(2)}) async-start(bf16[8,64,512]{2,1,0:T(8,128)(2,1)} %get-tuple-element.191), calls=%async_computation | async-start | bytes 1048576 | tf_op jit(solution)/shard_map/all_to_all | solution.py:901
  14.4 7.1 %collective-permute-start.2 = (bf16[128,512]{1,0:T(8,128)(2,1)}, bf16[128,512]{1,0:T(8,128)(2,1)S(1)}, u32[]{:S(2)}, u32[]{:S(2)}) collective-permute-start(bf16[128,512]{1,0:T(8,128)(2,1)} %refs_12_.3), channel_id=1, source_target_pairs={{0,2},{1,3},{2,0},{3,1},{4,6},{5,7},{6,4},{7,5},{8,10},{9,11},{10,... | collective-permute-start | bytes 393224 | tf_op jit(solution)/shard_map/ppermute | solution.py:845
  15.9 5.6 %collective-permute-start.1 = (bf16[8,128]{1,0:T(8,128)(2,1)S(1)}, bf16[8,128]{1,0:T(8,128)(2,1)S(1)}, u32[]{:S(2)}, u32[]{:S(2)}) collective-permute-start(bf16[8,128]{1,0:T(8,128)(2,1)S(1)} %pad_maximum_fusion.refs_4_.refs_2_.refs_8_), channel_id=1, source_target_pairs={{0,2},{1,3},{2,0},{3,1},{4,6},{5,7},{6,4},{7,5},{8,10},{9,11},{10,... | collective-permute-start | bytes 6152 | tf_op jit(solution)/shard_map/ppermute | solution.py:845
  21.5 25.0 %collective-permute-start.9 = (bf16[2,512,512]{2,1,0:T(8,128)(2,1)}, bf16[2,512,512]{2,1,0:T(8,128)(2,1)}, u32[]{:S(2)}, u32[]{:S(2)}) collective-permute-start(bf16[2,512,512]{2,1,0:T(8,128)(2,1)} %copy-done), channel_id=1, source_target_pairs={{0,2},{1,3},{2,0},{3,1},{4,6},{5,7},{6,4},{7,5},{8,10},{9,11},{10,... | collective-permute-start | bytes 3145736 | tf_op jit(solution)/shard_map/ppermute | solution.py:845
  27.0 4.0 %collective-permute-start.3 = (bf16[256,512]{1,0:T(8,128)(2,1)}, bf16[256,512]{1,0:T(8,128)(2,1)}, u32[]{:S(2)}, u32[]{:S(2)}) collective-permute-start(bf16[256,512]{1,0:T(8,128)(2,1)} %get-tuple-element.189.refs_1_), channel_id=1, source_target_pairs={{0,1},{1,0},{2,3},{3,2},{4,5},{5,4},{6,7},{7,6},{8,9},{9,8},{10,11... | collective-permute-start | bytes 786440 | tf_op jit(solution)/shard_map/ppermute | solution.py:848
  27.1 3.9 %collective-permute-start.4 = (bf16[256,512]{1,0:T(8,128)(2,1)}, bf16[256,512]{1,0:T(8,128)(2,1)}, u32[]{:S(2)}, u32[]{:S(2)}) collective-permute-start(bf16[256,512]{1,0:T(8,128)(2,1)} %get-tuple-element.190.refs_2_), channel_id=1, source_target_pairs={{0,1},{1,0},{2,3},{3,2},{4,5},{5,4},{6,7},{7,6},{8,9},{9,8},{10,11... | collective-permute-start | bytes 786440 | tf_op jit(solution)/shard_map/ppermute | solution.py:848
  27.6 8.3 %collective-permute-start.6 = (bf16[1024,128]{1,0:T(8,128)(2,1)S(1)}, bf16[1024,128]{1,0:T(8,128)(2,1)S(1)}, u32[]{:S(2)}, u32[]{:S(2)}) collective-permute-start(bf16[1024,128]{1,0:T(8,128)(2,1)S(1)} %collective-permute-done.5.refs_0_), channel_id=1, source_target_pairs={{0,4},{4,0},{8,12},{12,8},{16,20},{20,16},{24,28},{28,24},{1,5},{5... | collective-permute-start | bytes 786440 | tf_op jit(solution)/shard_map/ppermute | solution.py:851
  40.2 1.6 %collective-permute-start.7 = (bf16[256,512]{1,0:T(8,128)(2,1)S(1)}, bf16[256,512]{1,0:T(8,128)(2,1)S(1)}, u32[]{:S(2)}, u32[]{:S(2)}) collective-permute-start(bf16[256,512]{1,0:T(8,128)(2,1)S(1)} %get-tuple-element.206.refs_1_), channel_id=1, source_target_pairs={{0,1},{1,0},{2,3},{3,2},{4,5},{5,4},{6,7},{7,6},{8,9},{9,8},{10,11... | collective-permute-start | bytes 786440 | tf_op jit(solution)/shard_map/ppermute | solution.py:848
  40.3 1.9 %collective-permute-start.8 = (bf16[256,512]{1,0:T(8,128)(2,1)S(1)}, bf16[256,512]{1,0:T(8,128)(2,1)S(1)}, u32[]{:S(2)}, u32[]{:S(2)}) collective-permute-start(bf16[256,512]{1,0:T(8,128)(2,1)S(1)} %get-tuple-element.207.refs_2_), channel_id=1, source_target_pairs={{0,1},{1,0},{2,3},{3,2},{4,5},{5,4},{6,7},{7,6},{8,9},{9,8},{10,11... | collective-permute-start | bytes 786440 | tf_op jit(solution)/shard_map/ppermute | solution.py:848
  50.1 4.9 %collective-permute-start.10 = (bf16[256,512]{1,0:T(8,128)(2,1)S(1)}, bf16[256,512]{1,0:T(8,128)(2,1)S(1)}, u32[]{:S(2)}, u32[]{:S(2)}) collective-permute-start(bf16[256,512]{1,0:T(8,128)(2,1)S(1)} %get-tuple-element.218.refs_1_), channel_id=1, source_target_pairs={{0,1},{1,0},{2,3},{3,2},{4,5},{5,4},{6,7},{7,6},{8,9},{9,8},{10,11... | collective-permute-start | bytes 786440 | tf_op jit(solution)/shard_map/ppermute | solution.py:848
  52.1 14.3 %collective-permute-start.14 = (bf16[1,512,512]{2,1,0:T(8,128)(2,1)S(1)}, bf16[1,512,512]{2,1,0:T(8,128)(2,1)S(1)}, u32[]{:S(2)}, u32[]{:S(2)}) collective-permute-start(bf16[1,512,512]{2,1,0:T(8,128)(2,1)S(1)} %get-tuple-element.239), channel_id=1, source_target_pairs={{0,2},{1,3},{2,0},{3,1},{4,6},{5,7},{6,4},{7,5},{8,10},{9,11},{10,... | collective-permute-start | bytes 1572872 | tf_op jit(solution)/shard_map/ppermute | solution.py:845
  53.3 2.2 %collective-permute-start.11 = (bf16[256,512]{1,0:T(8,128)(2,1)S(1)}, bf16[256,512]{1,0:T(8,128)(2,1)S(1)}, u32[]{:S(2)}, u32[]{:S(2)}) collective-permute-start(bf16[256,512]{1,0:T(8,128)(2,1)S(1)} %get-tuple-element.219.refs_2_), channel_id=1, source_target_pairs={{0,1},{1,0},{2,3},{3,2},{4,5},{5,4},{6,7},{7,6},{8,9},{9,8},{10,11... | collective-permute-start | bytes 786440 | tf_op jit(solution)/shard_map/ppermute | solution.py:848
  53.5 14.1 %collective-permute-start.15 = (bf16[2,256,512]{2,1,0:T(8,128)(2,1)S(1)}, bf16[2,256,512]{2,1,0:T(8,128)(2,1)S(1)}, u32[]{:S(2)}, u32[]{:S(2)}) collective-permute-start(bf16[2,256,512]{2,1,0:T(8,128)(2,1)S(1)} %get-tuple-element.241), channel_id=1, source_target_pairs={{0,4},{4,0},{8,12},{12,8},{16,20},{20,16},{24,28},{28,24},{1,5},{5... | collective-permute-start | bytes 1572872 | tf_op jit(solution)/shard_map/ppermute | solution.py:851
  55.0 7.2 %collective-permute-start.16 = (bf16[256,512]{1,0:T(8,128)(2,1)S(1)}, bf16[256,512]{1,0:T(8,128)(2,1)S(1)}, u32[]{:S(2)}, u32[]{:S(2)}) collective-permute-start(bf16[256,512]{1,0:T(8,128)(2,1)S(1)} %get-tuple-element.251.refs_14_), channel_id=1, source_target_pairs={{0,1},{1,0},{2,3},{3,2},{4,5},{5,4},{6,7},{7,6},{8,9},{9,8},{10,11... | collective-permute-start | bytes 786440 | tf_op jit(solution)/shard_map/ppermute | solution.py:848
  55.0 7.6 %collective-permute-start.17 = (bf16[256,512]{1,0:T(8,128)(2,1)S(1)}, bf16[256,512]{1,0:T(8,128)(2,1)S(1)}, u32[]{:S(2)}, u32[]{:S(2)}) collective-permute-start(bf16[256,512]{1,0:T(8,128)(2,1)S(1)} %get-tuple-element.252.refs_15_), channel_id=1, source_target_pairs={{0,1},{1,0},{2,3},{3,2},{4,5},{5,4},{6,7},{7,6},{8,9},{9,8},{10,11... | collective-permute-start | bytes 786440 | tf_op jit(solution)/shard_map/ppermute | solution.py:848
  62.0 7.9 %collective-permute-start.12 = (bf16[256,512]{1,0:T(8,128)(2,1)S(1)}, bf16[256,512]{1,0:T(8,128)(2,1)S(1)}, u32[]{:S(2)}, u32[]{:S(2)}) collective-permute-start(bf16[256,512]{1,0:T(8,128)(2,1)S(1)} %get-tuple-element.230.refs_1_), channel_id=1, source_target_pairs={{0,1},{1,0},{2,3},{3,2},{4,5},{5,4},{6,7},{7,6},{8,9},{9,8},{10,11... | collective-permute-start | bytes 786440 | tf_op jit(solution)/shard_map/ppermute | solution.py:848
  62.2 8.8 %collective-permute-start.13 = (bf16[256,512]{1,0:T(8,128)(2,1)S(1)}, bf16[256,512]{1,0:T(8,128)(2,1)S(1)}, u32[]{:S(2)}, u32[]{:S(2)}) collective-permute-start(bf16[256,512]{1,0:T(8,128)(2,1)S(1)} %get-tuple-element.231.refs_2_), channel_id=1, source_target_pairs={{0,1},{1,0},{2,3},{3,2},{4,5},{5,4},{6,7},{7,6},{8,9},{9,8},{10,11... | collective-permute-start | bytes 786440 | tf_op jit(solution)/shard_map/ppermute | solution.py:848
  65.7 10.8 %collective-permute-start.20 = (bf16[256,512]{1,0:T(8,128)(2,1)S(1)}, bf16[256,512]{1,0:T(8,128)(2,1)S(1)}, u32[]{:S(2)}, u32[]{:S(2)}) collective-permute-start(bf16[256,512]{1,0:T(8,128)(2,1)S(1)} %get-tuple-element.269.refs_4_), channel_id=1, source_target_pairs={{0,1},{1,0},{2,3},{3,2},{4,5},{5,4},{6,7},{7,6},{8,9},{9,8},{10,11... | collective-permute-start | bytes 786440 | tf_op jit(solution)/shard_map/ppermute | solution.py:848
  66.4 10.2 %collective-permute-start.21 = (bf16[256,512]{1,0:T(8,128)(2,1)S(1)}, bf16[256,512]{1,0:T(8,128)(2,1)S(1)}, u32[]{:S(2)}, u32[]{:S(2)}) collective-permute-start(bf16[256,512]{1,0:T(8,128)(2,1)S(1)} %get-tuple-element.270.refs_5_), channel_id=1, source_target_pairs={{0,1},{1,0},{2,3},{3,2},{4,5},{5,4},{6,7},{7,6},{8,9},{9,8},{10,11... | collective-permute-start | bytes 786440 | tf_op jit(solution)/shard_map/ppermute | solution.py:848
  68.3 9.3 %collective-permute-start.18 = (bf16[1,256,512]{2,1,0:T(8,128)(2,1)S(1)}, bf16[1,256,512]{2,1,0:T(8,128)(2,1)S(1)}, u32[]{:S(2)}, u32[]{:S(2)}) collective-permute-start(bf16[1,256,512]{2,1,0:T(8,128)(2,1)S(1)} %get-tuple-element.267), channel_id=1, source_target_pairs={{0,4},{4,0},{8,12},{12,8},{16,20},{20,16},{24,28},{28,24},{1,5},{5... | collective-permute-start | bytes 786440 | tf_op jit(solution)/shard_map/ppermute | solution.py:851
  69.9 7.7 %collective-permute-start.19 = (bf16[1,256,512]{2,1,0:T(8,128)(2,1)S(1)}, bf16[1,256,512]{2,1,0:T(8,128)(2,1)S(1)}, u32[]{:S(2)}, u32[]{:S(2)}) collective-permute-start(bf16[1,256,512]{2,1,0:T(8,128)(2,1)S(1)} %get-tuple-element.268), channel_id=1, source_target_pairs={{0,2},{1,3},{2,0},{3,1},{4,6},{5,7},{6,4},{7,5},{8,10},{9,11},{10,... | collective-permute-start | bytes 786440 | tf_op jit(solution)/shard_map/ppermute | solution.py:845
  70.9 16.4 %collective-permute-start.26 = (bf16[2,256,512]{2,1,0:T(8,128)(2,1)S(1)}, bf16[2,256,512]{2,1,0:T(8,128)(2,1)S(1)}, u32[]{:S(2)}, u32[]{:S(2)}) collective-permute-start(bf16[2,256,512]{2,1,0:T(8,128)(2,1)S(1)} %get-tuple-element.289), channel_id=1, source_target_pairs={{0,4},{4,0},{8,12},{12,8},{16,20},{20,16},{24,28},{28,24},{1,5},{5... | collective-permute-start | bytes 1572872 | tf_op jit(solution)/shard_map/ppermute | solution.py:851
  78.4 9.1 %collective-permute-start.25 = (bf16[2,192,512]{2,1,0:T(8,128)(2,1)S(1)}, bf16[2,192,512]{2,1,0:T(8,128)(2,1)S(1)}, u32[]{:S(2)}, u32[]{:S(2)}) collective-permute-start(bf16[2,192,512]{2,1,0:T(8,128)(2,1)S(1)} %get-tuple-element.287), channel_id=1, source_target_pairs={{0,8},{4,12},{8,0},{12,4},{16,24},{20,28},{24,16},{28,20},{1,9},{5... | collective-permute-start | bytes 1179656 | tf_op jit(solution)/shard_map/ppermute | solution.py:851
  80.0 11.7 %collective-permute-start.24 = (bf16[1,512,512]{2,1,0:T(8,128)(2,1)S(1)}, bf16[1,512,512]{2,1,0:T(8,128)(2,1)S(1)}, u32[]{:S(2)}, u32[]{:S(2)}) collective-permute-start(bf16[1,512,512]{2,1,0:T(8,128)(2,1)S(1)} %get-tuple-element.285), channel_id=1, source_target_pairs={{0,2},{1,3},{2,0},{3,1},{4,6},{5,7},{6,4},{7,5},{8,10},{9,11},{10,... | collective-permute-start | bytes 1572872 | tf_op jit(solution)/shard_map/ppermute | solution.py:845
  85.8 7.8 %collective-permute-start.22 = (bf16[256,512]{1,0:T(8,128)(2,1)S(1)}, bf16[256,512]{1,0:T(8,128)(2,1)S(1)}, u32[]{:S(2)}, u32[]{:S(2)}) collective-permute-start(bf16[256,512]{1,0:T(8,128)(2,1)S(1)} %get-tuple-element.273.refs_1_), channel_id=1, source_target_pairs={{0,1},{1,0},{2,3},{3,2},{4,5},{5,4},{6,7},{7,6},{8,9},{9,8},{10,11... | collective-permute-start | bytes 786440 | tf_op jit(solution)/shard_map/ppermute | solution.py:848
  85.9 10.3 %collective-permute-start.23 = (bf16[256,512]{1,0:T(8,128)(2,1)S(1)}, bf16[256,512]{1,0:T(8,128)(2,1)S(1)}, u32[]{:S(2)}, u32[]{:S(2)}) collective-permute-start(bf16[256,512]{1,0:T(8,128)(2,1)S(1)} %get-tuple-element.274.refs_2_), channel_id=1, source_target_pairs={{0,1},{1,0},{2,3},{3,2},{4,5},{5,4},{6,7},{7,6},{8,9},{9,8},{10,11... | collective-permute-start | bytes 786440 | tf_op jit(solution)/shard_map/ppermute | solution.py:848
  88.1 9.6 %collective-permute-start.27 = (bf16[2,128,512]{2,1,0:T(8,128)(2,1)S(1)}, bf16[2,128,512]{2,1,0:T(8,128)(2,1)S(1)}, u32[]{:S(2)}, u32[]{:S(2)}) collective-permute-start(bf16[2,128,512]{2,1,0:T(8,128)(2,1)S(1)} %get-tuple-element.297), channel_id=1, source_target_pairs={{0,8},{4,12},{8,0},{12,4},{16,24},{20,28},{24,16},{28,20},{1,9},{5... | collective-permute-start | bytes 786440 | tf_op jit(solution)/shard_map/ppermute | solution.py:851
  89.7 8.0 %collective-permute-start.28 = (bf16[1,128,512]{2,1,0:T(8,128)(2,1)S(1)}, bf16[1,128,512]{2,1,0:T(8,128)(2,1)S(1)}, u32[]{:S(2)}, u32[]{:S(2)}) collective-permute-start(bf16[1,128,512]{2,1,0:T(8,128)(2,1)S(1)} %get-tuple-element.300), channel_id=1, source_target_pairs={{0,4},{4,0},{8,12},{12,8},{16,20},{20,16},{24,28},{28,24},{1,5},{5... | collective-permute-start | bytes 393224 | tf_op jit(solution)/shard_map/ppermute | solution.py:851
  92.4 7.7 %collective-permute-start.30 = (bf16[1,256,512]{2,1,0:T(8,128)(2,1)S(1)}, bf16[1,256,512]{2,1,0:T(8,128)(2,1)S(1)}, u32[]{:S(2)}, u32[]{:S(2)}) collective-permute-start(bf16[1,256,512]{2,1,0:T(8,128)(2,1)S(1)} %get-tuple-element.305), channel_id=1, source_target_pairs={{0,4},{4,0},{8,12},{12,8},{16,20},{20,16},{24,28},{28,24},{1,5},{5... | collective-permute-start | bytes 786440 | tf_op jit(solution)/shard_map/ppermute | solution.py:851
  93.6 11.9 %collective-permute-start.31 = (bf16[2,128,512]{2,1,0:T(8,128)(2,1)S(1)}, bf16[2,128,512]{2,1,0:T(8,128)(2,1)S(1)}, u32[]{:S(2)}, u32[]{:S(2)}) collective-permute-start(bf16[2,128,512]{2,1,0:T(8,128)(2,1)S(1)} %get-tuple-element.306.refs_4_), channel_id=1, source_target_pairs={{0,16},{4,20},{8,24},{12,28},{16,0},{20,4},{24,8},{28,12},{1,17},{... | collective-permute-start | bytes 786440 | tf_op jit(solution)/shard_map/ppermute | solution.py:851
  98.4 7.1 %collective-permute-start.29 = (bf16[1,144,512]{2,1,0:T(8,128)(2,1)S(1)}, bf16[1,144,512]{2,1,0:T(8,128)(2,1)S(1)}, u32[]{:S(2)}, u32[]{:S(2)}) collective-permute-start(bf16[1,144,512]{2,1,0:T(8,128)(2,1)S(1)} %get-tuple-element.303), channel_id=1, source_target_pairs={{0,2},{1,3},{2,0},{3,1},{4,6},{5,7},{6,4},{7,5},{8,10},{9,11},{10,... | collective-permute-start | bytes 442376 | tf_op jit(solution)/shard_map/ppermute | solution.py:845
  106.2 37.0 %collective-permute-start.32 = (bf16[1024,512]{1,0:T(8,128)(2,1)S(1)}, bf16[1024,512]{1,0:T(8,128)(2,1)S(1)}, u32[]{:S(2)}, u32[]{:S(2)}) collective-permute-start(bf16[1024,512]{1,0:T(8,128)(2,1)S(1)} %get-tuple-element.309.refs_0_), channel_id=1, source_target_pairs={{0,2},{1,3},{2,0},{3,1},{4,6},{5,7},{6,4},{7,5},{8,10},{9,11},{10,... | collective-permute-start | bytes 3145736 | tf_op jit(solution)/shard_map/ppermute | solution.py:845
  107.5 11.6 %collective-permute-start.34 = (bf16[2,128,512]{2,1,0:T(8,128)(2,1)S(1)}, bf16[2,128,512]{2,1,0:T(8,128)(2,1)S(1)}, u32[]{:S(2)}, u32[]{:S(2)}) collective-permute-start(bf16[2,128,512]{2,1,0:T(8,128)(2,1)S(1)} %get-tuple-element.312.refs_4_), channel_id=1, source_target_pairs={{0,8},{4,12},{8,0},{12,4},{16,24},{20,28},{24,16},{28,20},{1,9},{5... | collective-permute-start | bytes 786440 | tf_op jit(solution)/shard_map/ppermute | solution.py:851
  107.5 11.6 %collective-permute-start.33 = (bf16[1,128,512]{2,1,0:T(8,128)(2,1)S(1)}, bf16[1,128,512]{2,1,0:T(8,128)(2,1)S(1)}, u32[]{:S(2)}, u32[]{:S(2)}) collective-permute-start(bf16[1,128,512]{2,1,0:T(8,128)(2,1)S(1)} %get-tuple-element.310), channel_id=1, source_target_pairs={{0,8},{4,12},{8,0},{12,4},{16,24},{20,28},{24,16},{28,20},{1,9},{5... | collective-permute-start | bytes 393224 | tf_op jit(solution)/shard_map/ppermute | solution.py:851
  109.6 9.6 %collective-permute-start.35 = (bf16[1,128,512]{2,1,0:T(8,128)(2,1)S(1)}, bf16[1,128,512]{2,1,0:T(8,128)(2,1)S(1)}, u32[]{:S(2)}, u32[]{:S(2)}) collective-permute-start(bf16[1,128,512]{2,1,0:T(8,128)(2,1)S(1)} %get-tuple-element.313.refs_6_), channel_id=1, source_target_pairs={{0,16},{4,20},{8,24},{12,28},{16,0},{20,4},{24,8},{28,12},{1,17},{... | collective-permute-start | bytes 393224 | tf_op jit(solution)/shard_map/ppermute | solution.py:851
  119.8 7.5 %collective-permute-start.36 = (bf16[1,144,512]{2,1,0:T(8,128)(2,1)S(1)}, bf16[1,144,512]{2,1,0:T(8,128)(2,1)S(1)}, u32[]{:S(2)}, u32[]{:S(2)}) collective-permute-start(bf16[1,144,512]{2,1,0:T(8,128)(2,1)S(1)} %get-tuple-element.315.refs_0_), channel_id=1, source_target_pairs={{0,16},{4,20},{8,24},{12,28},{16,0},{20,4},{24,8},{28,12},{1,17},{... | collective-permute-start | bytes 442376 | tf_op jit(solution)/shard_map/ppermute | solution.py:851
  121.2 6.1 %collective-permute-start.37 = (bf16[1,128,512]{2,1,0:T(8,128)(2,1)S(1)}, bf16[1,128,512]{2,1,0:T(8,128)(2,1)S(1)}, u32[]{:S(2)}, u32[]{:S(2)}) collective-permute-start(bf16[1,128,512]{2,1,0:T(8,128)(2,1)S(1)} %get-tuple-element.316.refs_2_), channel_id=1, source_target_pairs={{0,8},{4,12},{8,0},{12,4},{16,24},{20,28},{24,16},{28,20},{1,9},{5... | collective-permute-start | bytes 393224 | tf_op jit(solution)/shard_map/ppermute | solution.py:851
  127.9 9.3 %collective-permute-start.40 = (bf16[1,256,512]{2,1,0:T(8,128)(2,1)S(1)}, bf16[1,256,512]{2,1,0:T(8,128)(2,1)S(1)}, u32[]{:S(2)}, u32[]{:S(2)}) collective-permute-start(bf16[1,256,512]{2,1,0:T(8,128)(2,1)S(1)} %get-tuple-element.321.refs_0_), channel_id=1, source_target_pairs={{0,4},{4,0},{8,12},{12,8},{16,20},{20,16},{24,28},{28,24},{1,5},{5... | collective-permute-start | bytes 786440 | tf_op jit(solution)/shard_map/ppermute | solution.py:851
  129.5 17.5 %collective-permute-start.42 = (bf16[2,256,512]{2,1,0:T(8,128)(2,1)S(1)}, bf16[2,256,512]{2,1,0:T(8,128)(2,1)S(1)}, u32[]{:S(2)}, u32[]{:S(2)}) collective-permute-start(bf16[2,256,512]{2,1,0:T(8,128)(2,1)S(1)} %get-tuple-element.329.refs_0_), channel_id=1, source_target_pairs={{0,4},{4,0},{8,12},{12,8},{16,20},{20,16},{24,28},{28,24},{1,5},{5... | collective-permute-start | bytes 1572872 | tf_op jit(solution)/shard_map/ppermute | solution.py:851
  130.0 8.9 %collective-permute-start.38 = (bf16[1,144,512]{2,1,0:T(8,128)(2,1)S(1)}, bf16[1,144,512]{2,1,0:T(8,128)(2,1)S(1)}, u32[]{:S(2)}, u32[]{:S(2)}) collective-permute-start(bf16[1,144,512]{2,1,0:T(8,128)(2,1)S(1)} %get-tuple-element.318.refs_0_), channel_id=1, source_target_pairs={{0,8},{4,12},{8,0},{12,4},{16,24},{20,28},{24,16},{28,20},{1,9},{5... | collective-permute-start | bytes 442376 | tf_op jit(solution)/shard_map/ppermute | solution.py:851
  131.4 7.5 %collective-permute-start.39 = (bf16[1,128,512]{2,1,0:T(8,128)(2,1)S(1)}, bf16[1,128,512]{2,1,0:T(8,128)(2,1)S(1)}, u32[]{:S(2)}, u32[]{:S(2)}) collective-permute-start(bf16[1,128,512]{2,1,0:T(8,128)(2,1)S(1)} %get-tuple-element.320), channel_id=1, source_target_pairs={{0,2},{1,3},{2,0},{3,1},{4,6},{5,7},{6,4},{7,5},{8,10},{9,11},{10,... | collective-permute-start | bytes 393224 | tf_op jit(solution)/shard_map/ppermute | solution.py:845
  139.5 11.2 %collective-permute-start.43 = (bf16[1,272,512]{2,1,0:T(8,128)(2,1)S(1)}, bf16[1,272,512]{2,1,0:T(8,128)(2,1)S(1)}, u32[]{:S(2)}, u32[]{:S(2)}) collective-permute-start(bf16[1,272,512]{2,1,0:T(8,128)(2,1)S(1)} %get-tuple-element.333.refs_0_), channel_id=1, source_target_pairs={{0,4},{4,0},{8,12},{12,8},{16,20},{20,16},{24,28},{28,24},{1,5},{5... | collective-permute-start | bytes 835592 | tf_op jit(solution)/shard_map/ppermute | solution.py:851
  141.1 8.2 %collective-permute-start.41 = (bf16[1,128,512]{2,1,0:T(8,128)(2,1)S(1)}, bf16[1,128,512]{2,1,0:T(8,128)(2,1)S(1)}, u32[]{:S(2)}, u32[]{:S(2)}) collective-permute-start(bf16[1,128,512]{2,1,0:T(8,128)(2,1)S(1)} %get-tuple-element.328), channel_id=1, source_target_pairs={{0,16},{4,20},{8,24},{12,28},{16,0},{20,4},{24,8},{28,12},{1,17},{... | collective-permute-start | bytes 393224 | tf_op jit(solution)/shard_map/ppermute | solution.py:851
  (1 other events, 1.0 us)

commit v3 on v2

--- a/solution.py
+++ b/solution.py
@@ -266,76 +266,92 @@
     return allowed
 
 
-def head_rows(value, j):
-    row = lax.broadcasted_iota(jnp.int32, value.shape, 0)
-    return jnp.where((row >= HDIM) == bool(j), value, jnp.zeros_like(value))
-
-
-def attend_forward(q, k, v, own, keys, heads, totals, banded):
+def both_heads(value):
+    return jnp.concatenate([head_lanes(value, 0), head_lanes(value, 1)], axis=0)
+
+
+def own_rows(value):
+    half = value.shape[1] // 2
+    row = lax.broadcasted_iota(jnp.int32, (value.shape[0], half), 0)
+    return jnp.where(row < HDIM, value[:, :half], value[:, half:])
+
+
+def pair_columns(at):
+    return slice(2 * at * BLOCK, 2 * (at + 1) * BLOCK)
+
+
+def attend_forward(q, k, v, own, keys, heads, totals, raised_all, shares, banded):
     seq, wide = q.shape
     columns = key_columns(keys)
+    blocks = row_blocks(seq)
     for pair in range(wide // LANES):
         lanes = slice(pair * LANES, (pair + 1) * LANES)
-        turned = [head_rows(v[:, lanes].T, j) for j in (0, 1)]
-        for block in row_blocks(seq):
+        for at, block in enumerate(blocks):
             span = span_of(block, k.shape[0], banded)
             allowed = allowed_of(own, columns, block, span, banded)
-            query, keyset = q[block, lanes] * 0.125, k[span, lanes]
-            mixed = None
+            allowed = jnp.concatenate([allowed, allowed], axis=1)
+            scores = dot_right(k[span, lanes], both_heads(q[block, lanes] * 0.125))
+            scores = jnp.where(allowed, scores, -1e30)
+            maxima = jnp.max(scores, axis=0, keepdims=True)
+            raised = jnp.exp(scores - maxima)
+            total = jnp.sum(raised, axis=0, keepdims=True)
+            raised_all[span, pair_columns(at)] = raised.astype(BF16)
+            shares[:, pair_columns(at)] = 1.0 / total
+            logs = maxima + jnp.log(total)
             for j in (0, 1):
-                scores = jnp.where(allowed, dot_right(keyset, head_lanes(query, j)), -1e30)
-                maxima = jnp.max(scores, axis=0, keepdims=True)
-                raised = jnp.exp(scores - maxima)
-                total = jnp.sum(raised, axis=0, keepdims=True)
-                chances = (raised * (1.0 / total)).astype(BF16)
-                term = dot(turned[j][:, span], chances)
-                mixed = term if mixed is None else mixed + term
-                totals[2 * pair + j : 2 * pair + j + 1, block] = maxima + jnp.log(total)
-            heads[block, lanes] = mixed.T.astype(BF16)
-
-
-def attend_backward(q, k, v, own, keys, totals, grad_heads, dq, dk, dv, sum_k, sum_v, banded):
+                totals[2 * pair + j : 2 * pair + j + 1, block] = logs[:, j * BLOCK : (j + 1) * BLOCK]
+        turned = v[:, lanes].T
+        if not banded:
+            mixed = dot(turned, raised_all[...]) * shares[...]
+        for at, block in enumerate(blocks):
+            if banded:
+                span = span_of(block, k.shape[0], banded)
+                part = dot(turned[:, span], raised_all[span, pair_columns(at)]) * shares[:, pair_columns(at)]
+            else:
+                part = mixed[:, pair_columns(at)]
+            heads[block, lanes] = own_rows(part).T.astype(BF16)
+
+
+def attend_backward(q, k, v, own, keys, totals, grad_heads, dq, dk, dv, work, banded):
     seq, wide = q.shape
     columns = key_columns(keys)
+    blocks = row_blocks(seq)
+    scores_all, query_all = work[:2]
     for pair in range(wide // LANES):
         lanes = slice(pair * LANES, (pair + 1) * LANES)
-        turned = [head_rows(k[:, lanes].T, j) for j in (0, 1)]
-        for at, block in enumerate(row_blocks(seq)):
+        for at, block in enumerate(blocks):
             span = span_of(block, k.shape[0], banded)
             allowed = allowed_of(own, columns, block, span, banded)
-            query, keyset, values = q[block, lanes] * 0.125, k[span, lanes], v[span, lanes]
-            grad = grad_heads[block, lanes]
-            grad_query = grad_key = grad_value = None
-            for j in (0, 1):
-                head = 2 * pair + j
-                part, own_grad = head_lanes(query, j), head_lanes(grad, j)
-                scores = jnp.where(allowed, dot_right(keyset, part), -1e30)
-                chances = jnp.exp(scores - totals[head : head + 1, block])
-                by_value = dot(chances.astype(BF16), own_grad)
-                weighted = chances * dot_right(values, own_grad)
-                mean = jnp.sum(weighted, axis=0, keepdims=True)
-                grad_scores = (weighted - chances * mean).astype(BF16)
-                by_query, by_key = dot(turned[j][:, span], grad_scores), dot(grad_scores, part)
-                if j == 0:
-                    grad_query, grad_key, grad_value = by_query, by_key, by_value
-                else:
-                    grad_query, grad_key, grad_value = grad_query + by_query, grad_key + by_key, grad_value + by_value
-            dq[block, lanes] = (grad_query.T * 0.125).astype(BF16)
+            allowed = jnp.concatenate([allowed, allowed], axis=1)
+            query, grad = both_heads(q[block, lanes] * 0.125), both_heads(grad_heads[block, lanes])
+            query_all[pair_columns(at), :] = query
+            logs = jnp.concatenate([totals[2 * pair + j : 2 * pair + j + 1, block] for j in (0, 1)], axis=1)
+            scores = jnp.where(allowed, dot_right(k[span, lanes], query), -1e30)
+            chances = jnp.exp(scores - logs)
             if banded:
-                early = block.start - span.start
-                sum_k[block, lanes] = grad_key[early:]
-                sum_v[block, lanes] = grad_value[early:]
-                if early:
-                    sum_k[span.start : block.start, lanes] += grad_key[:early]
-                    sum_v[span.start : block.start, lanes] += grad_value[:early]
-            elif at == 0:
-                sum_k[:, lanes] = grad_key
-                sum_v[:, lanes] = grad_value
+                work[2][span, pair_columns(at)] = chances.astype(BF16)
+                work[3][pair_columns(at), :] = grad
             else:
-                sum_k[:, lanes] += grad_key
-                sum_v[:, lanes] += grad_value
-    dk[...] = sum_k[...].astype(BF16)
-    dv[...] = sum_v[...].astype(BF16)
+                grad_value = dot(chances.astype(BF16), grad)
+                work[2][...] = grad_value if at == 0 else work[2][...] + grad_value
+            weighted = chances * dot_right(v[span, lanes], grad)
+            mean = jnp.sum(weighted, axis=0, keepdims=True)
+            scores_all[span, pair_columns(at)] = (weighted - chances * mean).astype(BF16)
+        turned = k[:, lanes].T
+        if not banded:
+            grad_query = dot(turned, scores_all[...])
+            dk[:, lanes] = dot(scores_all[...], query_all[...]).astype(BF16)
+            dv[:, lanes] = work[2][...].astype(BF16)
+        for at, block in enumerate(blocks):
+            if banded:
+                span = span_of(block, k.shape[0], banded)
+                part = dot(turned[:, span], scores_all[span, pair_columns(at)])
+                met = slice(pair_columns(at).start, pair_columns(min(at + 1, len(blocks) - 1)).stop)
+                dk[block, lanes] = dot(scores_all[block, met], query_all[met, :]).astype(BF16)
+                dv[block, lanes] = dot(work[2][block, met], work[3][met, :]).astype(BF16)
+            else:
+                part = grad_query[:, pair_columns(at)]
+            dq[block, lanes] = (own_rows(part).T * 0.125).astype(BF16)
 
 
 def team_total(mine, theirs, block):
@@ -369,7 +385,7 @@
     v[...] = (dot(normed[...], w[2]) + row_of(bias, 1)).astype(BF16)
     own = molecules[0:1, :]
     flow.send(q, k, v)
-    attend_forward(q, k, v, own, own, heads, totals, True)
+    attend_forward(q, k, v, own, own, heads, totals, *refs[-2:], True)
     flow.send(totals)
     if last:
         project_out(flow, [*done, heads], w_out, refs[5 : 5 + FRONT])
@@ -422,7 +438,7 @@
             normed[block, :] = (norm * row_of(vectors, GAIN + 1) + row_of(vectors, SHIFT + 1)).astype(BF16)
     flow.need(w)
     q[...] = (dot(normed[...], w[...]) + row_of(bias, 2)).astype(BF16)
-    attend_forward(q, k, v, molecules[0:1, :], molecules[1:2, :], heads, totals, False)
+    attend_forward(q, k, v, molecules[0:1, :], molecules[1:2, :], heads, totals, *refs[-2:], False)
     if last:
         project_out(flow, [*done, heads], w_out, refs[3 : 3 + FRONT])
 
@@ -497,7 +513,7 @@
     grad_cross, low, refs = refs[0], refs[1], refs[2:]
     (dq, dk, dv, bias_sums), refs = [refs[i * n : (i + 1) * n] for i in range(4)], refs[4 * n :]
     parts_out, sums, refs = refs[:BACK], refs[BACK], refs[BACK + 1 :]
-    grad_heads, sum_k, sum_v = refs[:n], refs[n], refs[n + 1]
+    grad_heads, work = refs[:n], refs[n:]
     seq, width = after_cross.shape
     rows = [jnp.zeros((1, width), F32)] * 3
     for block in row_blocks(seq):
@@ -516,7 +532,7 @@
     own, keys = molecules[0:1, :], molecules[1:2, :]
     for i in range(n):
         attend_backward(
-            q[i], k[i], v[i], own, keys, totals[i], grad_heads[i], dq[i], dk[i], dv[i], sum_k, sum_v, False
+            q[i], k[i], v[i], own, keys, totals[i], grad_heads[i], dq[i], dk[i], dv[i], work, False
         )
         column_sums(bias_sums[i], (dq[i], dv[i]))
     flow.need(*w)
@@ -571,7 +587,7 @@
     grad_cross, vectors, molecules, q, k, v, totals, refs = *refs[:7], refs[7:]
     w_out, refs = refs[:n], refs[n:]
     normed, heads, grad_self, low, dq, dk, dv, bias_sums, sums, refs = *refs[:9], refs[9:]
-    first, send, grad_heads, sum_k, sum_v = refs
+    first, send, grad_heads, work = *refs[:3], refs[3:]
     seq, width = after_self.shape
     rows = [jnp.zeros((1, width), F32)] * 3
     for block in row_blocks(seq):
@@ -589,7 +605,7 @@
     spread_grad_heads(low, w_out, [first, grad_heads] if n == 2 else [grad_heads])
     own = molecules[0:1, :]
     flow.need(q, k, v, totals)
-    attend_backward(q, k, v, own, own, totals, grad_heads, dq, dk, dv, sum_k, sum_v, True)
+    attend_backward(q, k, v, own, own, totals, grad_heads, dq, dk, dv, work, True)
     column_sums(bias_sums, (dq, dv))
     grads = [dot_left(a[...], b[...]) for a, b in ((dq, normed), (dk, normed), (dv, normed), (heads, low))]
     if n == 2:
@@ -606,10 +622,10 @@
     if n == 2:
         molecules, q, k, v, totals, grad_heads, normed, heads, low, refs = *refs[:9], refs[9:]
         bias_sums, keep, parts_out, refs = refs[0], refs[1], refs[2 : 2 + BACK], refs[2 + BACK :]
-        dq, dk, dv, sum_k, sum_v = refs
+        dq, dk, dv, work = *refs[:3], refs[3:]
         own = molecules[0:1, :]
         flow.need(q, k, v, totals)
-        attend_backward(q, k, v, own, own, totals, grad_heads, dq, dk, dv, sum_k, sum_v, True)
+        attend_backward(q, k, v, own, own, totals, grad_heads, dq, dk, dv, work, True)
         column_sums(bias_sums, (dq, dv))
         put_grads(keep, [dot_left(a[...], b[...]) for a, b in ((dq, normed), (dk, normed), (dv, normed), (heads, low))])
         pieces = [(dq, dk, dv), grads_last]
@@ -745,7 +761,7 @@
         out[k] = jnp.concatenate(parts, axis=0).astype(out.dtype)
 
 
-def join_kernel(ride, bit, flow, where, near, got, out):
+def join_kernel(ride, pad, bit, flow, where, near, got, out):
     half = near.shape[1] - (SMALL if ride else 0)
     for value, side in ((near, where[3 + bit]), (got, 1 - where[3 + bit])):
         rows = pl.ds(pl.multiple_of(side * half, half), half)
@@ -753,6 +769,8 @@
             out[p, rows, :] = value[p, :half]
     if ride:
         out[0, 2 * half :, :] = (near[0, half:].astype(F32) + got[0, half:].astype(F32)).astype(BF16)
+    if pad:
+        out[:, 2 * half :, :] = jnp.zeros((out.shape[0], pad, out.shape[2]), out.dtype)
 
 
 def joined(where, bit, near, got, p, ride=0):
@@ -785,8 +803,17 @@
     out[...] = value[3 * size :]
 
 
+def joined_inside(where, bit, near, got, p, pad):
+    half = (near.shape[1] - pad) // 2
+    first, parts = where[3 + bit] == 0, []
+    for k in (0, 1):
+        a, b = near[p, k * half : (k + 1) * half], got[p, k * half : (k + 1) * half]
+        parts += [jnp.where(first, a, b), jnp.where(first, b, a)]
+    return jnp.concatenate(parts, axis=0).astype(F32)
+
+
 def cross_grads_kernel(bit, flow, where, near, got, query, kv, out):
-    value = joined(where, bit, near, got, 0)
+    value = joined_inside(where, bit, near, got, 0, 2 * SMALL)
     size = out.shape[0]
     query[...] = value[:size].T
     for k in (0, 1):
@@ -907,6 +934,8 @@
     b_heads = [bias_own, bias_other] if apart else [jnp.concatenate([bias_own, bias_other], axis=1)]
     b_in = b_heads if apart else [b[4:].reshape(1, unit) for b in (bias_own, bias_other)]
 
+    forward_work = [pltpu.VMEM((seq, 2 * seq), BF16), pltpu.VMEM((1, 2 * seq), F32)]
+    cross_work = [pltpu.VMEM((mem_len, 2 * seq), BF16), pltpu.VMEM((1, 2 * seq), F32)]
     heads_self, saved_self = [], []
     for i in range(n):
         last = i == n - 1
@@ -915,7 +944,7 @@
         if last:
             ins += [*w_self_out, *heads_self]
             outs += front
-        got = run(functools.partial(self_forward_kernel, n, i), ins, outs, name=f"self_forward_{i}")
+        got = run(functools.partial(self_forward_kernel, n, i), ins, outs, scratch=forward_work, name=f"self_forward_{i}")
         if i == 0:
             normed_self, got = got[0], got[1:]
             early = (normed_self, other_qkv, bias_other, other_self_out)
@@ -958,7 +987,7 @@
         if last:
             ins += [*w_cross_out, *heads_cross]
             outs += front
-        got = run(functools.partial(cross_forward_kernel, n, i), ins, outs, name=f"cross_forward_{i}")
+        got = run(functools.partial(cross_forward_kernel, n, i), ins, outs, scratch=cross_work, name=f"cross_forward_{i}")
         if i == 0:
             after_self, normed_cross, got = got[0], got[1], got[2:]
         saved_cross.append((got[0], *kv, got[2]))
@@ -982,7 +1011,8 @@
     out_terms = team_parts(parts[:BACK])
 
     class Reduction:
-        def __init__(self, keeps, sends, axes):
+        def __init__(self, keeps, sends, axes, pad=0, turned=False):
+            self.pad, self.turned = pad, turned
             self.keeps, self.axes, self.ride, self.carry = keeps, axes, [], []
             self.gots = [swap(s, a) for s, a in zip(sends, axes[0])]
             self.halved = [b for b in axes[0] if b != "row"][:1]
@@ -993,8 +1023,9 @@
             if self.chunk is not None:
                 bit, small = self.halved.pop(), SMALL if self.ride else 0
                 planes, size, _ = self.chunk.shape
-                outs = [((planes, 2 * size - small, width), BF16)]
-                return functools.partial(join_kernel, bool(small), bit), [self.chunk, self.got], outs
+                pad = self.pad if len(self.halved) == 1 else 0
+                outs = [((planes, 2 * size - small + pad, width), BF16)]
+                return functools.partial(join_kernel, bool(small), pad, bit), [self.chunk, self.got], outs
             axes, keeps, size = self.axes, self.keeps, self.size
             planes = sum(k.shape[0] for k in keeps)
             bit, ride, at, rows = 0, [], None, size
@@ -1034,6 +1065,8 @@
 
         def take(self, got):
             if self.chunk is not None or len(self.axes) == 1:
+                if self.chunk is None and self.turned:
+                    self.halved[:2] = self.halved[1::-1]
                 self.chunk = got[0]
                 self.got = swap(self.chunk, self.halved[-1])
             else:
@@ -1066,7 +1099,9 @@
     by_out = Reduction([keep_out], [send_out], [["row"], [0], [1]])
     by_in = Reduction([keep_in], [send_in], [[0], ["row"], [1]])
 
-    scratch = [pltpu.VMEM((seq, wide), BF16)] * n + [pltpu.VMEM((seq, wide), F32)] * 2
+    all_scores = [pltpu.VMEM((mem_len, 2 * seq), BF16), pltpu.VMEM((2 * seq, LANES), BF16)]
+    scratch = [pltpu.VMEM((seq, wide), BF16)] * n + all_scores + [pltpu.VMEM((mem_len, LANES), F32)]
+    self_work = [pltpu.VMEM((seq, 2 * seq), BF16), pltpu.VMEM((2 * seq, LANES), BF16)] * 2
     bias_sum = ((2, wide), F32)
 
     def saved_of(saved):
@@ -1090,7 +1125,7 @@
         [((2, 2 * head, width), F32), ((2, 2 * head, width), BF16)] + back + [whole],
         name="cross_weights",
     )
-    by_cross = Reduction([keep], [send], [[0], [1], ["row"]] + [[k] for k in range(2, bits)])
+    by_cross = Reduction([keep], [send], [[0], [1], ["row"]] + [[k] for k in range(2, bits)], pad=2 * SMALL, turned=True)
     advance("fold_ffn", by_out, by_in)
 
     group = ((1, 4 * head, width), F32)
@@ -1099,7 +1134,7 @@
         functools.partial(self_backward_kernel, n),
         ins + [*w_self_out, normed_self, heads_self[-1]],
         [full, whole] + [local] * 3 + [bias_sum, ((3, width), F32), local if n == 2 else group, (group[0], BF16)],
-        scratch=scratch[-3:],
+        scratch=[pltpu.VMEM((seq, wide), BF16)] + self_work,
         name="self_backward",
     )
     by_self = Reduction([first], [send], [["row"]] + [[k] for k in range(bits)])
@@ -1120,18 +1155,20 @@
         functools.partial(self_backward_rest_kernel, n),
         ins,
         outs,
-        scratch=[pltpu.VMEM((seq, wide), BF16)] * 3 + scratch[-2:] if n == 2 else [],
+        scratch=[pltpu.VMEM((seq, wide), BF16)] * 3 + self_work if n == 2 else [],
         name="self_backward_rest",
     )
     self_bias_sums = [last_sums]
     if n == 2:
         self_bias_sums, by_self.keeps, got = [got[0], last_sums], [got[1]], got[2:]
     terms = team_parts(got)
+    moved = [*given, by_ffn.gots[0]]
+    moved_at = by_ffn.extra_at if along else None
+    advance("ffn_2", by_ffn)
     sent, more = [blocks, ((1, 8 * SMALL, width), BF16)], None
     if along:
-        more = (functools.partial(memory_send_kernel, 1, by_ffn.extra_at, 0), [*given, by_ffn.gots[0]], sent)
+        more = (functools.partial(memory_send_kernel, 1, moved_at, 0), moved, sent)
     given = advance("cross_1", by_cross, more=more)
-    advance("ffn_2", by_ffn)
     advance("self_1", by_self)
 
     fits = apart and 4 * head == width and unit == width
@@ -1166,9 +1203,10 @@
     by_self.ride, by_self.ride_at = [small_own, by_cross.gots[0]], by_cross.size
     if along:
         memory_state = [given[0], other(given[1])]
-    advance("all_1", by_cross, by_self, by_ffn)
-    got_both = other(later(both, by_self.keeps[0]))
-    advance("all_2", by_self, by_ffn, by_cross)
+    advance("ffn_3", by_ffn)
+    advance("self_cross_2", by_self, by_cross)
+    got_both = other(later(both, by_cross.keeps[0]))
+    advance("all_3", by_self, by_ffn, by_cross)
     if not along:
         mine, theirs = jnp.concatenate(mem_terms[:BACK]), jnp.concatenate(mem_terms[BACK:])
         total = (mine.astype(F32) + theirs.astype(F32)).astype(BF16)
@@ -1179,7 +1217,7 @@
         grad_memory = lax.all_to_all(
             blocks, ("dp", "mp"), split_axis=0, concat_axis=0, tiled=True, axis_index_groups=same_seat
         ).astype(F32)
-    advance("self_cross_3", by_self, by_cross)
+    advance("self_cross_4", by_self, by_cross)
 
     def cross_grads():
         return run(
@@ -1189,15 +1227,12 @@
             name="cross_grads",
         )
 
-    cross_results = None
-    if by_cross.ready():
-        cross_results = cross_grads()
     more = (functools.partial(memory_send_kernel, "row", 0, 2), memory_state, sent) if along else None
     while more or not (by_self.ready() and by_cross.ready() and by_ffn.ready()):
-        given = advance("rest", by_self, by_cross, by_ffn, more=more)
+        given = advance("rest", by_self, more=more)
         if more:
             memory_state, more = [given[0], data_swap(given[1], 2)], None
-    grad_cross_q, grad_cross_kv, grad_cross_out = cross_results or cross_grads()
+        advance("rest_cross", by_ffn, by_cross)
     mixed, grad_inputs = run(
         place_rows_kernel,
         [both, got_both],
@@ -1210,6 +1245,7 @@
         [far(((width, unit), F32)), far(((unit, width), F32))],
         name="ffn_grads",
     )
+    grad_cross_q, grad_cross_kv, grad_cross_out = cross_grads()
     if along:
         (grad_memory,) = run(
             functools.partial(memory_end_kernel, 2, 0),

time: 153 us -> 149 us (0.974)
  Pallas kernels: 68 us -> 63 us
  waiting for transfers between devices: 31.1 us -> 35.3 us
  starting transfers between devices: 51.2 us -> 47.5 us
    ppermute x11, waiting for transfers between devices: 1.73 us -> 10.6 us  [other(): return lax.ppermute(value, 'mp', across)]
    pallas_call x30 -> x31, Pallas kernels: 68 us -> 63 us  [__call__(): pl.pallas_call(body, in_specs=[words] + specs + after_specs, out_specs=[f...]
    ppermute x19, waiting for transfers between devices: 27.9 us -> 23.2 us  [data_swap(): return lax.ppermute(value, 'dp', [(i, i ^ 1 << k) for i in range(dp)])]
    ppermute x19, starting transfers between devices: 27.9 us -> 25 us  [data_swap(): return lax.ppermute(value, 'dp', [(i, i ^ 1 << k) for i in range(dp)])]
  transfers between devices with their start and end apart: 45 -> 45, of which waited for: 15 -> 20; matrix products, arithmetic and copies ran while one was open for 0% -> 0% of each run, Pallas kernels for 41% -> 39%
where the time goes in v3:
time: 149 us; the launch traced here: 148 us
  Pallas kernels  63 us (42%)
  starting transfers between devices  47.5 us (32%)
  waiting for transfers between devices  35.3 us (24%)
    pallas_call x31, Pallas kernels, __call__(): pl.pallas_call(body, in_specs=[words] + specs + after_specs, out_specs=[f...  63 us
    ppermute x19, starting transfers between devices, data_swap(): return lax.ppermute(value, 'dp', [(i, i ^ 1 << k) for i in range(dp)])  25 us
    ppermute x19, waiting for transfers between devices, data_swap(): return lax.ppermute(value, 'dp', [(i, i ^ 1 << k) for i in range(dp)])  23.2 us
    ppermute x11, starting transfers between devices, other(): return lax.ppermute(value, 'mp', across)  13 us
    ppermute x11, waiting for transfers between devices, other(): return lax.ppermute(value, 'mp', across)  10.6 us
    all_to_all x1, starting transfers between devices, shards(): lax.all_to_all(memory_part, 'dp', split_axis=0, concat_axis=0, tiled=True)  6.27 us
    ppermute x14, starting transfers between devices, seat_swap(): return lax.ppermute(value, 'mp', [(i, i ^ step) for i in range(mp)])  3.23 us
  transfers between devices with their start and end apart: 45, of which 20 were waited for; matrix products, arithmetic and copies ran while one was open for 0% of the time, Pallas kernels for 39%

profile of v3, /device:TPU:0, one launch (start us, length us, event | category | flops | bytes accessed | tf_op | source)
XLA Modules:
  0.0 148.1 jit_solution(11119322844070386245)
XLA Ops:
  0.6 3.0 %collective-permute-start = (bf16[3,512,128]{2,1,0:T(8,128)(2,1)}, bf16[3,512,128]{2,1,0:T(8,128)(2,1)S(1)}, u32[]{:S(2)}, u32[]{:S(2)}) collective-permute-start(bf16[3,512,128]{2,1,0:T(8,128)(2,1)} %refs_0_.3), channel_id=1, source_target_pairs={{0,2},{1,3},{2,0},{3,1},{4,6},{5,7},{6,4},{7,5},{8,10},{9,11},{10,... | collective-permute-start | bytes 1179656 | tf_op jit(solution)/shard_map/ppermute | solution.py:872
  3.8 3.3 %setup.1 = (bf16[1024,128]{1,0:T(8,128)(2,1)S(1)}, bf16[2,512,512]{2,1,0:T(8,128)(2,1)S(1)}, bf16[512,512]{1,0:T(8,128)(2,1)S(1)}, bf16[512,512]{1,0:T(8,128)(2,...) custom-call(s32[6]{0:T(128)S(1)} %stack.27.where_ref, ...), custom_call_target="tpu_custom_call" | custom-call | flops 1000000 | bytes 300000 | tf_op jit(solution)/shard_map/setup/pallas_call | solution.py:146
  8.1 6.3 %all-to-all-start = ((bf16[8,64,512]{2,1,0:T(8,128)(2,1)}), bf16[8,64,512]{2,1,0:T(8,128)(2,1)S(1)}, u32[]{:S(2)}, u32[]{:S(2)}) async-start(bf16[8,64,512]{2,1,0:T(8,128)(2,1)} %get-tuple-element.192), calls=%async_computation | async-start | bytes 1048576 | tf_op jit(solution)/shard_map/all_to_all | solution.py:928
  14.4 1.5 %collective-permute-start.2 = (bf16[128,512]{1,0:T(8,128)(2,1)}, bf16[128,512]{1,0:T(8,128)(2,1)S(1)}, u32[]{:S(2)}, u32[]{:S(2)}) collective-permute-start(bf16[128,512]{1,0:T(8,128)(2,1)} %refs_12_.3), channel_id=1, source_target_pairs={{0,2},{1,3},{2,0},{3,1},{4,6},{5,7},{6,4},{7,5},{8,10},{9,11},{10,... | collective-permute-start | bytes 393224 | tf_op jit(solution)/shard_map/ppermute | solution.py:872
  16.5 3.1 %self_forward_0.1 = (bf16[512,512]{1,0:T(8,128)(2,1)S(1)}, bf16[512,128]{1,0:T(8,128)(2,1)}, bf16[512,128]{1,0:T(8,128)(2,1)}, bf16[512,128]{1,0:T(8,128)(2,1)},...) custom-call(s32[6]{0:T(128)S(1)} %stack.27.where_ref, ...), custom_call_target="tpu_custom_call" | custom-call | flops 1000000 | bytes 300000 | tf_op jit(solution)/shard_map/self_forward_0/pallas_call | solution.py:146
  19.5 1.9 %collective-permute-done.1.refs_4_.refs_3_.refs_5_ = bf16[8,128]{1,0:T(8,128)(2,1)S(1)} collective-permute-done((bf16[8,128]{1,0:T(8,128)(2,1)S(1)}, bf16[8,128]{1,0:T(8,128)(2,1)S(1)}, u32[]{:S(2)}, u32[]{:S(2)}) %collective-permute-start.1) | collective-permute-done | bytes 2080 | tf_op jit(solution)/shard_map/ppermute | solution.py:872
  21.5 1.8 %collective-permute-start.9 = (bf16[2,512,512]{2,1,0:T(8,128)(2,1)}, bf16[2,512,512]{2,1,0:T(8,128)(2,1)}, u32[]{:S(2)}, u32[]{:S(2)}) collective-permute-start(bf16[2,512,512]{2,1,0:T(8,128)(2,1)} %copy-done), channel_id=1, source_target_pairs={{0,2},{1,3},{2,0},{3,1},{4,6},{5,7},{6,4},{7,5},{8,10},{9,11},{10,... | collective-permute-start | bytes 3145736 | tf_op jit(solution)/shard_map/ppermute | solution.py:872
  23.3 2.9 %self_forward_1.1 = (bf16[512,128]{1,0:T(8,128)(2,1)}, bf16[512,128]{1,0:T(8,128)(2,1)}, bf16[512,128]{1,0:T(8,128)(2,1)}, bf16[512,128]{1,0:T(8,128)(2,1)S(1)},...) custom-call(s32[6]{0:T(128)S(1)} %stack.27.where_ref, ...), custom_call_target="tpu_custom_call" | custom-call | flops 1000000 | bytes 300000 | tf_op jit(solution)/shard_map/self_forward_1/pallas_call | solution.py:146
  26.8 1.5 %collective-permute-start.6 = (bf16[1024,128]{1,0:T(8,128)(2,1)S(1)}, bf16[1024,128]{1,0:T(8,128)(2,1)S(1)}, u32[]{:S(2)}, u32[]{:S(2)}) collective-permute-start(bf16[1024,128]{1,0:T(8,128)(2,1)S(1)} %collective-permute-done.5.refs_0_), channel_id=1, source_target_pairs={{0,4},{4,0},{8,12},{12,8},{16,20},{20,16},{24,28},{28,24},{1,5},{5... | collective-permute-start | bytes 786440 | tf_op jit(solution)/shard_map/ppermute | solution.py:878
  28.3 1.9 %memory_0.1 = (bf16[512,128]{1,0:T(8,128)(2,1)S(1)}, bf16[512,128]{1,0:T(8,128)(2,1)S(1)}, f32[8,128]{1,0:T(8,128)}) custom-call(s32[6]{0:T(128)S(1)} %stack.27.where_ref, bf16[512,512]{1,0:T(8,128)(2,1)S(1)} %bitcast.10, bf16[2,512,128]{2,1,0:T(8,128)(2,1)} %refs_8_.3, bf16[8,128]{1,0:T(8,128)(2,1)S(1)} %pad_maximum_fusion.refs_4_.refs_2_.refs_8_, ...), custom_call_target="tpu_custom_call" | custom-call | flops 1000000 | bytes 300000 | tf_op jit(solution)/shard_map/memory_0/pallas_call | solution.py:146
  30.3 3.6 %cross_forward_0.1 = (f32[512,512]{1,0:T(8,128)S(1)}, bf16[512,512]{1,0:T(8,128)(2,1)S(1)}, bf16[512,128]{1,0:T(8,128)(2,1)S(1)}, bf16[512,128]{1,0:T(8,128)(2,1...) custom-call(s32[6]{0:T(128)S(1)} %stack.27.where_ref, bf16[512,512]{1,0:T(8,128)(2,1)S(1)} %get-tuple-element.183.refs_0_, ...), custom_call_target="tpu_custom_call" | custom-call | flops 1000000 | bytes 300000 | tf_op jit(solution)/shard_map/cross_forward_0/pallas_call | solution.py:146
  36.1 2.5 %cross_forward_1.1 = (bf16[512,128]{1,0:T(8,128)(2,1)S(1)}, bf16[512,128]{1,0:T(8,128)(2,1)S(1)}, f32[2,512]{1,0:T(2,128)S(1)}, bf16[256,512]{1,0:T(8,128)(2,1)S...) custom-call(s32[6]{0:T(128)S(1)} %stack.27.where_ref, bf16[512,512]{1,0:T(8,128)(2,1)S(1)} %get-tuple-element.198.refs_0_.refs_10_, ...), custom_call_target="tpu_custom_call" | custom-call | flops 1000000 | bytes 300000 | tf_op jit(solution)/shard_map/cross_forward_1/pallas_call | solution.py:146
  40.5 4.3 %ffn_0.1 = (f32[512,512]{1,0:T(8,128)S(1)}, bf16[512,512]{1,0:T(8,128)(2,1)S(1)}, bf16[512,512]{1,0:T(8,128)(2,1)S(1)}, bf16[512,512]{1,0:T(8,128)(2,1)S(1)}, bf...) custom-call(s32[6]{0:T(128)S(1)} %stack.27.where_ref, ...), custom_call_target="tpu_custom_call" | custom-call | flops 1000000 | bytes 300000 | tf_op jit(solution)/shard_map/ffn_0/pallas_call | solution.py:146
  44.9 1.4 collective-permute-done.9.refs_4_
  46.2 3.4 %ffn_1.2 = (bf16[512,512]{1,0:T(8,128)(2,1)S(1)}, bf16[512,512]{1,0:T(8,128)(2,1)S(1)}, bf16[256,512]{1,0:T(8,128)(2,1)S(1)}, bf16[256,512]{1,0:T(8,128)(2,1)S(1...) custom-call(s32[6]{0:T(128)S(1)} %stack.27.where_ref, ...), custom_call_target="tpu_custom_call" | custom-call | flops 1000000 | bytes 300000 | tf_op jit(solution)/shard_map/ffn_1/pallas_call | solution.py:146
  49.7 1.8 %ffn_weights.1 = (f32[2,512]{1,0:T(2,128)S(1)}, f32[1,512,512]{2,1,0:T(8,128)S(1)}, bf16[1,512,512]{2,1,0:T(8,128)(2,1)S(1)}, f32[2,256,512]{2,1,0:T(8,128)S(1)}...) custom-call(s32[6]{0:T(128)S(1)} %stack.27.where_ref, bf16[512,512]{1,0:T(8,128)(2,1)S(1)} %get-tuple-element.225.refs_0_, ...), custom_call_target="tpu_custom_call" | custom-call | flops 1000000 | bytes 300000 | tf_op jit(solution)/shard_map/ffn_weights/pallas_call | solution.py:146
  51.6 1.5 %collective-permute-start.14 = (bf16[1,512,512]{2,1,0:T(8,128)(2,1)S(1)}, bf16[1,512,512]{2,1,0:T(8,128)(2,1)S(1)}, u32[]{:S(2)}, u32[]{:S(2)}) collective-permute-start(bf16[1,512,512]{2,1,0:T(8,128)(2,1)S(1)} %get-tuple-element.240), channel_id=1, source_target_pairs={{0,2},{1,3},{2,0},{3,1},{4,6},{5,7},{6,4},{7,5},{8,10},{9,11},{10,... | collective-permute-start | bytes 1572872 | tf_op jit(solution)/shard_map/ppermute | solution.py:872
  53.3 1.5 %collective-permute-start.15 = (bf16[2,256,512]{2,1,0:T(8,128)(2,1)S(1)}, bf16[2,256,512]{2,1,0:T(8,128)(2,1)S(1)}, u32[]{:S(2)}, u32[]{:S(2)}) collective-permute-start(bf16[2,256,512]{2,1,0:T(8,128)(2,1)S(1)} %get-tuple-element.242), channel_id=1, source_target_pairs={{0,4},{4,0},{8,12},{12,8},{16,20},{20,16},{24,28},{28,24},{1,5},{5... | collective-permute-start | bytes 1572872 | tf_op jit(solution)/shard_map/ppermute | solution.py:878
  55.3 5.9 %cross_backward.1 = (f32[512,512]{1,0:T(8,128)S(1)}, bf16[512,512]{1,0:T(8,128)(2,1)S(1)}, bf16[512,128]{1,0:T(8,128)(2,1)S(1)}, bf16[512,128]{1,0:T(8,128)(2,1)...) custom-call(s32[6]{0:T(128)S(1)} %stack.27.where_ref, ...), custom_call_target="tpu_custom_call" | custom-call | flops 1000000 | bytes 300000 | tf_op jit(solution)/shard_map/cross_backward/pallas_call | solution.py:146
  61.8 3.0 %cross_weights.1 = (f32[2,256,512]{2,1,0:T(8,128)S(1)}, bf16[2,256,512]{2,1,0:T(8,128)(2,1)S(1)}, bf16[256,512]{1,0:T(8,128)(2,1)S(1)}, bf16[256,512]{1,0:T(8,12...) custom-call(s32[6]{0:T(128)S(1)} %stack.27.where_ref, bf16[512,128]{1,0:T(8,128)(2,1)S(1)} %get-tuple-element.243.refs_0_, ...), custom_call_target="tpu_custom_call" | custom-call | flops 1000000 | bytes 300000 | tf_op jit(solution)/shard_map/cross_weights/pallas_call | solution.py:146
  66.0 1.4 collective-permute-done.15.refs_3_
  68.1 1.6 %collective-permute-start.18 = (bf16[1,256,512]{2,1,0:T(8,128)(2,1)S(1)}, bf16[1,256,512]{2,1,0:T(8,128)(2,1)S(1)}, u32[]{:S(2)}, u32[]{:S(2)}) collective-permute-start(bf16[1,256,512]{2,1,0:T(8,128)(2,1)S(1)} %get-tuple-element.268), channel_id=1, source_target_pairs={{0,4},{4,0},{8,12},{12,8},{16,20},{20,16},{24,28},{28,24},{1,5},{5... | collective-permute-start | bytes 786440 | tf_op jit(solution)/shard_map/ppermute | solution.py:878
  70.8 4.1 %self_backward.1 = (f32[512,512]{1,0:T(8,128)S(1)}, bf16[512,512]{1,0:T(8,128)(2,1)S(1)}, bf16[512,128]{1,0:T(8,128)(2,1)S(1)}, bf16[512,128]{1,0:T(8,128)(2,1)S...) custom-call(s32[6]{0:T(128)S(1)} %stack.27.where_ref, ...), custom_call_target="tpu_custom_call" | custom-call | flops 1000000 | bytes 300000 | tf_op jit(solution)/shard_map/self_backward/pallas_call | solution.py:146
  75.0 2.5 %collective-permute-done.18.refs_2_ = bf16[1,256,512]{2,1,0:T(8,128)(2,1)S(1)} collective-permute-done((bf16[1,256,512]{2,1,0:T(8,128)(2,1)S(1)}, bf16[1,256,512]{2,1,0:T(8,128)(2,1)S(1)}, u32[]{:S(2)}, u32[]{:S(2)}) %collective-permute-start.18) | collective-permute-done | bytes 262176 | tf_op jit(solution)/shard_map/ppermute | solution.py:878
  78.1 1.6 %collective-permute-start.26 = (bf16[2,192,512]{2,1,0:T(8,128)(2,1)S(1)}, bf16[2,192,512]{2,1,0:T(8,128)(2,1)S(1)}, u32[]{:S(2)}, u32[]{:S(2)}) collective-permute-start(bf16[2,192,512]{2,1,0:T(8,128)(2,1)S(1)} %get-tuple-element.290), channel_id=1, source_target_pairs={{0,8},{4,12},{8,0},{12,4},{16,24},{20,28},{24,16},{28,20},{1,9},{5... | collective-permute-start | bytes 1179656 | tf_op jit(solution)/shard_map/ppermute | solution.py:878
  80.5 4.0 %self_backward_rest.1 = (f32[2,128]{1,0:T(2,128)S(1)}, f32[1,512,512]{2,1,0:T(8,128)S(1)}, bf16[256,512]{1,0:T(8,128)(2,1)S(1)}, bf16[256,512]{1,0:T(8,128)(2,1)S(1)}, f32[8,128]{1,0:T(8,128)}) custom-call(s32[6]{0:T(128)S(1)} %stack.27.where_ref, bf16[3,512,128]{2,1,0:T(8,128)(2,1)} %refs_0_.3, ...), custom_call_target="tpu_custom_call" | custom-call | flops 1000000 | bytes 300000 | tf_op jit(solution)/shard_map/self_backward_rest/pallas_call | solution.py:146
  85.1 2.1 %collective-permute-done.26.refs_1_.refs_3_ = bf16[2,192,512]{2,1,0:T(8,128)(2,1)S(1)} collective-permute-done((bf16[2,192,512]{2,1,0:T(8,128)(2,1)S(1)}, bf16[2,192,512]{2,1,0:T(8,128)(2,1)S(1)}, u32[]{:S(2)}, u32[]{:S(2)}) %collective-permute-start.26) | collective-permute-done | bytes 393248 | tf_op jit(solution)/shard_map/ppermute | solution.py:878
  88.5 1.6 %collective-permute-start.28 = (bf16[2,128,512]{2,1,0:T(8,128)(2,1)S(1)}, bf16[2,128,512]{2,1,0:T(8,128)(2,1)S(1)}, u32[]{:S(2)}, u32[]{:S(2)}) collective-permute-start(bf16[2,128,512]{2,1,0:T(8,128)(2,1)S(1)} %get-tuple-element.300), channel_id=1, source_target_pairs={{0,8},{4,12},{8,0},{12,4},{16,24},{20,28},{24,16},{28,20},{1,9},{5... | collective-permute-start | bytes 786440 | tf_op jit(solution)/shard_map/ppermute | solution.py:878
  91.3 2.6 %collective-permute-start.31 = (bf16[2,128,512]{2,1,0:T(8,128)(2,1)S(1)}, bf16[2,128,512]{2,1,0:T(8,128)(2,1)S(1)}, u32[]{:S(2)}, u32[]{:S(2)}) collective-permute-start(bf16[2,128,512]{2,1,0:T(8,128)(2,1)S(1)} %get-tuple-element.307.refs_0_), channel_id=1, source_target_pairs={{0,16},{4,20},{8,24},{12,28},{16,0},{20,4},{24,8},{28,12},{1,17},{... | collective-permute-start | bytes 786440 | tf_op jit(solution)/shard_map/ppermute | solution.py:878
  95.5 1.7 %input_backward.1 = (bf16[1024,512]{1,0:T(8,128)(2,1)S(1)}, bf16[16,512]{1,0:T(8,128)(2,1)S(1)}, bf16[16,512]{1,0:T(8,128)(2,1)S(1)}, f32[8,128]{1,0:T(8,128)}) custom-call(s32[6]{0:T(128)S(1)} %stack.27.where_ref, bf16[512,512]{1,0:T(8,128)(2,1)S(1)} %get-tuple-element.183.refs_0_, bf16[256,512]{1,0:T(8,128)(2,1)S(1)} %get-tuple-element.274.refs_1_, ...), custom_call_target="tpu_custom_call" | custom-call | flops 1000000 | bytes 300000 | tf_op jit(solution)/shard_map/input_backward/pallas_call | solution.py:146
  99.2 1.4 collective-permute-start.30
  100.6 3.2 %collective-permute-done.31.refs_1_ = bf16[2,128,512]{2,1,0:T(8,128)(2,1)S(1)} collective-permute-done((bf16[2,128,512]{2,1,0:T(8,128)(2,1)S(1)}, bf16[2,128,512]{2,1,0:T(8,128)(2,1)S(1)}, u32[]{:S(2)}, u32[]{:S(2)}) %collective-permute-start.31) | collective-permute-done | bytes 262176 | tf_op jit(solution)/shard_map/ppermute | solution.py:878
  104.4 1.5 %collective-permute-done.30.refs_3_ = bf16[1,144,512]{2,1,0:T(8,128)(2,1)S(1)} collective-permute-done((bf16[1,144,512]{2,1,0:T(8,128)(2,1)S(1)}, bf16[1,144,512]{2,1,0:T(8,128)(2,1)S(1)}, u32[]{:S(2)}, u32[]{:S(2)}) %collective-permute-start.30) | collective-permute-done | bytes 147488 | tf_op jit(solution)/shard_map/ppermute | solution.py:872
  106.5 1.5 %collective-permute-start.32 = (bf16[1024,512]{1,0:T(8,128)(2,1)S(1)}, bf16[1024,512]{1,0:T(8,128)(2,1)S(1)}, u32[]{:S(2)}, u32[]{:S(2)}) collective-permute-start(bf16[1024,512]{1,0:T(8,128)(2,1)S(1)} %get-tuple-element.311.refs_0_), channel_id=1, source_target_pairs={{0,2},{1,3},{2,0},{3,1},{4,6},{5,7},{6,4},{7,5},{8,10},{9,11},{10,... | collective-permute-start | bytes 3145736 | tf_op jit(solution)/shard_map/ppermute | solution.py:872
  108.2 1.8 %collective-permute-start.33 = (bf16[1,128,512]{2,1,0:T(8,128)(2,1)S(1)}, bf16[1,128,512]{2,1,0:T(8,128)(2,1)S(1)}, u32[]{:S(2)}, u32[]{:S(2)}) collective-permute-start(bf16[1,128,512]{2,1,0:T(8,128)(2,1)S(1)} %get-tuple-element.313), channel_id=1, source_target_pairs={{0,8},{4,12},{8,0},{12,4},{16,24},{20,28},{24,16},{28,20},{1,9},{5... | collective-permute-start | bytes 393224 | tf_op jit(solution)/shard_map/ppermute | solution.py:878
  110.0 1.4 collective-permute-start.35
  111.5 2.9 %collective-permute-done.34.refs_5_ = bf16[2,128,512]{2,1,0:T(8,128)(2,1)S(1)} collective-permute-done((bf16[2,128,512]{2,1,0:T(8,128)(2,1)S(1)}, bf16[2,128,512]{2,1,0:T(8,128)(2,1)S(1)}, u32[]{:S(2)}, u32[]{:S(2)}) %collective-permute-start.34) | collective-permute-done | bytes 262176 | tf_op jit(solution)/shard_map/ppermute | solution.py:878
  114.4 4.4 %collective-permute-done.33.refs_1_ = bf16[1,128,512]{2,1,0:T(8,128)(2,1)S(1)} collective-permute-done((bf16[1,128,512]{2,1,0:T(8,128)(2,1)S(1)}, bf16[1,128,512]{2,1,0:T(8,128)(2,1)S(1)}, u32[]{:S(2)}, u32[]{:S(2)}) %collective-permute-start.33) | collective-permute-done | bytes 131104 | tf_op jit(solution)/shard_map/ppermute | solution.py:878
  119.5 2.6 %collective-permute-start.37 = (bf16[1,128,512]{2,1,0:T(8,128)(2,1)S(1)}, bf16[1,128,512]{2,1,0:T(8,128)(2,1)S(1)}, u32[]{:S(2)}, u32[]{:S(2)}) collective-permute-start(bf16[1,128,512]{2,1,0:T(8,128)(2,1)S(1)} %get-tuple-element.318.refs_2_), channel_id=1, source_target_pairs={{0,4},{4,0},{8,12},{12,8},{16,20},{20,16},{24,28},{28,24},{1,5},{5... | collective-permute-start | bytes 393224 | tf_op jit(solution)/shard_map/ppermute | solution.py:878
  122.2 3.6 %collective-permute-done.37.refs_3_ = bf16[1,128,512]{2,1,0:T(8,128)(2,1)S(1)} collective-permute-done((bf16[1,128,512]{2,1,0:T(8,128)(2,1)S(1)}, bf16[1,128,512]{2,1,0:T(8,128)(2,1)S(1)}, u32[]{:S(2)}, u32[]{:S(2)}) %collective-permute-start.37) | collective-permute-done | bytes 131104 | tf_op jit(solution)/shard_map/ppermute | solution.py:878
  126.8 2.4 %collective-permute-start.38 = (bf16[1,144,512]{2,1,0:T(8,128)(2,1)S(1)}, bf16[1,144,512]{2,1,0:T(8,128)(2,1)S(1)}, u32[]{:S(2)}, u32[]{:S(2)}) collective-permute-start(bf16[1,144,512]{2,1,0:T(8,128)(2,1)S(1)} %get-tuple-element.320.refs_0_), channel_id=1, source_target_pairs={{0,8},{4,12},{8,0},{12,4},{16,24},{20,28},{24,16},{28,20},{1,9},{5... | collective-permute-start | bytes 442376 | tf_op jit(solution)/shard_map/ppermute | solution.py:878
  129.7 4.5 %collective-permute-done.39.refs_3_ = bf16[1,128,512]{2,1,0:T(8,128)(2,1)S(1)} collective-permute-done((bf16[1,128,512]{2,1,0:T(8,128)(2,1)S(1)}, bf16[1,128,512]{2,1,0:T(8,128)(2,1)S(1)}, u32[]{:S(2)}, u32[]{:S(2)}) %collective-permute-start.39) | collective-permute-done | bytes 131104 | tf_op jit(solution)/shard_map/ppermute | solution.py:872
  134.8 2.7 %collective-permute-start.43 = (bf16[1,272,512]{2,1,0:T(8,128)(2,1)S(1)}, bf16[1,272,512]{2,1,0:T(8,128)(2,1)S(1)}, u32[]{:S(2)}, u32[]{:S(2)}) collective-permute-start(bf16[1,272,512]{2,1,0:T(8,128)(2,1)S(1)} %get-tuple-element.335.refs_0_), channel_id=1, source_target_pairs={{0,4},{4,0},{8,12},{12,8},{16,20},{20,16},{24,28},{28,24},{1,5},{5... | collective-permute-start | bytes 835592 | tf_op jit(solution)/shard_map/ppermute | solution.py:878
  138.3 2.3 %place_rows.1 = (bf16[2,512,512]{2,1,0:T(8,128)(2,1)}, f32[2,512,512]{2,1,0:T(8,128)}, f32[8,128]{1,0:T(8,128)}) custom-call(s32[6]{0:T(128)S(1)} %stack.27.where_ref, bf16[1024,512]{1,0:T(8,128)(2,1)S(1)} %get-tuple-element.311.refs_0_, bf16[1024,512]{1,0:T(8,128)(2,1)S(1)} %collective-permute-done.32.refs_1_, f32[8,128]{1,0:T(8,128)} %get-tuple-element.324.refs_2_), custom_call_target="tpu_custom_call" | custom-call | flops 1000000 | bytes 300000 | tf_op jit(solution)/shard_map/place_rows/pallas_call | solution.py:146
  140.6 2.2 %ffn_grads.1 = (f32[512,512]{1,0:T(8,128)}, f32[512,512]{1,0:T(8,128)}, f32[8,128]{1,0:T(8,128)}) custom-call(s32[6]{0:T(128)S(1)} %stack.27.where_ref, bf16[2,256,512]{2,1,0:T(8,128)(2,1)S(1)} %get-tuple-element.330.refs_0_, bf16[2,256,512]{2,1,0:T(8,128)(2,1)S(1)} %collective-permute-done.42.refs_1_, f32[8,128]{1,0:T(8,128)} %get-tuple-element.331.refs_2_), custom_call_target="tpu_custom_call" | custom-call | flops 1000000 | bytes 300000 | tf_op jit(solution)/shard_map/ffn_grads/pallas_call | solution.py:146
  142.8 1.6 %cross_grads.1 = (f32[512,128]{1,0:T(8,128)}, f32[2,512,128]{2,1,0:T(8,128)}, f32[128,512]{1,0:T(8,128)}, f32[8,128]{1,0:T(8,128)}) custom-call(s32[6]{0:T(128)S(1)} %stack.27.where_ref, bf16[1,288,512]{2,1,0:T(8,128)(2,1)S(1)} %get-tuple-element.329.refs_0_, bf16[1,288,512]{2,1,0:T(8,128)(2,1)S(1)} %collective-permute-done.41.refs_1_, ...), custom_call_target="tpu_custom_call" | custom-call | flops 1000000 | bytes 300000 | tf_op jit(solution)/shard_map/cross_grads/pallas_call | solution.py:146
  144.7 1.4 memory_end.1
  146.1 1.8 %self_grads.1 = (f32[3,512,128]{2,1,0:T(8,128)}, f32[128,512]{1,0:T(8,128)}, f32[3,512]{1,0:T(4,128)}, f32[3,512]{1,0:T(4,128)}, f32[3,512]{1,0:T(4,128)}, /*ind...) custom-call(s32[6]{0:T(128)S(1)} %stack.27.where_ref, ...), custom_call_target="tpu_custom_call" | custom-call | flops 1000000 | bytes 300000 | tf_op jit(solution)/shard_map/self_grads/pallas_call | solution.py:146
  (83 shorter events, 24.0 us)
Async XLA Ops:
  0.6 20.8 %collective-permute-start = (bf16[3,512,128]{2,1,0:T(8,128)(2,1)}, bf16[3,512,128]{2,1,0:T(8,128)(2,1)S(1)}, u32[]{:S(2)}, u32[]{:S(2)}) collective-permute-start(bf16[3,512,128]{2,1,0:T(8,128)(2,1)} %refs_0_.3), channel_id=1, source_target_pairs={{0,2},{1,3},{2,0},{3,1},{4,6},{5,7},{6,4},{7,5},{8,10},{9,11},{10,... | collective-permute-start | bytes 1179656 | tf_op jit(solution)/shard_map/ppermute | solution.py:872
  3.8 12.1 %copy-start.1 = (bf16[512]{0:T(512)(128)(2,1)S(1)}, bf16[512]{0:T(512)(128)(2,1)}, u32[]{:S(2)}) copy-start(bf16[512]{0:T(512)(128)(2,1)} %param.36) | copy-start | bytes 3076
  3.8 12.1 %copy-start.2 = (bf16[2,128]{1,0:T(2,128)(2,1)S(1)}, bf16[2,128]{1,0:T(2,128)(2,1)}, u32[]{:S(2)}) copy-start(bf16[2,128]{1,0:T(2,128)(2,1)} %param.33) | copy-start | bytes 1540
  3.8 12.1 %copy-start.3 = (bf16[2,128]{1,0:T(2,128)(2,1)S(1)}, bf16[2,128]{1,0:T(2,128)(2,1)}, u32[]{:S(2)}) copy-start(bf16[2,128]{1,0:T(2,128)(2,1)} %param.29) | copy-start | bytes 1540
  8.0 13.4 %collective-permute-start.5 = (bf16[1024,128]{1,0:T(8,128)(2,1)S(1)}, bf16[1024,128]{1,0:T(8,128)(2,1)S(1)}, u32[]{:S(2)}, u32[]{:S(2)}) collective-permute-start(bf16[1024,128]{1,0:T(8,128)(2,1)S(1)} %get-tuple-element.199), channel_id=1, source_target_pairs={{0,2},{1,3},{2,0},{3,1},{4,6},{5,7},{6,4},{7,5},{8,10},{9,11},{10,... | collective-permute-start | bytes 786440 | tf_op jit(solution)/shard_map/ppermute | solution.py:872
  8.1 20.2 %all-to-all-start = ((bf16[8,64,512]{2,1,0:T(8,128)(2,1)}), bf16[8,64,512]{2,1,0:T(8,128)(2,1)S(1)}, u32[]{:S(2)}, u32[]{:S(2)}) async-start(bf16[8,64,512]{2,1,0:T(8,128)(2,1)} %get-tuple-element.192), calls=%async_computation | async-start | bytes 1048576 | tf_op jit(solution)/shard_map/all_to_all | solution.py:928
  14.4 7.1 %collective-permute-start.2 = (bf16[128,512]{1,0:T(8,128)(2,1)}, bf16[128,512]{1,0:T(8,128)(2,1)S(1)}, u32[]{:S(2)}, u32[]{:S(2)}) collective-permute-start(bf16[128,512]{1,0:T(8,128)(2,1)} %refs_12_.3), channel_id=1, source_target_pairs={{0,2},{1,3},{2,0},{3,1},{4,6},{5,7},{6,4},{7,5},{8,10},{9,11},{10,... | collective-permute-start | bytes 393224 | tf_op jit(solution)/shard_map/ppermute | solution.py:872
  15.9 5.6 %collective-permute-start.1 = (bf16[8,128]{1,0:T(8,128)(2,1)S(1)}, bf16[8,128]{1,0:T(8,128)(2,1)S(1)}, u32[]{:S(2)}, u32[]{:S(2)}) collective-permute-start(bf16[8,128]{1,0:T(8,128)(2,1)S(1)} %pad_maximum_fusion.refs_4_.refs_2_.refs_8_), channel_id=1, source_target_pairs={{0,2},{1,3},{2,0},{3,1},{4,6},{5,7},{6,4},{7,5},{8,10},{9,11},{10,... | collective-permute-start | bytes 6152 | tf_op jit(solution)/shard_map/ppermute | solution.py:872
  21.5 24.7 %collective-permute-start.9 = (bf16[2,512,512]{2,1,0:T(8,128)(2,1)}, bf16[2,512,512]{2,1,0:T(8,128)(2,1)}, u32[]{:S(2)}, u32[]{:S(2)}) collective-permute-start(bf16[2,512,512]{2,1,0:T(8,128)(2,1)} %copy-done), channel_id=1, source_target_pairs={{0,2},{1,3},{2,0},{3,1},{4,6},{5,7},{6,4},{7,5},{8,10},{9,11},{10,... | collective-permute-start | bytes 3145736 | tf_op jit(solution)/shard_map/ppermute | solution.py:872
  26.2 4.1 %collective-permute-start.3 = (bf16[256,512]{1,0:T(8,128)(2,1)}, bf16[256,512]{1,0:T(8,128)(2,1)}, u32[]{:S(2)}, u32[]{:S(2)}) collective-permute-start(bf16[256,512]{1,0:T(8,128)(2,1)} %get-tuple-element.190.refs_1_), channel_id=1, source_target_pairs={{0,1},{1,0},{2,3},{3,2},{4,5},{5,4},{6,7},{7,6},{8,9},{9,8},{10,11... | collective-permute-start | bytes 786440 | tf_op jit(solution)/shard_map/ppermute | solution.py:875
  26.3 4.0 %collective-permute-start.4 = (bf16[256,512]{1,0:T(8,128)(2,1)}, bf16[256,512]{1,0:T(8,128)(2,1)}, u32[]{:S(2)}, u32[]{:S(2)}) collective-permute-start(bf16[256,512]{1,0:T(8,128)(2,1)} %get-tuple-element.191.refs_2_), channel_id=1, source_target_pairs={{0,1},{1,0},{2,3},{3,2},{4,5},{5,4},{6,7},{7,6},{8,9},{9,8},{10,11... | collective-permute-start | bytes 786440 | tf_op jit(solution)/shard_map/ppermute | solution.py:875
  26.8 8.3 %collective-permute-start.6 = (bf16[1024,128]{1,0:T(8,128)(2,1)S(1)}, bf16[1024,128]{1,0:T(8,128)(2,1)S(1)}, u32[]{:S(2)}, u32[]{:S(2)}) collective-permute-start(bf16[1024,128]{1,0:T(8,128)(2,1)S(1)} %collective-permute-done.5.refs_0_), channel_id=1, source_target_pairs={{0,4},{4,0},{8,12},{12,8},{16,20},{20,16},{24,28},{28,24},{1,5},{5... | collective-permute-start | bytes 786440 | tf_op jit(solution)/shard_map/ppermute | solution.py:878
  38.6 1.6 %collective-permute-start.7 = (bf16[256,512]{1,0:T(8,128)(2,1)S(1)}, bf16[256,512]{1,0:T(8,128)(2,1)S(1)}, u32[]{:S(2)}, u32[]{:S(2)}) collective-permute-start(bf16[256,512]{1,0:T(8,128)(2,1)S(1)} %get-tuple-element.207.refs_1_), channel_id=1, source_target_pairs={{0,1},{1,0},{2,3},{3,2},{4,5},{5,4},{6,7},{7,6},{8,9},{9,8},{10,11... | collective-permute-start | bytes 786440 | tf_op jit(solution)/shard_map/ppermute | solution.py:875
  38.7 1.9 %collective-permute-start.8 = (bf16[256,512]{1,0:T(8,128)(2,1)S(1)}, bf16[256,512]{1,0:T(8,128)(2,1)S(1)}, u32[]{:S(2)}, u32[]{:S(2)}) collective-permute-start(bf16[256,512]{1,0:T(8,128)(2,1)S(1)} %get-tuple-element.208.refs_2_), channel_id=1, source_target_pairs={{0,1},{1,0},{2,3},{3,2},{4,5},{5,4},{6,7},{7,6},{8,9},{9,8},{10,11... | collective-permute-start | bytes 786440 | tf_op jit(solution)/shard_map/ppermute | solution.py:875
  49.6 5.1 %collective-permute-start.10 = (bf16[256,512]{1,0:T(8,128)(2,1)S(1)}, bf16[256,512]{1,0:T(8,128)(2,1)S(1)}, u32[]{:S(2)}, u32[]{:S(2)}) collective-permute-start(bf16[256,512]{1,0:T(8,128)(2,1)S(1)} %get-tuple-element.219.refs_1_), channel_id=1, source_target_pairs={{0,1},{1,0},{2,3},{3,2},{4,5},{5,4},{6,7},{7,6},{8,9},{9,8},{10,11... | collective-permute-start | bytes 786440 | tf_op jit(solution)/shard_map/ppermute | solution.py:875
  51.6 14.4 %collective-permute-start.14 = (bf16[1,512,512]{2,1,0:T(8,128)(2,1)S(1)}, bf16[1,512,512]{2,1,0:T(8,128)(2,1)S(1)}, u32[]{:S(2)}, u32[]{:S(2)}) collective-permute-start(bf16[1,512,512]{2,1,0:T(8,128)(2,1)S(1)} %get-tuple-element.240), channel_id=1, source_target_pairs={{0,2},{1,3},{2,0},{3,1},{4,6},{5,7},{6,4},{7,5},{8,10},{9,11},{10,... | collective-permute-start | bytes 1572872 | tf_op jit(solution)/shard_map/ppermute | solution.py:872
  53.0 2.2 %collective-permute-start.11 = (bf16[256,512]{1,0:T(8,128)(2,1)S(1)}, bf16[256,512]{1,0:T(8,128)(2,1)S(1)}, u32[]{:S(2)}, u32[]{:S(2)}) collective-permute-start(bf16[256,512]{1,0:T(8,128)(2,1)S(1)} %get-tuple-element.220.refs_2_), channel_id=1, source_target_pairs={{0,1},{1,0},{2,3},{3,2},{4,5},{5,4},{6,7},{7,6},{8,9},{9,8},{10,11... | collective-permute-start | bytes 786440 | tf_op jit(solution)/shard_map/ppermute | solution.py:875
  53.3 14.1 %collective-permute-start.15 = (bf16[2,256,512]{2,1,0:T(8,128)(2,1)S(1)}, bf16[2,256,512]{2,1,0:T(8,128)(2,1)S(1)}, u32[]{:S(2)}, u32[]{:S(2)}) collective-permute-start(bf16[2,256,512]{2,1,0:T(8,128)(2,1)S(1)} %get-tuple-element.242), channel_id=1, source_target_pairs={{0,4},{4,0},{8,12},{12,8},{16,20},{20,16},{24,28},{28,24},{1,5},{5... | collective-permute-start | bytes 1572872 | tf_op jit(solution)/shard_map/ppermute | solution.py:878
  54.8 6.6 %collective-permute-start.16 = (bf16[256,512]{1,0:T(8,128)(2,1)S(1)}, bf16[256,512]{1,0:T(8,128)(2,1)S(1)}, u32[]{:S(2)}, u32[]{:S(2)}) collective-permute-start(bf16[256,512]{1,0:T(8,128)(2,1)S(1)} %get-tuple-element.252.refs_14_), channel_id=1, source_target_pairs={{0,1},{1,0},{2,3},{3,2},{4,5},{5,4},{6,7},{7,6},{8,9},{9,8},{10,11... | collective-permute-start | bytes 786440 | tf_op jit(solution)/shard_map/ppermute | solution.py:875
  54.8 7.0 %collective-permute-start.17 = (bf16[256,512]{1,0:T(8,128)(2,1)S(1)}, bf16[256,512]{1,0:T(8,128)(2,1)S(1)}, u32[]{:S(2)}, u32[]{:S(2)}) collective-permute-start(bf16[256,512]{1,0:T(8,128)(2,1)S(1)} %get-tuple-element.253.refs_15_), channel_id=1, source_target_pairs={{0,1},{1,0},{2,3},{3,2},{4,5},{5,4},{6,7},{7,6},{8,9},{9,8},{10,11... | collective-permute-start | bytes 786440 | tf_op jit(solution)/shard_map/ppermute | solution.py:875
  61.2 8.5 %collective-permute-start.12 = (bf16[256,512]{1,0:T(8,128)(2,1)S(1)}, bf16[256,512]{1,0:T(8,128)(2,1)S(1)}, u32[]{:S(2)}, u32[]{:S(2)}) collective-permute-start(bf16[256,512]{1,0:T(8,128)(2,1)S(1)} %get-tuple-element.231.refs_1_), channel_id=1, source_target_pairs={{0,1},{1,0},{2,3},{3,2},{4,5},{5,4},{6,7},{7,6},{8,9},{9,8},{10,11... | collective-permute-start | bytes 786440 | tf_op jit(solution)/shard_map/ppermute | solution.py:875
  61.3 8.9 %collective-permute-start.13 = (bf16[256,512]{1,0:T(8,128)(2,1)S(1)}, bf16[256,512]{1,0:T(8,128)(2,1)S(1)}, u32[]{:S(2)}, u32[]{:S(2)}) collective-permute-start(bf16[256,512]{1,0:T(8,128)(2,1)S(1)} %get-tuple-element.232.refs_2_), channel_id=1, source_target_pairs={{0,1},{1,0},{2,3},{3,2},{4,5},{5,4},{6,7},{7,6},{8,9},{9,8},{10,11... | collective-permute-start | bytes 786440 | tf_op jit(solution)/shard_map/ppermute | solution.py:875
  64.8 10.1 %collective-permute-start.20 = (bf16[256,512]{1,0:T(8,128)(2,1)S(1)}, bf16[256,512]{1,0:T(8,128)(2,1)S(1)}, u32[]{:S(2)}, u32[]{:S(2)}) collective-permute-start(bf16[256,512]{1,0:T(8,128)(2,1)S(1)} %get-tuple-element.270.refs_4_), channel_id=1, source_target_pairs={{0,1},{1,0},{2,3},{3,2},{4,5},{5,4},{6,7},{7,6},{8,9},{9,8},{10,11... | collective-permute-start | bytes 786440 | tf_op jit(solution)/shard_map/ppermute | solution.py:875
  66.0 9.0 %collective-permute-start.21 = (bf16[256,512]{1,0:T(8,128)(2,1)S(1)}, bf16[256,512]{1,0:T(8,128)(2,1)S(1)}, u32[]{:S(2)}, u32[]{:S(2)}) collective-permute-start(bf16[256,512]{1,0:T(8,128)(2,1)S(1)} %get-tuple-element.271.refs_5_), channel_id=1, source_target_pairs={{0,1},{1,0},{2,3},{3,2},{4,5},{5,4},{6,7},{7,6},{8,9},{9,8},{10,11... | collective-permute-start | bytes 786440 | tf_op jit(solution)/shard_map/ppermute | solution.py:875
  68.1 9.3 %collective-permute-start.18 = (bf16[1,256,512]{2,1,0:T(8,128)(2,1)S(1)}, bf16[1,256,512]{2,1,0:T(8,128)(2,1)S(1)}, u32[]{:S(2)}, u32[]{:S(2)}) collective-permute-start(bf16[1,256,512]{2,1,0:T(8,128)(2,1)S(1)} %get-tuple-element.268), channel_id=1, source_target_pairs={{0,4},{4,0},{8,12},{12,8},{16,20},{20,16},{24,28},{28,24},{1,5},{5... | collective-permute-start | bytes 786440 | tf_op jit(solution)/shard_map/ppermute | solution.py:878
  69.7 7.7 %collective-permute-start.19 = (bf16[1,256,512]{2,1,0:T(8,128)(2,1)S(1)}, bf16[1,256,512]{2,1,0:T(8,128)(2,1)S(1)}, u32[]{:S(2)}, u32[]{:S(2)}) collective-permute-start(bf16[1,256,512]{2,1,0:T(8,128)(2,1)S(1)} %get-tuple-element.269), channel_id=1, source_target_pairs={{0,2},{1,3},{2,0},{3,1},{4,6},{5,7},{6,4},{7,5},{8,10},{9,11},{10,... | collective-permute-start | bytes 786440 | tf_op jit(solution)/shard_map/ppermute | solution.py:872
  70.2 17.6 %collective-permute-start.25 = (bf16[2,256,512]{2,1,0:T(8,128)(2,1)S(1)}, bf16[2,256,512]{2,1,0:T(8,128)(2,1)S(1)}, u32[]{:S(2)}, u32[]{:S(2)}) collective-permute-start(bf16[2,256,512]{2,1,0:T(8,128)(2,1)S(1)} %get-tuple-element.288), channel_id=1, source_target_pairs={{0,4},{4,0},{8,12},{12,8},{16,20},{20,16},{24,28},{28,24},{1,5},{5... | collective-permute-start | bytes 1572872 | tf_op jit(solution)/shard_map/ppermute | solution.py:878
  78.1 9.1 %collective-permute-start.26 = (bf16[2,192,512]{2,1,0:T(8,128)(2,1)S(1)}, bf16[2,192,512]{2,1,0:T(8,128)(2,1)S(1)}, u32[]{:S(2)}, u32[]{:S(2)}) collective-permute-start(bf16[2,192,512]{2,1,0:T(8,128)(2,1)S(1)} %get-tuple-element.290), channel_id=1, source_target_pairs={{0,8},{4,12},{8,0},{12,4},{16,24},{20,28},{24,16},{28,20},{1,9},{5... | collective-permute-start | bytes 1179656 | tf_op jit(solution)/shard_map/ppermute | solution.py:878
  79.8 11.5 %collective-permute-start.24 = (bf16[1,512,512]{2,1,0:T(8,128)(2,1)S(1)}, bf16[1,512,512]{2,1,0:T(8,128)(2,1)S(1)}, u32[]{:S(2)}, u32[]{:S(2)}) collective-permute-start(bf16[1,512,512]{2,1,0:T(8,128)(2,1)S(1)} %get-tuple-element.286), channel_id=1, source_target_pairs={{0,2},{1,3},{2,0},{3,1},{4,6},{5,7},{6,4},{7,5},{8,10},{9,11},{10,... | collective-permute-start | bytes 1572872 | tf_op jit(solution)/shard_map/ppermute | solution.py:872
  84.5 10.0 %collective-permute-start.22 = (bf16[256,512]{1,0:T(8,128)(2,1)S(1)}, bf16[256,512]{1,0:T(8,128)(2,1)S(1)}, u32[]{:S(2)}, u32[]{:S(2)}) collective-permute-start(bf16[256,512]{1,0:T(8,128)(2,1)S(1)} %get-tuple-element.274.refs_1_), channel_id=1, source_target_pairs={{0,1},{1,0},{2,3},{3,2},{4,5},{5,4},{6,7},{7,6},{8,9},{9,8},{10,11... | collective-permute-start | bytes 786440 | tf_op jit(solution)/shard_map/ppermute | solution.py:875
  84.6 10.9 %collective-permute-start.23 = (bf16[256,512]{1,0:T(8,128)(2,1)S(1)}, bf16[256,512]{1,0:T(8,128)(2,1)S(1)}, u32[]{:S(2)}, u32[]{:S(2)}) collective-permute-start(bf16[256,512]{1,0:T(8,128)(2,1)S(1)} %get-tuple-element.275.refs_2_), channel_id=1, source_target_pairs={{0,1},{1,0},{2,3},{3,2},{4,5},{5,4},{6,7},{7,6},{8,9},{9,8},{10,11... | collective-permute-start | bytes 786440 | tf_op jit(solution)/shard_map/ppermute | solution.py:875
  88.5 10.0 %collective-permute-start.28 = (bf16[2,128,512]{2,1,0:T(8,128)(2,1)S(1)}, bf16[2,128,512]{2,1,0:T(8,128)(2,1)S(1)}, u32[]{:S(2)}, u32[]{:S(2)}) collective-permute-start(bf16[2,128,512]{2,1,0:T(8,128)(2,1)S(1)} %get-tuple-element.300), channel_id=1, source_target_pairs={{0,8},{4,12},{8,0},{12,4},{16,24},{20,28},{24,16},{28,20},{1,9},{5... | collective-permute-start | bytes 786440 | tf_op jit(solution)/shard_map/ppermute | solution.py:878
  90.2 7.1 %collective-permute-start.29 = (bf16[1,128,512]{2,1,0:T(8,128)(2,1)S(1)}, bf16[1,128,512]{2,1,0:T(8,128)(2,1)S(1)}, u32[]{:S(2)}, u32[]{:S(2)}) collective-permute-start(bf16[1,128,512]{2,1,0:T(8,128)(2,1)S(1)} %get-tuple-element.303), channel_id=1, source_target_pairs={{0,4},{4,0},{8,12},{12,8},{16,20},{20,16},{24,28},{28,24},{1,5},{5... | collective-permute-start | bytes 393224 | tf_op jit(solution)/shard_map/ppermute | solution.py:878
  91.3 12.5 %collective-permute-start.31 = (bf16[2,128,512]{2,1,0:T(8,128)(2,1)S(1)}, bf16[2,128,512]{2,1,0:T(8,128)(2,1)S(1)}, u32[]{:S(2)}, u32[]{:S(2)}) collective-permute-start(bf16[2,128,512]{2,1,0:T(8,128)(2,1)S(1)} %get-tuple-element.307.refs_0_), channel_id=1, source_target_pairs={{0,16},{4,20},{8,24},{12,28},{16,0},{20,4},{24,8},{28,12},{1,17},{... | collective-permute-start | bytes 786440 | tf_op jit(solution)/shard_map/ppermute | solution.py:878
  94.6 9.8 %collective-permute-start.27 = (bf16[1,256,512]{2,1,0:T(8,128)(2,1)S(1)}, bf16[1,256,512]{2,1,0:T(8,128)(2,1)S(1)}, u32[]{:S(2)}, u32[]{:S(2)}) collective-permute-start(bf16[1,256,512]{2,1,0:T(8,128)(2,1)S(1)} %get-tuple-element.298), channel_id=1, source_target_pairs={{0,4},{4,0},{8,12},{12,8},{16,20},{20,16},{24,28},{28,24},{1,5},{5... | collective-permute-start | bytes 786440 | tf_op jit(solution)/shard_map/ppermute | solution.py:878
  99.2 6.7 %collective-permute-start.30 = (bf16[1,144,512]{2,1,0:T(8,128)(2,1)S(1)}, bf16[1,144,512]{2,1,0:T(8,128)(2,1)S(1)}, u32[]{:S(2)}, u32[]{:S(2)}) collective-permute-start(bf16[1,144,512]{2,1,0:T(8,128)(2,1)S(1)} %get-tuple-element.306), channel_id=1, source_target_pairs={{0,2},{1,3},{2,0},{3,1},{4,6},{5,7},{6,4},{7,5},{8,10},{9,11},{10,... | collective-permute-start | bytes 442376 | tf_op jit(solution)/shard_map/ppermute | solution.py:872
  106.5 31.8 %collective-permute-start.32 = (bf16[1024,512]{1,0:T(8,128)(2,1)S(1)}, bf16[1024,512]{1,0:T(8,128)(2,1)S(1)}, u32[]{:S(2)}, u32[]{:S(2)}) collective-permute-start(bf16[1024,512]{1,0:T(8,128)(2,1)S(1)} %get-tuple-element.311.refs_0_), channel_id=1, source_target_pairs={{0,2},{1,3},{2,0},{3,1},{4,6},{5,7},{6,4},{7,5},{8,10},{9,11},{10,... | collective-permute-start | bytes 3145736 | tf_op jit(solution)/shard_map/ppermute | solution.py:872
  108.0 6.4 %collective-permute-start.34 = (bf16[2,128,512]{2,1,0:T(8,128)(2,1)S(1)}, bf16[2,128,512]{2,1,0:T(8,128)(2,1)S(1)}, u32[]{:S(2)}, u32[]{:S(2)}) collective-permute-start(bf16[2,128,512]{2,1,0:T(8,128)(2,1)S(1)} %get-tuple-element.315.refs_4_), channel_id=1, source_target_pairs={{0,8},{4,12},{8,0},{12,4},{16,24},{20,28},{24,16},{28,20},{1,9},{5... | collective-permute-start | bytes 786440 | tf_op jit(solution)/shard_map/ppermute | solution.py:878
  108.2 10.5 %collective-permute-start.33 = (bf16[1,128,512]{2,1,0:T(8,128)(2,1)S(1)}, bf16[1,128,512]{2,1,0:T(8,128)(2,1)S(1)}, u32[]{:S(2)}, u32[]{:S(2)}) collective-permute-start(bf16[1,128,512]{2,1,0:T(8,128)(2,1)S(1)} %get-tuple-element.313), channel_id=1, source_target_pairs={{0,8},{4,12},{8,0},{12,4},{16,24},{20,28},{24,16},{28,20},{1,9},{5... | collective-permute-start | bytes 393224 | tf_op jit(solution)/shard_map/ppermute | solution.py:878
  110.0 8.7 %collective-permute-start.35 = (bf16[1,128,512]{2,1,0:T(8,128)(2,1)S(1)}, bf16[1,128,512]{2,1,0:T(8,128)(2,1)S(1)}, u32[]{:S(2)}, u32[]{:S(2)}) collective-permute-start(bf16[1,128,512]{2,1,0:T(8,128)(2,1)S(1)} %get-tuple-element.310.refs_6_), channel_id=1, source_target_pairs={{0,16},{4,20},{8,24},{12,28},{16,0},{20,4},{24,8},{28,12},{1,17},{... | collective-permute-start | bytes 393224 | tf_op jit(solution)/shard_map/ppermute | solution.py:878
  119.4 6.8 %collective-permute-start.36 = (bf16[1,144,512]{2,1,0:T(8,128)(2,1)S(1)}, bf16[1,144,512]{2,1,0:T(8,128)(2,1)S(1)}, u32[]{:S(2)}, u32[]{:S(2)}) collective-permute-start(bf16[1,144,512]{2,1,0:T(8,128)(2,1)S(1)} %get-tuple-element.317.refs_0_), channel_id=1, source_target_pairs={{0,16},{4,20},{8,24},{12,28},{16,0},{20,4},{24,8},{28,12},{1,17},{... | collective-permute-start | bytes 442376 | tf_op jit(solution)/shard_map/ppermute | solution.py:878
  119.5 6.3 %collective-permute-start.37 = (bf16[1,128,512]{2,1,0:T(8,128)(2,1)S(1)}, bf16[1,128,512]{2,1,0:T(8,128)(2,1)S(1)}, u32[]{:S(2)}, u32[]{:S(2)}) collective-permute-start(bf16[1,128,512]{2,1,0:T(8,128)(2,1)S(1)} %get-tuple-element.318.refs_2_), channel_id=1, source_target_pairs={{0,4},{4,0},{8,12},{12,8},{16,20},{20,16},{24,28},{28,24},{1,5},{5... | collective-permute-start | bytes 393224 | tf_op jit(solution)/shard_map/ppermute | solution.py:878
  122.1 18.4 %collective-permute-start.42 = (bf16[2,256,512]{2,1,0:T(8,128)(2,1)S(1)}, bf16[2,256,512]{2,1,0:T(8,128)(2,1)S(1)}, u32[]{:S(2)}, u32[]{:S(2)}) collective-permute-start(bf16[2,256,512]{2,1,0:T(8,128)(2,1)S(1)} %get-tuple-element.330.refs_0_), channel_id=1, source_target_pairs={{0,4},{4,0},{8,12},{12,8},{16,20},{20,16},{24,28},{28,24},{1,5},{5... | collective-permute-start | bytes 1572872 | tf_op jit(solution)/shard_map/ppermute | solution.py:878
  126.8 7.4 %collective-permute-start.38 = (bf16[1,144,512]{2,1,0:T(8,128)(2,1)S(1)}, bf16[1,144,512]{2,1,0:T(8,128)(2,1)S(1)}, u32[]{:S(2)}, u32[]{:S(2)}) collective-permute-start(bf16[1,144,512]{2,1,0:T(8,128)(2,1)S(1)} %get-tuple-element.320.refs_0_), channel_id=1, source_target_pairs={{0,8},{4,12},{8,0},{12,4},{16,24},{20,28},{24,16},{28,20},{1,9},{5... | collective-permute-start | bytes 442376 | tf_op jit(solution)/shard_map/ppermute | solution.py:878
  129.2 5.0 %collective-permute-start.39 = (bf16[1,128,512]{2,1,0:T(8,128)(2,1)S(1)}, bf16[1,128,512]{2,1,0:T(8,128)(2,1)S(1)}, u32[]{:S(2)}, u32[]{:S(2)}) collective-permute-start(bf16[1,128,512]{2,1,0:T(8,128)(2,1)S(1)} %get-tuple-element.322), channel_id=1, source_target_pairs={{0,2},{1,3},{2,0},{3,1},{4,6},{5,7},{6,4},{7,5},{8,10},{9,11},{10,... | collective-permute-start | bytes 393224 | tf_op jit(solution)/shard_map/ppermute | solution.py:872
  129.7 13.2 %collective-permute-start.41 = (bf16[1,288,512]{2,1,0:T(8,128)(2,1)S(1)}, bf16[1,288,512]{2,1,0:T(8,128)(2,1)S(1)}, u32[]{:S(2)}, u32[]{:S(2)}) collective-permute-start(bf16[1,288,512]{2,1,0:T(8,128)(2,1)S(1)} %get-tuple-element.329.refs_0_), channel_id=1, source_target_pairs={{0,8},{4,12},{8,0},{12,4},{16,24},{20,28},{24,16},{28,20},{1,9},{5... | collective-permute-start | bytes 884744 | tf_op jit(solution)/shard_map/ppermute | solution.py:878
  134.8 11.3 %collective-permute-start.43 = (bf16[1,272,512]{2,1,0:T(8,128)(2,1)S(1)}, bf16[1,272,512]{2,1,0:T(8,128)(2,1)S(1)}, u32[]{:S(2)}, u32[]{:S(2)}) collective-permute-start(bf16[1,272,512]{2,1,0:T(8,128)(2,1)S(1)} %get-tuple-element.335.refs_0_), channel_id=1, source_target_pairs={{0,4},{4,0},{8,12},{12,8},{16,20},{20,16},{24,28},{28,24},{1,5},{5... | collective-permute-start | bytes 835592 | tf_op jit(solution)/shard_map/ppermute | solution.py:878
  137.5 7.2 %collective-permute-start.40 = (bf16[1,128,512]{2,1,0:T(8,128)(2,1)S(1)}, bf16[1,128,512]{2,1,0:T(8,128)(2,1)S(1)}, u32[]{:S(2)}, u32[]{:S(2)}) collective-permute-start(bf16[1,128,512]{2,1,0:T(8,128)(2,1)S(1)} %get-tuple-element.328), channel_id=1, source_target_pairs={{0,16},{4,20},{8,24},{12,28},{16,0},{20,4},{24,8},{28,12},{1,17},{... | collective-permute-start | bytes 393224 | tf_op jit(solution)/shard_map/ppermute | solution.py:878
  (1 other events, 1.0 us)

commit v4 on v3

--- a/solution.py
+++ b/solution.py
@@ -207,7 +207,7 @@
 def setup_kernel(packing, flow, where, *refs):
     group_tokens, bucket_group, lengths, inputs, cotangent, memory, segments, gains, shifts, biases, refs = *refs[:10], refs[10:]
     if packing:
-        query, kv, out, w_in, w_out, cross, ffn, refs = *refs[:7], refs[7:]
+        query, kv, out, w_in, w_out, cross, ffn, own_kv, refs = *refs[:8], refs[8:]
     x, cot, memory_part, vectors, molecules, tokens_now, group_now, lengths_now, word_sems, sems = refs
     words = start_all([(group_tokens, tokens_now), (bucket_group, group_now), (lengths, lengths_now)], word_sems)
     moves = [(memory.at[:, where[0]], memory_part), (inputs.at[where[0]], x), (cotangent.at[where[0]], cot)]
@@ -224,7 +224,7 @@
         for k in range(count):
             lanes = pl.ds(pl.multiple_of((where[3] * count + k) * wide, wide), wide)
             moves.append((out.at[:, lanes], cross.at[3 * half + k * size : 3 * half + (k + 1) * size, :]))
-        moves += [(w_in, ffn.at[0]), (w_out, ffn.at[1])]
+        moves += [(w_in, ffn.at[0]), (w_out, ffn.at[1]), (kv, own_kv)]
     copies = start_all(moves, sems)
     for copy in words:
         copy.wait()
@@ -796,14 +796,14 @@
                 target[i : i + 1, :] = small[9:10, at : at + wide]
         rest[2][...] = small[10:11]
     flow.send(gains, shifts, biases, *rest)
-    value = joined(where, bit, near, got, 0, SMALL)
+    value = joined_inside(where, bit, near, got, 0, SMALL)
     size = out.shape[0]
     for k in range(3):
         qkv[k] = value[k * size : (k + 1) * size].T
     out[...] = value[3 * size :]
 
 
-def joined_inside(where, bit, near, got, p, pad):
+def joined_inside(where, bit, near, got, p, pad=0):
     half = (near.shape[1] - pad) // 2
     first, parts = where[3 + bit] == 0, []
     for k in (0, 1):
@@ -813,7 +813,7 @@
 
 
 def cross_grads_kernel(bit, flow, where, near, got, query, kv, out):
-    value = joined_inside(where, bit, near, got, 0, 2 * SMALL)
+    value = joined(where, bit, near, got, 0, 2 * SMALL)
     size = out.shape[0]
     query[...] = value[:size].T
     for k in (0, 1):
@@ -822,9 +822,9 @@
 
 
 def ffn_grads_kernel(bit, flow, where, near, got, grad_in, grad_out):
-    grad_out[...] = joined(where, bit, near, got, 0)
+    grad_out[...] = joined_inside(where, bit, near, got, 0)
     flow.send(grad_out)
-    grad_in[...] = joined(where, bit, near, got, 1).T
+    grad_in[...] = joined_inside(where, bit, near, got, 1).T
 
 
 def place_rows_kernel(flow, where, own, got, mixed, grad):
@@ -913,13 +913,14 @@
     outs = [whole, whole, ((dp,) + memory.shape[1:], BF16), ((VECTORS, width), F32), ((2, seq), jnp.int32)]
     if packing:
         ins += [Raw(v) for v in (cross_q, cross_kv, cross_out, ffn_in, ffn_out)]
-        outs = [((3 * width // 2 + cross_out.size // head // 2, head), BF16), ((2,) + ffn_in.shape, BF16)] + outs
+        packs = [((3 * width // 2 + cross_out.size // head // 2, head), BF16), ((2,) + ffn_in.shape, BF16)]
+        outs = packs + [(cross_kv.shape, BF16)] + outs
     *packed, x, cot, memory_part, vectors, molecules = run(
         functools.partial(setup_kernel, packing),
         ins,
         outs,
         scratch=[pltpu.SMEM(v.shape, jnp.int32) for v in (group_tokens, bucket_group, mem_lengths)]
-        + [pltpu.SemaphoreType.DMA((3,)), pltpu.SemaphoreType.DMA((8 + width // head // 2,))],
+        + [pltpu.SemaphoreType.DMA((3,)), pltpu.SemaphoreType.DMA((9 + width // head // 2,))],
         name="setup",
     )
     if packing:
@@ -959,7 +960,8 @@
 
     heads_cross, saved_cross = [], []
     if apart:
-        w_cross_q, w_cross_kv, w_cross_out = [far(cross_q)], [far(cross_kv)], [far(cross_out)]
+        w_cross_q, w_cross_out = [far(cross_q)], [far(cross_out)]
+        w_cross_kv = [packed[2] if packing else far(cross_kv)]
     else:
         w_cross_q = pieces(cross_q, other_cross[0], 1)
         w_cross_kv = pieces(cross_kv, other_cross[1], 2)
@@ -1125,7 +1127,7 @@
         [((2, 2 * head, width), F32), ((2, 2 * head, width), BF16)] + back + [whole],
         name="cross_weights",
     )
-    by_cross = Reduction([keep], [send], [[0], [1], ["row"]] + [[k] for k in range(2, bits)], pad=2 * SMALL, turned=True)
+    by_cross = Reduction([keep], [send], [[0], [1], ["row"]] + [[k] for k in range(2, bits)], pad=2 * SMALL)
     advance("fold_ffn", by_out, by_in)
 
     group = ((1, 4 * head, width), F32)
@@ -1137,9 +1139,10 @@
         scratch=[pltpu.VMEM((seq, wide), BF16)] + self_work,
         name="self_backward",
     )
-    by_self = Reduction([first], [send], [["row"]] + [[k] for k in range(bits)])
+    by_self = Reduction([first], [send], [["row"]] + [[k] for k in range(bits)], turned=True)
     by_ffn = by_out
     by_ffn.keeps, by_ffn.gots = by_out.keeps + by_in.keeps, by_out.gots + by_in.gots
+    by_ffn.turned = True
     by_ffn.axes = [[0]] + [[k] for k in range(1, bits)]
     mem_terms = team_parts(memory_terms)
     share = width // mp
@@ -1219,50 +1222,52 @@
         ).astype(F32)
     advance("self_cross_4", by_self, by_cross)
 
-    def cross_grads():
-        return run(
-            functools.partial(cross_grads_kernel, by_cross.halved[0]),
-            [by_cross.chunk, by_cross.got],
-            [far(((width, head), F32)), far(((2, width, head), F32)), far(((head, width), F32))],
-            name="cross_grads",
-        )
-
     more = (functools.partial(memory_send_kernel, "row", 0, 2), memory_state, sent) if along else None
     while more or not (by_self.ready() and by_cross.ready() and by_ffn.ready()):
         given = advance("rest", by_self, more=more)
         if more:
             memory_state, more = [given[0], data_swap(given[1], 2)], None
         advance("rest_cross", by_ffn, by_cross)
-    mixed, grad_inputs = run(
-        place_rows_kernel,
-        [both, got_both],
-        [far(((rows, seq, width), BF16)), far(((rows, seq, width), F32))],
-        name="place_rows",
-    )
-    grad_ffn_in, grad_ffn_out = run(
-        functools.partial(ffn_grads_kernel, by_ffn.halved[0]),
-        [by_ffn.chunk, by_ffn.got],
-        [far(((width, unit), F32)), far(((unit, width), F32))],
-        name="ffn_grads",
-    )
-    grad_cross_q, grad_cross_kv, grad_cross_out = cross_grads()
+    (mixed, grad_inputs), (grad_ffn_in, grad_ffn_out) = run.batch(
+        [
+            (
+                place_rows_kernel,
+                [both, got_both],
+                [far(((rows, seq, width), BF16)), far(((rows, seq, width), F32))],
+            ),
+            (
+                functools.partial(ffn_grads_kernel, by_ffn.halved[0]),
+                [by_ffn.chunk, by_ffn.got],
+                [far(((width, unit), F32)), far(((unit, width), F32))],
+            ),
+        ],
+        name="rows_and_ffn_grads",
+    )
+    grad_cross_q, grad_cross_kv, grad_cross_out = run(
+        functools.partial(cross_grads_kernel, by_cross.halved[0]),
+        [by_cross.chunk, by_cross.got],
+        [far(((width, head), F32)), far(((2, width, head), F32)), far(((head, width), F32))],
+        name="cross_grads",
+    )
+    parts = []
     if along:
-        (grad_memory,) = run(
-            functools.partial(memory_end_kernel, 2, 0),
-            memory_state,
-            [far(((16, mem_len // dp, share), F32))],
-            name="memory_end",
-        )
+        end = functools.partial(memory_end_kernel, 2, 0)
+        parts = [(end, memory_state, [far(((16, mem_len // dp, share), F32))])]
     if fits:
         outs = [((2, head), F32), ((2, head), F32), ((1, unit), F32)]
     else:
         outs = [((lines, width), F32)]
-    grad_self_qkv, grad_self_out, grad_gain, grad_shift, grad_out_bias, *rest = run(
-        functools.partial(self_grads_kernel, by_self.halved[0]),
-        [by_self.chunk, by_self.got],
-        [far(((3, width, head), F32)), far(((head, width), F32))] + [far(((3, width), F32))] * 3 + [far(v) for v in outs],
-        name="self_grads",
-    )
+    outs = [((3, width, head), F32), ((head, width), F32)] + [((3, width), F32)] * 3 + outs
+    parts.append(
+        (
+            functools.partial(self_grads_kernel, by_self.halved[0]),
+            [by_self.chunk, by_self.got],
+            [far(v) for v in outs],
+        )
+    )
+    *got, (grad_self_qkv, grad_self_out, grad_gain, grad_shift, grad_out_bias, *rest) = run.batch(parts, name="last_grads")
+    if along:
+        grad_memory = got[0][0]
     if fits:
         grad_self_bias, grad_cross_bias, grad_ffn_bias = rest[0], rest[1], rest[2].reshape(-1)
     else:

time: 149 us -> 146 us (0.980)
  Pallas kernels: 63 us -> 59 us
  starting transfers between devices: 47.5 us -> 51.1 us
  waiting for transfers between devices: 35.3 us -> 33.1 us
    pallas_call x31 -> x29, Pallas kernels: 63 us -> 59 us  [__call__(): pl.pallas_call(body, in_specs=[words] + specs + after_specs, out_specs=[f...]
    ppermute x19, starting transfers between devices: 25 us -> 28.1 us  [data_swap(): return lax.ppermute(value, 'dp', [(i, i ^ 1 << k) for i in range(dp)])]
    ppermute x11, waiting for transfers between devices: 10.6 us -> 8.58 us  [other(): return lax.ppermute(value, 'mp', across)]
  transfers between devices with their start and end apart: 45 -> 45, of which waited for: 20 -> 19; matrix products, arithmetic and copies ran while one was open for 0% -> 0% of each run, Pallas kernels for 39% -> 36%
where the time goes in v4:
time: 146 us
  Pallas kernels  59 us (40%)
  starting transfers between devices  51.1 us (35%)
  waiting for transfers between devices  33.1 us (23%)
    pallas_call x29, Pallas kernels, __call__(): pl.pallas_call(body, in_specs=[words] + specs + after_specs, out_specs=[f...  59 us
    ppermute x19, starting transfers between devices, data_swap(): return lax.ppermute(value, 'dp', [(i, i ^ 1 << k) for i in range(dp)])  28.1 us
    ppermute x19, waiting for transfers between devices, data_swap(): return lax.ppermute(value, 'dp', [(i, i ^ 1 << k) for i in range(dp)])  22.9 us
    ppermute x11, starting transfers between devices, other(): return lax.ppermute(value, 'mp', across)  13.5 us
    ppermute x11, waiting for transfers between devices, other(): return lax.ppermute(value, 'mp', across)  8.58 us
    all_to_all x1, starting transfers between devices, shards(): lax.all_to_all(memory_part, 'dp', split_axis=0, concat_axis=0, tiled=True)  6.27 us
    ppermute x14, starting transfers between devices, seat_swap(): return lax.ppermute(value, 'mp', [(i, i ^ step) for i in range(mp)])  3.23 us
  transfers between devices with their start and end apart: 45, of which 19 were waited for; matrix products, arithmetic and copies ran while one was open for 0% of the time, Pallas kernels for 36%

profile of v4, /device:TPU:0, one launch (start us, length us, event | category | flops | bytes accessed | tf_op | source)
XLA Modules:
  0.0 145.6 jit_solution(12429335514791272862)
XLA Ops:
  0.6 3.0 %collective-permute-start = (bf16[3,512,128]{2,1,0:T(8,128)(2,1)}, bf16[3,512,128]{2,1,0:T(8,128)(2,1)S(1)}, u32[]{:S(2)}, u32[]{:S(2)}) collective-permute-start(bf16[3,512,128]{2,1,0:T(8,128)(2,1)} %refs_0_.3), channel_id=1, source_target_pairs={{0,2},{1,3},{2,0},{3,1},{4,6},{5,7},{6,4},{7,5},{8,10},{9,11},{10,... | collective-permute-start | bytes 1179656 | tf_op jit(solution)/shard_map/ppermute | solution.py:872
  3.8 3.5 %setup.1 = (bf16[1024,128]{1,0:T(8,128)(2,1)}, bf16[2,512,512]{2,1,0:T(8,128)(2,1)S(1)}, bf16[2,512,128]{2,1,0:T(8,128)(2,1)S(1)}, bf16[512,512]{1,0:T(8,128)(2,...) custom-call(s32[6]{0:T(128)S(1)} %stack.27.where_ref, ...), custom_call_target="tpu_custom_call" | custom-call | flops 1000000 | bytes 300000 | tf_op jit(solution)/shard_map/setup/pallas_call | solution.py:146
  8.3 6.3 %all-to-all-start = ((bf16[8,64,512]{2,1,0:T(8,128)(2,1)}), bf16[8,64,512]{2,1,0:T(8,128)(2,1)S(1)}, u32[]{:S(2)}, u32[]{:S(2)}) async-start(bf16[8,64,512]{2,1,0:T(8,128)(2,1)} %get-tuple-element.191), calls=%async_computation | async-start | bytes 1048576 | tf_op jit(solution)/shard_map/all_to_all | solution.py:929
  14.5 1.6 %collective-permute-start.2 = (bf16[128,512]{1,0:T(8,128)(2,1)S(1)}, bf16[128,512]{1,0:T(8,128)(2,1)S(1)}, u32[]{:S(2)}, u32[]{:S(2)}) collective-permute-start(bf16[128,512]{1,0:T(8,128)(2,1)S(1)} %copy-done.1), channel_id=1, source_target_pairs={{0,2},{1,3},{2,0},{3,1},{4,6},{5,7},{6,4},{7,5},{8,10},{9,11},{10,... | collective-permute-start | bytes 393224 | tf_op jit(solution)/shard_map/ppermute | solution.py:872
  16.7 3.1 %self_forward_0.1 = (bf16[512,512]{1,0:T(8,128)(2,1)S(1)}, bf16[512,128]{1,0:T(8,128)(2,1)}, bf16[512,128]{1,0:T(8,128)(2,1)}, bf16[512,128]{1,0:T(8,128)(2,1)},...) custom-call(s32[6]{0:T(128)S(1)} %stack.27.where_ref, ...), custom_call_target="tpu_custom_call" | custom-call | flops 1000000 | bytes 300000 | tf_op jit(solution)/shard_map/self_forward_0/pallas_call | solution.py:146
  19.8 1.7 %collective-permute-done.1.refs_4_.refs_3_.refs_5_ = bf16[8,128]{1,0:T(8,128)(2,1)S(1)} collective-permute-done((bf16[8,128]{1,0:T(8,128)(2,1)S(1)}, bf16[8,128]{1,0:T(8,128)(2,1)S(1)}, u32[]{:S(2)}, u32[]{:S(2)}) %collective-permute-start.1) | collective-permute-done | bytes 2080 | tf_op jit(solution)/shard_map/ppermute | solution.py:872
  21.5 1.8 %collective-permute-start.9 = (bf16[2,512,512]{2,1,0:T(8,128)(2,1)}, bf16[2,512,512]{2,1,0:T(8,128)(2,1)}, u32[]{:S(2)}, u32[]{:S(2)}) collective-permute-start(bf16[2,512,512]{2,1,0:T(8,128)(2,1)} %copy-done), channel_id=1, source_target_pairs={{0,2},{1,3},{2,0},{3,1},{4,6},{5,7},{6,4},{7,5},{8,10},{9,11},{10,... | collective-permute-start | bytes 3145736 | tf_op jit(solution)/shard_map/ppermute | solution.py:872
  23.3 2.9 %self_forward_1.1 = (bf16[512,128]{1,0:T(8,128)(2,1)}, bf16[512,128]{1,0:T(8,128)(2,1)}, bf16[512,128]{1,0:T(8,128)(2,1)}, bf16[512,128]{1,0:T(8,128)(2,1)S(1)},...) custom-call(s32[6]{0:T(128)S(1)} %stack.27.where_ref, ...), custom_call_target="tpu_custom_call" | custom-call | flops 1000000 | bytes 300000 | tf_op jit(solution)/shard_map/self_forward_1/pallas_call | solution.py:146
  26.8 1.5 %collective-permute-start.6 = (bf16[1024,128]{1,0:T(8,128)(2,1)S(1)}, bf16[1024,128]{1,0:T(8,128)(2,1)}, u32[]{:S(2)}, u32[]{:S(2)}) collective-permute-start(bf16[1024,128]{1,0:T(8,128)(2,1)S(1)} %collective-permute-done.5.refs_0_), channel_id=1, source_target_pairs={{0,4},{4,0},{8,12},{12,8},{16,20},{20,16},{24,28},{28,24},{1,5},{5... | collective-permute-start | bytes 786440 | tf_op jit(solution)/shard_map/ppermute | solution.py:878
  29.5 3.6 %cross_forward_0.1 = (f32[512,512]{1,0:T(8,128)S(1)}, bf16[512,512]{1,0:T(8,128)(2,1)S(1)}, bf16[512,128]{1,0:T(8,128)(2,1)S(1)}, bf16[512,128]{1,0:T(8,128)(2,1...) custom-call(s32[6]{0:T(128)S(1)} %stack.27.where_ref, bf16[512,512]{1,0:T(8,128)(2,1)S(1)} %get-tuple-element.182.refs_0_, ...), custom_call_target="tpu_custom_call" | custom-call | flops 1000000 | bytes 300000 | tf_op jit(solution)/shard_map/cross_forward_0/pallas_call | solution.py:146
  33.1 2.1 %collective-permute-done.6.refs_1_ = bf16[1024,128]{1,0:T(8,128)(2,1)} collective-permute-done((bf16[1024,128]{1,0:T(8,128)(2,1)S(1)}, bf16[1024,128]{1,0:T(8,128)(2,1)}, u32[]{:S(2)}, u32[]{:S(2)}) %collective-permute-start.6) | collective-permute-done | bytes 262176 | tf_op jit(solution)/shard_map/ppermute | solution.py:878
  35.2 1.4 memory_1.1
  36.6 2.5 %cross_forward_1.1 = (bf16[512,128]{1,0:T(8,128)(2,1)S(1)}, bf16[512,128]{1,0:T(8,128)(2,1)S(1)}, f32[2,512]{1,0:T(2,128)S(1)}, bf16[256,512]{1,0:T(8,128)(2,1)S...) custom-call(s32[6]{0:T(128)S(1)} %stack.27.where_ref, bf16[512,512]{1,0:T(8,128)(2,1)S(1)} %get-tuple-element.198.refs_0_.refs_10_, ...), custom_call_target="tpu_custom_call" | custom-call | flops 1000000 | bytes 300000 | tf_op jit(solution)/shard_map/cross_forward_1/pallas_call | solution.py:146
  41.1 4.3 %ffn_0.1 = (f32[512,512]{1,0:T(8,128)S(1)}, bf16[512,512]{1,0:T(8,128)(2,1)S(1)}, bf16[512,512]{1,0:T(8,128)(2,1)S(1)}, bf16[512,512]{1,0:T(8,128)(2,1)S(1)}, bf...) custom-call(s32[6]{0:T(128)S(1)} %stack.27.where_ref, ...), custom_call_target="tpu_custom_call" | custom-call | flops 1000000 | bytes 300000 | tf_op jit(solution)/shard_map/ffn_0/pallas_call | solution.py:146
  46.2 3.4 %ffn_1.2 = (bf16[512,512]{1,0:T(8,128)(2,1)S(1)}, bf16[512,512]{1,0:T(8,128)(2,1)S(1)}, bf16[256,512]{1,0:T(8,128)(2,1)S(1)}, bf16[256,512]{1,0:T(8,128)(2,1)S(1...) custom-call(s32[6]{0:T(128)S(1)} %stack.27.where_ref, ...), custom_call_target="tpu_custom_call" | custom-call | flops 1000000 | bytes 300000 | tf_op jit(solution)/shard_map/ffn_1/pallas_call | solution.py:146
  49.7 1.8 %ffn_weights.1 = (f32[2,512]{1,0:T(2,128)S(1)}, f32[1,512,512]{2,1,0:T(8,128)S(1)}, bf16[1,512,512]{2,1,0:T(8,128)(2,1)S(1)}, f32[2,256,512]{2,1,0:T(8,128)S(1)}...) custom-call(s32[6]{0:T(128)S(1)} %stack.27.where_ref, bf16[512,512]{1,0:T(8,128)(2,1)S(1)} %get-tuple-element.225.refs_0_, ...), custom_call_target="tpu_custom_call" | custom-call | flops 1000000 | bytes 300000 | tf_op jit(solution)/shard_map/ffn_weights/pallas_call | solution.py:146
  51.6 1.5 %collective-permute-start.14 = (bf16[1,512,512]{2,1,0:T(8,128)(2,1)S(1)}, bf16[1,512,512]{2,1,0:T(8,128)(2,1)S(1)}, u32[]{:S(2)}, u32[]{:S(2)}) collective-permute-start(bf16[1,512,512]{2,1,0:T(8,128)(2,1)S(1)} %get-tuple-element.240), channel_id=1, source_target_pairs={{0,2},{1,3},{2,0},{3,1},{4,6},{5,7},{6,4},{7,5},{8,10},{9,11},{10,... | collective-permute-start | bytes 1572872 | tf_op jit(solution)/shard_map/ppermute | solution.py:872
  53.3 1.5 %collective-permute-start.15 = (bf16[2,256,512]{2,1,0:T(8,128)(2,1)S(1)}, bf16[2,256,512]{2,1,0:T(8,128)(2,1)S(1)}, u32[]{:S(2)}, u32[]{:S(2)}) collective-permute-start(bf16[2,256,512]{2,1,0:T(8,128)(2,1)S(1)} %get-tuple-element.242), channel_id=1, source_target_pairs={{0,4},{4,0},{8,12},{12,8},{16,20},{20,16},{24,28},{28,24},{1,5},{5... | collective-permute-start | bytes 1572872 | tf_op jit(solution)/shard_map/ppermute | solution.py:878
  55.3 5.9 %cross_backward.1 = (f32[512,512]{1,0:T(8,128)S(1)}, bf16[512,512]{1,0:T(8,128)(2,1)S(1)}, bf16[512,128]{1,0:T(8,128)(2,1)S(1)}, bf16[512,128]{1,0:T(8,128)(2,1)...) custom-call(s32[6]{0:T(128)S(1)} %stack.27.where_ref, ...), custom_call_target="tpu_custom_call" | custom-call | flops 1000000 | bytes 300000 | tf_op jit(solution)/shard_map/cross_backward/pallas_call | solution.py:146
  61.8 2.0 %cross_weights.1 = (f32[2,256,512]{2,1,0:T(8,128)S(1)}, bf16[2,256,512]{2,1,0:T(8,128)(2,1)S(1)}, bf16[256,512]{1,0:T(8,128)(2,1)S(1)}, bf16[256,512]{1,0:T(8,12...) custom-call(s32[6]{0:T(128)S(1)} %stack.27.where_ref, bf16[512,128]{1,0:T(8,128)(2,1)S(1)} %get-tuple-element.243.refs_0_, ...), custom_call_target="tpu_custom_call" | custom-call | flops 1000000 | bytes 300000 | tf_op jit(solution)/shard_map/cross_weights/pallas_call | solution.py:146
  64.0 1.9 %collective-permute-done.14.refs_1_ = bf16[1,512,512]{2,1,0:T(8,128)(2,1)S(1)} collective-permute-done((bf16[1,512,512]{2,1,0:T(8,128)(2,1)S(1)}, bf16[1,512,512]{2,1,0:T(8,128)(2,1)S(1)}, u32[]{:S(2)}, u32[]{:S(2)}) %collective-permute-start.14) | collective-permute-done | bytes 524320 | tf_op jit(solution)/shard_map/ppermute | solution.py:872
  66.0 1.4 collective-permute-done.15.refs_3_
  68.1 1.6 %collective-permute-start.18 = (bf16[1,256,512]{2,1,0:T(8,128)(2,1)S(1)}, bf16[1,256,512]{2,1,0:T(8,128)(2,1)S(1)}, u32[]{:S(2)}, u32[]{:S(2)}) collective-permute-start(bf16[1,256,512]{2,1,0:T(8,128)(2,1)S(1)} %get-tuple-element.268), channel_id=1, source_target_pairs={{0,4},{4,0},{8,12},{12,8},{16,20},{20,16},{24,28},{28,24},{1,5},{5... | collective-permute-start | bytes 786440 | tf_op jit(solution)/shard_map/ppermute | solution.py:878
  70.8 4.1 %self_backward.1 = (f32[512,512]{1,0:T(8,128)S(1)}, bf16[512,512]{1,0:T(8,128)(2,1)S(1)}, bf16[512,128]{1,0:T(8,128)(2,1)S(1)}, bf16[512,128]{1,0:T(8,128)(2,1)S...) custom-call(s32[6]{0:T(128)S(1)} %stack.27.where_ref, ...), custom_call_target="tpu_custom_call" | custom-call | flops 1000000 | bytes 300000 | tf_op jit(solution)/shard_map/self_backward/pallas_call | solution.py:146
  75.0 2.5 %collective-permute-done.18.refs_2_ = bf16[1,256,512]{2,1,0:T(8,128)(2,1)S(1)} collective-permute-done((bf16[1,256,512]{2,1,0:T(8,128)(2,1)S(1)}, bf16[1,256,512]{2,1,0:T(8,128)(2,1)S(1)}, u32[]{:S(2)}, u32[]{:S(2)}) %collective-permute-start.18) | collective-permute-done | bytes 262176 | tf_op jit(solution)/shard_map/ppermute | solution.py:878
  78.1 1.6 %collective-permute-start.26 = (bf16[2,192,512]{2,1,0:T(8,128)(2,1)S(1)}, bf16[2,192,512]{2,1,0:T(8,128)(2,1)S(1)}, u32[]{:S(2)}, u32[]{:S(2)}) collective-permute-start(bf16[2,192,512]{2,1,0:T(8,128)(2,1)S(1)} %get-tuple-element.290), channel_id=1, source_target_pairs={{0,8},{4,12},{8,0},{12,4},{16,24},{20,28},{24,16},{28,20},{1,9},{5... | collective-permute-start | bytes 1179656 | tf_op jit(solution)/shard_map/ppermute | solution.py:878
  80.5 4.0 %self_backward_rest.1 = (f32[2,128]{1,0:T(2,128)S(1)}, f32[1,512,512]{2,1,0:T(8,128)S(1)}, bf16[256,512]{1,0:T(8,128)(2,1)S(1)}, bf16[256,512]{1,0:T(8,128)(2,1)S(1)}, f32[8,128]{1,0:T(8,128)}) custom-call(s32[6]{0:T(128)S(1)} %stack.27.where_ref, bf16[3,512,128]{2,1,0:T(8,128)(2,1)} %refs_0_.3, ...), custom_call_target="tpu_custom_call" | custom-call | flops 1000000 | bytes 300000 | tf_op jit(solution)/shard_map/self_backward_rest/pallas_call | solution.py:146
  85.1 2.1 %collective-permute-done.26.refs_1_.refs_3_ = bf16[2,192,512]{2,1,0:T(8,128)(2,1)S(1)} collective-permute-done((bf16[2,192,512]{2,1,0:T(8,128)(2,1)S(1)}, bf16[2,192,512]{2,1,0:T(8,128)(2,1)S(1)}, u32[]{:S(2)}, u32[]{:S(2)}) %collective-permute-start.26) | collective-permute-done | bytes 393248 | tf_op jit(solution)/shard_map/ppermute | solution.py:878
  88.5 1.6 %collective-permute-start.28 = (bf16[2,128,512]{2,1,0:T(8,128)(2,1)S(1)}, bf16[2,128,512]{2,1,0:T(8,128)(2,1)S(1)}, u32[]{:S(2)}, u32[]{:S(2)}) collective-permute-start(bf16[2,128,512]{2,1,0:T(8,128)(2,1)S(1)} %get-tuple-element.300), channel_id=1, source_target_pairs={{0,8},{4,12},{8,0},{12,4},{16,24},{20,28},{24,16},{28,20},{1,9},{5... | collective-permute-start | bytes 786440 | tf_op jit(solution)/shard_map/ppermute | solution.py:878
  91.3 2.6 %collective-permute-start.31 = (bf16[2,128,512]{2,1,0:T(8,128)(2,1)S(1)}, bf16[2,128,512]{2,1,0:T(8,128)(2,1)S(1)}, u32[]{:S(2)}, u32[]{:S(2)}) collective-permute-start(bf16[2,128,512]{2,1,0:T(8,128)(2,1)S(1)} %get-tuple-element.307.refs_0_), channel_id=1, source_target_pairs={{0,16},{4,20},{8,24},{12,28},{16,0},{20,4},{24,8},{28,12},{1,17},{... | collective-permute-start | bytes 786440 | tf_op jit(solution)/shard_map/ppermute | solution.py:878
  95.5 1.7 %input_backward.1 = (bf16[1024,512]{1,0:T(8,128)(2,1)S(1)}, bf16[16,512]{1,0:T(8,128)(2,1)S(1)}, bf16[16,512]{1,0:T(8,128)(2,1)S(1)}, f32[8,128]{1,0:T(8,128)}) custom-call(s32[6]{0:T(128)S(1)} %stack.27.where_ref, bf16[512,512]{1,0:T(8,128)(2,1)S(1)} %get-tuple-element.182.refs_0_, bf16[256,512]{1,0:T(8,128)(2,1)S(1)} %get-tuple-element.274.refs_1_, ...), custom_call_target="tpu_custom_call" | custom-call | flops 1000000 | bytes 300000 | tf_op jit(solution)/shard_map/input_backward/pallas_call | solution.py:146
  99.2 1.4 collective-permute-start.30
  100.6 3.1 %collective-permute-done.31.refs_1_ = bf16[2,128,512]{2,1,0:T(8,128)(2,1)S(1)} collective-permute-done((bf16[2,128,512]{2,1,0:T(8,128)(2,1)S(1)}, bf16[2,128,512]{2,1,0:T(8,128)(2,1)S(1)}, u32[]{:S(2)}, u32[]{:S(2)}) %collective-permute-start.31) | collective-permute-done | bytes 262176 | tf_op jit(solution)/shard_map/ppermute | solution.py:878
  104.4 1.5 %collective-permute-done.30.refs_3_ = bf16[1,144,512]{2,1,0:T(8,128)(2,1)S(1)} collective-permute-done((bf16[1,144,512]{2,1,0:T(8,128)(2,1)S(1)}, bf16[1,144,512]{2,1,0:T(8,128)(2,1)S(1)}, u32[]{:S(2)}, u32[]{:S(2)}) %collective-permute-start.30) | collective-permute-done | bytes 147488 | tf_op jit(solution)/shard_map/ppermute | solution.py:872
  106.5 1.5 %collective-permute-start.32 = (bf16[1024,512]{1,0:T(8,128)(2,1)S(1)}, bf16[1024,512]{1,0:T(8,128)(2,1)S(1)}, u32[]{:S(2)}, u32[]{:S(2)}) collective-permute-start(bf16[1024,512]{1,0:T(8,128)(2,1)S(1)} %get-tuple-element.311.refs_0_), channel_id=1, source_target_pairs={{0,2},{1,3},{2,0},{3,1},{4,6},{5,7},{6,4},{7,5},{8,10},{9,11},{10,... | collective-permute-start | bytes 3145736 | tf_op jit(solution)/shard_map/ppermute | solution.py:872
  108.0 2.6 %collective-permute-start.34 = (bf16[2,128,512]{2,1,0:T(8,128)(2,1)S(1)}, bf16[2,128,512]{2,1,0:T(8,128)(2,1)S(1)}, u32[]{:S(2)}, u32[]{:S(2)}) collective-permute-start(bf16[2,128,512]{2,1,0:T(8,128)(2,1)S(1)} %get-tuple-element.315.refs_4_), channel_id=1, source_target_pairs={{0,4},{4,0},{8,12},{12,8},{16,20},{20,16},{24,28},{28,24},{1,5},{5... | collective-permute-start | bytes 786440 | tf_op jit(solution)/shard_map/ppermute | solution.py:878
  110.6 1.9 %collective-permute-start.35 = (bf16[1,128,512]{2,1,0:T(8,128)(2,1)S(1)}, bf16[1,128,512]{2,1,0:T(8,128)(2,1)S(1)}, u32[]{:S(2)}, u32[]{:S(2)}) collective-permute-start(bf16[1,128,512]{2,1,0:T(8,128)(2,1)S(1)} %get-tuple-element.310.refs_6_), channel_id=1, source_target_pairs={{0,16},{4,20},{8,24},{12,28},{16,0},{20,4},{24,8},{28,12},{1,17},{... | collective-permute-start | bytes 393224 | tf_op jit(solution)/shard_map/ppermute | solution.py:878
  112.5 2.4 %collective-permute-done.34.refs_5_ = bf16[2,128,512]{2,1,0:T(8,128)(2,1)S(1)} collective-permute-done((bf16[2,128,512]{2,1,0:T(8,128)(2,1)S(1)}, bf16[2,128,512]{2,1,0:T(8,128)(2,1)S(1)}, u32[]{:S(2)}, u32[]{:S(2)}) %collective-permute-start.34) | collective-permute-done | bytes 262176 | tf_op jit(solution)/shard_map/ppermute | solution.py:878
  114.9 2.0 %collective-permute-done.33.refs_1_ = bf16[1,128,512]{2,1,0:T(8,128)(2,1)S(1)} collective-permute-done((bf16[1,128,512]{2,1,0:T(8,128)(2,1)S(1)}, bf16[1,128,512]{2,1,0:T(8,128)(2,1)S(1)}, u32[]{:S(2)}, u32[]{:S(2)}) %collective-permute-start.33) | collective-permute-done | bytes 131104 | tf_op jit(solution)/shard_map/ppermute | solution.py:878
  117.6 1.8 %collective-permute-start.37 = (bf16[1,144,512]{2,1,0:T(8,128)(2,1)S(1)}, bf16[1,144,512]{2,1,0:T(8,128)(2,1)S(1)}, u32[]{:S(2)}, u32[]{:S(2)}) collective-permute-start(bf16[1,144,512]{2,1,0:T(8,128)(2,1)S(1)} %get-tuple-element.318.refs_0_), channel_id=1, source_target_pairs={{0,16},{4,20},{8,24},{12,28},{16,0},{20,4},{24,8},{28,12},{1,17},{... | collective-permute-start | bytes 442376 | tf_op jit(solution)/shard_map/ppermute | solution.py:878
  121.5 5.2 %collective-permute-done.38.refs_3_ = bf16[1,128,512]{2,1,0:T(8,128)(2,1)S(1)} collective-permute-done((bf16[1,128,512]{2,1,0:T(8,128)(2,1)S(1)}, bf16[1,128,512]{2,1,0:T(8,128)(2,1)S(1)}, u32[]{:S(2)}, u32[]{:S(2)}) %collective-permute-start.38) | collective-permute-done | bytes 131104 | tf_op jit(solution)/shard_map/ppermute | solution.py:878
  127.3 1.6 %collective-permute-start.39 = (bf16[1,144,512]{2,1,0:T(8,128)(2,1)S(1)}, bf16[1,144,512]{2,1,0:T(8,128)(2,1)S(1)}, u32[]{:S(2)}, u32[]{:S(2)}) collective-permute-start(bf16[1,144,512]{2,1,0:T(8,128)(2,1)S(1)} %get-tuple-element.321.refs_0_), channel_id=1, source_target_pairs={{0,4},{4,0},{8,12},{12,8},{16,20},{20,16},{24,28},{28,24},{1,5},{5... | collective-permute-start | bytes 442376 | tf_op jit(solution)/shard_map/ppermute | solution.py:878
  129.8 1.9 %collective-permute-start.43 = (bf16[1,288,512]{2,1,0:T(8,128)(2,1)S(1)}, bf16[1,288,512]{2,1,0:T(8,128)(2,1)S(1)}, u32[]{:S(2)}, u32[]{:S(2)}) collective-permute-start(bf16[1,288,512]{2,1,0:T(8,128)(2,1)S(1)} %get-tuple-element.331.refs_0_), channel_id=1, source_target_pairs={{0,4},{4,0},{8,12},{12,8},{16,20},{20,16},{24,28},{28,24},{1,5},{5... | collective-permute-start | bytes 884744 | tf_op jit(solution)/shard_map/ppermute | solution.py:878
  131.7 2.2 %collective-permute-done.40.refs_3_ = bf16[1,128,512]{2,1,0:T(8,128)(2,1)S(1)} collective-permute-done((bf16[1,128,512]{2,1,0:T(8,128)(2,1)S(1)}, bf16[1,128,512]{2,1,0:T(8,128)(2,1)S(1)}, u32[]{:S(2)}, u32[]{:S(2)}) %collective-permute-start.40) | collective-permute-done | bytes 131104 | tf_op jit(solution)/shard_map/ppermute | solution.py:872
  135.5 2.4 %collective-permute-start.41 = (bf16[1,128,512]{2,1,0:T(8,128)(2,1)S(1)}, bf16[1,128,512]{2,1,0:T(8,128)(2,1)S(1)}, u32[]{:S(2)}, u32[]{:S(2)}) collective-permute-start(bf16[1,128,512]{2,1,0:T(8,128)(2,1)S(1)} %get-tuple-element.329), channel_id=1, source_target_pairs={{0,16},{4,20},{8,24},{12,28},{16,0},{20,4},{24,8},{28,12},{1,17},{... | collective-permute-start | bytes 393224 | tf_op jit(solution)/shard_map/ppermute | solution.py:878
  138.6 3.2 %rows_and_ffn_grads.1 = (bf16[2,512,512]{2,1,0:T(8,128)(2,1)}, f32[2,512,512]{2,1,0:T(8,128)}, f32[512,512]{1,0:T(8,128)}, f32[512,512]{1,0:T(8,128)}, f32[8,128]{1,0:T(8,128)}) custom-call(s32[6]{0:T(128)S(1)} %stack.27.where_ref, bf16[1024,512]{1,0:T(8,128)(2,1)S(1)} %get-tuple-element.311.refs_0_, bf16[1024,512]{1,0:T(8,128)(2,1)S(1)} %collective-permute-done.32.refs_1_, ...), custom_call_target="tpu_custom_call" | custom-call | flops 1000000 | bytes 300000 | tf_op jit(solution)/shard_map/rows_and_ffn_grads/pallas_call | solution.py:146
  141.8 1.6 %cross_grads.1 = (f32[512,128]{1,0:T(8,128)}, f32[2,512,128]{2,1,0:T(8,128)}, f32[128,512]{1,0:T(8,128)}, f32[8,128]{1,0:T(8,128)}) custom-call(s32[6]{0:T(128)S(1)} %stack.27.where_ref, bf16[1,288,512]{2,1,0:T(8,128)(2,1)S(1)} %get-tuple-element.331.refs_0_, bf16[1,288,512]{2,1,0:T(8,128)(2,1)S(1)} %collective-permute-done.43.refs_1_, ...), custom_call_target="tpu_custom_call" | custom-call | flops 1000000 | bytes 300000 | tf_op jit(solution)/shard_map/cross_grads/pallas_call | solution.py:146
  143.4 1.9 %last_grads.1 = (f32[16,64,128]{2,1,0:T(8,128)}, f32[3,512,128]{2,1,0:T(8,128)}, f32[128,512]{1,0:T(8,128)}, f32[3,512]{1,0:T(4,128)}, f32[3,512]{1,0:T(4,128)},...) custom-call(s32[6]{0:T(128)S(1)} %stack.27.where_ref, ...), custom_call_target="tpu_custom_call" | custom-call | flops 1000000 | bytes 300000 | tf_op jit(solution)/shard_map/last_grads/pallas_call | solution.py:146
  (83 shorter events, 25.2 us)
Async XLA Ops:
  0.6 20.8 %collective-permute-start = (bf16[3,512,128]{2,1,0:T(8,128)(2,1)}, bf16[3,512,128]{2,1,0:T(8,128)(2,1)S(1)}, u32[]{:S(2)}, u32[]{:S(2)}) collective-permute-start(bf16[3,512,128]{2,1,0:T(8,128)(2,1)} %refs_0_.3), channel_id=1, source_target_pairs={{0,2},{1,3},{2,0},{3,1},{4,6},{5,7},{6,4},{7,5},{8,10},{9,11},{10,... | collective-permute-start | bytes 1179656 | tf_op jit(solution)/shard_map/ppermute | solution.py:872
  3.8 12.4 %copy-start.2 = (bf16[512]{0:T(512)(128)(2,1)S(1)}, bf16[512]{0:T(512)(128)(2,1)}, u32[]{:S(2)}) copy-start(bf16[512]{0:T(512)(128)(2,1)} %param.36) | copy-start | bytes 3076
  3.8 12.4 %copy-start.3 = (bf16[2,128]{1,0:T(2,128)(2,1)S(1)}, bf16[2,128]{1,0:T(2,128)(2,1)}, u32[]{:S(2)}) copy-start(bf16[2,128]{1,0:T(2,128)(2,1)} %param.33) | copy-start | bytes 1540
  3.8 12.4 %copy-start.4 = (bf16[2,128]{1,0:T(2,128)(2,1)S(1)}, bf16[2,128]{1,0:T(2,128)(2,1)}, u32[]{:S(2)}) copy-start(bf16[2,128]{1,0:T(2,128)(2,1)} %param.29) | copy-start | bytes 1540
  8.2 13.3 %collective-permute-start.5 = (bf16[1024,128]{1,0:T(8,128)(2,1)}, bf16[1024,128]{1,0:T(8,128)(2,1)S(1)}, u32[]{:S(2)}, u32[]{:S(2)}) collective-permute-start(bf16[1024,128]{1,0:T(8,128)(2,1)} %get-tuple-element.199), channel_id=1, source_target_pairs={{0,2},{1,3},{2,0},{3,1},{4,6},{5,7},{6,4},{7,5},{8,10},{9,11},{10,... | collective-permute-start | bytes 786440 | tf_op jit(solution)/shard_map/ppermute | solution.py:872
  8.3 20.2 %all-to-all-start = ((bf16[8,64,512]{2,1,0:T(8,128)(2,1)}), bf16[8,64,512]{2,1,0:T(8,128)(2,1)S(1)}, u32[]{:S(2)}, u32[]{:S(2)}) async-start(bf16[8,64,512]{2,1,0:T(8,128)(2,1)} %get-tuple-element.191), calls=%async_computation | async-start | bytes 1048576 | tf_op jit(solution)/shard_map/all_to_all | solution.py:929
  14.5 6.9 %collective-permute-start.2 = (bf16[128,512]{1,0:T(8,128)(2,1)S(1)}, bf16[128,512]{1,0:T(8,128)(2,1)S(1)}, u32[]{:S(2)}, u32[]{:S(2)}) collective-permute-start(bf16[128,512]{1,0:T(8,128)(2,1)S(1)} %copy-done.1), channel_id=1, source_target_pairs={{0,2},{1,3},{2,0},{3,1},{4,6},{5,7},{6,4},{7,5},{8,10},{9,11},{10,... | collective-permute-start | bytes 393224 | tf_op jit(solution)/shard_map/ppermute | solution.py:872
  16.1 5.3 %collective-permute-start.1 = (bf16[8,128]{1,0:T(8,128)(2,1)S(1)}, bf16[8,128]{1,0:T(8,128)(2,1)S(1)}, u32[]{:S(2)}, u32[]{:S(2)}) collective-permute-start(bf16[8,128]{1,0:T(8,128)(2,1)S(1)} %pad_maximum_fusion.refs_4_.refs_2_.refs_8_), channel_id=1, source_target_pairs={{0,2},{1,3},{2,0},{3,1},{4,6},{5,7},{6,4},{7,5},{8,10},{9,11},{10,... | collective-permute-start | bytes 6152 | tf_op jit(solution)/shard_map/ppermute | solution.py:872
  21.5 24.7 %collective-permute-start.9 = (bf16[2,512,512]{2,1,0:T(8,128)(2,1)}, bf16[2,512,512]{2,1,0:T(8,128)(2,1)}, u32[]{:S(2)}, u32[]{:S(2)}) collective-permute-start(bf16[2,512,512]{2,1,0:T(8,128)(2,1)} %copy-done), channel_id=1, source_target_pairs={{0,2},{1,3},{2,0},{3,1},{4,6},{5,7},{6,4},{7,5},{8,10},{9,11},{10,... | collective-permute-start | bytes 3145736 | tf_op jit(solution)/shard_map/ppermute | solution.py:872
  26.2 3.3 %collective-permute-start.3 = (bf16[256,512]{1,0:T(8,128)(2,1)}, bf16[256,512]{1,0:T(8,128)(2,1)}, u32[]{:S(2)}, u32[]{:S(2)}) collective-permute-start(bf16[256,512]{1,0:T(8,128)(2,1)} %get-tuple-element.189.refs_1_), channel_id=1, source_target_pairs={{0,1},{1,0},{2,3},{3,2},{4,5},{5,4},{6,7},{7,6},{8,9},{9,8},{10,11... | collective-permute-start | bytes 786440 | tf_op jit(solution)/shard_map/ppermute | solution.py:875
  26.3 3.2 %collective-permute-start.4 = (bf16[256,512]{1,0:T(8,128)(2,1)}, bf16[256,512]{1,0:T(8,128)(2,1)}, u32[]{:S(2)}, u32[]{:S(2)}) collective-permute-start(bf16[256,512]{1,0:T(8,128)(2,1)} %get-tuple-element.190.refs_2_), channel_id=1, source_target_pairs={{0,1},{1,0},{2,3},{3,2},{4,5},{5,4},{6,7},{7,6},{8,9},{9,8},{10,11... | collective-permute-start | bytes 786440 | tf_op jit(solution)/shard_map/ppermute | solution.py:875
  26.8 8.4 %collective-permute-start.6 = (bf16[1024,128]{1,0:T(8,128)(2,1)S(1)}, bf16[1024,128]{1,0:T(8,128)(2,1)}, u32[]{:S(2)}, u32[]{:S(2)}) collective-permute-start(bf16[1024,128]{1,0:T(8,128)(2,1)S(1)} %collective-permute-done.5.refs_0_), channel_id=1, source_target_pairs={{0,4},{4,0},{8,12},{12,8},{16,20},{20,16},{24,28},{28,24},{1,5},{5... | collective-permute-start | bytes 786440 | tf_op jit(solution)/shard_map/ppermute | solution.py:878
  39.1 1.6 %collective-permute-start.7 = (bf16[256,512]{1,0:T(8,128)(2,1)S(1)}, bf16[256,512]{1,0:T(8,128)(2,1)S(1)}, u32[]{:S(2)}, u32[]{:S(2)}) collective-permute-start(bf16[256,512]{1,0:T(8,128)(2,1)S(1)} %get-tuple-element.207.refs_1_), channel_id=1, source_target_pairs={{0,1},{1,0},{2,3},{3,2},{4,5},{5,4},{6,7},{7,6},{8,9},{9,8},{10,11... | collective-permute-start | bytes 786440 | tf_op jit(solution)/shard_map/ppermute | solution.py:875
  39.2 1.9 %collective-permute-start.8 = (bf16[256,512]{1,0:T(8,128)(2,1)S(1)}, bf16[256,512]{1,0:T(8,128)(2,1)S(1)}, u32[]{:S(2)}, u32[]{:S(2)}) collective-permute-start(bf16[256,512]{1,0:T(8,128)(2,1)S(1)} %get-tuple-element.208.refs_2_), channel_id=1, source_target_pairs={{0,1},{1,0},{2,3},{3,2},{4,5},{5,4},{6,7},{7,6},{8,9},{9,8},{10,11... | collective-permute-start | bytes 786440 | tf_op jit(solution)/shard_map/ppermute | solution.py:875
  49.6 5.1 %collective-permute-start.10 = (bf16[256,512]{1,0:T(8,128)(2,1)S(1)}, bf16[256,512]{1,0:T(8,128)(2,1)S(1)}, u32[]{:S(2)}, u32[]{:S(2)}) collective-permute-start(bf16[256,512]{1,0:T(8,128)(2,1)S(1)} %get-tuple-element.219.refs_1_), channel_id=1, source_target_pairs={{0,1},{1,0},{2,3},{3,2},{4,5},{5,4},{6,7},{7,6},{8,9},{9,8},{10,11... | collective-permute-start | bytes 786440 | tf_op jit(solution)/shard_map/ppermute | solution.py:875
  51.6 14.4 %collective-permute-start.14 = (bf16[1,512,512]{2,1,0:T(8,128)(2,1)S(1)}, bf16[1,512,512]{2,1,0:T(8,128)(2,1)S(1)}, u32[]{:S(2)}, u32[]{:S(2)}) collective-permute-start(bf16[1,512,512]{2,1,0:T(8,128)(2,1)S(1)} %get-tuple-element.240), channel_id=1, source_target_pairs={{0,2},{1,3},{2,0},{3,1},{4,6},{5,7},{6,4},{7,5},{8,10},{9,11},{10,... | collective-permute-start | bytes 1572872 | tf_op jit(solution)/shard_map/ppermute | solution.py:872
  53.0 2.2 %collective-permute-start.11 = (bf16[256,512]{1,0:T(8,128)(2,1)S(1)}, bf16[256,512]{1,0:T(8,128)(2,1)S(1)}, u32[]{:S(2)}, u32[]{:S(2)}) collective-permute-start(bf16[256,512]{1,0:T(8,128)(2,1)S(1)} %get-tuple-element.220.refs_2_), channel_id=1, source_target_pairs={{0,1},{1,0},{2,3},{3,2},{4,5},{5,4},{6,7},{7,6},{8,9},{9,8},{10,11... | collective-permute-start | bytes 786440 | tf_op jit(solution)/shard_map/ppermute | solution.py:875
  53.3 14.1 %collective-permute-start.15 = (bf16[2,256,512]{2,1,0:T(8,128)(2,1)S(1)}, bf16[2,256,512]{2,1,0:T(8,128)(2,1)S(1)}, u32[]{:S(2)}, u32[]{:S(2)}) collective-permute-start(bf16[2,256,512]{2,1,0:T(8,128)(2,1)S(1)} %get-tuple-element.242), channel_id=1, source_target_pairs={{0,4},{4,0},{8,12},{12,8},{16,20},{20,16},{24,28},{28,24},{1,5},{5... | collective-permute-start | bytes 1572872 | tf_op jit(solution)/shard_map/ppermute | solution.py:878
  54.8 6.6 %collective-permute-start.16 = (bf16[256,512]{1,0:T(8,128)(2,1)S(1)}, bf16[256,512]{1,0:T(8,128)(2,1)S(1)}, u32[]{:S(2)}, u32[]{:S(2)}) collective-permute-start(bf16[256,512]{1,0:T(8,128)(2,1)S(1)} %get-tuple-element.252.refs_14_), channel_id=1, source_target_pairs={{0,1},{1,0},{2,3},{3,2},{4,5},{5,4},{6,7},{7,6},{8,9},{9,8},{10,11... | collective-permute-start | bytes 786440 | tf_op jit(solution)/shard_map/ppermute | solution.py:875
  54.8 7.0 %collective-permute-start.17 = (bf16[256,512]{1,0:T(8,128)(2,1)S(1)}, bf16[256,512]{1,0:T(8,128)(2,1)S(1)}, u32[]{:S(2)}, u32[]{:S(2)}) collective-permute-start(bf16[256,512]{1,0:T(8,128)(2,1)S(1)} %get-tuple-element.253.refs_15_), channel_id=1, source_target_pairs={{0,1},{1,0},{2,3},{3,2},{4,5},{5,4},{6,7},{7,6},{8,9},{9,8},{10,11... | collective-permute-start | bytes 786440 | tf_op jit(solution)/shard_map/ppermute | solution.py:875
  61.2 8.5 %collective-permute-start.12 = (bf16[256,512]{1,0:T(8,128)(2,1)S(1)}, bf16[256,512]{1,0:T(8,128)(2,1)S(1)}, u32[]{:S(2)}, u32[]{:S(2)}) collective-permute-start(bf16[256,512]{1,0:T(8,128)(2,1)S(1)} %get-tuple-element.231.refs_1_), channel_id=1, source_target_pairs={{0,1},{1,0},{2,3},{3,2},{4,5},{5,4},{6,7},{7,6},{8,9},{9,8},{10,11... | collective-permute-start | bytes 786440 | tf_op jit(solution)/shard_map/ppermute | solution.py:875
  61.3 8.9 %collective-permute-start.13 = (bf16[256,512]{1,0:T(8,128)(2,1)S(1)}, bf16[256,512]{1,0:T(8,128)(2,1)S(1)}, u32[]{:S(2)}, u32[]{:S(2)}) collective-permute-start(bf16[256,512]{1,0:T(8,128)(2,1)S(1)} %get-tuple-element.232.refs_2_), channel_id=1, source_target_pairs={{0,1},{1,0},{2,3},{3,2},{4,5},{5,4},{6,7},{7,6},{8,9},{9,8},{10,11... | collective-permute-start | bytes 786440 | tf_op jit(solution)/shard_map/ppermute | solution.py:875
  63.9 11.1 %collective-permute-start.20 = (bf16[256,512]{1,0:T(8,128)(2,1)S(1)}, bf16[256,512]{1,0:T(8,128)(2,1)S(1)}, u32[]{:S(2)}, u32[]{:S(2)}) collective-permute-start(bf16[256,512]{1,0:T(8,128)(2,1)S(1)} %get-tuple-element.270.refs_4_), channel_id=1, source_target_pairs={{0,1},{1,0},{2,3},{3,2},{4,5},{5,4},{6,7},{7,6},{8,9},{9,8},{10,11... | collective-permute-start | bytes 786440 | tf_op jit(solution)/shard_map/ppermute | solution.py:875
  66.0 9.0 %collective-permute-start.21 = (bf16[256,512]{1,0:T(8,128)(2,1)S(1)}, bf16[256,512]{1,0:T(8,128)(2,1)S(1)}, u32[]{:S(2)}, u32[]{:S(2)}) collective-permute-start(bf16[256,512]{1,0:T(8,128)(2,1)S(1)} %get-tuple-element.271.refs_5_), channel_id=1, source_target_pairs={{0,1},{1,0},{2,3},{3,2},{4,5},{5,4},{6,7},{7,6},{8,9},{9,8},{10,11... | collective-permute-start | bytes 786440 | tf_op jit(solution)/shard_map/ppermute | solution.py:875
  68.1 9.3 %collective-permute-start.18 = (bf16[1,256,512]{2,1,0:T(8,128)(2,1)S(1)}, bf16[1,256,512]{2,1,0:T(8,128)(2,1)S(1)}, u32[]{:S(2)}, u32[]{:S(2)}) collective-permute-start(bf16[1,256,512]{2,1,0:T(8,128)(2,1)S(1)} %get-tuple-element.268), channel_id=1, source_target_pairs={{0,4},{4,0},{8,12},{12,8},{16,20},{20,16},{24,28},{28,24},{1,5},{5... | collective-permute-start | bytes 786440 | tf_op jit(solution)/shard_map/ppermute | solution.py:878
  69.7 7.7 %collective-permute-start.19 = (bf16[1,256,512]{2,1,0:T(8,128)(2,1)S(1)}, bf16[1,256,512]{2,1,0:T(8,128)(2,1)S(1)}, u32[]{:S(2)}, u32[]{:S(2)}) collective-permute-start(bf16[1,256,512]{2,1,0:T(8,128)(2,1)S(1)} %get-tuple-element.269), channel_id=1, source_target_pairs={{0,2},{1,3},{2,0},{3,1},{4,6},{5,7},{6,4},{7,5},{8,10},{9,11},{10,... | collective-permute-start | bytes 786440 | tf_op jit(solution)/shard_map/ppermute | solution.py:872
  70.2 17.6 %collective-permute-start.25 = (bf16[2,256,512]{2,1,0:T(8,128)(2,1)S(1)}, bf16[2,256,512]{2,1,0:T(8,128)(2,1)S(1)}, u32[]{:S(2)}, u32[]{:S(2)}) collective-permute-start(bf16[2,256,512]{2,1,0:T(8,128)(2,1)S(1)} %get-tuple-element.288), channel_id=1, source_target_pairs={{0,4},{4,0},{8,12},{12,8},{16,20},{20,16},{24,28},{28,24},{1,5},{5... | collective-permute-start | bytes 1572872 | tf_op jit(solution)/shard_map/ppermute | solution.py:878
  78.1 9.1 %collective-permute-start.26 = (bf16[2,192,512]{2,1,0:T(8,128)(2,1)S(1)}, bf16[2,192,512]{2,1,0:T(8,128)(2,1)S(1)}, u32[]{:S(2)}, u32[]{:S(2)}) collective-permute-start(bf16[2,192,512]{2,1,0:T(8,128)(2,1)S(1)} %get-tuple-element.290), channel_id=1, source_target_pairs={{0,8},{4,12},{8,0},{12,4},{16,24},{20,28},{24,16},{28,20},{1,9},{5... | collective-permute-start | bytes 1179656 | tf_op jit(solution)/shard_map/ppermute | solution.py:878
  79.8 11.5 %collective-permute-start.24 = (bf16[1,512,512]{2,1,0:T(8,128)(2,1)S(1)}, bf16[1,512,512]{2,1,0:T(8,128)(2,1)S(1)}, u32[]{:S(2)}, u32[]{:S(2)}) collective-permute-start(bf16[1,512,512]{2,1,0:T(8,128)(2,1)S(1)} %get-tuple-element.286), channel_id=1, source_target_pairs={{0,2},{1,3},{2,0},{3,1},{4,6},{5,7},{6,4},{7,5},{8,10},{9,11},{10,... | collective-permute-start | bytes 1572872 | tf_op jit(solution)/shard_map/ppermute | solution.py:872
  84.5 10.0 %collective-permute-start.22 = (bf16[256,512]{1,0:T(8,128)(2,1)S(1)}, bf16[256,512]{1,0:T(8,128)(2,1)S(1)}, u32[]{:S(2)}, u32[]{:S(2)}) collective-permute-start(bf16[256,512]{1,0:T(8,128)(2,1)S(1)} %get-tuple-element.274.refs_1_), channel_id=1, source_target_pairs={{0,1},{1,0},{2,3},{3,2},{4,5},{5,4},{6,7},{7,6},{8,9},{9,8},{10,11... | collective-permute-start | bytes 786440 | tf_op jit(solution)/shard_map/ppermute | solution.py:875
  84.6 10.9 %collective-permute-start.23 = (bf16[256,512]{1,0:T(8,128)(2,1)S(1)}, bf16[256,512]{1,0:T(8,128)(2,1)S(1)}, u32[]{:S(2)}, u32[]{:S(2)}) collective-permute-start(bf16[256,512]{1,0:T(8,128)(2,1)S(1)} %get-tuple-element.275.refs_2_), channel_id=1, source_target_pairs={{0,1},{1,0},{2,3},{3,2},{4,5},{5,4},{6,7},{7,6},{8,9},{9,8},{10,11... | collective-permute-start | bytes 786440 | tf_op jit(solution)/shard_map/ppermute | solution.py:875
  88.5 10.0 %collective-permute-start.28 = (bf16[2,128,512]{2,1,0:T(8,128)(2,1)S(1)}, bf16[2,128,512]{2,1,0:T(8,128)(2,1)S(1)}, u32[]{:S(2)}, u32[]{:S(2)}) collective-permute-start(bf16[2,128,512]{2,1,0:T(8,128)(2,1)S(1)} %get-tuple-element.300), channel_id=1, source_target_pairs={{0,8},{4,12},{8,0},{12,4},{16,24},{20,28},{24,16},{28,20},{1,9},{5... | collective-permute-start | bytes 786440 | tf_op jit(solution)/shard_map/ppermute | solution.py:878
  90.2 7.1 %collective-permute-start.29 = (bf16[1,128,512]{2,1,0:T(8,128)(2,1)S(1)}, bf16[1,128,512]{2,1,0:T(8,128)(2,1)S(1)}, u32[]{:S(2)}, u32[]{:S(2)}) collective-permute-start(bf16[1,128,512]{2,1,0:T(8,128)(2,1)S(1)} %get-tuple-element.303), channel_id=1, source_target_pairs={{0,4},{4,0},{8,12},{12,8},{16,20},{20,16},{24,28},{28,24},{1,5},{5... | collective-permute-start | bytes 393224 | tf_op jit(solution)/shard_map/ppermute | solution.py:878
  91.3 12.4 %collective-permute-start.31 = (bf16[2,128,512]{2,1,0:T(8,128)(2,1)S(1)}, bf16[2,128,512]{2,1,0:T(8,128)(2,1)S(1)}, u32[]{:S(2)}, u32[]{:S(2)}) collective-permute-start(bf16[2,128,512]{2,1,0:T(8,128)(2,1)S(1)} %get-tuple-element.307.refs_0_), channel_id=1, source_target_pairs={{0,16},{4,20},{8,24},{12,28},{16,0},{20,4},{24,8},{28,12},{1,17},{... | collective-permute-start | bytes 786440 | tf_op jit(solution)/shard_map/ppermute | solution.py:878
  94.6 9.8 %collective-permute-start.27 = (bf16[1,256,512]{2,1,0:T(8,128)(2,1)S(1)}, bf16[1,256,512]{2,1,0:T(8,128)(2,1)S(1)}, u32[]{:S(2)}, u32[]{:S(2)}) collective-permute-start(bf16[1,256,512]{2,1,0:T(8,128)(2,1)S(1)} %get-tuple-element.298), channel_id=1, source_target_pairs={{0,4},{4,0},{8,12},{12,8},{16,20},{20,16},{24,28},{28,24},{1,5},{5... | collective-permute-start | bytes 786440 | tf_op jit(solution)/shard_map/ppermute | solution.py:878
  99.2 6.7 %collective-permute-start.30 = (bf16[1,144,512]{2,1,0:T(8,128)(2,1)S(1)}, bf16[1,144,512]{2,1,0:T(8,128)(2,1)S(1)}, u32[]{:S(2)}, u32[]{:S(2)}) collective-permute-start(bf16[1,144,512]{2,1,0:T(8,128)(2,1)S(1)} %get-tuple-element.306), channel_id=1, source_target_pairs={{0,2},{1,3},{2,0},{3,1},{4,6},{5,7},{6,4},{7,5},{8,10},{9,11},{10,... | collective-permute-start | bytes 442376 | tf_op jit(solution)/shard_map/ppermute | solution.py:872
  106.5 32.1 %collective-permute-start.32 = (bf16[1024,512]{1,0:T(8,128)(2,1)S(1)}, bf16[1024,512]{1,0:T(8,128)(2,1)S(1)}, u32[]{:S(2)}, u32[]{:S(2)}) collective-permute-start(bf16[1024,512]{1,0:T(8,128)(2,1)S(1)} %get-tuple-element.311.refs_0_), channel_id=1, source_target_pairs={{0,2},{1,3},{2,0},{3,1},{4,6},{5,7},{6,4},{7,5},{8,10},{9,11},{10,... | collective-permute-start | bytes 3145736 | tf_op jit(solution)/shard_map/ppermute | solution.py:872
  108.0 6.9 %collective-permute-start.34 = (bf16[2,128,512]{2,1,0:T(8,128)(2,1)S(1)}, bf16[2,128,512]{2,1,0:T(8,128)(2,1)S(1)}, u32[]{:S(2)}, u32[]{:S(2)}) collective-permute-start(bf16[2,128,512]{2,1,0:T(8,128)(2,1)S(1)} %get-tuple-element.315.refs_4_), channel_id=1, source_target_pairs={{0,4},{4,0},{8,12},{12,8},{16,20},{20,16},{24,28},{28,24},{1,5},{5... | collective-permute-start | bytes 786440 | tf_op jit(solution)/shard_map/ppermute | solution.py:878
  110.6 6.4 %collective-permute-start.33 = (bf16[1,128,512]{2,1,0:T(8,128)(2,1)S(1)}, bf16[1,128,512]{2,1,0:T(8,128)(2,1)S(1)}, u32[]{:S(2)}, u32[]{:S(2)}) collective-permute-start(bf16[1,128,512]{2,1,0:T(8,128)(2,1)S(1)} %get-tuple-element.313), channel_id=1, source_target_pairs={{0,8},{4,12},{8,0},{12,4},{16,24},{20,28},{24,16},{28,20},{1,9},{5... | collective-permute-start | bytes 393224 | tf_op jit(solution)/shard_map/ppermute | solution.py:878
  110.6 6.4 %collective-permute-start.35 = (bf16[1,128,512]{2,1,0:T(8,128)(2,1)S(1)}, bf16[1,128,512]{2,1,0:T(8,128)(2,1)S(1)}, u32[]{:S(2)}, u32[]{:S(2)}) collective-permute-start(bf16[1,128,512]{2,1,0:T(8,128)(2,1)S(1)} %get-tuple-element.310.refs_6_), channel_id=1, source_target_pairs={{0,16},{4,20},{8,24},{12,28},{16,0},{20,4},{24,8},{28,12},{1,17},{... | collective-permute-start | bytes 393224 | tf_op jit(solution)/shard_map/ppermute | solution.py:878
  117.6 9.1 %collective-permute-start.37 = (bf16[1,144,512]{2,1,0:T(8,128)(2,1)S(1)}, bf16[1,144,512]{2,1,0:T(8,128)(2,1)S(1)}, u32[]{:S(2)}, u32[]{:S(2)}) collective-permute-start(bf16[1,144,512]{2,1,0:T(8,128)(2,1)S(1)} %get-tuple-element.318.refs_0_), channel_id=1, source_target_pairs={{0,16},{4,20},{8,24},{12,28},{16,0},{20,4},{24,8},{28,12},{1,17},{... | collective-permute-start | bytes 442376 | tf_op jit(solution)/shard_map/ppermute | solution.py:878
  119.4 7.3 %collective-permute-start.38 = (bf16[1,128,512]{2,1,0:T(8,128)(2,1)S(1)}, bf16[1,128,512]{2,1,0:T(8,128)(2,1)S(1)}, u32[]{:S(2)}, u32[]{:S(2)}) collective-permute-start(bf16[1,128,512]{2,1,0:T(8,128)(2,1)S(1)} %get-tuple-element.319.refs_2_), channel_id=1, source_target_pairs={{0,8},{4,12},{8,0},{12,4},{16,24},{20,28},{24,16},{28,20},{1,9},{5... | collective-permute-start | bytes 393224 | tf_op jit(solution)/shard_map/ppermute | solution.py:878
  120.6 17.9 %collective-permute-start.36 = (bf16[2,256,512]{2,1,0:T(8,128)(2,1)S(1)}, bf16[2,256,512]{2,1,0:T(8,128)(2,1)S(1)}, u32[]{:S(2)}, u32[]{:S(2)}) collective-permute-start(bf16[2,256,512]{2,1,0:T(8,128)(2,1)S(1)} %get-tuple-element.317.refs_2_), channel_id=1, source_target_pairs={{0,8},{4,12},{8,0},{12,4},{16,24},{20,28},{24,16},{28,20},{1,9},{5... | collective-permute-start | bytes 1572872 | tf_op jit(solution)/shard_map/ppermute | solution.py:878
  127.3 6.6 %collective-permute-start.39 = (bf16[1,144,512]{2,1,0:T(8,128)(2,1)S(1)}, bf16[1,144,512]{2,1,0:T(8,128)(2,1)S(1)}, u32[]{:S(2)}, u32[]{:S(2)}) collective-permute-start(bf16[1,144,512]{2,1,0:T(8,128)(2,1)S(1)} %get-tuple-element.321.refs_0_), channel_id=1, source_target_pairs={{0,4},{4,0},{8,12},{12,8},{16,20},{20,16},{24,28},{28,24},{1,5},{5... | collective-permute-start | bytes 442376 | tf_op jit(solution)/shard_map/ppermute | solution.py:878
  128.9 5.0 %collective-permute-start.40 = (bf16[1,128,512]{2,1,0:T(8,128)(2,1)S(1)}, bf16[1,128,512]{2,1,0:T(8,128)(2,1)S(1)}, u32[]{:S(2)}, u32[]{:S(2)}) collective-permute-start(bf16[1,128,512]{2,1,0:T(8,128)(2,1)S(1)} %get-tuple-element.323), channel_id=1, source_target_pairs={{0,2},{1,3},{2,0},{3,1},{4,6},{5,7},{6,4},{7,5},{8,10},{9,11},{10,... | collective-permute-start | bytes 393224 | tf_op jit(solution)/shard_map/ppermute | solution.py:872
  129.8 12.0 %collective-permute-start.43 = (bf16[1,288,512]{2,1,0:T(8,128)(2,1)S(1)}, bf16[1,288,512]{2,1,0:T(8,128)(2,1)S(1)}, u32[]{:S(2)}, u32[]{:S(2)}) collective-permute-start(bf16[1,288,512]{2,1,0:T(8,128)(2,1)S(1)} %get-tuple-element.331.refs_0_), channel_id=1, source_target_pairs={{0,4},{4,0},{8,12},{12,8},{16,20},{20,16},{24,28},{28,24},{1,5},{5... | collective-permute-start | bytes 884744 | tf_op jit(solution)/shard_map/ppermute | solution.py:878
  134.5 8.9 %collective-permute-start.42 = (bf16[1,272,512]{2,1,0:T(8,128)(2,1)S(1)}, bf16[1,272,512]{2,1,0:T(8,128)(2,1)S(1)}, u32[]{:S(2)}, u32[]{:S(2)}) collective-permute-start(bf16[1,272,512]{2,1,0:T(8,128)(2,1)S(1)} %get-tuple-element.330.refs_2_), channel_id=1, source_target_pairs={{0,8},{4,12},{8,0},{12,4},{16,24},{20,28},{24,16},{28,20},{1,9},{5... | collective-permute-start | bytes 835592 | tf_op jit(solution)/shard_map/ppermute | solution.py:878
  135.5 7.9 %collective-permute-start.41 = (bf16[1,128,512]{2,1,0:T(8,128)(2,1)S(1)}, bf16[1,128,512]{2,1,0:T(8,128)(2,1)S(1)}, u32[]{:S(2)}, u32[]{:S(2)}) collective-permute-start(bf16[1,128,512]{2,1,0:T(8,128)(2,1)S(1)} %get-tuple-element.329), channel_id=1, source_target_pairs={{0,16},{4,20},{8,24},{12,28},{16,0},{20,4},{24,8},{28,12},{1,17},{... | collective-permute-start | bytes 393224 | tf_op jit(solution)/shard_map/ppermute | solution.py:878
  (2 other events, 11.7 us)

commit v5 on v4

--- a/solution.py
+++ b/solution.py
@@ -1222,32 +1222,32 @@
         ).astype(F32)
     advance("self_cross_4", by_self, by_cross)
 
+    mixed, grad_inputs = run(
+        place_rows_kernel,
+        [both, got_both],
+        [far(((rows, seq, width), BF16)), far(((rows, seq, width), F32))],
+        name="place_rows",
+    )
     more = (functools.partial(memory_send_kernel, "row", 0, 2), memory_state, sent) if along else None
     while more or not (by_self.ready() and by_cross.ready() and by_ffn.ready()):
         given = advance("rest", by_self, more=more)
         if more:
             memory_state, more = [given[0], data_swap(given[1], 2)], None
         advance("rest_cross", by_ffn, by_cross)
-    (mixed, grad_inputs), (grad_ffn_in, grad_ffn_out) = run.batch(
+    (grad_ffn_in, grad_ffn_out), (grad_cross_q, grad_cross_kv, grad_cross_out) = run.batch(
         [
-            (
-                place_rows_kernel,
-                [both, got_both],
-                [far(((rows, seq, width), BF16)), far(((rows, seq, width), F32))],
-            ),
             (
                 functools.partial(ffn_grads_kernel, by_ffn.halved[0]),
                 [by_ffn.chunk, by_ffn.got],
                 [far(((width, unit), F32)), far(((unit, width), F32))],
             ),
+            (
+                functools.partial(cross_grads_kernel, by_cross.halved[0]),
+                [by_cross.chunk, by_cross.got],
+                [far(((width, head), F32)), far(((2, width, head), F32)), far(((head, width), F32))],
+            ),
         ],
-        name="rows_and_ffn_grads",
-    )
-    grad_cross_q, grad_cross_kv, grad_cross_out = run(
-        functools.partial(cross_grads_kernel, by_cross.halved[0]),
-        [by_cross.chunk, by_cross.got],
-        [far(((width, head), F32)), far(((2, width, head), F32)), far(((head, width), F32))],
-        name="cross_grads",
+        name="ffn_and_cross_grads",
     )
     parts = []
     if along:

time: 146 us -> 146 us (level)
  starting transfers between devices: 51.1 us -> 49.6 us
    ppermute x19, waiting for transfers between devices: 22.9 us -> 24.5 us  [data_swap(): return lax.ppermute(value, 'dp', [(i, i ^ 1 << k) for i in range(dp)])]
  transfers between devices with their start and end apart: 45 -> 45, of which waited for: 19 -> 21; matrix products, arithmetic and copies ran while one was open for 0% -> 0% of each run, Pallas kernels for 36% -> 37%
where the time goes in v5:
time: 146 us; the launch traced here: 145 us
  Pallas kernels  59.2 us (41%)
  starting transfers between devices  49.6 us (34%)
  waiting for transfers between devices  34.1 us (23%)
    pallas_call x29, Pallas kernels, __call__(): pl.pallas_call(body, in_specs=[words] + specs + after_specs, out_specs=[f...  59.2 us
    ppermute x19, starting transfers between devices, data_swap(): return lax.ppermute(value, 'dp', [(i, i ^ 1 << k) for i in range(dp)])  26.8 us
    ppermute x19, waiting for transfers between devices, data_swap(): return lax.ppermute(value, 'dp', [(i, i ^ 1 << k) for i in range(dp)])  24.5 us
    ppermute x11, starting transfers between devices, other(): return lax.ppermute(value, 'mp', across)  13.4 us
    ppermute x11, waiting for transfers between devices, other(): return lax.ppermute(value, 'mp', across)  7.86 us
    all_to_all x1, starting transfers between devices, shards(): lax.all_to_all(memory_part, 'dp', split_axis=0, concat_axis=0, tiled=True)  6.27 us
    ppermute x14, starting transfers between devices, seat_swap(): return lax.ppermute(value, 'mp', [(i, i ^ step) for i in range(mp)])  3.23 us
  transfers between devices with their start and end apart: 45, of which 21 were waited for; matrix products, arithmetic and copies ran while one was open for 0% of the time, Pallas kernels for 37%

profile of v5, /device:TPU:0, one launch (start us, length us, event | category | flops | bytes accessed | tf_op | source)
XLA Modules:
  0.0 145.1 jit_solution(14290035329940953280)
XLA Ops:
  0.6 3.0 %collective-permute-start = (bf16[3,512,128]{2,1,0:T(8,128)(2,1)}, bf16[3,512,128]{2,1,0:T(8,128)(2,1)S(1)}, u32[]{:S(2)}, u32[]{:S(2)}) collective-permute-start(bf16[3,512,128]{2,1,0:T(8,128)(2,1)} %refs_0_.3), channel_id=1, source_target_pairs={{0,2},{1,3},{2,0},{3,1},{4,6},{5,7},{6,4},{7,5},{8,10},{9,11},{10,... | collective-permute-start | bytes 1179656 | tf_op jit(solution)/shard_map/ppermute | solution.py:872
  3.8 3.5 %setup.1 = (bf16[1024,128]{1,0:T(8,128)(2,1)}, bf16[2,512,512]{2,1,0:T(8,128)(2,1)S(1)}, bf16[2,512,128]{2,1,0:T(8,128)(2,1)S(1)}, bf16[512,512]{1,0:T(8,128)(2,...) custom-call(s32[6]{0:T(128)S(1)} %stack.27.where_ref, ...), custom_call_target="tpu_custom_call" | custom-call | flops 1000000 | bytes 300000 | tf_op jit(solution)/shard_map/setup/pallas_call | solution.py:146
  8.3 6.3 %all-to-all-start = ((bf16[8,64,512]{2,1,0:T(8,128)(2,1)}), bf16[8,64,512]{2,1,0:T(8,128)(2,1)S(1)}, u32[]{:S(2)}, u32[]{:S(2)}) async-start(bf16[8,64,512]{2,1,0:T(8,128)(2,1)} %get-tuple-element.191), calls=%async_computation | async-start | bytes 1048576 | tf_op jit(solution)/shard_map/all_to_all | solution.py:929
  14.5 1.6 %collective-permute-start.2 = (bf16[128,512]{1,0:T(8,128)(2,1)S(1)}, bf16[128,512]{1,0:T(8,128)(2,1)S(1)}, u32[]{:S(2)}, u32[]{:S(2)}) collective-permute-start(bf16[128,512]{1,0:T(8,128)(2,1)S(1)} %copy-done.1), channel_id=1, source_target_pairs={{0,2},{1,3},{2,0},{3,1},{4,6},{5,7},{6,4},{7,5},{8,10},{9,11},{10,... | collective-permute-start | bytes 393224 | tf_op jit(solution)/shard_map/ppermute | solution.py:872
  16.7 3.1 %self_forward_0.1 = (bf16[512,512]{1,0:T(8,128)(2,1)S(1)}, bf16[512,128]{1,0:T(8,128)(2,1)}, bf16[512,128]{1,0:T(8,128)(2,1)}, bf16[512,128]{1,0:T(8,128)(2,1)},...) custom-call(s32[6]{0:T(128)S(1)} %stack.27.where_ref, ...), custom_call_target="tpu_custom_call" | custom-call | flops 1000000 | bytes 300000 | tf_op jit(solution)/shard_map/self_forward_0/pallas_call | solution.py:146
  19.8 1.7 %collective-permute-done.1.refs_4_.refs_3_.refs_5_ = bf16[8,128]{1,0:T(8,128)(2,1)S(1)} collective-permute-done((bf16[8,128]{1,0:T(8,128)(2,1)S(1)}, bf16[8,128]{1,0:T(8,128)(2,1)S(1)}, u32[]{:S(2)}, u32[]{:S(2)}) %collective-permute-start.1) | collective-permute-done | bytes 2080 | tf_op jit(solution)/shard_map/ppermute | solution.py:872
  21.5 1.8 %collective-permute-start.9 = (bf16[2,512,512]{2,1,0:T(8,128)(2,1)}, bf16[2,512,512]{2,1,0:T(8,128)(2,1)}, u32[]{:S(2)}, u32[]{:S(2)}) collective-permute-start(bf16[2,512,512]{2,1,0:T(8,128)(2,1)} %copy-done), channel_id=1, source_target_pairs={{0,2},{1,3},{2,0},{3,1},{4,6},{5,7},{6,4},{7,5},{8,10},{9,11},{10,... | collective-permute-start | bytes 3145736 | tf_op jit(solution)/shard_map/ppermute | solution.py:872
  23.3 2.9 %self_forward_1.1 = (bf16[512,128]{1,0:T(8,128)(2,1)}, bf16[512,128]{1,0:T(8,128)(2,1)}, bf16[512,128]{1,0:T(8,128)(2,1)}, bf16[512,128]{1,0:T(8,128)(2,1)S(1)},...) custom-call(s32[6]{0:T(128)S(1)} %stack.27.where_ref, ...), custom_call_target="tpu_custom_call" | custom-call | flops 1000000 | bytes 300000 | tf_op jit(solution)/shard_map/self_forward_1/pallas_call | solution.py:146
  26.8 1.5 %collective-permute-start.6 = (bf16[1024,128]{1,0:T(8,128)(2,1)S(1)}, bf16[1024,128]{1,0:T(8,128)(2,1)}, u32[]{:S(2)}, u32[]{:S(2)}) collective-permute-start(bf16[1024,128]{1,0:T(8,128)(2,1)S(1)} %collective-permute-done.5.refs_0_), channel_id=1, source_target_pairs={{0,4},{4,0},{8,12},{12,8},{16,20},{20,16},{24,28},{28,24},{1,5},{5... | collective-permute-start | bytes 786440 | tf_op jit(solution)/shard_map/ppermute | solution.py:878
  29.5 3.6 %cross_forward_0.1 = (f32[512,512]{1,0:T(8,128)S(1)}, bf16[512,512]{1,0:T(8,128)(2,1)S(1)}, bf16[512,128]{1,0:T(8,128)(2,1)S(1)}, bf16[512,128]{1,0:T(8,128)(2,1...) custom-call(s32[6]{0:T(128)S(1)} %stack.27.where_ref, bf16[512,512]{1,0:T(8,128)(2,1)S(1)} %get-tuple-element.182.refs_0_, ...), custom_call_target="tpu_custom_call" | custom-call | flops 1000000 | bytes 300000 | tf_op jit(solution)/shard_map/cross_forward_0/pallas_call | solution.py:146
  33.1 2.1 %collective-permute-done.6.refs_1_ = bf16[1024,128]{1,0:T(8,128)(2,1)} collective-permute-done((bf16[1024,128]{1,0:T(8,128)(2,1)S(1)}, bf16[1024,128]{1,0:T(8,128)(2,1)}, u32[]{:S(2)}, u32[]{:S(2)}) %collective-permute-start.6) | collective-permute-done | bytes 262176 | tf_op jit(solution)/shard_map/ppermute | solution.py:878
  35.2 1.4 memory_1.1
  36.6 2.5 %cross_forward_1.1 = (bf16[512,128]{1,0:T(8,128)(2,1)S(1)}, bf16[512,128]{1,0:T(8,128)(2,1)S(1)}, f32[2,512]{1,0:T(2,128)S(1)}, bf16[256,512]{1,0:T(8,128)(2,1)S...) custom-call(s32[6]{0:T(128)S(1)} %stack.27.where_ref, bf16[512,512]{1,0:T(8,128)(2,1)S(1)} %get-tuple-element.198.refs_0_.refs_10_, ...), custom_call_target="tpu_custom_call" | custom-call | flops 1000000 | bytes 300000 | tf_op jit(solution)/shard_map/cross_forward_1/pallas_call | solution.py:146
  41.1 4.3 %ffn_0.1 = (f32[512,512]{1,0:T(8,128)S(1)}, bf16[512,512]{1,0:T(8,128)(2,1)S(1)}, bf16[512,512]{1,0:T(8,128)(2,1)S(1)}, bf16[512,512]{1,0:T(8,128)(2,1)S(1)}, bf...) custom-call(s32[6]{0:T(128)S(1)} %stack.27.where_ref, ...), custom_call_target="tpu_custom_call" | custom-call | flops 1000000 | bytes 300000 | tf_op jit(solution)/shard_map/ffn_0/pallas_call | solution.py:146
  46.2 3.4 %ffn_1.2 = (bf16[512,512]{1,0:T(8,128)(2,1)S(1)}, bf16[512,512]{1,0:T(8,128)(2,1)S(1)}, bf16[256,512]{1,0:T(8,128)(2,1)S(1)}, bf16[256,512]{1,0:T(8,128)(2,1)S(1...) custom-call(s32[6]{0:T(128)S(1)} %stack.27.where_ref, ...), custom_call_target="tpu_custom_call" | custom-call | flops 1000000 | bytes 300000 | tf_op jit(solution)/shard_map/ffn_1/pallas_call | solution.py:146
  49.7 1.8 %ffn_weights.1 = (f32[2,512]{1,0:T(2,128)S(1)}, f32[1,512,512]{2,1,0:T(8,128)S(1)}, bf16[1,512,512]{2,1,0:T(8,128)(2,1)S(1)}, f32[2,256,512]{2,1,0:T(8,128)S(1)}...) custom-call(s32[6]{0:T(128)S(1)} %stack.27.where_ref, bf16[512,512]{1,0:T(8,128)(2,1)S(1)} %get-tuple-element.225.refs_0_, ...), custom_call_target="tpu_custom_call" | custom-call | flops 1000000 | bytes 300000 | tf_op jit(solution)/shard_map/ffn_weights/pallas_call | solution.py:146
  51.6 1.5 %collective-permute-start.14 = (bf16[1,512,512]{2,1,0:T(8,128)(2,1)S(1)}, bf16[1,512,512]{2,1,0:T(8,128)(2,1)S(1)}, u32[]{:S(2)}, u32[]{:S(2)}) collective-permute-start(bf16[1,512,512]{2,1,0:T(8,128)(2,1)S(1)} %get-tuple-element.240), channel_id=1, source_target_pairs={{0,2},{1,3},{2,0},{3,1},{4,6},{5,7},{6,4},{7,5},{8,10},{9,11},{10,... | collective-permute-start | bytes 1572872 | tf_op jit(solution)/shard_map/ppermute | solution.py:872
  53.3 1.5 %collective-permute-start.15 = (bf16[2,256,512]{2,1,0:T(8,128)(2,1)S(1)}, bf16[2,256,512]{2,1,0:T(8,128)(2,1)S(1)}, u32[]{:S(2)}, u32[]{:S(2)}) collective-permute-start(bf16[2,256,512]{2,1,0:T(8,128)(2,1)S(1)} %get-tuple-element.242), channel_id=1, source_target_pairs={{0,4},{4,0},{8,12},{12,8},{16,20},{20,16},{24,28},{28,24},{1,5},{5... | collective-permute-start | bytes 1572872 | tf_op jit(solution)/shard_map/ppermute | solution.py:878
  55.3 5.9 %cross_backward.1 = (f32[512,512]{1,0:T(8,128)S(1)}, bf16[512,512]{1,0:T(8,128)(2,1)S(1)}, bf16[512,128]{1,0:T(8,128)(2,1)S(1)}, bf16[512,128]{1,0:T(8,128)(2,1)...) custom-call(s32[6]{0:T(128)S(1)} %stack.27.where_ref, ...), custom_call_target="tpu_custom_call" | custom-call | flops 1000000 | bytes 300000 | tf_op jit(solution)/shard_map/cross_backward/pallas_call | solution.py:146
  61.8 2.0 %cross_weights.1 = (f32[2,256,512]{2,1,0:T(8,128)S(1)}, bf16[2,256,512]{2,1,0:T(8,128)(2,1)S(1)}, bf16[256,512]{1,0:T(8,128)(2,1)S(1)}, bf16[256,512]{1,0:T(8,12...) custom-call(s32[6]{0:T(128)S(1)} %stack.27.where_ref, bf16[512,128]{1,0:T(8,128)(2,1)S(1)} %get-tuple-element.243.refs_0_, ...), custom_call_target="tpu_custom_call" | custom-call | flops 1000000 | bytes 300000 | tf_op jit(solution)/shard_map/cross_weights/pallas_call | solution.py:146
  64.0 1.9 %collective-permute-done.14.refs_1_ = bf16[1,512,512]{2,1,0:T(8,128)(2,1)S(1)} collective-permute-done((bf16[1,512,512]{2,1,0:T(8,128)(2,1)S(1)}, bf16[1,512,512]{2,1,0:T(8,128)(2,1)S(1)}, u32[]{:S(2)}, u32[]{:S(2)}) %collective-permute-start.14) | collective-permute-done | bytes 524320 | tf_op jit(solution)/shard_map/ppermute | solution.py:872
  66.0 1.4 collective-permute-done.15.refs_3_
  68.1 1.6 %collective-permute-start.18 = (bf16[1,256,512]{2,1,0:T(8,128)(2,1)S(1)}, bf16[1,256,512]{2,1,0:T(8,128)(2,1)S(1)}, u32[]{:S(2)}, u32[]{:S(2)}) collective-permute-start(bf16[1,256,512]{2,1,0:T(8,128)(2,1)S(1)} %get-tuple-element.268), channel_id=1, source_target_pairs={{0,4},{4,0},{8,12},{12,8},{16,20},{20,16},{24,28},{28,24},{1,5},{5... | collective-permute-start | bytes 786440 | tf_op jit(solution)/shard_map/ppermute | solution.py:878
  70.8 4.1 %self_backward.1 = (f32[512,512]{1,0:T(8,128)S(1)}, bf16[512,512]{1,0:T(8,128)(2,1)S(1)}, bf16[512,128]{1,0:T(8,128)(2,1)S(1)}, bf16[512,128]{1,0:T(8,128)(2,1)S...) custom-call(s32[6]{0:T(128)S(1)} %stack.27.where_ref, ...), custom_call_target="tpu_custom_call" | custom-call | flops 1000000 | bytes 300000 | tf_op jit(solution)/shard_map/self_backward/pallas_call | solution.py:146
  75.0 2.5 %collective-permute-done.18.refs_2_ = bf16[1,256,512]{2,1,0:T(8,128)(2,1)S(1)} collective-permute-done((bf16[1,256,512]{2,1,0:T(8,128)(2,1)S(1)}, bf16[1,256,512]{2,1,0:T(8,128)(2,1)S(1)}, u32[]{:S(2)}, u32[]{:S(2)}) %collective-permute-start.18) | collective-permute-done | bytes 262176 | tf_op jit(solution)/shard_map/ppermute | solution.py:878
  78.1 1.6 %collective-permute-start.26 = (bf16[2,192,512]{2,1,0:T(8,128)(2,1)S(1)}, bf16[2,192,512]{2,1,0:T(8,128)(2,1)S(1)}, u32[]{:S(2)}, u32[]{:S(2)}) collective-permute-start(bf16[2,192,512]{2,1,0:T(8,128)(2,1)S(1)} %get-tuple-element.290), channel_id=1, source_target_pairs={{0,8},{4,12},{8,0},{12,4},{16,24},{20,28},{24,16},{28,20},{1,9},{5... | collective-permute-start | bytes 1179656 | tf_op jit(solution)/shard_map/ppermute | solution.py:878
  80.5 4.0 %self_backward_rest.1 = (f32[2,128]{1,0:T(2,128)S(1)}, f32[1,512,512]{2,1,0:T(8,128)S(1)}, bf16[256,512]{1,0:T(8,128)(2,1)S(1)}, bf16[256,512]{1,0:T(8,128)(2,1)S(1)}, f32[8,128]{1,0:T(8,128)}) custom-call(s32[6]{0:T(128)S(1)} %stack.27.where_ref, bf16[3,512,128]{2,1,0:T(8,128)(2,1)} %refs_0_.3, ...), custom_call_target="tpu_custom_call" | custom-call | flops 1000000 | bytes 300000 | tf_op jit(solution)/shard_map/self_backward_rest/pallas_call | solution.py:146
  85.1 2.1 %collective-permute-done.26.refs_1_.refs_3_ = bf16[2,192,512]{2,1,0:T(8,128)(2,1)S(1)} collective-permute-done((bf16[2,192,512]{2,1,0:T(8,128)(2,1)S(1)}, bf16[2,192,512]{2,1,0:T(8,128)(2,1)S(1)}, u32[]{:S(2)}, u32[]{:S(2)}) %collective-permute-start.26) | collective-permute-done | bytes 393248 | tf_op jit(solution)/shard_map/ppermute | solution.py:878
  88.5 1.6 %collective-permute-start.28 = (bf16[2,128,512]{2,1,0:T(8,128)(2,1)S(1)}, bf16[2,128,512]{2,1,0:T(8,128)(2,1)S(1)}, u32[]{:S(2)}, u32[]{:S(2)}) collective-permute-start(bf16[2,128,512]{2,1,0:T(8,128)(2,1)S(1)} %get-tuple-element.300), channel_id=1, source_target_pairs={{0,8},{4,12},{8,0},{12,4},{16,24},{20,28},{24,16},{28,20},{1,9},{5... | collective-permute-start | bytes 786440 | tf_op jit(solution)/shard_map/ppermute | solution.py:878
  91.3 2.6 %collective-permute-start.31 = (bf16[2,128,512]{2,1,0:T(8,128)(2,1)S(1)}, bf16[2,128,512]{2,1,0:T(8,128)(2,1)S(1)}, u32[]{:S(2)}, u32[]{:S(2)}) collective-permute-start(bf16[2,128,512]{2,1,0:T(8,128)(2,1)S(1)} %get-tuple-element.307.refs_0_), channel_id=1, source_target_pairs={{0,16},{4,20},{8,24},{12,28},{16,0},{20,4},{24,8},{28,12},{1,17},{... | collective-permute-start | bytes 786440 | tf_op jit(solution)/shard_map/ppermute | solution.py:878
  95.5 1.7 %input_backward.1 = (bf16[1024,512]{1,0:T(8,128)(2,1)S(1)}, bf16[16,512]{1,0:T(8,128)(2,1)S(1)}, bf16[16,512]{1,0:T(8,128)(2,1)S(1)}, f32[8,128]{1,0:T(8,128)}) custom-call(s32[6]{0:T(128)S(1)} %stack.27.where_ref, bf16[512,512]{1,0:T(8,128)(2,1)S(1)} %get-tuple-element.182.refs_0_, bf16[256,512]{1,0:T(8,128)(2,1)S(1)} %get-tuple-element.274.refs_1_, ...), custom_call_target="tpu_custom_call" | custom-call | flops 1000000 | bytes 300000 | tf_op jit(solution)/shard_map/input_backward/pallas_call | solution.py:146
  99.2 1.5 collective-permute-start.30
  100.6 3.1 %collective-permute-done.31.refs_1_ = bf16[2,128,512]{2,1,0:T(8,128)(2,1)S(1)} collective-permute-done((bf16[2,128,512]{2,1,0:T(8,128)(2,1)S(1)}, bf16[2,128,512]{2,1,0:T(8,128)(2,1)S(1)}, u32[]{:S(2)}, u32[]{:S(2)}) %collective-permute-start.31) | collective-permute-done | bytes 262176 | tf_op jit(solution)/shard_map/ppermute | solution.py:878
  104.4 1.5 %collective-permute-done.30.refs_3_ = bf16[1,144,512]{2,1,0:T(8,128)(2,1)S(1)} collective-permute-done((bf16[1,144,512]{2,1,0:T(8,128)(2,1)S(1)}, bf16[1,144,512]{2,1,0:T(8,128)(2,1)S(1)}, u32[]{:S(2)}, u32[]{:S(2)}) %collective-permute-start.30) | collective-permute-done | bytes 147488 | tf_op jit(solution)/shard_map/ppermute | solution.py:872
  106.5 1.4 collective-permute-start.32
  108.0 2.6 %collective-permute-start.34 = (bf16[2,128,512]{2,1,0:T(8,128)(2,1)S(1)}, bf16[2,128,512]{2,1,0:T(8,128)(2,1)S(1)}, u32[]{:S(2)}, u32[]{:S(2)}) collective-permute-start(bf16[2,128,512]{2,1,0:T(8,128)(2,1)S(1)} %get-tuple-element.315.refs_4_), channel_id=1, source_target_pairs={{0,4},{4,0},{8,12},{12,8},{16,20},{20,16},{24,28},{28,24},{1,5},{5... | collective-permute-start | bytes 786440 | tf_op jit(solution)/shard_map/ppermute | solution.py:878
  110.6 1.9 %collective-permute-start.35 = (bf16[1,128,512]{2,1,0:T(8,128)(2,1)S(1)}, bf16[1,128,512]{2,1,0:T(8,128)(2,1)S(1)}, u32[]{:S(2)}, u32[]{:S(2)}) collective-permute-start(bf16[1,128,512]{2,1,0:T(8,128)(2,1)S(1)} %get-tuple-element.310.refs_6_), channel_id=1, source_target_pairs={{0,16},{4,20},{8,24},{12,28},{16,0},{20,4},{24,8},{28,12},{1,17},{... | collective-permute-start | bytes 393224 | tf_op jit(solution)/shard_map/ppermute | solution.py:878
  112.5 2.4 %collective-permute-done.34.refs_5_ = bf16[2,128,512]{2,1,0:T(8,128)(2,1)S(1)} collective-permute-done((bf16[2,128,512]{2,1,0:T(8,128)(2,1)S(1)}, bf16[2,128,512]{2,1,0:T(8,128)(2,1)S(1)}, u32[]{:S(2)}, u32[]{:S(2)}) %collective-permute-start.34) | collective-permute-done | bytes 262176 | tf_op jit(solution)/shard_map/ppermute | solution.py:878
  114.9 2.0 %collective-permute-done.33.refs_1_ = bf16[1,128,512]{2,1,0:T(8,128)(2,1)S(1)} collective-permute-done((bf16[1,128,512]{2,1,0:T(8,128)(2,1)S(1)}, bf16[1,128,512]{2,1,0:T(8,128)(2,1)S(1)}, u32[]{:S(2)}, u32[]{:S(2)}) %collective-permute-start.33) | collective-permute-done | bytes 131104 | tf_op jit(solution)/shard_map/ppermute | solution.py:878
  117.6 1.8 %collective-permute-start.36 = (bf16[1,144,512]{2,1,0:T(8,128)(2,1)S(1)}, bf16[1,144,512]{2,1,0:T(8,128)(2,1)S(1)}, u32[]{:S(2)}, u32[]{:S(2)}) collective-permute-start(bf16[1,144,512]{2,1,0:T(8,128)(2,1)S(1)} %get-tuple-element.317.refs_0_), channel_id=1, source_target_pairs={{0,16},{4,20},{8,24},{12,28},{16,0},{20,4},{24,8},{28,12},{1,17},{... | collective-permute-start | bytes 442376 | tf_op jit(solution)/shard_map/ppermute | solution.py:878
  121.4 5.3 %collective-permute-done.37.refs_3_ = bf16[1,128,512]{2,1,0:T(8,128)(2,1)S(1)} collective-permute-done((bf16[1,128,512]{2,1,0:T(8,128)(2,1)S(1)}, bf16[1,128,512]{2,1,0:T(8,128)(2,1)S(1)}, u32[]{:S(2)}, u32[]{:S(2)}) %collective-permute-start.37) | collective-permute-done | bytes 131104 | tf_op jit(solution)/shard_map/ppermute | solution.py:878
  127.3 1.6 %collective-permute-start.38 = (bf16[1,144,512]{2,1,0:T(8,128)(2,1)S(1)}, bf16[1,144,512]{2,1,0:T(8,128)(2,1)S(1)}, u32[]{:S(2)}, u32[]{:S(2)}) collective-permute-start(bf16[1,144,512]{2,1,0:T(8,128)(2,1)S(1)} %get-tuple-element.323.refs_0_), channel_id=1, source_target_pairs={{0,4},{4,0},{8,12},{12,8},{16,20},{20,16},{24,28},{28,24},{1,5},{5... | collective-permute-start | bytes 442376 | tf_op jit(solution)/shard_map/ppermute | solution.py:878
  130.1 2.3 %place_rows.1 = (bf16[2,512,512]{2,1,0:T(8,128)(2,1)}, f32[2,512,512]{2,1,0:T(8,128)}, f32[8,128]{1,0:T(8,128)}) custom-call(s32[6]{0:T(128)S(1)} %stack.27.where_ref, bf16[1024,512]{1,0:T(8,128)(2,1)S(1)} %get-tuple-element.311.refs_0_, bf16[1024,512]{1,0:T(8,128)(2,1)S(1)} %collective-permute-done.32.refs_1_, f32[8,128]{1,0:T(8,128)} %get-tuple-element.320.refs_2_), custom_call_target="tpu_custom_call" | custom-call | flops 1000000 | bytes 300000 | tf_op jit(solution)/shard_map/place_rows/pallas_call | solution.py:146
  132.4 1.4 collective-permute-done.39.refs_3_
  135.5 2.5 %collective-permute-start.40 = (bf16[1,128,512]{2,1,0:T(8,128)(2,1)S(1)}, bf16[1,128,512]{2,1,0:T(8,128)(2,1)S(1)}, u32[]{:S(2)}, u32[]{:S(2)}) collective-permute-start(bf16[1,128,512]{2,1,0:T(8,128)(2,1)S(1)} %get-tuple-element.328), channel_id=1, source_target_pairs={{0,16},{4,20},{8,24},{12,28},{16,0},{20,4},{24,8},{28,12},{1,17},{... | collective-permute-start | bytes 393224 | tf_op jit(solution)/shard_map/ppermute | solution.py:878
  138.6 2.7 %ffn_and_cross_grads.1 = (f32[512,512]{1,0:T(8,128)}, f32[512,512]{1,0:T(8,128)}, f32[512,128]{1,0:T(8,128)}, f32[2,512,128]{2,1,0:T(8,128)}, f32[128,512]{1,0:T(8,128)}, /*index=5*/f32[8,128]{1,0:T(8,128)}) custom-call(s32[6]{0:T(128)S(1)} %stack.27.where_ref, bf16[2,256,512]{2,1,0:T(8,128)(2,1)S(1)} %get-tuple-element.330.refs_0_, ...), custom_call_target="tpu_custom_call" | custom-call | flops 1000000 | bytes 300000 | tf_op jit(solution)/shard_map/ffn_and_cross_grads/pallas_call | solution.py:146
  141.4 1.5 %collective-permute-done.41.refs_3_ = bf16[1,272,512]{2,1,0:T(8,128)(2,1)S(1)} collective-permute-done((bf16[1,272,512]{2,1,0:T(8,128)(2,1)S(1)}, bf16[1,272,512]{2,1,0:T(8,128)(2,1)S(1)}, u32[]{:S(2)}, u32[]{:S(2)}) %collective-permute-start.41) | collective-permute-done | bytes 278560 | tf_op jit(solution)/shard_map/ppermute | solution.py:878
  143.0 1.9 %last_grads.1 = (f32[16,64,128]{2,1,0:T(8,128)}, f32[3,512,128]{2,1,0:T(8,128)}, f32[128,512]{1,0:T(8,128)}, f32[3,512]{1,0:T(4,128)}, f32[3,512]{1,0:T(4,128)},...) custom-call(s32[6]{0:T(128)S(1)} %stack.27.where_ref, ...), custom_call_target="tpu_custom_call" | custom-call | flops 1000000 | bytes 300000 | tf_op jit(solution)/shard_map/last_grads/pallas_call | solution.py:146
  (83 shorter events, 25.7 us)
Async XLA Ops:
  0.6 20.8 %collective-permute-start = (bf16[3,512,128]{2,1,0:T(8,128)(2,1)}, bf16[3,512,128]{2,1,0:T(8,128)(2,1)S(1)}, u32[]{:S(2)}, u32[]{:S(2)}) collective-permute-start(bf16[3,512,128]{2,1,0:T(8,128)(2,1)} %refs_0_.3), channel_id=1, source_target_pairs={{0,2},{1,3},{2,0},{3,1},{4,6},{5,7},{6,4},{7,5},{8,10},{9,11},{10,... | collective-permute-start | bytes 1179656 | tf_op jit(solution)/shard_map/ppermute | solution.py:872
  3.8 12.4 %copy-start.2 = (bf16[512]{0:T(512)(128)(2,1)S(1)}, bf16[512]{0:T(512)(128)(2,1)}, u32[]{:S(2)}) copy-start(bf16[512]{0:T(512)(128)(2,1)} %param.36) | copy-start | bytes 3076
  3.8 12.4 %copy-start.3 = (bf16[2,128]{1,0:T(2,128)(2,1)S(1)}, bf16[2,128]{1,0:T(2,128)(2,1)}, u32[]{:S(2)}) copy-start(bf16[2,128]{1,0:T(2,128)(2,1)} %param.33) | copy-start | bytes 1540
  3.8 12.4 %copy-start.4 = (bf16[2,128]{1,0:T(2,128)(2,1)S(1)}, bf16[2,128]{1,0:T(2,128)(2,1)}, u32[]{:S(2)}) copy-start(bf16[2,128]{1,0:T(2,128)(2,1)} %param.29) | copy-start | bytes 1540
  8.2 13.3 %collective-permute-start.5 = (bf16[1024,128]{1,0:T(8,128)(2,1)}, bf16[1024,128]{1,0:T(8,128)(2,1)S(1)}, u32[]{:S(2)}, u32[]{:S(2)}) collective-permute-start(bf16[1024,128]{1,0:T(8,128)(2,1)} %get-tuple-element.199), channel_id=1, source_target_pairs={{0,2},{1,3},{2,0},{3,1},{4,6},{5,7},{6,4},{7,5},{8,10},{9,11},{10,... | collective-permute-start | bytes 786440 | tf_op jit(solution)/shard_map/ppermute | solution.py:872
  8.3 20.2 %all-to-all-start = ((bf16[8,64,512]{2,1,0:T(8,128)(2,1)}), bf16[8,64,512]{2,1,0:T(8,128)(2,1)S(1)}, u32[]{:S(2)}, u32[]{:S(2)}) async-start(bf16[8,64,512]{2,1,0:T(8,128)(2,1)} %get-tuple-element.191), calls=%async_computation | async-start | bytes 1048576 | tf_op jit(solution)/shard_map/all_to_all | solution.py:929
  14.5 6.9 %collective-permute-start.2 = (bf16[128,512]{1,0:T(8,128)(2,1)S(1)}, bf16[128,512]{1,0:T(8,128)(2,1)S(1)}, u32[]{:S(2)}, u32[]{:S(2)}) collective-permute-start(bf16[128,512]{1,0:T(8,128)(2,1)S(1)} %copy-done.1), channel_id=1, source_target_pairs={{0,2},{1,3},{2,0},{3,1},{4,6},{5,7},{6,4},{7,5},{8,10},{9,11},{10,... | collective-permute-start | bytes 393224 | tf_op jit(solution)/shard_map/ppermute | solution.py:872
  16.1 5.3 %collective-permute-start.1 = (bf16[8,128]{1,0:T(8,128)(2,1)S(1)}, bf16[8,128]{1,0:T(8,128)(2,1)S(1)}, u32[]{:S(2)}, u32[]{:S(2)}) collective-permute-start(bf16[8,128]{1,0:T(8,128)(2,1)S(1)} %pad_maximum_fusion.refs_4_.refs_2_.refs_8_), channel_id=1, source_target_pairs={{0,2},{1,3},{2,0},{3,1},{4,6},{5,7},{6,4},{7,5},{8,10},{9,11},{10,... | collective-permute-start | bytes 6152 | tf_op jit(solution)/shard_map/ppermute | solution.py:872
  21.5 24.7 %collective-permute-start.9 = (bf16[2,512,512]{2,1,0:T(8,128)(2,1)}, bf16[2,512,512]{2,1,0:T(8,128)(2,1)}, u32[]{:S(2)}, u32[]{:S(2)}) collective-permute-start(bf16[2,512,512]{2,1,0:T(8,128)(2,1)} %copy-done), channel_id=1, source_target_pairs={{0,2},{1,3},{2,0},{3,1},{4,6},{5,7},{6,4},{7,5},{8,10},{9,11},{10,... | collective-permute-start | bytes 3145736 | tf_op jit(solution)/shard_map/ppermute | solution.py:872
  26.2 3.3 %collective-permute-start.3 = (bf16[256,512]{1,0:T(8,128)(2,1)}, bf16[256,512]{1,0:T(8,128)(2,1)}, u32[]{:S(2)}, u32[]{:S(2)}) collective-permute-start(bf16[256,512]{1,0:T(8,128)(2,1)} %get-tuple-element.189.refs_1_), channel_id=1, source_target_pairs={{0,1},{1,0},{2,3},{3,2},{4,5},{5,4},{6,7},{7,6},{8,9},{9,8},{10,11... | collective-permute-start | bytes 786440 | tf_op jit(solution)/shard_map/ppermute | solution.py:875
  26.3 3.2 %collective-permute-start.4 = (bf16[256,512]{1,0:T(8,128)(2,1)}, bf16[256,512]{1,0:T(8,128)(2,1)}, u32[]{:S(2)}, u32[]{:S(2)}) collective-permute-start(bf16[256,512]{1,0:T(8,128)(2,1)} %get-tuple-element.190.refs_2_), channel_id=1, source_target_pairs={{0,1},{1,0},{2,3},{3,2},{4,5},{5,4},{6,7},{7,6},{8,9},{9,8},{10,11... | collective-permute-start | bytes 786440 | tf_op jit(solution)/shard_map/ppermute | solution.py:875
  26.8 8.4 %collective-permute-start.6 = (bf16[1024,128]{1,0:T(8,128)(2,1)S(1)}, bf16[1024,128]{1,0:T(8,128)(2,1)}, u32[]{:S(2)}, u32[]{:S(2)}) collective-permute-start(bf16[1024,128]{1,0:T(8,128)(2,1)S(1)} %collective-permute-done.5.refs_0_), channel_id=1, source_target_pairs={{0,4},{4,0},{8,12},{12,8},{16,20},{20,16},{24,28},{28,24},{1,5},{5... | collective-permute-start | bytes 786440 | tf_op jit(solution)/shard_map/ppermute | solution.py:878
  39.1 1.6 %collective-permute-start.7 = (bf16[256,512]{1,0:T(8,128)(2,1)S(1)}, bf16[256,512]{1,0:T(8,128)(2,1)S(1)}, u32[]{:S(2)}, u32[]{:S(2)}) collective-permute-start(bf16[256,512]{1,0:T(8,128)(2,1)S(1)} %get-tuple-element.207.refs_1_), channel_id=1, source_target_pairs={{0,1},{1,0},{2,3},{3,2},{4,5},{5,4},{6,7},{7,6},{8,9},{9,8},{10,11... | collective-permute-start | bytes 786440 | tf_op jit(solution)/shard_map/ppermute | solution.py:875
  39.2 1.9 %collective-permute-start.8 = (bf16[256,512]{1,0:T(8,128)(2,1)S(1)}, bf16[256,512]{1,0:T(8,128)(2,1)S(1)}, u32[]{:S(2)}, u32[]{:S(2)}) collective-permute-start(bf16[256,512]{1,0:T(8,128)(2,1)S(1)} %get-tuple-element.208.refs_2_), channel_id=1, source_target_pairs={{0,1},{1,0},{2,3},{3,2},{4,5},{5,4},{6,7},{7,6},{8,9},{9,8},{10,11... | collective-permute-start | bytes 786440 | tf_op jit(solution)/shard_map/ppermute | solution.py:875
  49.6 5.1 %collective-permute-start.10 = (bf16[256,512]{1,0:T(8,128)(2,1)S(1)}, bf16[256,512]{1,0:T(8,128)(2,1)S(1)}, u32[]{:S(2)}, u32[]{:S(2)}) collective-permute-start(bf16[256,512]{1,0:T(8,128)(2,1)S(1)} %get-tuple-element.219.refs_1_), channel_id=1, source_target_pairs={{0,1},{1,0},{2,3},{3,2},{4,5},{5,4},{6,7},{7,6},{8,9},{9,8},{10,11... | collective-permute-start | bytes 786440 | tf_op jit(solution)/shard_map/ppermute | solution.py:875
  51.6 14.4 %collective-permute-start.14 = (bf16[1,512,512]{2,1,0:T(8,128)(2,1)S(1)}, bf16[1,512,512]{2,1,0:T(8,128)(2,1)S(1)}, u32[]{:S(2)}, u32[]{:S(2)}) collective-permute-start(bf16[1,512,512]{2,1,0:T(8,128)(2,1)S(1)} %get-tuple-element.240), channel_id=1, source_target_pairs={{0,2},{1,3},{2,0},{3,1},{4,6},{5,7},{6,4},{7,5},{8,10},{9,11},{10,... | collective-permute-start | bytes 1572872 | tf_op jit(solution)/shard_map/ppermute | solution.py:872
  53.0 2.2 %collective-permute-start.11 = (bf16[256,512]{1,0:T(8,128)(2,1)S(1)}, bf16[256,512]{1,0:T(8,128)(2,1)S(1)}, u32[]{:S(2)}, u32[]{:S(2)}) collective-permute-start(bf16[256,512]{1,0:T(8,128)(2,1)S(1)} %get-tuple-element.220.refs_2_), channel_id=1, source_target_pairs={{0,1},{1,0},{2,3},{3,2},{4,5},{5,4},{6,7},{7,6},{8,9},{9,8},{10,11... | collective-permute-start | bytes 786440 | tf_op jit(solution)/shard_map/ppermute | solution.py:875
  53.3 14.1 %collective-permute-start.15 = (bf16[2,256,512]{2,1,0:T(8,128)(2,1)S(1)}, bf16[2,256,512]{2,1,0:T(8,128)(2,1)S(1)}, u32[]{:S(2)}, u32[]{:S(2)}) collective-permute-start(bf16[2,256,512]{2,1,0:T(8,128)(2,1)S(1)} %get-tuple-element.242), channel_id=1, source_target_pairs={{0,4},{4,0},{8,12},{12,8},{16,20},{20,16},{24,28},{28,24},{1,5},{5... | collective-permute-start | bytes 1572872 | tf_op jit(solution)/shard_map/ppermute | solution.py:878
  54.8 6.6 %collective-permute-start.16 = (bf16[256,512]{1,0:T(8,128)(2,1)S(1)}, bf16[256,512]{1,0:T(8,128)(2,1)S(1)}, u32[]{:S(2)}, u32[]{:S(2)}) collective-permute-start(bf16[256,512]{1,0:T(8,128)(2,1)S(1)} %get-tuple-element.252.refs_14_), channel_id=1, source_target_pairs={{0,1},{1,0},{2,3},{3,2},{4,5},{5,4},{6,7},{7,6},{8,9},{9,8},{10,11... | collective-permute-start | bytes 786440 | tf_op jit(solution)/shard_map/ppermute | solution.py:875
  54.8 7.0 %collective-permute-start.17 = (bf16[256,512]{1,0:T(8,128)(2,1)S(1)}, bf16[256,512]{1,0:T(8,128)(2,1)S(1)}, u32[]{:S(2)}, u32[]{:S(2)}) collective-permute-start(bf16[256,512]{1,0:T(8,128)(2,1)S(1)} %get-tuple-element.253.refs_15_), channel_id=1, source_target_pairs={{0,1},{1,0},{2,3},{3,2},{4,5},{5,4},{6,7},{7,6},{8,9},{9,8},{10,11... | collective-permute-start | bytes 786440 | tf_op jit(solution)/shard_map/ppermute | solution.py:875
  61.2 8.5 %collective-permute-start.12 = (bf16[256,512]{1,0:T(8,128)(2,1)S(1)}, bf16[256,512]{1,0:T(8,128)(2,1)S(1)}, u32[]{:S(2)}, u32[]{:S(2)}) collective-permute-start(bf16[256,512]{1,0:T(8,128)(2,1)S(1)} %get-tuple-element.231.refs_1_), channel_id=1, source_target_pairs={{0,1},{1,0},{2,3},{3,2},{4,5},{5,4},{6,7},{7,6},{8,9},{9,8},{10,11... | collective-permute-start | bytes 786440 | tf_op jit(solution)/shard_map/ppermute | solution.py:875
  61.3 8.9 %collective-permute-start.13 = (bf16[256,512]{1,0:T(8,128)(2,1)S(1)}, bf16[256,512]{1,0:T(8,128)(2,1)S(1)}, u32[]{:S(2)}, u32[]{:S(2)}) collective-permute-start(bf16[256,512]{1,0:T(8,128)(2,1)S(1)} %get-tuple-element.232.refs_2_), channel_id=1, source_target_pairs={{0,1},{1,0},{2,3},{3,2},{4,5},{5,4},{6,7},{7,6},{8,9},{9,8},{10,11... | collective-permute-start | bytes 786440 | tf_op jit(solution)/shard_map/ppermute | solution.py:875
  63.9 11.1 %collective-permute-start.20 = (bf16[256,512]{1,0:T(8,128)(2,1)S(1)}, bf16[256,512]{1,0:T(8,128)(2,1)S(1)}, u32[]{:S(2)}, u32[]{:S(2)}) collective-permute-start(bf16[256,512]{1,0:T(8,128)(2,1)S(1)} %get-tuple-element.270.refs_4_), channel_id=1, source_target_pairs={{0,1},{1,0},{2,3},{3,2},{4,5},{5,4},{6,7},{7,6},{8,9},{9,8},{10,11... | collective-permute-start | bytes 786440 | tf_op jit(solution)/shard_map/ppermute | solution.py:875
  66.0 9.0 %collective-permute-start.21 = (bf16[256,512]{1,0:T(8,128)(2,1)S(1)}, bf16[256,512]{1,0:T(8,128)(2,1)S(1)}, u32[]{:S(2)}, u32[]{:S(2)}) collective-permute-start(bf16[256,512]{1,0:T(8,128)(2,1)S(1)} %get-tuple-element.271.refs_5_), channel_id=1, source_target_pairs={{0,1},{1,0},{2,3},{3,2},{4,5},{5,4},{6,7},{7,6},{8,9},{9,8},{10,11... | collective-permute-start | bytes 786440 | tf_op jit(solution)/shard_map/ppermute | solution.py:875
  68.1 9.3 %collective-permute-start.18 = (bf16[1,256,512]{2,1,0:T(8,128)(2,1)S(1)}, bf16[1,256,512]{2,1,0:T(8,128)(2,1)S(1)}, u32[]{:S(2)}, u32[]{:S(2)}) collective-permute-start(bf16[1,256,512]{2,1,0:T(8,128)(2,1)S(1)} %get-tuple-element.268), channel_id=1, source_target_pairs={{0,4},{4,0},{8,12},{12,8},{16,20},{20,16},{24,28},{28,24},{1,5},{5... | collective-permute-start | bytes 786440 | tf_op jit(solution)/shard_map/ppermute | solution.py:878
  69.7 7.7 %collective-permute-start.19 = (bf16[1,256,512]{2,1,0:T(8,128)(2,1)S(1)}, bf16[1,256,512]{2,1,0:T(8,128)(2,1)S(1)}, u32[]{:S(2)}, u32[]{:S(2)}) collective-permute-start(bf16[1,256,512]{2,1,0:T(8,128)(2,1)S(1)} %get-tuple-element.269), channel_id=1, source_target_pairs={{0,2},{1,3},{2,0},{3,1},{4,6},{5,7},{6,4},{7,5},{8,10},{9,11},{10,... | collective-permute-start | bytes 786440 | tf_op jit(solution)/shard_map/ppermute | solution.py:872
  70.2 17.6 %collective-permute-start.25 = (bf16[2,256,512]{2,1,0:T(8,128)(2,1)S(1)}, bf16[2,256,512]{2,1,0:T(8,128)(2,1)S(1)}, u32[]{:S(2)}, u32[]{:S(2)}) collective-permute-start(bf16[2,256,512]{2,1,0:T(8,128)(2,1)S(1)} %get-tuple-element.288), channel_id=1, source_target_pairs={{0,4},{4,0},{8,12},{12,8},{16,20},{20,16},{24,28},{28,24},{1,5},{5... | collective-permute-start | bytes 1572872 | tf_op jit(solution)/shard_map/ppermute | solution.py:878
  78.1 9.1 %collective-permute-start.26 = (bf16[2,192,512]{2,1,0:T(8,128)(2,1)S(1)}, bf16[2,192,512]{2,1,0:T(8,128)(2,1)S(1)}, u32[]{:S(2)}, u32[]{:S(2)}) collective-permute-start(bf16[2,192,512]{2,1,0:T(8,128)(2,1)S(1)} %get-tuple-element.290), channel_id=1, source_target_pairs={{0,8},{4,12},{8,0},{12,4},{16,24},{20,28},{24,16},{28,20},{1,9},{5... | collective-permute-start | bytes 1179656 | tf_op jit(solution)/shard_map/ppermute | solution.py:878
  79.8 11.5 %collective-permute-start.24 = (bf16[1,512,512]{2,1,0:T(8,128)(2,1)S(1)}, bf16[1,512,512]{2,1,0:T(8,128)(2,1)S(1)}, u32[]{:S(2)}, u32[]{:S(2)}) collective-permute-start(bf16[1,512,512]{2,1,0:T(8,128)(2,1)S(1)} %get-tuple-element.286), channel_id=1, source_target_pairs={{0,2},{1,3},{2,0},{3,1},{4,6},{5,7},{6,4},{7,5},{8,10},{9,11},{10,... | collective-permute-start | bytes 1572872 | tf_op jit(solution)/shard_map/ppermute | solution.py:872
  84.5 10.1 %collective-permute-start.22 = (bf16[256,512]{1,0:T(8,128)(2,1)S(1)}, bf16[256,512]{1,0:T(8,128)(2,1)S(1)}, u32[]{:S(2)}, u32[]{:S(2)}) collective-permute-start(bf16[256,512]{1,0:T(8,128)(2,1)S(1)} %get-tuple-element.274.refs_1_), channel_id=1, source_target_pairs={{0,1},{1,0},{2,3},{3,2},{4,5},{5,4},{6,7},{7,6},{8,9},{9,8},{10,11... | collective-permute-start | bytes 786440 | tf_op jit(solution)/shard_map/ppermute | solution.py:875
  84.6 10.9 %collective-permute-start.23 = (bf16[256,512]{1,0:T(8,128)(2,1)S(1)}, bf16[256,512]{1,0:T(8,128)(2,1)S(1)}, u32[]{:S(2)}, u32[]{:S(2)}) collective-permute-start(bf16[256,512]{1,0:T(8,128)(2,1)S(1)} %get-tuple-element.275.refs_2_), channel_id=1, source_target_pairs={{0,1},{1,0},{2,3},{3,2},{4,5},{5,4},{6,7},{7,6},{8,9},{9,8},{10,11... | collective-permute-start | bytes 786440 | tf_op jit(solution)/shard_map/ppermute | solution.py:875
  88.5 10.0 %collective-permute-start.28 = (bf16[2,128,512]{2,1,0:T(8,128)(2,1)S(1)}, bf16[2,128,512]{2,1,0:T(8,128)(2,1)S(1)}, u32[]{:S(2)}, u32[]{:S(2)}) collective-permute-start(bf16[2,128,512]{2,1,0:T(8,128)(2,1)S(1)} %get-tuple-element.300), channel_id=1, source_target_pairs={{0,8},{4,12},{8,0},{12,4},{16,24},{20,28},{24,16},{28,20},{1,9},{5... | collective-permute-start | bytes 786440 | tf_op jit(solution)/shard_map/ppermute | solution.py:878
  90.2 7.1 %collective-permute-start.29 = (bf16[1,128,512]{2,1,0:T(8,128)(2,1)S(1)}, bf16[1,128,512]{2,1,0:T(8,128)(2,1)S(1)}, u32[]{:S(2)}, u32[]{:S(2)}) collective-permute-start(bf16[1,128,512]{2,1,0:T(8,128)(2,1)S(1)} %get-tuple-element.303), channel_id=1, source_target_pairs={{0,4},{4,0},{8,12},{12,8},{16,20},{20,16},{24,28},{28,24},{1,5},{5... | collective-permute-start | bytes 393224 | tf_op jit(solution)/shard_map/ppermute | solution.py:878
  91.3 12.4 %collective-permute-start.31 = (bf16[2,128,512]{2,1,0:T(8,128)(2,1)S(1)}, bf16[2,128,512]{2,1,0:T(8,128)(2,1)S(1)}, u32[]{:S(2)}, u32[]{:S(2)}) collective-permute-start(bf16[2,128,512]{2,1,0:T(8,128)(2,1)S(1)} %get-tuple-element.307.refs_0_), channel_id=1, source_target_pairs={{0,16},{4,20},{8,24},{12,28},{16,0},{20,4},{24,8},{28,12},{1,17},{... | collective-permute-start | bytes 786440 | tf_op jit(solution)/shard_map/ppermute | solution.py:878
  94.6 9.8 %collective-permute-start.27 = (bf16[1,256,512]{2,1,0:T(8,128)(2,1)S(1)}, bf16[1,256,512]{2,1,0:T(8,128)(2,1)S(1)}, u32[]{:S(2)}, u32[]{:S(2)}) collective-permute-start(bf16[1,256,512]{2,1,0:T(8,128)(2,1)S(1)} %get-tuple-element.298), channel_id=1, source_target_pairs={{0,4},{4,0},{8,12},{12,8},{16,20},{20,16},{24,28},{28,24},{1,5},{5... | collective-permute-start | bytes 786440 | tf_op jit(solution)/shard_map/ppermute | solution.py:878
  99.2 6.7 %collective-permute-start.30 = (bf16[1,144,512]{2,1,0:T(8,128)(2,1)S(1)}, bf16[1,144,512]{2,1,0:T(8,128)(2,1)S(1)}, u32[]{:S(2)}, u32[]{:S(2)}) collective-permute-start(bf16[1,144,512]{2,1,0:T(8,128)(2,1)S(1)} %get-tuple-element.306), channel_id=1, source_target_pairs={{0,2},{1,3},{2,0},{3,1},{4,6},{5,7},{6,4},{7,5},{8,10},{9,11},{10,... | collective-permute-start | bytes 442376 | tf_op jit(solution)/shard_map/ppermute | solution.py:872
  106.5 23.6 %collective-permute-start.32 = (bf16[1024,512]{1,0:T(8,128)(2,1)S(1)}, bf16[1024,512]{1,0:T(8,128)(2,1)S(1)}, u32[]{:S(2)}, u32[]{:S(2)}) collective-permute-start(bf16[1024,512]{1,0:T(8,128)(2,1)S(1)} %get-tuple-element.311.refs_0_), channel_id=1, source_target_pairs={{0,2},{1,3},{2,0},{3,1},{4,6},{5,7},{6,4},{7,5},{8,10},{9,11},{10,... | collective-permute-start | bytes 3145736 | tf_op jit(solution)/shard_map/ppermute | solution.py:872
  108.0 7.0 %collective-permute-start.34 = (bf16[2,128,512]{2,1,0:T(8,128)(2,1)S(1)}, bf16[2,128,512]{2,1,0:T(8,128)(2,1)S(1)}, u32[]{:S(2)}, u32[]{:S(2)}) collective-permute-start(bf16[2,128,512]{2,1,0:T(8,128)(2,1)S(1)} %get-tuple-element.315.refs_4_), channel_id=1, source_target_pairs={{0,4},{4,0},{8,12},{12,8},{16,20},{20,16},{24,28},{28,24},{1,5},{5... | collective-permute-start | bytes 786440 | tf_op jit(solution)/shard_map/ppermute | solution.py:878
  110.6 6.4 %collective-permute-start.33 = (bf16[1,128,512]{2,1,0:T(8,128)(2,1)S(1)}, bf16[1,128,512]{2,1,0:T(8,128)(2,1)S(1)}, u32[]{:S(2)}, u32[]{:S(2)}) collective-permute-start(bf16[1,128,512]{2,1,0:T(8,128)(2,1)S(1)} %get-tuple-element.313), channel_id=1, source_target_pairs={{0,8},{4,12},{8,0},{12,4},{16,24},{20,28},{24,16},{28,20},{1,9},{5... | collective-permute-start | bytes 393224 | tf_op jit(solution)/shard_map/ppermute | solution.py:878
  110.6 6.4 %collective-permute-start.35 = (bf16[1,128,512]{2,1,0:T(8,128)(2,1)S(1)}, bf16[1,128,512]{2,1,0:T(8,128)(2,1)S(1)}, u32[]{:S(2)}, u32[]{:S(2)}) collective-permute-start(bf16[1,128,512]{2,1,0:T(8,128)(2,1)S(1)} %get-tuple-element.310.refs_6_), channel_id=1, source_target_pairs={{0,16},{4,20},{8,24},{12,28},{16,0},{20,4},{24,8},{28,12},{1,17},{... | collective-permute-start | bytes 393224 | tf_op jit(solution)/shard_map/ppermute | solution.py:878
  117.6 9.1 %collective-permute-start.36 = (bf16[1,144,512]{2,1,0:T(8,128)(2,1)S(1)}, bf16[1,144,512]{2,1,0:T(8,128)(2,1)S(1)}, u32[]{:S(2)}, u32[]{:S(2)}) collective-permute-start(bf16[1,144,512]{2,1,0:T(8,128)(2,1)S(1)} %get-tuple-element.317.refs_0_), channel_id=1, source_target_pairs={{0,16},{4,20},{8,24},{12,28},{16,0},{20,4},{24,8},{28,12},{1,17},{... | collective-permute-start | bytes 442376 | tf_op jit(solution)/shard_map/ppermute | solution.py:878
  119.4 7.3 %collective-permute-start.37 = (bf16[1,128,512]{2,1,0:T(8,128)(2,1)S(1)}, bf16[1,128,512]{2,1,0:T(8,128)(2,1)S(1)}, u32[]{:S(2)}, u32[]{:S(2)}) collective-permute-start(bf16[1,128,512]{2,1,0:T(8,128)(2,1)S(1)} %get-tuple-element.318.refs_2_), channel_id=1, source_target_pairs={{0,8},{4,12},{8,0},{12,4},{16,24},{20,28},{24,16},{28,20},{1,9},{5... | collective-permute-start | bytes 393224 | tf_op jit(solution)/shard_map/ppermute | solution.py:878
  120.6 18.0 %collective-permute-start.42 = (bf16[2,256,512]{2,1,0:T(8,128)(2,1)S(1)}, bf16[2,256,512]{2,1,0:T(8,128)(2,1)S(1)}, u32[]{:S(2)}, u32[]{:S(2)}) collective-permute-start(bf16[2,256,512]{2,1,0:T(8,128)(2,1)S(1)} %get-tuple-element.330.refs_0_), channel_id=1, source_target_pairs={{0,8},{4,12},{8,0},{12,4},{16,24},{20,28},{24,16},{28,20},{1,9},{5... | collective-permute-start | bytes 1572872 | tf_op jit(solution)/shard_map/ppermute | solution.py:878
  127.3 6.6 %collective-permute-start.38 = (bf16[1,144,512]{2,1,0:T(8,128)(2,1)S(1)}, bf16[1,144,512]{2,1,0:T(8,128)(2,1)S(1)}, u32[]{:S(2)}, u32[]{:S(2)}) collective-permute-start(bf16[1,144,512]{2,1,0:T(8,128)(2,1)S(1)} %get-tuple-element.323.refs_0_), channel_id=1, source_target_pairs={{0,4},{4,0},{8,12},{12,8},{16,20},{20,16},{24,28},{28,24},{1,5},{5... | collective-permute-start | bytes 442376 | tf_op jit(solution)/shard_map/ppermute | solution.py:878
  128.9 5.0 %collective-permute-start.39 = (bf16[1,128,512]{2,1,0:T(8,128)(2,1)S(1)}, bf16[1,128,512]{2,1,0:T(8,128)(2,1)S(1)}, u32[]{:S(2)}, u32[]{:S(2)}) collective-permute-start(bf16[1,128,512]{2,1,0:T(8,128)(2,1)S(1)} %get-tuple-element.325), channel_id=1, source_target_pairs={{0,2},{1,3},{2,0},{3,1},{4,6},{5,7},{6,4},{7,5},{8,10},{9,11},{10,... | collective-permute-start | bytes 393224 | tf_op jit(solution)/shard_map/ppermute | solution.py:872
  129.7 8.2 %collective-permute-start.43 = (bf16[1,288,512]{2,1,0:T(8,128)(2,1)S(1)}, bf16[1,288,512]{2,1,0:T(8,128)(2,1)S(1)}, u32[]{:S(2)}, u32[]{:S(2)}) collective-permute-start(bf16[1,288,512]{2,1,0:T(8,128)(2,1)S(1)} %get-tuple-element.331.refs_2_), channel_id=1, source_target_pairs={{0,4},{4,0},{8,12},{12,8},{16,20},{20,16},{24,28},{28,24},{1,5},{5... | collective-permute-start | bytes 884744 | tf_op jit(solution)/shard_map/ppermute | solution.py:878
  134.5 8.5 %collective-permute-start.41 = (bf16[1,272,512]{2,1,0:T(8,128)(2,1)S(1)}, bf16[1,272,512]{2,1,0:T(8,128)(2,1)S(1)}, u32[]{:S(2)}, u32[]{:S(2)}) collective-permute-start(bf16[1,272,512]{2,1,0:T(8,128)(2,1)S(1)} %get-tuple-element.329.refs_2_), channel_id=1, source_target_pairs={{0,8},{4,12},{8,0},{12,4},{16,24},{20,28},{24,16},{28,20},{1,9},{5... | collective-permute-start | bytes 835592 | tf_op jit(solution)/shard_map/ppermute | solution.py:878
  135.5 6.0 %collective-permute-start.40 = (bf16[1,128,512]{2,1,0:T(8,128)(2,1)S(1)}, bf16[1,128,512]{2,1,0:T(8,128)(2,1)S(1)}, u32[]{:S(2)}, u32[]{:S(2)}) collective-permute-start(bf16[1,128,512]{2,1,0:T(8,128)(2,1)S(1)} %get-tuple-element.328), channel_id=1, source_target_pairs={{0,16},{4,20},{8,24},{12,28},{16,0},{20,4},{24,8},{28,12},{1,17},{... | collective-permute-start | bytes 393224 | tf_op jit(solution)/shard_map/ppermute | solution.py:878
  (2 other events, 11.7 us)

commit v6 on v5

--- a/solution.py
+++ b/solution.py
@@ -1221,6 +1221,8 @@
             blocks, ("dp", "mp"), split_axis=0, concat_axis=0, tiled=True, axis_index_groups=same_seat
         ).astype(F32)
     advance("self_cross_4", by_self, by_cross)
+    if by_ffn.ready():
+        by_ffn.got = swap(later(by_ffn.chunk, by_cross.chunk), by_ffn.halved[0])
 
     mixed, grad_inputs = run(
         place_rows_kernel,

time: 146 us -> 148 us (1.014)
  transfers between devices with their start and end apart: 45 -> 45, of which waited for: 21 -> 21; matrix products, arithmetic and copies ran while one was open for 0% -> 0% of each run, Pallas kernels for 37% -> 36%
where the time goes in v6:
time: 148 us; the launch traced here: 147 us
  Pallas kernels  59.2 us (40%)
  starting transfers between devices  51 us (34%)
  waiting for transfers between devices  34.8 us (24%)
    pallas_call x29, Pallas kernels, __call__(): pl.pallas_call(body, in_specs=[words] + specs + after_specs, out_specs=[f...  59.2 us
    ppermute x19, starting transfers between devices, data_swap(): return lax.ppermute(value, 'dp', [(i, i ^ 1 << k) for i in range(dp)])  28.2 us
    ppermute x19, waiting for transfers between devices, data_swap(): return lax.ppermute(value, 'dp', [(i, i ^ 1 << k) for i in range(dp)])  25.3 us
    ppermute x11, starting transfers between devices, other(): return lax.ppermute(value, 'mp', across)  13.4 us
    ppermute x11, waiting for transfers between devices, other(): return lax.ppermute(value, 'mp', across)  7.88 us
    all_to_all x1, starting transfers between devices, shards(): lax.all_to_all(memory_part, 'dp', split_axis=0, concat_axis=0, tiled=True)  6.27 us
    ppermute x14, starting transfers between devices, seat_swap(): return lax.ppermute(value, 'mp', [(i, i ^ step) for i in range(mp)])  3.23 us
  transfers between devices with their start and end apart: 45, of which 21 were waited for; matrix products, arithmetic and copies ran while one was open for 0% of the time, Pallas kernels for 36%

profile of v6, /device:TPU:0, one launch (start us, length us, event | category | flops | bytes accessed | tf_op | source)
XLA Modules:
  0.0 147.3 jit_solution(2537517894087104597)
XLA Ops:
  0.6 3.0 %collective-permute-start = (bf16[3,512,128]{2,1,0:T(8,128)(2,1)}, bf16[3,512,128]{2,1,0:T(8,128)(2,1)S(1)}, u32[]{:S(2)}, u32[]{:S(2)}) collective-permute-start(bf16[3,512,128]{2,1,0:T(8,128)(2,1)} %refs_0_.3), channel_id=1, source_target_pairs={{0,2},{1,3},{2,0},{3,1},{4,6},{5,7},{6,4},{7,5},{8,10},{9,11},{10,... | collective-permute-start | bytes 1179656 | tf_op jit(solution)/shard_map/ppermute | solution.py:872
  3.8 3.5 %setup.1 = (bf16[1024,128]{1,0:T(8,128)(2,1)}, bf16[2,512,512]{2,1,0:T(8,128)(2,1)S(1)}, bf16[2,512,128]{2,1,0:T(8,128)(2,1)S(1)}, bf16[512,512]{1,0:T(8,128)(2,...) custom-call(s32[6]{0:T(128)S(1)} %stack.27.where_ref, ...), custom_call_target="tpu_custom_call" | custom-call | flops 1000000 | bytes 300000 | tf_op jit(solution)/shard_map/setup/pallas_call | solution.py:146
  8.3 6.3 %all-to-all-start = ((bf16[8,64,512]{2,1,0:T(8,128)(2,1)}), bf16[8,64,512]{2,1,0:T(8,128)(2,1)S(1)}, u32[]{:S(2)}, u32[]{:S(2)}) async-start(bf16[8,64,512]{2,1,0:T(8,128)(2,1)} %get-tuple-element.192), calls=%async_computation | async-start | bytes 1048576 | tf_op jit(solution)/shard_map/all_to_all | solution.py:929
  14.5 1.6 %collective-permute-start.2 = (bf16[128,512]{1,0:T(8,128)(2,1)S(1)}, bf16[128,512]{1,0:T(8,128)(2,1)S(1)}, u32[]{:S(2)}, u32[]{:S(2)}) collective-permute-start(bf16[128,512]{1,0:T(8,128)(2,1)S(1)} %copy-done.1), channel_id=1, source_target_pairs={{0,2},{1,3},{2,0},{3,1},{4,6},{5,7},{6,4},{7,5},{8,10},{9,11},{10,... | collective-permute-start | bytes 393224 | tf_op jit(solution)/shard_map/ppermute | solution.py:872
  16.7 3.1 %self_forward_0.1 = (bf16[512,512]{1,0:T(8,128)(2,1)S(1)}, bf16[512,128]{1,0:T(8,128)(2,1)}, bf16[512,128]{1,0:T(8,128)(2,1)}, bf16[512,128]{1,0:T(8,128)(2,1)},...) custom-call(s32[6]{0:T(128)S(1)} %stack.27.where_ref, ...), custom_call_target="tpu_custom_call" | custom-call | flops 1000000 | bytes 300000 | tf_op jit(solution)/shard_map/self_forward_0/pallas_call | solution.py:146
  19.8 1.7 %collective-permute-done.1.refs_4_.refs_3_.refs_5_ = bf16[8,128]{1,0:T(8,128)(2,1)S(1)} collective-permute-done((bf16[8,128]{1,0:T(8,128)(2,1)S(1)}, bf16[8,128]{1,0:T(8,128)(2,1)S(1)}, u32[]{:S(2)}, u32[]{:S(2)}) %collective-permute-start.1) | collective-permute-done | bytes 2080 | tf_op jit(solution)/shard_map/ppermute | solution.py:872
  21.5 1.8 %collective-permute-start.9 = (bf16[2,512,512]{2,1,0:T(8,128)(2,1)}, bf16[2,512,512]{2,1,0:T(8,128)(2,1)}, u32[]{:S(2)}, u32[]{:S(2)}) collective-permute-start(bf16[2,512,512]{2,1,0:T(8,128)(2,1)} %copy-done), channel_id=1, source_target_pairs={{0,2},{1,3},{2,0},{3,1},{4,6},{5,7},{6,4},{7,5},{8,10},{9,11},{10,... | collective-permute-start | bytes 3145736 | tf_op jit(solution)/shard_map/ppermute | solution.py:872
  23.3 2.9 %self_forward_1.1 = (bf16[512,128]{1,0:T(8,128)(2,1)}, bf16[512,128]{1,0:T(8,128)(2,1)}, bf16[512,128]{1,0:T(8,128)(2,1)}, bf16[512,128]{1,0:T(8,128)(2,1)S(1)},...) custom-call(s32[6]{0:T(128)S(1)} %stack.27.where_ref, ...), custom_call_target="tpu_custom_call" | custom-call | flops 1000000 | bytes 300000 | tf_op jit(solution)/shard_map/self_forward_1/pallas_call | solution.py:146
  26.8 1.5 %collective-permute-start.6 = (bf16[1024,128]{1,0:T(8,128)(2,1)S(1)}, bf16[1024,128]{1,0:T(8,128)(2,1)}, u32[]{:S(2)}, u32[]{:S(2)}) collective-permute-start(bf16[1024,128]{1,0:T(8,128)(2,1)S(1)} %collective-permute-done.5.refs_0_), channel_id=1, source_target_pairs={{0,4},{4,0},{8,12},{12,8},{16,20},{20,16},{24,28},{28,24},{1,5},{5... | collective-permute-start | bytes 786440 | tf_op jit(solution)/shard_map/ppermute | solution.py:878
  29.5 3.6 %cross_forward_0.1 = (f32[512,512]{1,0:T(8,128)S(1)}, bf16[512,512]{1,0:T(8,128)(2,1)S(1)}, bf16[512,128]{1,0:T(8,128)(2,1)S(1)}, bf16[512,128]{1,0:T(8,128)(2,1...) custom-call(s32[6]{0:T(128)S(1)} %stack.27.where_ref, bf16[512,512]{1,0:T(8,128)(2,1)S(1)} %get-tuple-element.183.refs_0_, ...), custom_call_target="tpu_custom_call" | custom-call | flops 1000000 | bytes 300000 | tf_op jit(solution)/shard_map/cross_forward_0/pallas_call | solution.py:146
  33.1 2.1 %collective-permute-done.6.refs_1_ = bf16[1024,128]{1,0:T(8,128)(2,1)} collective-permute-done((bf16[1024,128]{1,0:T(8,128)(2,1)S(1)}, bf16[1024,128]{1,0:T(8,128)(2,1)}, u32[]{:S(2)}, u32[]{:S(2)}) %collective-permute-start.6) | collective-permute-done | bytes 262176 | tf_op jit(solution)/shard_map/ppermute | solution.py:878
  35.2 1.4 memory_1.1
  36.6 2.5 %cross_forward_1.1 = (bf16[512,128]{1,0:T(8,128)(2,1)S(1)}, bf16[512,128]{1,0:T(8,128)(2,1)S(1)}, f32[2,512]{1,0:T(2,128)S(1)}, bf16[256,512]{1,0:T(8,128)(2,1)S...) custom-call(s32[6]{0:T(128)S(1)} %stack.27.where_ref, bf16[512,512]{1,0:T(8,128)(2,1)S(1)} %get-tuple-element.199.refs_0_.refs_10_, ...), custom_call_target="tpu_custom_call" | custom-call | flops 1000000 | bytes 300000 | tf_op jit(solution)/shard_map/cross_forward_1/pallas_call | solution.py:146
  41.1 4.3 %ffn_0.1 = (f32[512,512]{1,0:T(8,128)S(1)}, bf16[512,512]{1,0:T(8,128)(2,1)S(1)}, bf16[512,512]{1,0:T(8,128)(2,1)S(1)}, bf16[512,512]{1,0:T(8,128)(2,1)S(1)}, bf...) custom-call(s32[6]{0:T(128)S(1)} %stack.27.where_ref, ...), custom_call_target="tpu_custom_call" | custom-call | flops 1000000 | bytes 300000 | tf_op jit(solution)/shard_map/ffn_0/pallas_call | solution.py:146
  46.2 3.4 %ffn_1.2 = (bf16[512,512]{1,0:T(8,128)(2,1)S(1)}, bf16[512,512]{1,0:T(8,128)(2,1)S(1)}, bf16[256,512]{1,0:T(8,128)(2,1)S(1)}, bf16[256,512]{1,0:T(8,128)(2,1)S(1...) custom-call(s32[6]{0:T(128)S(1)} %stack.27.where_ref, ...), custom_call_target="tpu_custom_call" | custom-call | flops 1000000 | bytes 300000 | tf_op jit(solution)/shard_map/ffn_1/pallas_call | solution.py:146
  49.7 1.8 %ffn_weights.1 = (f32[2,512]{1,0:T(2,128)S(1)}, f32[1,512,512]{2,1,0:T(8,128)S(1)}, bf16[1,512,512]{2,1,0:T(8,128)(2,1)S(1)}, f32[2,256,512]{2,1,0:T(8,128)S(1)}...) custom-call(s32[6]{0:T(128)S(1)} %stack.27.where_ref, bf16[512,512]{1,0:T(8,128)(2,1)S(1)} %get-tuple-element.226.refs_0_, ...), custom_call_target="tpu_custom_call" | custom-call | flops 1000000 | bytes 300000 | tf_op jit(solution)/shard_map/ffn_weights/pallas_call | solution.py:146
  51.6 1.5 %collective-permute-start.14 = (bf16[1,512,512]{2,1,0:T(8,128)(2,1)S(1)}, bf16[1,512,512]{2,1,0:T(8,128)(2,1)S(1)}, u32[]{:S(2)}, u32[]{:S(2)}) collective-permute-start(bf16[1,512,512]{2,1,0:T(8,128)(2,1)S(1)} %get-tuple-element.241), channel_id=1, source_target_pairs={{0,2},{1,3},{2,0},{3,1},{4,6},{5,7},{6,4},{7,5},{8,10},{9,11},{10,... | collective-permute-start | bytes 1572872 | tf_op jit(solution)/shard_map/ppermute | solution.py:872
  53.3 1.5 %collective-permute-start.15 = (bf16[2,256,512]{2,1,0:T(8,128)(2,1)S(1)}, bf16[2,256,512]{2,1,0:T(8,128)(2,1)S(1)}, u32[]{:S(2)}, u32[]{:S(2)}) collective-permute-start(bf16[2,256,512]{2,1,0:T(8,128)(2,1)S(1)} %get-tuple-element.243), channel_id=1, source_target_pairs={{0,4},{4,0},{8,12},{12,8},{16,20},{20,16},{24,28},{28,24},{1,5},{5... | collective-permute-start | bytes 1572872 | tf_op jit(solution)/shard_map/ppermute | solution.py:878
  55.3 5.9 %cross_backward.1 = (f32[512,512]{1,0:T(8,128)S(1)}, bf16[512,512]{1,0:T(8,128)(2,1)S(1)}, bf16[512,128]{1,0:T(8,128)(2,1)S(1)}, bf16[512,128]{1,0:T(8,128)(2,1)...) custom-call(s32[6]{0:T(128)S(1)} %stack.27.where_ref, ...), custom_call_target="tpu_custom_call" | custom-call | flops 1000000 | bytes 300000 | tf_op jit(solution)/shard_map/cross_backward/pallas_call | solution.py:146
  61.8 2.0 %cross_weights.1 = (f32[2,256,512]{2,1,0:T(8,128)S(1)}, bf16[2,256,512]{2,1,0:T(8,128)(2,1)S(1)}, bf16[256,512]{1,0:T(8,128)(2,1)S(1)}, bf16[256,512]{1,0:T(8,12...) custom-call(s32[6]{0:T(128)S(1)} %stack.27.where_ref, bf16[512,128]{1,0:T(8,128)(2,1)S(1)} %get-tuple-element.244.refs_0_, ...), custom_call_target="tpu_custom_call" | custom-call | flops 1000000 | bytes 300000 | tf_op jit(solution)/shard_map/cross_weights/pallas_call | solution.py:146
  64.0 1.9 %collective-permute-done.14.refs_1_ = bf16[1,512,512]{2,1,0:T(8,128)(2,1)S(1)} collective-permute-done((bf16[1,512,512]{2,1,0:T(8,128)(2,1)S(1)}, bf16[1,512,512]{2,1,0:T(8,128)(2,1)S(1)}, u32[]{:S(2)}, u32[]{:S(2)}) %collective-permute-start.14) | collective-permute-done | bytes 524320 | tf_op jit(solution)/shard_map/ppermute | solution.py:872
  66.0 1.4 collective-permute-done.15.refs_3_
  68.1 1.6 %collective-permute-start.18 = (bf16[1,256,512]{2,1,0:T(8,128)(2,1)S(1)}, bf16[1,256,512]{2,1,0:T(8,128)(2,1)S(1)}, u32[]{:S(2)}, u32[]{:S(2)}) collective-permute-start(bf16[1,256,512]{2,1,0:T(8,128)(2,1)S(1)} %get-tuple-element.269), channel_id=1, source_target_pairs={{0,4},{4,0},{8,12},{12,8},{16,20},{20,16},{24,28},{28,24},{1,5},{5... | collective-permute-start | bytes 786440 | tf_op jit(solution)/shard_map/ppermute | solution.py:878
  70.8 4.1 %self_backward.1 = (f32[512,512]{1,0:T(8,128)S(1)}, bf16[512,512]{1,0:T(8,128)(2,1)S(1)}, bf16[512,128]{1,0:T(8,128)(2,1)S(1)}, bf16[512,128]{1,0:T(8,128)(2,1)S...) custom-call(s32[6]{0:T(128)S(1)} %stack.27.where_ref, ...), custom_call_target="tpu_custom_call" | custom-call | flops 1000000 | bytes 300000 | tf_op jit(solution)/shard_map/self_backward/pallas_call | solution.py:146
  75.0 2.5 %collective-permute-done.18.refs_2_ = bf16[1,256,512]{2,1,0:T(8,128)(2,1)S(1)} collective-permute-done((bf16[1,256,512]{2,1,0:T(8,128)(2,1)S(1)}, bf16[1,256,512]{2,1,0:T(8,128)(2,1)S(1)}, u32[]{:S(2)}, u32[]{:S(2)}) %collective-permute-start.18) | collective-permute-done | bytes 262176 | tf_op jit(solution)/shard_map/ppermute | solution.py:878
  78.1 1.6 %collective-permute-start.26 = (bf16[2,192,512]{2,1,0:T(8,128)(2,1)S(1)}, bf16[2,192,512]{2,1,0:T(8,128)(2,1)S(1)}, u32[]{:S(2)}, u32[]{:S(2)}) collective-permute-start(bf16[2,192,512]{2,1,0:T(8,128)(2,1)S(1)} %get-tuple-element.291), channel_id=1, source_target_pairs={{0,8},{4,12},{8,0},{12,4},{16,24},{20,28},{24,16},{28,20},{1,9},{5... | collective-permute-start | bytes 1179656 | tf_op jit(solution)/shard_map/ppermute | solution.py:878
  80.5 4.0 %self_backward_rest.1 = (f32[2,128]{1,0:T(2,128)S(1)}, f32[1,512,512]{2,1,0:T(8,128)S(1)}, bf16[256,512]{1,0:T(8,128)(2,1)S(1)}, bf16[256,512]{1,0:T(8,128)(2,1)S(1)}, f32[8,128]{1,0:T(8,128)}) custom-call(s32[6]{0:T(128)S(1)} %stack.27.where_ref, bf16[3,512,128]{2,1,0:T(8,128)(2,1)} %refs_0_.3, ...), custom_call_target="tpu_custom_call" | custom-call | flops 1000000 | bytes 300000 | tf_op jit(solution)/shard_map/self_backward_rest/pallas_call | solution.py:146
  85.1 2.1 %collective-permute-done.26.refs_1_.refs_3_ = bf16[2,192,512]{2,1,0:T(8,128)(2,1)S(1)} collective-permute-done((bf16[2,192,512]{2,1,0:T(8,128)(2,1)S(1)}, bf16[2,192,512]{2,1,0:T(8,128)(2,1)S(1)}, u32[]{:S(2)}, u32[]{:S(2)}) %collective-permute-start.26) | collective-permute-done | bytes 393248 | tf_op jit(solution)/shard_map/ppermute | solution.py:878
  88.5 1.6 %collective-permute-start.28 = (bf16[2,128,512]{2,1,0:T(8,128)(2,1)S(1)}, bf16[2,128,512]{2,1,0:T(8,128)(2,1)S(1)}, u32[]{:S(2)}, u32[]{:S(2)}) collective-permute-start(bf16[2,128,512]{2,1,0:T(8,128)(2,1)S(1)} %get-tuple-element.301), channel_id=1, source_target_pairs={{0,8},{4,12},{8,0},{12,4},{16,24},{20,28},{24,16},{28,20},{1,9},{5... | collective-permute-start | bytes 786440 | tf_op jit(solution)/shard_map/ppermute | solution.py:878
  91.3 2.6 %collective-permute-start.31 = (bf16[2,128,512]{2,1,0:T(8,128)(2,1)S(1)}, bf16[2,128,512]{2,1,0:T(8,128)(2,1)S(1)}, u32[]{:S(2)}, u32[]{:S(2)}) collective-permute-start(bf16[2,128,512]{2,1,0:T(8,128)(2,1)S(1)} %get-tuple-element.308.refs_0_), channel_id=1, source_target_pairs={{0,16},{4,20},{8,24},{12,28},{16,0},{20,4},{24,8},{28,12},{1,17},{... | collective-permute-start | bytes 786440 | tf_op jit(solution)/shard_map/ppermute | solution.py:878
  95.5 1.7 %input_backward.1 = (bf16[1024,512]{1,0:T(8,128)(2,1)S(1)}, bf16[16,512]{1,0:T(8,128)(2,1)S(1)}, bf16[16,512]{1,0:T(8,128)(2,1)S(1)}, f32[8,128]{1,0:T(8,128)}) custom-call(s32[6]{0:T(128)S(1)} %stack.27.where_ref, bf16[512,512]{1,0:T(8,128)(2,1)S(1)} %get-tuple-element.183.refs_0_, bf16[256,512]{1,0:T(8,128)(2,1)S(1)} %get-tuple-element.275.refs_1_, ...), custom_call_target="tpu_custom_call" | custom-call | flops 1000000 | bytes 300000 | tf_op jit(solution)/shard_map/input_backward/pallas_call | solution.py:146
  99.2 1.5 collective-permute-start.30
  100.6 3.1 %collective-permute-done.31.refs_1_ = bf16[2,128,512]{2,1,0:T(8,128)(2,1)S(1)} collective-permute-done((bf16[2,128,512]{2,1,0:T(8,128)(2,1)S(1)}, bf16[2,128,512]{2,1,0:T(8,128)(2,1)S(1)}, u32[]{:S(2)}, u32[]{:S(2)}) %collective-permute-start.31) | collective-permute-done | bytes 262176 | tf_op jit(solution)/shard_map/ppermute | solution.py:878
  104.4 1.5 %collective-permute-done.30.refs_3_ = bf16[1,144,512]{2,1,0:T(8,128)(2,1)S(1)} collective-permute-done((bf16[1,144,512]{2,1,0:T(8,128)(2,1)S(1)}, bf16[1,144,512]{2,1,0:T(8,128)(2,1)S(1)}, u32[]{:S(2)}, u32[]{:S(2)}) %collective-permute-start.30) | collective-permute-done | bytes 147488 | tf_op jit(solution)/shard_map/ppermute | solution.py:872
  106.5 1.4 collective-permute-start.32
  108.0 2.6 %collective-permute-start.34 = (bf16[2,128,512]{2,1,0:T(8,128)(2,1)S(1)}, bf16[2,128,512]{2,1,0:T(8,128)(2,1)S(1)}, u32[]{:S(2)}, u32[]{:S(2)}) collective-permute-start(bf16[2,128,512]{2,1,0:T(8,128)(2,1)S(1)} %get-tuple-element.316.refs_4_), channel_id=1, source_target_pairs={{0,4},{4,0},{8,12},{12,8},{16,20},{20,16},{24,28},{28,24},{1,5},{5... | collective-permute-start | bytes 786440 | tf_op jit(solution)/shard_map/ppermute | solution.py:878
  110.6 1.9 %collective-permute-start.35 = (bf16[1,128,512]{2,1,0:T(8,128)(2,1)S(1)}, bf16[1,128,512]{2,1,0:T(8,128)(2,1)S(1)}, u32[]{:S(2)}, u32[]{:S(2)}) collective-permute-start(bf16[1,128,512]{2,1,0:T(8,128)(2,1)S(1)} %get-tuple-element.311.refs_6_), channel_id=1, source_target_pairs={{0,16},{4,20},{8,24},{12,28},{16,0},{20,4},{24,8},{28,12},{1,17},{... | collective-permute-start | bytes 393224 | tf_op jit(solution)/shard_map/ppermute | solution.py:878
  112.5 2.4 %collective-permute-done.34.refs_5_ = bf16[2,128,512]{2,1,0:T(8,128)(2,1)S(1)} collective-permute-done((bf16[2,128,512]{2,1,0:T(8,128)(2,1)S(1)}, bf16[2,128,512]{2,1,0:T(8,128)(2,1)S(1)}, u32[]{:S(2)}, u32[]{:S(2)}) %collective-permute-start.34) | collective-permute-done | bytes 262176 | tf_op jit(solution)/shard_map/ppermute | solution.py:878
  114.9 2.0 %collective-permute-done.33.refs_1_ = bf16[1,128,512]{2,1,0:T(8,128)(2,1)S(1)} collective-permute-done((bf16[1,128,512]{2,1,0:T(8,128)(2,1)S(1)}, bf16[1,128,512]{2,1,0:T(8,128)(2,1)S(1)}, u32[]{:S(2)}, u32[]{:S(2)}) %collective-permute-start.33) | collective-permute-done | bytes 131104 | tf_op jit(solution)/shard_map/ppermute | solution.py:878
  117.6 1.8 %collective-permute-start.36 = (bf16[1,144,512]{2,1,0:T(8,128)(2,1)S(1)}, bf16[1,144,512]{2,1,0:T(8,128)(2,1)S(1)}, u32[]{:S(2)}, u32[]{:S(2)}) collective-permute-start(bf16[1,144,512]{2,1,0:T(8,128)(2,1)S(1)} %get-tuple-element.318.refs_0_), channel_id=1, source_target_pairs={{0,16},{4,20},{8,24},{12,28},{16,0},{20,4},{24,8},{28,12},{1,17},{... | collective-permute-start | bytes 442376 | tf_op jit(solution)/shard_map/ppermute | solution.py:878
  120.6 5.5 %collective-permute-done.37.refs_3_ = bf16[1,128,512]{2,1,0:T(8,128)(2,1)S(1)} collective-permute-done((bf16[1,128,512]{2,1,0:T(8,128)(2,1)S(1)}, bf16[1,128,512]{2,1,0:T(8,128)(2,1)S(1)}, u32[]{:S(2)}, u32[]{:S(2)}) %collective-permute-start.37) | collective-permute-done | bytes 131104 | tf_op jit(solution)/shard_map/ppermute | solution.py:878
  126.7 2.2 %collective-permute-start.42 = (bf16[2,256,512]{2,1,0:T(8,128)(2,1)S(1)}, bf16[2,256,512]{2,1,0:T(8,128)(2,1)S(1)}, u32[]{:S(2)}, u32[]{:S(2)}) collective-permute-start(bf16[2,256,512]{2,1,0:T(8,128)(2,1)S(1)} %get-tuple-element.333.refs_0_), channel_id=1, source_target_pairs={{0,8},{4,12},{8,0},{12,4},{16,24},{20,28},{24,16},{28,20},{1,9},{5... | collective-permute-start | bytes 1572872 | tf_op jit(solution)/shard_map/ppermute | solution.py:878
  128.8 2.0 %collective-permute-start.38 = (bf16[1,144,512]{2,1,0:T(8,128)(2,1)S(1)}, bf16[1,144,512]{2,1,0:T(8,128)(2,1)S(1)}, u32[]{:S(2)}, u32[]{:S(2)}) collective-permute-start(bf16[1,144,512]{2,1,0:T(8,128)(2,1)S(1)} %get-tuple-element.324.refs_0_), channel_id=1, source_target_pairs={{0,4},{4,0},{8,12},{12,8},{16,20},{20,16},{24,28},{28,24},{1,5},{5... | collective-permute-start | bytes 442376 | tf_op jit(solution)/shard_map/ppermute | solution.py:878
  132.1 2.3 %place_rows.1 = (bf16[2,512,512]{2,1,0:T(8,128)(2,1)}, f32[2,512,512]{2,1,0:T(8,128)}, f32[8,128]{1,0:T(8,128)}) custom-call(s32[6]{0:T(128)S(1)} %stack.27.where_ref, bf16[1024,512]{1,0:T(8,128)(2,1)S(1)} %get-tuple-element.312.refs_0_, bf16[1024,512]{1,0:T(8,128)(2,1)S(1)} %collective-permute-done.32.refs_1_, f32[8,128]{1,0:T(8,128)} %get-tuple-element.321.refs_2_), custom_call_target="tpu_custom_call" | custom-call | flops 1000000 | bytes 300000 | tf_op jit(solution)/shard_map/place_rows/pallas_call | solution.py:146
  134.4 1.5 collective-permute-done.39.refs_3_
  136.6 3.0 %collective-permute-start.40 = (bf16[1,128,512]{2,1,0:T(8,128)(2,1)S(1)}, bf16[1,128,512]{2,1,0:T(8,128)(2,1)S(1)}, u32[]{:S(2)}, u32[]{:S(2)}) collective-permute-start(bf16[1,128,512]{2,1,0:T(8,128)(2,1)S(1)} %get-tuple-element.329), channel_id=1, source_target_pairs={{0,16},{4,20},{8,24},{12,28},{16,0},{20,4},{24,8},{28,12},{1,17},{... | collective-permute-start | bytes 393224 | tf_op jit(solution)/shard_map/ppermute | solution.py:878
  140.7 2.7 %ffn_and_cross_grads.1 = (f32[512,512]{1,0:T(8,128)}, f32[512,512]{1,0:T(8,128)}, f32[512,128]{1,0:T(8,128)}, f32[2,512,128]{2,1,0:T(8,128)}, f32[128,512]{1,0:T(8,128)}, /*index=5*/f32[8,128]{1,0:T(8,128)}) custom-call(s32[6]{0:T(128)S(1)} %stack.27.where_ref, bf16[2,256,512]{2,1,0:T(8,128)(2,1)S(1)} %get-tuple-element.333.refs_0_, ...), custom_call_target="tpu_custom_call" | custom-call | flops 1000000 | bytes 300000 | tf_op jit(solution)/shard_map/ffn_and_cross_grads/pallas_call | solution.py:146
  145.1 1.9 %last_grads.1 = (f32[16,64,128]{2,1,0:T(8,128)}, f32[3,512,128]{2,1,0:T(8,128)}, f32[128,512]{1,0:T(8,128)}, f32[3,512]{1,0:T(4,128)}, f32[3,512]{1,0:T(4,128)},...) custom-call(s32[6]{0:T(128)S(1)} %stack.27.where_ref, ...), custom_call_target="tpu_custom_call" | custom-call | flops 1000000 | bytes 300000 | tf_op jit(solution)/shard_map/last_grads/pallas_call | solution.py:146
  (83 shorter events, 26.1 us)
Async XLA Ops:
  0.6 20.8 %collective-permute-start = (bf16[3,512,128]{2,1,0:T(8,128)(2,1)}, bf16[3,512,128]{2,1,0:T(8,128)(2,1)S(1)}, u32[]{:S(2)}, u32[]{:S(2)}) collective-permute-start(bf16[3,512,128]{2,1,0:T(8,128)(2,1)} %refs_0_.3), channel_id=1, source_target_pairs={{0,2},{1,3},{2,0},{3,1},{4,6},{5,7},{6,4},{7,5},{8,10},{9,11},{10,... | collective-permute-start | bytes 1179656 | tf_op jit(solution)/shard_map/ppermute | solution.py:872
  3.8 12.4 %copy-start.2 = (bf16[512]{0:T(512)(128)(2,1)S(1)}, bf16[512]{0:T(512)(128)(2,1)}, u32[]{:S(2)}) copy-start(bf16[512]{0:T(512)(128)(2,1)} %param.36) | copy-start | bytes 3076
  3.8 12.4 %copy-start.3 = (bf16[2,128]{1,0:T(2,128)(2,1)S(1)}, bf16[2,128]{1,0:T(2,128)(2,1)}, u32[]{:S(2)}) copy-start(bf16[2,128]{1,0:T(2,128)(2,1)} %param.33) | copy-start | bytes 1540
  3.8 12.4 %copy-start.4 = (bf16[2,128]{1,0:T(2,128)(2,1)S(1)}, bf16[2,128]{1,0:T(2,128)(2,1)}, u32[]{:S(2)}) copy-start(bf16[2,128]{1,0:T(2,128)(2,1)} %param.29) | copy-start | bytes 1540
  8.2 13.3 %collective-permute-start.5 = (bf16[1024,128]{1,0:T(8,128)(2,1)}, bf16[1024,128]{1,0:T(8,128)(2,1)S(1)}, u32[]{:S(2)}, u32[]{:S(2)}) collective-permute-start(bf16[1024,128]{1,0:T(8,128)(2,1)} %get-tuple-element.200), channel_id=1, source_target_pairs={{0,2},{1,3},{2,0},{3,1},{4,6},{5,7},{6,4},{7,5},{8,10},{9,11},{10,... | collective-permute-start | bytes 786440 | tf_op jit(solution)/shard_map/ppermute | solution.py:872
  8.3 20.2 %all-to-all-start = ((bf16[8,64,512]{2,1,0:T(8,128)(2,1)}), bf16[8,64,512]{2,1,0:T(8,128)(2,1)S(1)}, u32[]{:S(2)}, u32[]{:S(2)}) async-start(bf16[8,64,512]{2,1,0:T(8,128)(2,1)} %get-tuple-element.192), calls=%async_computation | async-start | bytes 1048576 | tf_op jit(solution)/shard_map/all_to_all | solution.py:929
  14.5 6.9 %collective-permute-start.2 = (bf16[128,512]{1,0:T(8,128)(2,1)S(1)}, bf16[128,512]{1,0:T(8,128)(2,1)S(1)}, u32[]{:S(2)}, u32[]{:S(2)}) collective-permute-start(bf16[128,512]{1,0:T(8,128)(2,1)S(1)} %copy-done.1), channel_id=1, source_target_pairs={{0,2},{1,3},{2,0},{3,1},{4,6},{5,7},{6,4},{7,5},{8,10},{9,11},{10,... | collective-permute-start | bytes 393224 | tf_op jit(solution)/shard_map/ppermute | solution.py:872
  16.1 5.3 %collective-permute-start.1 = (bf16[8,128]{1,0:T(8,128)(2,1)S(1)}, bf16[8,128]{1,0:T(8,128)(2,1)S(1)}, u32[]{:S(2)}, u32[]{:S(2)}) collective-permute-start(bf16[8,128]{1,0:T(8,128)(2,1)S(1)} %pad_maximum_fusion.refs_4_.refs_2_.refs_8_), channel_id=1, source_target_pairs={{0,2},{1,3},{2,0},{3,1},{4,6},{5,7},{6,4},{7,5},{8,10},{9,11},{10,... | collective-permute-start | bytes 6152 | tf_op jit(solution)/shard_map/ppermute | solution.py:872
  21.5 24.7 %collective-permute-start.9 = (bf16[2,512,512]{2,1,0:T(8,128)(2,1)}, bf16[2,512,512]{2,1,0:T(8,128)(2,1)}, u32[]{:S(2)}, u32[]{:S(2)}) collective-permute-start(bf16[2,512,512]{2,1,0:T(8,128)(2,1)} %copy-done), channel_id=1, source_target_pairs={{0,2},{1,3},{2,0},{3,1},{4,6},{5,7},{6,4},{7,5},{8,10},{9,11},{10,... | collective-permute-start | bytes 3145736 | tf_op jit(solution)/shard_map/ppermute | solution.py:872
  26.2 3.3 %collective-permute-start.3 = (bf16[256,512]{1,0:T(8,128)(2,1)}, bf16[256,512]{1,0:T(8,128)(2,1)}, u32[]{:S(2)}, u32[]{:S(2)}) collective-permute-start(bf16[256,512]{1,0:T(8,128)(2,1)} %get-tuple-element.190.refs_1_), channel_id=1, source_target_pairs={{0,1},{1,0},{2,3},{3,2},{4,5},{5,4},{6,7},{7,6},{8,9},{9,8},{10,11... | collective-permute-start | bytes 786440 | tf_op jit(solution)/shard_map/ppermute | solution.py:875
  26.3 3.2 %collective-permute-start.4 = (bf16[256,512]{1,0:T(8,128)(2,1)}, bf16[256,512]{1,0:T(8,128)(2,1)}, u32[]{:S(2)}, u32[]{:S(2)}) collective-permute-start(bf16[256,512]{1,0:T(8,128)(2,1)} %get-tuple-element.191.refs_2_), channel_id=1, source_target_pairs={{0,1},{1,0},{2,3},{3,2},{4,5},{5,4},{6,7},{7,6},{8,9},{9,8},{10,11... | collective-permute-start | bytes 786440 | tf_op jit(solution)/shard_map/ppermute | solution.py:875
  26.8 8.4 %collective-permute-start.6 = (bf16[1024,128]{1,0:T(8,128)(2,1)S(1)}, bf16[1024,128]{1,0:T(8,128)(2,1)}, u32[]{:S(2)}, u32[]{:S(2)}) collective-permute-start(bf16[1024,128]{1,0:T(8,128)(2,1)S(1)} %collective-permute-done.5.refs_0_), channel_id=1, source_target_pairs={{0,4},{4,0},{8,12},{12,8},{16,20},{20,16},{24,28},{28,24},{1,5},{5... | collective-permute-start | bytes 786440 | tf_op jit(solution)/shard_map/ppermute | solution.py:878
  39.1 1.6 %collective-permute-start.7 = (bf16[256,512]{1,0:T(8,128)(2,1)S(1)}, bf16[256,512]{1,0:T(8,128)(2,1)S(1)}, u32[]{:S(2)}, u32[]{:S(2)}) collective-permute-start(bf16[256,512]{1,0:T(8,128)(2,1)S(1)} %get-tuple-element.208.refs_1_), channel_id=1, source_target_pairs={{0,1},{1,0},{2,3},{3,2},{4,5},{5,4},{6,7},{7,6},{8,9},{9,8},{10,11... | collective-permute-start | bytes 786440 | tf_op jit(solution)/shard_map/ppermute | solution.py:875
  39.2 1.9 %collective-permute-start.8 = (bf16[256,512]{1,0:T(8,128)(2,1)S(1)}, bf16[256,512]{1,0:T(8,128)(2,1)S(1)}, u32[]{:S(2)}, u32[]{:S(2)}) collective-permute-start(bf16[256,512]{1,0:T(8,128)(2,1)S(1)} %get-tuple-element.209.refs_2_), channel_id=1, source_target_pairs={{0,1},{1,0},{2,3},{3,2},{4,5},{5,4},{6,7},{7,6},{8,9},{9,8},{10,11... | collective-permute-start | bytes 786440 | tf_op jit(solution)/shard_map/ppermute | solution.py:875
  49.6 5.1 %collective-permute-start.10 = (bf16[256,512]{1,0:T(8,128)(2,1)S(1)}, bf16[256,512]{1,0:T(8,128)(2,1)S(1)}, u32[]{:S(2)}, u32[]{:S(2)}) collective-permute-start(bf16[256,512]{1,0:T(8,128)(2,1)S(1)} %get-tuple-element.220.refs_1_), channel_id=1, source_target_pairs={{0,1},{1,0},{2,3},{3,2},{4,5},{5,4},{6,7},{7,6},{8,9},{9,8},{10,11... | collective-permute-start | bytes 786440 | tf_op jit(solution)/shard_map/ppermute | solution.py:875
  51.6 14.4 %collective-permute-start.14 = (bf16[1,512,512]{2,1,0:T(8,128)(2,1)S(1)}, bf16[1,512,512]{2,1,0:T(8,128)(2,1)S(1)}, u32[]{:S(2)}, u32[]{:S(2)}) collective-permute-start(bf16[1,512,512]{2,1,0:T(8,128)(2,1)S(1)} %get-tuple-element.241), channel_id=1, source_target_pairs={{0,2},{1,3},{2,0},{3,1},{4,6},{5,7},{6,4},{7,5},{8,10},{9,11},{10,... | collective-permute-start | bytes 1572872 | tf_op jit(solution)/shard_map/ppermute | solution.py:872
  53.0 2.2 %collective-permute-start.11 = (bf16[256,512]{1,0:T(8,128)(2,1)S(1)}, bf16[256,512]{1,0:T(8,128)(2,1)S(1)}, u32[]{:S(2)}, u32[]{:S(2)}) collective-permute-start(bf16[256,512]{1,0:T(8,128)(2,1)S(1)} %get-tuple-element.221.refs_2_), channel_id=1, source_target_pairs={{0,1},{1,0},{2,3},{3,2},{4,5},{5,4},{6,7},{7,6},{8,9},{9,8},{10,11... | collective-permute-start | bytes 786440 | tf_op jit(solution)/shard_map/ppermute | solution.py:875
  53.3 14.1 %collective-permute-start.15 = (bf16[2,256,512]{2,1,0:T(8,128)(2,1)S(1)}, bf16[2,256,512]{2,1,0:T(8,128)(2,1)S(1)}, u32[]{:S(2)}, u32[]{:S(2)}) collective-permute-start(bf16[2,256,512]{2,1,0:T(8,128)(2,1)S(1)} %get-tuple-element.243), channel_id=1, source_target_pairs={{0,4},{4,0},{8,12},{12,8},{16,20},{20,16},{24,28},{28,24},{1,5},{5... | collective-permute-start | bytes 1572872 | tf_op jit(solution)/shard_map/ppermute | solution.py:878
  54.8 6.6 %collective-permute-start.16 = (bf16[256,512]{1,0:T(8,128)(2,1)S(1)}, bf16[256,512]{1,0:T(8,128)(2,1)S(1)}, u32[]{:S(2)}, u32[]{:S(2)}) collective-permute-start(bf16[256,512]{1,0:T(8,128)(2,1)S(1)} %get-tuple-element.253.refs_14_), channel_id=1, source_target_pairs={{0,1},{1,0},{2,3},{3,2},{4,5},{5,4},{6,7},{7,6},{8,9},{9,8},{10,11... | collective-permute-start | bytes 786440 | tf_op jit(solution)/shard_map/ppermute | solution.py:875
  54.8 7.0 %collective-permute-start.17 = (bf16[256,512]{1,0:T(8,128)(2,1)S(1)}, bf16[256,512]{1,0:T(8,128)(2,1)S(1)}, u32[]{:S(2)}, u32[]{:S(2)}) collective-permute-start(bf16[256,512]{1,0:T(8,128)(2,1)S(1)} %get-tuple-element.254.refs_15_), channel_id=1, source_target_pairs={{0,1},{1,0},{2,3},{3,2},{4,5},{5,4},{6,7},{7,6},{8,9},{9,8},{10,11... | collective-permute-start | bytes 786440 | tf_op jit(solution)/shard_map/ppermute | solution.py:875
  61.2 8.5 %collective-permute-start.12 = (bf16[256,512]{1,0:T(8,128)(2,1)S(1)}, bf16[256,512]{1,0:T(8,128)(2,1)S(1)}, u32[]{:S(2)}, u32[]{:S(2)}) collective-permute-start(bf16[256,512]{1,0:T(8,128)(2,1)S(1)} %get-tuple-element.232.refs_1_), channel_id=1, source_target_pairs={{0,1},{1,0},{2,3},{3,2},{4,5},{5,4},{6,7},{7,6},{8,9},{9,8},{10,11... | collective-permute-start | bytes 786440 | tf_op jit(solution)/shard_map/ppermute | solution.py:875
  61.3 8.9 %collective-permute-start.13 = (bf16[256,512]{1,0:T(8,128)(2,1)S(1)}, bf16[256,512]{1,0:T(8,128)(2,1)S(1)}, u32[]{:S(2)}, u32[]{:S(2)}) collective-permute-start(bf16[256,512]{1,0:T(8,128)(2,1)S(1)} %get-tuple-element.233.refs_2_), channel_id=1, source_target_pairs={{0,1},{1,0},{2,3},{3,2},{4,5},{5,4},{6,7},{7,6},{8,9},{9,8},{10,11... | collective-permute-start | bytes 786440 | tf_op jit(solution)/shard_map/ppermute | solution.py:875
  63.9 11.1 %collective-permute-start.20 = (bf16[256,512]{1,0:T(8,128)(2,1)S(1)}, bf16[256,512]{1,0:T(8,128)(2,1)S(1)}, u32[]{:S(2)}, u32[]{:S(2)}) collective-permute-start(bf16[256,512]{1,0:T(8,128)(2,1)S(1)} %get-tuple-element.271.refs_4_), channel_id=1, source_target_pairs={{0,1},{1,0},{2,3},{3,2},{4,5},{5,4},{6,7},{7,6},{8,9},{9,8},{10,11... | collective-permute-start | bytes 786440 | tf_op jit(solution)/shard_map/ppermute | solution.py:875
  66.0 9.0 %collective-permute-start.21 = (bf16[256,512]{1,0:T(8,128)(2,1)S(1)}, bf16[256,512]{1,0:T(8,128)(2,1)S(1)}, u32[]{:S(2)}, u32[]{:S(2)}) collective-permute-start(bf16[256,512]{1,0:T(8,128)(2,1)S(1)} %get-tuple-element.272.refs_5_), channel_id=1, source_target_pairs={{0,1},{1,0},{2,3},{3,2},{4,5},{5,4},{6,7},{7,6},{8,9},{9,8},{10,11... | collective-permute-start | bytes 786440 | tf_op jit(solution)/shard_map/ppermute | solution.py:875
  68.1 9.3 %collective-permute-start.18 = (bf16[1,256,512]{2,1,0:T(8,128)(2,1)S(1)}, bf16[1,256,512]{2,1,0:T(8,128)(2,1)S(1)}, u32[]{:S(2)}, u32[]{:S(2)}) collective-permute-start(bf16[1,256,512]{2,1,0:T(8,128)(2,1)S(1)} %get-tuple-element.269), channel_id=1, source_target_pairs={{0,4},{4,0},{8,12},{12,8},{16,20},{20,16},{24,28},{28,24},{1,5},{5... | collective-permute-start | bytes 786440 | tf_op jit(solution)/shard_map/ppermute | solution.py:878
  69.7 7.7 %collective-permute-start.19 = (bf16[1,256,512]{2,1,0:T(8,128)(2,1)S(1)}, bf16[1,256,512]{2,1,0:T(8,128)(2,1)S(1)}, u32[]{:S(2)}, u32[]{:S(2)}) collective-permute-start(bf16[1,256,512]{2,1,0:T(8,128)(2,1)S(1)} %get-tuple-element.270), channel_id=1, source_target_pairs={{0,2},{1,3},{2,0},{3,1},{4,6},{5,7},{6,4},{7,5},{8,10},{9,11},{10,... | collective-permute-start | bytes 786440 | tf_op jit(solution)/shard_map/ppermute | solution.py:872
  70.2 17.6 %collective-permute-start.25 = (bf16[2,256,512]{2,1,0:T(8,128)(2,1)S(1)}, bf16[2,256,512]{2,1,0:T(8,128)(2,1)S(1)}, u32[]{:S(2)}, u32[]{:S(2)}) collective-permute-start(bf16[2,256,512]{2,1,0:T(8,128)(2,1)S(1)} %get-tuple-element.289), channel_id=1, source_target_pairs={{0,4},{4,0},{8,12},{12,8},{16,20},{20,16},{24,28},{28,24},{1,5},{5... | collective-permute-start | bytes 1572872 | tf_op jit(solution)/shard_map/ppermute | solution.py:878
  78.1 9.1 %collective-permute-start.26 = (bf16[2,192,512]{2,1,0:T(8,128)(2,1)S(1)}, bf16[2,192,512]{2,1,0:T(8,128)(2,1)S(1)}, u32[]{:S(2)}, u32[]{:S(2)}) collective-permute-start(bf16[2,192,512]{2,1,0:T(8,128)(2,1)S(1)} %get-tuple-element.291), channel_id=1, source_target_pairs={{0,8},{4,12},{8,0},{12,4},{16,24},{20,28},{24,16},{28,20},{1,9},{5... | collective-permute-start | bytes 1179656 | tf_op jit(solution)/shard_map/ppermute | solution.py:878
  79.8 11.5 %collective-permute-start.24 = (bf16[1,512,512]{2,1,0:T(8,128)(2,1)S(1)}, bf16[1,512,512]{2,1,0:T(8,128)(2,1)S(1)}, u32[]{:S(2)}, u32[]{:S(2)}) collective-permute-start(bf16[1,512,512]{2,1,0:T(8,128)(2,1)S(1)} %get-tuple-element.287), channel_id=1, source_target_pairs={{0,2},{1,3},{2,0},{3,1},{4,6},{5,7},{6,4},{7,5},{8,10},{9,11},{10,... | collective-permute-start | bytes 1572872 | tf_op jit(solution)/shard_map/ppermute | solution.py:872
  84.5 10.1 %collective-permute-start.22 = (bf16[256,512]{1,0:T(8,128)(2,1)S(1)}, bf16[256,512]{1,0:T(8,128)(2,1)S(1)}, u32[]{:S(2)}, u32[]{:S(2)}) collective-permute-start(bf16[256,512]{1,0:T(8,128)(2,1)S(1)} %get-tuple-element.275.refs_1_), channel_id=1, source_target_pairs={{0,1},{1,0},{2,3},{3,2},{4,5},{5,4},{6,7},{7,6},{8,9},{9,8},{10,11... | collective-permute-start | bytes 786440 | tf_op jit(solution)/shard_map/ppermute | solution.py:875
  84.6 10.9 %collective-permute-start.23 = (bf16[256,512]{1,0:T(8,128)(2,1)S(1)}, bf16[256,512]{1,0:T(8,128)(2,1)S(1)}, u32[]{:S(2)}, u32[]{:S(2)}) collective-permute-start(bf16[256,512]{1,0:T(8,128)(2,1)S(1)} %get-tuple-element.276.refs_2_), channel_id=1, source_target_pairs={{0,1},{1,0},{2,3},{3,2},{4,5},{5,4},{6,7},{7,6},{8,9},{9,8},{10,11... | collective-permute-start | bytes 786440 | tf_op jit(solution)/shard_map/ppermute | solution.py:875
  88.5 10.0 %collective-permute-start.28 = (bf16[2,128,512]{2,1,0:T(8,128)(2,1)S(1)}, bf16[2,128,512]{2,1,0:T(8,128)(2,1)S(1)}, u32[]{:S(2)}, u32[]{:S(2)}) collective-permute-start(bf16[2,128,512]{2,1,0:T(8,128)(2,1)S(1)} %get-tuple-element.301), channel_id=1, source_target_pairs={{0,8},{4,12},{8,0},{12,4},{16,24},{20,28},{24,16},{28,20},{1,9},{5... | collective-permute-start | bytes 786440 | tf_op jit(solution)/shard_map/ppermute | solution.py:878
  90.2 7.1 %collective-permute-start.29 = (bf16[1,128,512]{2,1,0:T(8,128)(2,1)S(1)}, bf16[1,128,512]{2,1,0:T(8,128)(2,1)S(1)}, u32[]{:S(2)}, u32[]{:S(2)}) collective-permute-start(bf16[1,128,512]{2,1,0:T(8,128)(2,1)S(1)} %get-tuple-element.304), channel_id=1, source_target_pairs={{0,4},{4,0},{8,12},{12,8},{16,20},{20,16},{24,28},{28,24},{1,5},{5... | collective-permute-start | bytes 393224 | tf_op jit(solution)/shard_map/ppermute | solution.py:878
  91.3 12.4 %collective-permute-start.31 = (bf16[2,128,512]{2,1,0:T(8,128)(2,1)S(1)}, bf16[2,128,512]{2,1,0:T(8,128)(2,1)S(1)}, u32[]{:S(2)}, u32[]{:S(2)}) collective-permute-start(bf16[2,128,512]{2,1,0:T(8,128)(2,1)S(1)} %get-tuple-element.308.refs_0_), channel_id=1, source_target_pairs={{0,16},{4,20},{8,24},{12,28},{16,0},{20,4},{24,8},{28,12},{1,17},{... | collective-permute-start | bytes 786440 | tf_op jit(solution)/shard_map/ppermute | solution.py:878
  94.6 9.8 %collective-permute-start.27 = (bf16[1,256,512]{2,1,0:T(8,128)(2,1)S(1)}, bf16[1,256,512]{2,1,0:T(8,128)(2,1)S(1)}, u32[]{:S(2)}, u32[]{:S(2)}) collective-permute-start(bf16[1,256,512]{2,1,0:T(8,128)(2,1)S(1)} %get-tuple-element.299), channel_id=1, source_target_pairs={{0,4},{4,0},{8,12},{12,8},{16,20},{20,16},{24,28},{28,24},{1,5},{5... | collective-permute-start | bytes 786440 | tf_op jit(solution)/shard_map/ppermute | solution.py:878
  99.2 6.7 %collective-permute-start.30 = (bf16[1,144,512]{2,1,0:T(8,128)(2,1)S(1)}, bf16[1,144,512]{2,1,0:T(8,128)(2,1)S(1)}, u32[]{:S(2)}, u32[]{:S(2)}) collective-permute-start(bf16[1,144,512]{2,1,0:T(8,128)(2,1)S(1)} %get-tuple-element.307), channel_id=1, source_target_pairs={{0,2},{1,3},{2,0},{3,1},{4,6},{5,7},{6,4},{7,5},{8,10},{9,11},{10,... | collective-permute-start | bytes 442376 | tf_op jit(solution)/shard_map/ppermute | solution.py:872
  106.5 25.5 %collective-permute-start.32 = (bf16[1024,512]{1,0:T(8,128)(2,1)S(1)}, bf16[1024,512]{1,0:T(8,128)(2,1)S(1)}, u32[]{:S(2)}, u32[]{:S(2)}) collective-permute-start(bf16[1024,512]{1,0:T(8,128)(2,1)S(1)} %get-tuple-element.312.refs_0_), channel_id=1, source_target_pairs={{0,2},{1,3},{2,0},{3,1},{4,6},{5,7},{6,4},{7,5},{8,10},{9,11},{10,... | collective-permute-start | bytes 3145736 | tf_op jit(solution)/shard_map/ppermute | solution.py:872
  108.0 7.0 %collective-permute-start.34 = (bf16[2,128,512]{2,1,0:T(8,128)(2,1)S(1)}, bf16[2,128,512]{2,1,0:T(8,128)(2,1)S(1)}, u32[]{:S(2)}, u32[]{:S(2)}) collective-permute-start(bf16[2,128,512]{2,1,0:T(8,128)(2,1)S(1)} %get-tuple-element.316.refs_4_), channel_id=1, source_target_pairs={{0,4},{4,0},{8,12},{12,8},{16,20},{20,16},{24,28},{28,24},{1,5},{5... | collective-permute-start | bytes 786440 | tf_op jit(solution)/shard_map/ppermute | solution.py:878
  110.6 6.4 %collective-permute-start.33 = (bf16[1,128,512]{2,1,0:T(8,128)(2,1)S(1)}, bf16[1,128,512]{2,1,0:T(8,128)(2,1)S(1)}, u32[]{:S(2)}, u32[]{:S(2)}) collective-permute-start(bf16[1,128,512]{2,1,0:T(8,128)(2,1)S(1)} %get-tuple-element.314), channel_id=1, source_target_pairs={{0,8},{4,12},{8,0},{12,4},{16,24},{20,28},{24,16},{28,20},{1,9},{5... | collective-permute-start | bytes 393224 | tf_op jit(solution)/shard_map/ppermute | solution.py:878
  110.6 6.4 %collective-permute-start.35 = (bf16[1,128,512]{2,1,0:T(8,128)(2,1)S(1)}, bf16[1,128,512]{2,1,0:T(8,128)(2,1)S(1)}, u32[]{:S(2)}, u32[]{:S(2)}) collective-permute-start(bf16[1,128,512]{2,1,0:T(8,128)(2,1)S(1)} %get-tuple-element.311.refs_6_), channel_id=1, source_target_pairs={{0,16},{4,20},{8,24},{12,28},{16,0},{20,4},{24,8},{28,12},{1,17},{... | collective-permute-start | bytes 393224 | tf_op jit(solution)/shard_map/ppermute | solution.py:878
  117.6 8.5 %collective-permute-start.36 = (bf16[1,144,512]{2,1,0:T(8,128)(2,1)S(1)}, bf16[1,144,512]{2,1,0:T(8,128)(2,1)S(1)}, u32[]{:S(2)}, u32[]{:S(2)}) collective-permute-start(bf16[1,144,512]{2,1,0:T(8,128)(2,1)S(1)} %get-tuple-element.318.refs_0_), channel_id=1, source_target_pairs={{0,16},{4,20},{8,24},{12,28},{16,0},{20,4},{24,8},{28,12},{1,17},{... | collective-permute-start | bytes 442376 | tf_op jit(solution)/shard_map/ppermute | solution.py:878
  119.4 6.6 %collective-permute-start.37 = (bf16[1,128,512]{2,1,0:T(8,128)(2,1)S(1)}, bf16[1,128,512]{2,1,0:T(8,128)(2,1)S(1)}, u32[]{:S(2)}, u32[]{:S(2)}) collective-permute-start(bf16[1,128,512]{2,1,0:T(8,128)(2,1)S(1)} %get-tuple-element.319.refs_2_), channel_id=1, source_target_pairs={{0,8},{4,12},{8,0},{12,4},{16,24},{20,28},{24,16},{28,20},{1,9},{5... | collective-permute-start | bytes 393224 | tf_op jit(solution)/shard_map/ppermute | solution.py:878
  126.7 14.1 %collective-permute-start.42 = (bf16[2,256,512]{2,1,0:T(8,128)(2,1)S(1)}, bf16[2,256,512]{2,1,0:T(8,128)(2,1)S(1)}, u32[]{:S(2)}, u32[]{:S(2)}) collective-permute-start(bf16[2,256,512]{2,1,0:T(8,128)(2,1)S(1)} %get-tuple-element.333.refs_0_), channel_id=1, source_target_pairs={{0,8},{4,12},{8,0},{12,4},{16,24},{20,28},{24,16},{28,20},{1,9},{5... | collective-permute-start | bytes 1572872 | tf_op jit(solution)/shard_map/ppermute | solution.py:878
  128.8 7.0 %collective-permute-start.38 = (bf16[1,144,512]{2,1,0:T(8,128)(2,1)S(1)}, bf16[1,144,512]{2,1,0:T(8,128)(2,1)S(1)}, u32[]{:S(2)}, u32[]{:S(2)}) collective-permute-start(bf16[1,144,512]{2,1,0:T(8,128)(2,1)S(1)} %get-tuple-element.324.refs_0_), channel_id=1, source_target_pairs={{0,4},{4,0},{8,12},{12,8},{16,20},{20,16},{24,28},{28,24},{1,5},{5... | collective-permute-start | bytes 442376 | tf_op jit(solution)/shard_map/ppermute | solution.py:878
  130.9 5.0 %collective-permute-start.39 = (bf16[1,128,512]{2,1,0:T(8,128)(2,1)S(1)}, bf16[1,128,512]{2,1,0:T(8,128)(2,1)S(1)}, u32[]{:S(2)}, u32[]{:S(2)}) collective-permute-start(bf16[1,128,512]{2,1,0:T(8,128)(2,1)S(1)} %get-tuple-element.326), channel_id=1, source_target_pairs={{0,2},{1,3},{2,0},{3,1},{4,6},{5,7},{6,4},{7,5},{8,10},{9,11},{10,... | collective-permute-start | bytes 393224 | tf_op jit(solution)/shard_map/ppermute | solution.py:872
  131.6 8.0 %collective-permute-start.43 = (bf16[1,288,512]{2,1,0:T(8,128)(2,1)S(1)}, bf16[1,288,512]{2,1,0:T(8,128)(2,1)S(1)}, u32[]{:S(2)}, u32[]{:S(2)}) collective-permute-start(bf16[1,288,512]{2,1,0:T(8,128)(2,1)S(1)} %get-tuple-element.332.refs_2_), channel_id=1, source_target_pairs={{0,4},{4,0},{8,12},{12,8},{16,20},{20,16},{24,28},{28,24},{1,5},{5... | collective-permute-start | bytes 884744 | tf_op jit(solution)/shard_map/ppermute | solution.py:878
  136.4 8.7 %collective-permute-start.41 = (bf16[1,272,512]{2,1,0:T(8,128)(2,1)S(1)}, bf16[1,272,512]{2,1,0:T(8,128)(2,1)S(1)}, u32[]{:S(2)}, u32[]{:S(2)}) collective-permute-start(bf16[1,272,512]{2,1,0:T(8,128)(2,1)S(1)} %get-tuple-element.330.refs_2_), channel_id=1, source_target_pairs={{0,8},{4,12},{8,0},{12,4},{16,24},{20,28},{24,16},{28,20},{1,9},{5... | collective-permute-start | bytes 835592 | tf_op jit(solution)/shard_map/ppermute | solution.py:878
  136.6 7.3 %collective-permute-start.40 = (bf16[1,128,512]{2,1,0:T(8,128)(2,1)S(1)}, bf16[1,128,512]{2,1,0:T(8,128)(2,1)S(1)}, u32[]{:S(2)}, u32[]{:S(2)}) collective-permute-start(bf16[1,128,512]{2,1,0:T(8,128)(2,1)S(1)} %get-tuple-element.329), channel_id=1, source_target_pairs={{0,16},{4,20},{8,24},{12,28},{16,0},{20,4},{24,8},{28,12},{1,17},{... | collective-permute-start | bytes 393224 | tf_op jit(solution)/shard_map/ppermute | solution.py:878
  (2 other events, 11.7 us)
